TPU v7x, 32 devices: a whole 2x2x4 slice. The times are simulated.
32 devices in a mesh: dp: 4 (over y, x), mp: 8 (over z, core).
Axes of the slice: x: 2, y: 2, z: 4, core: 2. Of those that a mesh axis runs over, the one named last changes fastest.
Arguments:
- inputs: bfloat16 [2, 10240, 2048], P(None, ('dp', 'mp')), may hold values from -6 to 6
- cotangent: bfloat16 [2, 10240, 2048], P(None, ('dp', 'mp')), may hold values from -6 to 6
- short_lengths: int32 [4, 4], P('dp'), may hold values from 1 to 1024, 2560 in all within a row
- long_lengths: int32 [4, 2], P('dp'), may hold values from 1 to 2048, 2560 in all within a row
- norm1_gain: float32 [2048], replicated, may hold values from 0.5 to 1.5
- norm1_bias: float32 [2048], replicated, may hold values from -3 to 3
- query_weight: bfloat16 [2048, 512], P(None, 'mp'), may hold values from -0.125 to 0.125
- key_weight: bfloat16 [2048, 512], P(None, 'mp'), may hold values from -0.125 to 0.125
- value_weight: bfloat16 [2048, 512], P(None, 'mp'), may hold values from -0.125 to 0.125
- query_kernel: float32 [3, 512], P(None, 'mp'), may hold values from -3 to 3
- key_kernel: float32 [3, 512], P(None, 'mp'), may hold values from -3 to 3
- value_kernel: float32 [3, 512], P(None, 'mp'), may hold values from -3 to 3
- out_weight: bfloat16 [512, 2048], P('mp'), may hold values from -2 to 2
- norm2_gain: float32 [2048], replicated, may hold values from 0.5 to 1.5
- norm2_bias: float32 [2048], replicated, may hold values from -3 to 3
- up_weight: bfloat16 [2048, 8192], P(None, 'mp'), may hold values from -0.125 to 0.125
- down_weight: bfloat16 [8192, 2048], P('mp'), may hold values from -0.0625 to 0.0625
Outputs:
- output: bfloat16 [2, 10240, 2048], P(None, ('dp', 'mp'))
- input_grad: float32 [2, 10240, 2048], P(None, ('dp', 'mp'))
- norm1_gain_grad: float32 [2048], replicated
- norm1_bias_grad: float32 [2048], replicated
- query_weight_grad: float32 [2048, 512], P(None, 'mp')
- key_weight_grad: float32 [2048, 512], P(None, 'mp')
- value_weight_grad: float32 [2048, 512], P(None, 'mp')
- query_kernel_grad: float32 [3, 512], P(None, 'mp')
- key_kernel_grad: float32 [3, 512], P(None, 'mp')
- value_kernel_grad: float32 [3, 512], P(None, 'mp')
- out_weight_grad: float32 [512, 2048], P('mp')
- norm2_gain_grad: float32 [2048], replicated
- norm2_bias_grad: float32 [2048], replicated
- up_weight_grad: float32 [2048, 8192], P(None, 'mp')
- down_weight_grad: float32 [8192, 2048], P('mp')
Inputs may be any that keep to these rules, and one draw needn't show every extreme that they name: `short_lengths`: row g lists, in order, the lengths of the documents packed into data group g's short buffer of 2560 tokens; each row sums to 2560 and its largest entry is 1024. `long_lengths`: row g lists, in order, the lengths of the documents packed into data group g's long buffer of 2560 tokens; each row sums to 2560 and its entries are at most 2048.
All inputs are finite; a program needn't handle non-finite values.
Results may differ from a plain program's by a relative error of at most 0.019.
Values may be sent and summed in bfloat16 or wider, within the bound.
A program may use at most 384 MiB of HBM per device.

v0:
```python
from functools import partial

import jax
import jax.numpy as jnp
from jax import lax
from jax.sharding import PartitionSpec as P

HD = 64


def layer_norm(rows, gain, shift):
    row_mean = jnp.mean(rows, axis=-1, keepdims=True)
    centered = rows - row_mean
    variance = jnp.mean(centered * centered, axis=-1, keepdims=True)
    return centered * lax.rsqrt(variance + 1e-05) * gain + shift


def positions(lengths, count):
    ends = jnp.cumsum(lengths)
    places = jnp.arange(count, dtype=jnp.int32)
    passed = (places[:, None] >= ends[None, :]).astype(jnp.int32)
    doc_ids = jnp.sum(passed, axis=1)
    starts = jnp.sum(passed * lengths[None, :], axis=1)
    return (doc_ids, places - starts)


def causal_conv(values, kernel, offsets):
    width = values.shape[1]
    one_back = jnp.concatenate([jnp.zeros((1, width), values.dtype), values[:-1]], axis=0)
    two_back = jnp.concatenate([jnp.zeros((2, width), values.dtype), values[:-2]], axis=0)
    one_back = jnp.where(offsets[:, None] >= 1, one_back, jnp.zeros_like(one_back))
    two_back = jnp.where(offsets[:, None] >= 2, two_back, jnp.zeros_like(two_back))
    return kernel[0] * values + kernel[1] * one_back + kernel[2] * two_back


def block_mask(doc_ids, first, last):
    query_places = first + jnp.arange(last - first, dtype=jnp.int32)
    key_places = jnp.arange(last, dtype=jnp.int32)
    same = doc_ids[first:last][:, None] == doc_ids[:last][None, :]
    return same & (query_places[:, None] >= key_places[None, :])


def block_scores(query, keys, doc_ids, first, last, scale):
    scores = (
        jnp.einsum("qd,kd->qk", query[first:last], keys[:last], preferred_element_type=jnp.float32)
        * scale
    )
    return jnp.where(block_mask(doc_ids, first, last), scores, -1e30)


def attend(query, keys, values, doc_ids, block, scale):
    outputs = []
    totals = []
    for first in range(0, query.shape[0], block):
        last = first + block
        masked = block_scores(query, keys, doc_ids, first, last, scale)
        top = jnp.max(masked, axis=1, keepdims=True)
        powered = jnp.exp(masked - top)
        summed = jnp.sum(powered, axis=1, keepdims=True)
        weights = (powered / summed).astype(jnp.bfloat16)
        outputs.append(jnp.dot(weights, values[:last], preferred_element_type=jnp.float32))
        totals.append(top + jnp.log(summed))
    return (jnp.concatenate(outputs, axis=0), jnp.concatenate(totals, axis=0))


def attend_back(query, keys, values, doc_ids, log_totals, grad_out, block, scale):
    grad_keys = jnp.zeros(keys.shape, jnp.float32)
    grad_values = jnp.zeros(values.shape, jnp.float32)
    grad_query = []
    for first in range(0, query.shape[0], block):
        last = first + block
        masked = block_scores(query, keys, doc_ids, first, last, scale)
        probs = jnp.exp(masked - log_totals[first:last])
        weights = probs.astype(jnp.bfloat16)
        grad_probs = jnp.einsum(
            "qd,kd->qk", grad_out[first:last], values[:last], preferred_element_type=jnp.float32
        )
        inner = jnp.sum(probs * grad_probs, axis=1, keepdims=True)
        grad_scores = (probs * (grad_probs - inner)).astype(jnp.bfloat16)
        grad_query.append(
            jnp.dot(grad_scores, keys[:last], preferred_element_type=jnp.float32) * scale
        )
        grad_keys = grad_keys.at[:last].add(
            jnp.einsum(
                "qk,qd->kd", grad_scores, query[first:last], preferred_element_type=jnp.float32
            )
            * scale
        )
        grad_values = grad_values.at[:last].add(
            jnp.einsum(
                "qk,qd->kd", weights, grad_out[first:last], preferred_element_type=jnp.float32
            )
        )
    return (jnp.concatenate(grad_query, axis=0), grad_keys, grad_values)


def project_rows(left, right):
    return jnp.dot(left, right, preferred_element_type=jnp.float32)


def project_back(left, right):
    return jnp.einsum("gc,dc->gd", left, right, preferred_element_type=jnp.float32)


def fold_rows(right, carry, piece):
    return carry + jnp.einsum("gd,gc->dc", piece, right, preferred_element_type=jnp.float32)


def gather_attention(normed):
    return lax.all_gather(normed, "mp", axis=0, tiled=True)


def gather_feed(second):
    return lax.all_gather(second, "mp", axis=0, tiled=True)


def per_device(
    inputs,
    cotangent,
    short_lengths,
    long_lengths,
    norm1_gain,
    norm1_bias,
    query_weight,
    key_weight,
    value_weight,
    query_kernel,
    key_kernel,
    value_kernel,
    out_weight,
    norm2_gain,
    norm2_bias,
    up_weight,
    down_weight,
):
    row_count = inputs.shape[1]
    group = row_count * lax.axis_size("mp")
    head_width = query_weight.shape[1]
    block = min(512, group)
    scale = HD ** (-0.5)
    joined = jnp.concatenate([query_weight, key_weight, value_weight], axis=1)
    kernels = jnp.concatenate([query_kernel, key_kernel, value_kernel], axis=1)
    layouts = [positions(short_lengths[0], group), positions(long_lengths[0], group)]
    joined_acc = jnp.zeros(joined.shape, jnp.float32)
    kernel_acc = jnp.zeros(kernels.shape, jnp.float32)
    out_acc = jnp.zeros(out_weight.shape, jnp.float32)
    up_acc = jnp.zeros(up_weight.shape, jnp.float32)
    down_acc = jnp.zeros(down_weight.shape, jnp.float32)
    norm_acc = [jnp.zeros(norm1_gain.shape, jnp.float32) for item in range(4)]
    results = []
    input_grads = []
    for index in range(2):
        rows = inputs[index].astype(jnp.float32)
        doc_ids, offsets = layouts[index]
        normed = layer_norm(rows, norm1_gain, norm1_bias).astype(jnp.bfloat16)
        gathered = gather_attention(normed)
        raw = jnp.dot(gathered, joined, preferred_element_type=jnp.float32)
        mixed = causal_conv(raw, kernels, offsets).astype(jnp.bfloat16)
        head = 0
        lower = head * HD
        query = mixed[:, lower : lower + HD]
        keys = mixed[:, head_width + lower : head_width + lower + HD]
        values = mixed[:, 2 * head_width + lower : 2 * head_width + lower + HD]
        attended, log_totals = attend(query, keys, values, doc_ids, block, scale)
        head_totals = [log_totals]
        attended_low = attended.astype(jnp.bfloat16)
        branch = lax.psum_scatter(
            project_rows(attended_low, out_weight), "mp", scatter_dimension=0, tiled=True
        )
        middle = rows + branch
        second = layer_norm(middle, norm2_gain, norm2_bias).astype(jnp.bfloat16)
        grad_rows = cotangent[index]
        gathered_two = gather_feed(second)
        pre = jnp.dot(gathered_two, up_weight, preferred_element_type=jnp.float32)
        hidden = jnp.square(jnp.maximum(pre, 0.0)).astype(jnp.bfloat16)
        feed = lax.psum_scatter(
            project_rows(hidden, down_weight).astype(jnp.bfloat16),
            "mp",
            scatter_dimension=0,
            tiled=True,
        ).astype(jnp.float32)
        results.append((middle + feed).astype(jnp.bfloat16))
        grads_all = lax.all_gather(grad_rows, "mp", axis=0, tiled=True)
        down_acc = down_acc + jnp.einsum(
            "gf,gd->fd", hidden, grads_all, preferred_element_type=jnp.float32
        )
        grad_hidden = jnp.einsum(
            "gd,fd->gf", grads_all, down_weight, preferred_element_type=jnp.float32
        )
        grad_pre = (grad_hidden * 2.0 * jnp.maximum(pre, 0.0)).astype(jnp.bfloat16)
        up_acc = fold_rows(grad_pre, up_acc, lax.all_gather(second, "mp", axis=0, tiled=True))
        grad_second = lax.psum_scatter(
            project_back(grad_pre, up_weight), "mp", scatter_dimension=0, tiled=True
        )
        unused, pull_two = jax.vjp(layer_norm, middle, norm2_gain, norm2_bias)
        grad_middle, grad_gain_two, grad_shift_two = pull_two(grad_second)
        grad_middle = grad_middle + grad_rows.astype(jnp.float32)
        branch_low = grad_middle.astype(jnp.bfloat16)
        branch_all = lax.all_gather(branch_low, "mp", axis=0, tiled=True)
        out_acc = out_acc + jnp.einsum(
            "gh,gd->hd", attended_low, branch_all, preferred_element_type=jnp.float32
        )
        grad_attended = jnp.einsum(
            "gd,hd->gh", branch_all, out_weight, preferred_element_type=jnp.float32
        ).astype(jnp.bfloat16)
        head = 0
        lower = head * HD
        query = mixed[:, lower : lower + HD]
        keys = mixed[:, head_width + lower : head_width + lower + HD]
        values = mixed[:, 2 * head_width + lower : 2 * head_width + lower + HD]
        grad_query, grad_keys, grad_values = attend_back(
            query, keys, values, doc_ids, head_totals[head], grad_attended, block, scale
        )
        query_parts = [grad_query]
        key_parts = [grad_keys]
        value_parts = [grad_values]
        grad_mixed = jnp.concatenate(query_parts + key_parts + value_parts, axis=1)
        unused_conv, pull_conv = jax.vjp(partial(causal_conv, offsets=offsets), raw, kernels)
        grad_raw, grad_kernels = pull_conv(grad_mixed)
        kernel_acc = kernel_acc + grad_kernels
        raw_low = grad_raw.astype(jnp.bfloat16)
        joined_acc = fold_rows(
            raw_low, joined_acc, lax.all_gather(normed, "mp", axis=0, tiled=True)
        )
        grad_normed = lax.psum_scatter(
            project_back(raw_low, joined).astype(jnp.bfloat16),
            "mp",
            scatter_dimension=0,
            tiled=True,
        ).astype(jnp.float32)
        unused_one, pull_one = jax.vjp(layer_norm, rows, norm1_gain, norm1_bias)
        grad_input, grad_gain_one, grad_shift_one = pull_one(grad_normed)
        input_grads.append(grad_middle + grad_input)
        norm_acc = [
            norm_acc[0] + grad_gain_one,
            norm_acc[1] + grad_shift_one,
            norm_acc[2] + grad_gain_two,
            norm_acc[3] + grad_shift_two,
        ]
    summed = (
        lax.psum(joined_acc.astype(jnp.bfloat16), "dp").astype(jnp.float32),
        lax.psum(kernel_acc.astype(jnp.bfloat16), "dp").astype(jnp.float32),
        lax.psum(out_acc.astype(jnp.bfloat16), "dp").astype(jnp.float32),
        lax.psum(up_acc.astype(jnp.bfloat16), "dp").astype(jnp.float32),
        lax.psum(down_acc.astype(jnp.bfloat16), "dp").astype(jnp.float32),
    )
    norm_totals = lax.psum((norm_acc[0], norm_acc[1], norm_acc[2], norm_acc[3]), ("dp", "mp"))
    joined_grad = summed[0]
    kernel_grad = summed[1]
    return (
        jnp.stack(results, axis=0),
        jnp.stack(input_grads, axis=0),
        norm_totals[0],
        norm_totals[1],
        joined_grad[:, :head_width],
        joined_grad[:, head_width : 2 * head_width],
        joined_grad[:, 2 * head_width :],
        kernel_grad[:, :head_width],
        kernel_grad[:, head_width : 2 * head_width],
        kernel_grad[:, 2 * head_width :],
        summed[2],
        norm_totals[2],
        norm_totals[3],
        summed[3],
        summed[4],
    )


def solution(mesh):
    return jax.shard_map(
        per_device,
        mesh=mesh,
        in_specs=(
            P(None, ("dp", "mp"), None),
            P(None, ("dp", "mp"), None),
            P("dp", None),
            P("dp", None),
            P(),
            P(),
            P(None, "mp"),
            P(None, "mp"),
            P(None, "mp"),
            P(None, "mp"),
            P(None, "mp"),
            P(None, "mp"),
            P("mp", None),
            P(),
            P(),
            P(None, "mp"),
            P("mp", None),
        ),
        out_specs=(
            P(None, ("dp", "mp"), None),
            P(None, ("dp", "mp"), None),
            P(),
            P(),
            P(None, "mp"),
            P(None, "mp"),
            P(None, "mp"),
            P(None, "mp"),
            P(None, "mp"),
            P(None, "mp"),
            P("mp", None),
            P(),
            P(),
            P(None, "mp"),
            P("mp", None),
        ),
        check_vma=False,
    )
```

profile of v0, /device:TPU:0, one launch (start us, length us, event | category | flops | bytes accessed | tf_op | source)
XLA Modules:
  0.0 2491.5 jit_solution(12175752411022375073)
XLA Ops:
  19.2 96.9 %all-gather.15.cloned.1.call-done = bf16[2560,2048]{1,0:T(8,128)(2,1)} async-done(((bf16[320,2048]{1,0:T(8,128)(2,1)}), bf16[2560,2048]{1,0:T(8,128)(2,1)}) %all-gather.15.cloned.1.call-update) | async-done | bytes 10485776 | tf_op jit(solution)/shard_map/all_gather | solution.py:110
  116.1 9.0 fusion.286
  125.1 91.0 %all-gather.11.cloned.1.call-done = bf16[2560,2048]{1,0:T(8,128)(2,1)} async-done(((bf16[320,2048]{1,0:T(8,128)(2,1)}), bf16[2560,2048]{1,0:T(8,128)(2,1)}) %all-gather.11.cloned.1.call-update) | async-done | bytes 10485776 | tf_op jit(solution)/shard_map/all_gather | solution.py:110
  216.1 7.8 fusion.283
  242.8 8.6 fusion.287
  265.3 8.7 fusion.284
  274.5 183.1 %reduce-scatter.13.cloned.1.call-done = f32[320,2048]{1,0:T(8,128)} async-done(((f32[2560,2048]{1,0:T(8,128)}), f32[320,2048]{1,0:T(8,128)}) %reduce-scatter.13.cloned.1.call-update) | async-done | bytes 2621456 | tf_op jit(solution)/shard_map/reduce_scatter | solution.py:167
  457.6 208.3 %reduce-scatter.9.cloned.1.call-done = f32[320,2048]{1,0:T(8,128)} async-done(((f32[2560,2048]{1,0:T(8,128)}), f32[320,2048]{1,0:T(8,128)}) %reduce-scatter.9.cloned.1.call-update) | async-done | bytes 2621456 | tf_op jit(solution)/shard_map/reduce_scatter | solution.py:167
  677.2 94.6 %all-gather.17.cloned.1.call-done = bf16[2560,2048]{1,0:T(8,128)(2,1)} async-done(((bf16[320,2048]{1,0:T(8,128)(2,1)}), bf16[2560,2048]{1,0:T(8,128)(2,1)}) %all-gather.17.cloned.1.call-update) | async-done | bytes 10485776 | tf_op jit(solution)/shard_map/all_gather | solution.py:114
  771.8 16.4 fusion.288
  788.2 82.9 %all-gather.25.cloned.1.call-done = bf16[1,2560,2048]{2,1,0:T(8,128)(2,1)} async-done(((bf16[1,320,2048]{2,1,0:T(8,128)(2,1)}), bf16[1,2560,2048]{2,1,0:T(8,128)(2,1)}) %all-gather.25.cloned.1.call-update) | async-done | bytes 10485776 | tf_op jit(solution)/shard_map/all_gather | solution.py:183
  871.1 17.0 multiply_convert_fusion
  890.5 14.4 fusion.290
  905.1 65.5 %all-gather.13.cloned.1.call-done = bf16[2560,2048]{1,0:T(8,128)(2,1)} async-done(((bf16[320,2048]{1,0:T(8,128)(2,1)}), bf16[2560,2048]{1,0:T(8,128)(2,1)}) %all-gather.13.cloned.1.call-update) | async-done | bytes 10485776 | tf_op jit(solution)/shard_map/all_gather | solution.py:114
  970.6 16.4 fusion.285
  987.0 83.1 %all-gather.23.cloned.1.call-done = bf16[1,2560,2048]{2,1,0:T(8,128)(2,1)} async-done(((bf16[1,320,2048]{2,1,0:T(8,128)(2,1)}), bf16[1,2560,2048]{2,1,0:T(8,128)(2,1)}) %all-gather.23.cloned.1.call-update) | async-done | bytes 10485776 | tf_op jit(solution)/shard_map/all_gather | solution.py:183
  1070.0 16.9 multiply_convert_fusion.1
  1089.3 14.4 fusion.289
  1104.0 17.4 convolution_convert_fusion.2
  1121.5 17.5 convolution_convert_fusion.3
  1139.1 139.4 %reduce-scatter.21.cloned.1.call-done = f32[320,2048]{1,0:T(8,128)} async-done(((f32[2560,2048]{1,0:T(8,128)}), f32[320,2048]{1,0:T(8,128)}) %reduce-scatter.21.cloned.1.call-update) | async-done | bytes 2621456 | tf_op jit(solution)/shard_map/reduce_scatter | solution.py:192
  1278.5 208.3 %reduce-scatter.17.cloned.1.call-done = f32[320,2048]{1,0:T(8,128)} async-done(((f32[2560,2048]{1,0:T(8,128)}), f32[320,2048]{1,0:T(8,128)}) %reduce-scatter.17.cloned.1.call-update) | async-done | bytes 2621456 | tf_op jit(solution)/shard_map/reduce_scatter | solution.py:192
  1486.8 4.8 multiply_reduce_fusion.7
  1491.7 105.2 %reduce-scatter.15.cloned.1.call-done = bf16[320,2048]{1,0:T(8,128)(2,1)} async-done(((bf16[2560,2048]{1,0:T(8,128)(2,1)}), bf16[320,2048]{1,0:T(8,128)(2,1)}) %reduce-scatter.15.cloned.1.call-update) | async-done | bytes 1310736 | tf_op jit(solution)/shard_map/reduce_scatter | solution.py:176
  1596.9 110.0 %reduce-scatter.11.cloned.1.call-done = bf16[320,2048]{1,0:T(8,128)(2,1)} async-done(((bf16[2560,2048]{1,0:T(8,128)(2,1)}), bf16[320,2048]{1,0:T(8,128)(2,1)}) %reduce-scatter.11.cloned.1.call-update) | async-done | bytes 1310736 | tf_op jit(solution)/shard_map/reduce_scatter | solution.py:176
  1706.9 6.2 fusion.262
  1718.2 20.1 fusion
  1738.2 19.9 add_convert_fusion
  1758.1 16.3 fusion.292
  1774.4 16.0 add_convert_fusion.1
  1790.4 23.9 all-gather.21.cloned.1.call-done
  1814.4 7.3 convolution_convert_fusion.4
  1826.3 87.9 %all-gather.19.cloned.1.call-done = bf16[2560,2048]{1,0:T(8,128)(2,1)} async-done(((bf16[320,2048]{1,0:T(8,128)(2,1)}), bf16[2560,2048]{1,0:T(8,128)(2,1)}) %all-gather.19.cloned.1.call-update) | async-done | bytes 10485776 | tf_op jit(solution)/shard_map/all_gather | solution.py:199
  1914.3 7.3 convolution_convert_fusion.5
  1950.5 3.5 multiply_reduce_fusion
  2000.9 3.3 multiply_reduce_fusion.16
  2004.3 5.2 multiply_reduce_fusion.19
  2014.4 6.3 fusion.293
  2023.9 7.1 convolution_convert_fusion
  2031.1 6.8 convolution_convert_fusion.1
  2041.5 10.2 psum.66
  2052.4 160.5 %all-reduce.22.cloned.1.call-done = (bf16[2048,192]{0,1:T(8,128)(2,1)}, bf16[64,2048]{1,0:T(8,128)(2,1)}, bf16[2048,1024]{1,0:T(8,128)(2,1)}, bf16[1024,2048]{1,0:T(8,128)(2,1)}) async-done(((bf16[2048,192]{0,1:T(8,128)(2,1)}, bf16[64,2048]{1,0:T(8,128)(2,1)}, bf16[2048,1024]{1,0:T(8,128)(2,1)}, bf16[1024,2048]{1,0:T(8,128)(2,1)}), (bf16[2048,192]{0,1:T(8,128)(2,1)}, bf16[64,2048]{1,0:T(8,128)(2,1)}, ...) | async-done | bytes 9437200 | tf_op jit(solution)/shard_map/psum | solution.py:241
  2214.6 7.0 convert_element_type.295
  2221.7 4.4 convert_element_type.297
  2227.3 97.2 %reduce-scatter.23.cloned.1.call-done = bf16[320,2048]{1,0:T(8,128)(2,1)} async-done(((bf16[2560,2048]{1,0:T(8,128)(2,1)}), bf16[320,2048]{1,0:T(8,128)(2,1)}) %reduce-scatter.23.cloned.1.call-update) | async-done | bytes 1310736 | tf_op jit(solution)/shard_map/reduce_scatter | solution.py:225
  2324.5 110.0 %reduce-scatter.19.cloned.1.call-done = bf16[320,2048]{1,0:T(8,128)(2,1)} async-done(((bf16[2560,2048]{1,0:T(8,128)(2,1)}), bf16[320,2048]{1,0:T(8,128)(2,1)}) %reduce-scatter.19.cloned.1.call-update) | async-done | bytes 1310736 | tf_op jit(solution)/shard_map/reduce_scatter | solution.py:225
  2434.5 3.4 fusion.55
  2446.0 38.7 %all-reduce.18 = (f32[2048]{0:T(1024)}, f32[2048]{0:T(1024)}, f32[2048]{0:T(1024)}, f32[2048]{0:T(1024)}) all-reduce(f32[2048]{0:T(1024)S(1)} %add.525, f32[2048]{0:T(1024)S(1)} %add.526, f32[2048]{0:T(1024)S(1)} %add.530, f32[2048]{0:T(1024)S(1)} %add.531), channel_id=1, replica_groups=mesh['dp'=4,'mp'=8] {'dp','mp'}, use_global_device_ids=true, to_apply=%region_62.63 | all-reduce | flops 8192 | bytes 65536 | tf_op jit(solution)/shard_map/psum | solution.py:247
  (590 shorter events, 168.5 us)
Async XLA Ops:
  7.2 235.6 %copy-start = (bf16[64,2048]{1,0:T(8,128)(2,1)S(1)}, bf16[64,2048]{1,0:T(8,128)(2,1)}, u32[]{:S(2)}) copy-start(bf16[64,2048]{1,0:T(8,128)(2,1)} %param.77) | copy-start | bytes 786436
  7.2 108.9 %all-gather.15.cloned.1.call-start = ((), (), s32[]{:S(2)}) async-start(), calls=%async_computation.12 | async-start | bytes 11796480 | tf_op jit(solution)/shard_map/all_gather | solution.py:110
  13.9 202.3 %all-gather.11.cloned.1.call-start = ((), (), s32[]{:S(2)}) async-start(), calls=%async_computation.8 | async-start | bytes 11796480 | tf_op jit(solution)/shard_map/all_gather | solution.py:110
  14.6 443.0 %reduce-scatter.13.cloned.1.call-start = ((), (), s32[]{:S(2)}) async-start(), calls=%async_computation.13 | async-start | bytes 23592960 | tf_op jit(solution)/shard_map/reduce_scatter | solution.py:167
  15.8 208.2 %copy-start.110 = (f32[1,192]{1,0:T(1,128)}, f32[1,192]{1,0:T(1,128)S(1)}, u32[]{:S(2)}) copy-start(f32[1,192]{1,0:T(1,128)S(1)} %get-tuple-element.372) | copy-start | bytes 2308
  15.8 208.2 %copy-start.112 = (f32[1,192]{1,0:T(1,128)}, f32[1,192]{1,0:T(1,128)S(1)}, u32[]{:S(2)}) copy-start(f32[1,192]{1,0:T(1,128)S(1)} %get-tuple-element.373) | copy-start | bytes 2308
  15.8 208.2 %copy-start.114 = (f32[1,192]{1,0:T(1,128)}, f32[1,192]{1,0:T(1,128)S(1)}, u32[]{:S(2)}) copy-start(f32[1,192]{1,0:T(1,128)S(1)} %get-tuple-element.374) | copy-start | bytes 2308
  16.0 208.0 %copy-start.78 = (pred[2560]{0:T(1024)(128)(4,1)}, pred[2560]{0:T(1024)(128)(4,1)S(1)}, u32[]{:S(2)}) copy-start(pred[2560]{0:T(1024)(128)(4,1)S(1)} %get-tuple-element.357) | copy-start | bytes 7684
  16.0 208.0 %copy-start.80 = (pred[2560]{0:T(1024)(128)(4,1)}, pred[2560]{0:T(1024)(128)(4,1)S(1)}, u32[]{:S(2)}) copy-start(pred[2560]{0:T(1024)(128)(4,1)S(1)} %get-tuple-element.358) | copy-start | bytes 7684
  16.0 208.0 %copy-start.82 = (pred[2560]{0:T(1024)(128)(4,1)}, pred[2560]{0:T(1024)(128)(4,1)S(1)}, u32[]{:S(2)}) copy-start(pred[2560]{0:T(1024)(128)(4,1)S(1)} %get-tuple-element.426) | copy-start | bytes 7684
  16.1 208.0 %copy-start.84 = (pred[2560]{0:T(1024)(128)(4,1)}, pred[2560]{0:T(1024)(128)(4,1)S(1)}, u32[]{:S(2)}) copy-start(pred[2560]{0:T(1024)(128)(4,1)S(1)} %get-tuple-element.427) | copy-start | bytes 7684
  251.4 414.6 %reduce-scatter.9.cloned.1.call-start = ((), (), s32[]{:S(2)}) async-start(), calls=%async_computation.9 | async-start | bytes 23592960 | tf_op jit(solution)/shard_map/reduce_scatter | solution.py:167
  274.1 497.8 %all-gather.17.cloned.1.call-start = ((), (), s32[]{:S(2)}) async-start(), calls=%async_computation.14 | async-start | bytes 11796480 | tf_op jit(solution)/shard_map/all_gather | solution.py:114
  673.9 197.2 %all-gather.25.cloned.1.call-start = ((), (), s32[]{:S(2)}) async-start(), calls=%async_computation.23 | async-start | bytes 11796480 | tf_op jit(solution)/shard_map/all_gather | solution.py:183
  675.7 294.9 %all-gather.13.cloned.1.call-start = ((), (), s32[]{:S(2)}) async-start(), calls=%async_computation.10 | async-start | bytes 11796480 | tf_op jit(solution)/shard_map/all_gather | solution.py:114
  676.4 393.6 %all-gather.23.cloned.1.call-start = ((), (), s32[]{:S(2)}) async-start(), calls=%async_computation.22 | async-start | bytes 11796480 | tf_op jit(solution)/shard_map/all_gather | solution.py:183
  677.2 601.3 %reduce-scatter.21.cloned.1.call-start = ((), (), s32[]{:S(2)}) async-start(), calls=%async_computation.19 | async-start | bytes 23592960 | tf_op jit(solution)/shard_map/reduce_scatter | solution.py:192
  871.1 19.3 copy-start.169
  904.9 581.9 %reduce-scatter.17.cloned.1.call-start = ((), (), s32[]{:S(2)}) async-start(), calls=%async_computation.16 | async-start | bytes 23592960 | tf_op jit(solution)/shard_map/reduce_scatter | solution.py:192
  1103.8 493.1 %reduce-scatter.15.cloned.1.call-start = ((), (), s32[]{:S(2)}) async-start(), calls=%async_computation.15 | async-start | bytes 11796480 | tf_op jit(solution)/shard_map/reduce_scatter | solution.py:176
  1121.4 585.4 %reduce-scatter.11.cloned.1.call-start = ((), (), s32[]{:S(2)}) async-start(), calls=%async_computation.11 | async-start | bytes 11796480 | tf_op jit(solution)/shard_map/reduce_scatter | solution.py:176
  1139.0 347.8 %copy-start.14 = (f32[320,2048]{1,0:T(8,128)S(1)}, f32[320,2048]{1,0:T(8,128)}, u32[]{:S(2)}) copy-start(f32[320,2048]{1,0:T(8,128)} %copy-done.13) | copy-start | bytes 7864324
  1139.0 347.8 %copy-start.69 = (f32[2048]{0:T(1024)S(1)}, f32[2048]{0:T(1024)}, u32[]{:S(2)}) copy-start(f32[2048]{0:T(1024)} %param.78) | copy-start | bytes 24580
  1139.0 347.8 %copy-start.75 = (f32[320]{0:T(512)S(1)}, f32[320]{0:T(512)}, u32[]{:S(2)}) copy-start(f32[320]{0:T(512)} %copy-done.74) | copy-start | bytes 3844
  1139.0 347.8 %copy-start.77 = (f32[320]{0:T(512)S(1)}, f32[320]{0:T(512)}, u32[]{:S(2)}) copy-start(f32[320]{0:T(512)} %copy-done.76) | copy-start | bytes 3844
  1139.0 347.8 %copy-start.87 = (f32[320]{0:T(512)S(1)}, f32[320]{0:T(512)}, u32[]{:S(2)}) copy-start(f32[320]{0:T(512)} %copy-done.86) | copy-start | bytes 3844
  1139.0 347.8 %copy-start.89 = (f32[320]{0:T(512)S(1)}, f32[320]{0:T(512)}, u32[]{:S(2)}) copy-start(f32[320]{0:T(512)} %copy-done.88) | copy-start | bytes 3844
  1139.1 352.6 %copy-start.103 = (f32[320]{0:T(512)S(1)}, f32[320]{0:T(512)}, u32[]{:S(2)}) copy-start(f32[320]{0:T(512)} %copy-done.102) | copy-start | bytes 3844
  1139.1 352.6 %copy-start.105 = (f32[320]{0:T(512)S(1)}, f32[320]{0:T(512)}, u32[]{:S(2)}) copy-start(f32[320]{0:T(512)} %copy-done.104) | copy-start | bytes 3844
  1139.1 675.3 %all-gather.21.cloned.1.call-start = ((), (), s32[]{:S(2)}) async-start(), calls=%async_computation.20 | async-start | bytes 11796480 | tf_op jit(solution)/shard_map/all_gather | solution.py:199
  1716.5 197.8 %all-gather.19.cloned.1.call-start = ((), (), s32[]{:S(2)}) async-start(), calls=%async_computation.17 | async-start | bytes 11796480 | tf_op jit(solution)/shard_map/all_gather | solution.py:199
  1717.0 495.8 %all-reduce.22.cloned.1.call-start = ((), (), s32[]{:S(2)}) async-start(), calls=%async_computation.24 | async-start | bytes 18874368 | tf_op jit(solution)/shard_map/psum | solution.py:241
  1718.1 39.9 %slice-start.18 = ((s8[5242880]{0:T(1024)(128)(4,1)}), s8[4194304]{0:T(1024)(128)(4,1)S(1)}, s32[]{:S(2)}) async-start(s8[5242880]{0:T(1024)(128)(4,1)} %bitcast.222), calls=%async_computation.43 | async-start | bytes 8388608
  1738.2 19.9 slice-start.19
  1738.2 36.2 %slice-start.15 = ((s8[10485760]{0:T(1024)(128)(4,1)}), s8[2097152]{0:T(1024)(128)(4,1)S(1)}, s32[]{:S(2)}) async-start(s8[10485760]{0:T(1024)(128)(4,1)} %bitcast.220), calls=%async_computation.40 | async-start | bytes 4194304
  1738.2 36.2 %slice-start.16 = ((s8[10485760]{0:T(1024)(128)(4,1)}), s8[4194304]{0:T(1024)(128)(4,1)S(1)}, s32[]{:S(2)}) async-start(s8[10485760]{0:T(1024)(128)(4,1)} %bitcast.220), calls=%async_computation.41 | async-start | bytes 8388608
  1790.4 31.2 %copy-start.33 = (f32[512,512]{0,1:T(8,128)S(1)}, f32[512,512]{0,1:T(8,128)}, u32[]{:S(2)}) copy-start(f32[512,512]{0,1:T(8,128)} %copy-done.32) | copy-start | bytes 3145732
  1826.3 95.2 %copy-start.35 = (f32[512,512]{0,1:T(8,128)S(1)}, f32[512,512]{0,1:T(8,128)}, u32[]{:S(2)}) copy-start(f32[512,512]{0,1:T(8,128)} %copy-done.34) | copy-start | bytes 3145732
  2023.9 300.6 %reduce-scatter.23.cloned.1.call-start = ((), (), s32[]{:S(2)}) async-start(), calls=%async_computation.21 | async-start | bytes 11796480 | tf_op jit(solution)/shard_map/reduce_scatter | solution.py:225
  2031.1 403.4 %reduce-scatter.19.cloned.1.call-start = ((), (), s32[]{:S(2)}) async-start(), calls=%async_computation.18 | async-start | bytes 11796480 | tf_op jit(solution)/shard_map/reduce_scatter | solution.py:225
  2226.1 208.3 %copy-start.2 = (bf16[2,320,2048]{2,1,0:T(8,128)(2,1)S(1)}, bf16[2,320,2048]{2,1,0:T(8,128)(2,1)}, u32[]{:S(2)}) copy-start(bf16[2,320,2048]{2,1,0:T(8,128)(2,1)} %param.65) | copy-start | bytes 7864324
  2226.1 208.3 %copy-start.67 = (f32[2048]{0:T(1024)S(1)}, f32[2048]{0:T(1024)}, u32[]{:S(2)}) copy-start(f32[2048]{0:T(1024)} %param.69) | copy-start | bytes 24580
  2226.1 208.3 %copy-start.71 = (f32[320]{0:T(512)S(1)}, f32[320]{0:T(512)}, u32[]{:S(2)}) copy-start(f32[320]{0:T(512)} %copy-done.70) | copy-start | bytes 3844
  2226.1 208.3 %copy-start.73 = (f32[320]{0:T(512)S(1)}, f32[320]{0:T(512)}, u32[]{:S(2)}) copy-start(f32[320]{0:T(512)} %copy-done.72) | copy-start | bytes 3844
  2227.3 210.5 %copy-start.101 = (f32[320]{0:T(512)S(1)}, f32[320]{0:T(512)}, u32[]{:S(2)}) copy-start(f32[320]{0:T(512)} %copy-done.100) | copy-start | bytes 3844
  2227.3 210.6 %copy-start.99 = (f32[320]{0:T(512)S(1)}, f32[320]{0:T(512)}, u32[]{:S(2)}) copy-start(f32[320]{0:T(512)} %copy-done.98) | copy-start | bytes 3844
  2227.3 210.6 %copy-start.95 = (f32[320]{0:T(512)S(1)}, f32[320]{0:T(512)}, u32[]{:S(2)}) copy-start(f32[320]{0:T(512)} %copy-done.94) | copy-start | bytes 3844
  2227.3 210.6 %copy-start.97 = (f32[320]{0:T(512)S(1)}, f32[320]{0:T(512)}, u32[]{:S(2)}) copy-start(f32[320]{0:T(512)} %copy-done.96) | copy-start | bytes 3844
  (162 other events, 522.6 us)
Sparse Core Ops, SparseCore 0:
  14.0 102.0 all-gather.14
  118.3 97.7 all-gather.10
  251.5 206.0 reduce-scatter.12
  459.8 206.0 reduce-scatter.8
  674.1 97.7 all-gather.16
  773.3 97.7 all-gather.24
  872.8 97.7 all-gather.12
  972.2 97.7 all-gather.22
  1072.4 206.0 reduce-scatter.20
  1280.7 206.0 reduce-scatter.16
  1489.1 107.7 reduce-scatter.14
  1599.1 107.7 reduce-scatter.10
  1716.6 97.7 all-gather.20
  1816.4 97.7 all-gather.18
  2024.0 188.8 all-reduce.21
  2215.0 109.4 reduce-scatter.22
  2326.6 107.7 reduce-scatter.18
where the time goes:
time: 2500 us; the launch traced here: 2490 us
  waiting for transfers between devices  1950 us (78%)
  matrix products  361 us (14%)
  other arithmetic  86.8 us (3%)
  blocking collectives  49 us (2%)
  local copies, waits for them, and re-layouts  25 us (1%)
    reduce_scatter x2, waiting for transfers between devices, per_device(): lax.psum_scatter(project_rows(attended_low, out_weight), 'mp', scatter_di...  391 us
    reduce_scatter x2, waiting for transfers between devices, per_device(): lax.psum_scatter(project_back(grad_pre, up_weight), 'mp', scatter_dimensi...  348 us
    reduce_scatter x2, waiting for transfers between devices, per_device(): lax.psum_scatter(project_rows(hidden, down_weight).astype(jnp.bfloat16),...  215 us
    reduce_scatter x2, waiting for transfers between devices, per_device(): lax.psum_scatter(project_back(raw_low, joined).astype(jnp.bfloat16), 'mp'...  207 us
    all_gather x2, waiting for transfers between devices, gather_attention(): return lax.all_gather(normed, 'mp', axis=0, tiled=True)  188 us
    all_gather x2, waiting for transfers between devices, per_device(): grads_all = lax.all_gather(grad_rows, 'mp', axis=0, tiled=True)  166 us
    psum x1, waiting for transfers between devices, per_device(): lax.psum(joined_acc.astype(jnp.bfloat16), 'dp').astype(jnp.float32)  161 us
    all_gather x2, waiting for transfers between devices, gather_feed(): return lax.all_gather(second, 'mp', axis=0, tiled=True)  160 us
  transfers between devices with their start and end apart: 17, of which 17 were waited for; matrix products, arithmetic and copies ran while one was open for 11% of the time, Pallas kernels for 0%

commit v1 on v0

v1 whole, which is shorter than its diff:
```python
from functools import partial

import jax
import jax.numpy as jnp
from jax import lax
from jax.experimental import pallas as pl
from jax.experimental.pallas import tpu as pltpu
from jax.sharding import PartitionSpec as P

HD = 64
BLOCK = 256
LOW = jnp.bfloat16
F32 = jnp.float32


def dot(left, right):
    return jnp.dot(left, right, preferred_element_type=F32)


def layer_norm(rows, gain, shift):
    row_mean = jnp.mean(rows, axis=-1, keepdims=True)
    centered = rows - row_mean
    variance = jnp.mean(centered * centered, axis=-1, keepdims=True)
    return centered * lax.rsqrt(variance + 1e-05) * gain + shift


def document_starts(lengths, count):
    ends = jnp.cumsum(lengths)
    places = jnp.arange(count, dtype=jnp.int32)
    passed = (places[:, None] >= ends[None, :]).astype(jnp.int32)
    return jnp.sum(passed * lengths[None, :], axis=1)


def allowed_pairs(start_row, key_block, query_block):
    keys = key_block * BLOCK + lax.broadcasted_iota(jnp.int32, (BLOCK, BLOCK), 0)
    queries = query_block * BLOCK + lax.broadcasted_iota(jnp.int32, (BLOCK, BLOCK), 1)
    return (keys <= queries) & (keys >= start_row)


def attend_kernel(first_ref, start_ref, mixed_ref, out_ref, wide_ref, total_ref, values_t):
    step = pl.program_id(0)

    @pl.when(step == 0)
    def _():
        def turn(at, carry):
            rows = pl.ds(pl.multiple_of(at * BLOCK, BLOCK), BLOCK)
            values_t[at] = mixed_ref[rows, 2 * HD : 3 * HD].T
            return carry

        lax.fori_loop(0, values_t.shape[0], turn, 0)

    here = pl.ds(pl.multiple_of(step * BLOCK, BLOCK), BLOCK)
    query_t = (mixed_ref[here, 0:HD] * HD ** (-0.5)).astype(LOW).T
    start_row = start_ref[...]

    def one(at, carry):
        top, summed, acc = carry
        rows = pl.ds(pl.multiple_of(at * BLOCK, BLOCK), BLOCK)
        scores = dot(mixed_ref[rows, HD : 2 * HD], query_t)
        scores = jnp.where(allowed_pairs(start_row, at, step), scores, -1e30)
        new_top = jnp.maximum(top, jnp.max(scores, axis=0, keepdims=True))
        powered = jnp.exp(scores - new_top)
        shrink = jnp.exp(top - new_top)
        summed = summed * shrink + jnp.sum(powered, axis=0, keepdims=True)
        acc = acc * shrink + dot(values_t[at], powered.astype(LOW))
        return new_top, summed, acc

    top, summed, acc = lax.fori_loop(
        first_ref[step],
        step + 1,
        one,
        (
            jnp.full((1, BLOCK), -1e30, F32),
            jnp.zeros((1, BLOCK), F32),
            jnp.zeros((HD, BLOCK), F32),
        ),
    )
    result = acc / summed
    wide_ref[...] = result
    out_ref[...] = result.T.astype(LOW)
    total_ref[...] = top + jnp.log(summed)


def attend(mixed, starts):
    group = mixed.shape[0]
    steps = group // BLOCK
    first = starts[::BLOCK] // BLOCK
    row = pl.BlockSpec((1, BLOCK), lambda i, first: (0, i))
    return pl.pallas_call(
        attend_kernel,
        grid_spec=pltpu.PrefetchScalarGridSpec(
            num_scalar_prefetch=1,
            grid=(steps,),
            in_specs=[row, pl.BlockSpec((group, 3 * HD), lambda i, first: (0, 0))],
            out_specs=[
                pl.BlockSpec((BLOCK, HD), lambda i, first: (i, 0)),
                pl.BlockSpec((HD, BLOCK), lambda i, first: (0, i)),
                row,
            ],
            scratch_shapes=[pltpu.VMEM((steps, HD, BLOCK), LOW)],
        ),
        out_shape=[
            jax.ShapeDtypeStruct((group, HD), LOW),
            jax.ShapeDtypeStruct((HD, group), F32),
            jax.ShapeDtypeStruct((1, group), F32),
        ],
        compiler_params=pltpu.CompilerParams(vmem_limit_bytes=32 * 1024 * 1024),
        cost_estimate=pl.CostEstimate(
            flops=4 * HD * group * group // 4,
            bytes_accessed=group * 2048,
            transcendentals=group * group // 4,
        ),
        name="attend",
    )(first, starts.reshape(1, group), mixed)


def attend_back_kernel(
    first_ref, start_ref, mixed_ref, grad_ref, wide_ref, total_ref, out_ref, keys_t, grad_keys, grad_values
):
    step = pl.program_id(0)

    @pl.when(step == 0)
    def _():
        def turn(at, carry):
            rows = pl.ds(pl.multiple_of(at * BLOCK, BLOCK), BLOCK)
            keys_t[at] = mixed_ref[rows, HD : 2 * HD].T
            return carry

        lax.fori_loop(0, keys_t.shape[0], turn, 0)
        grad_keys[...] = jnp.zeros(grad_keys.shape, F32)
        grad_values[...] = jnp.zeros(grad_values.shape, F32)

    here = pl.ds(pl.multiple_of(step * BLOCK, BLOCK), BLOCK)
    query = (mixed_ref[here, 0:HD] * HD ** (-0.5)).astype(LOW)
    query_t = query.T
    grad = grad_ref[...]
    grad_t = grad.T
    start_row = start_ref[...]
    total = total_ref[...]
    inner = jnp.sum(grad_t.astype(F32) * wide_ref[...], axis=0, keepdims=True)

    def one(at, acc):
        rows = pl.ds(pl.multiple_of(at * BLOCK, BLOCK), BLOCK)
        scores = dot(mixed_ref[rows, HD : 2 * HD], query_t)
        scores = jnp.where(allowed_pairs(start_row, at, step), scores, -1e30)
        probs = jnp.exp(scores - total)
        grad_probs = dot(mixed_ref[rows, 2 * HD : 3 * HD], grad_t)
        grad_scores = (probs * (grad_probs - inner)).astype(LOW)
        grad_values[rows, :] += dot(probs.astype(LOW), grad)
        grad_keys[rows, :] += dot(grad_scores, query)
        return acc + dot(keys_t[at], grad_scores)

    acc = lax.fori_loop(first_ref[step], step + 1, one, jnp.zeros((HD, BLOCK), F32))
    out_ref[here, 0:HD] = (acc * HD ** (-0.5)).T.astype(out_ref.dtype)

    @pl.when(step == pl.num_programs(0) - 1)
    def _():
        out_ref[:, HD : 2 * HD] = grad_keys[...].astype(out_ref.dtype)
        out_ref[:, 2 * HD : 3 * HD] = grad_values[...].astype(out_ref.dtype)


def attend_back(mixed, grad, wide, total, starts):
    group = mixed.shape[0]
    steps = group // BLOCK
    first = starts[::BLOCK] // BLOCK
    row = pl.BlockSpec((1, BLOCK), lambda i, first: (0, i))
    return pl.pallas_call(
        attend_back_kernel,
        grid_spec=pltpu.PrefetchScalarGridSpec(
            num_scalar_prefetch=1,
            grid=(steps,),
            in_specs=[
                row,
                pl.BlockSpec((group, 3 * HD), lambda i, first: (0, 0)),
                pl.BlockSpec((BLOCK, HD), lambda i, first: (i, 0)),
                pl.BlockSpec((HD, BLOCK), lambda i, first: (0, i)),
                row,
            ],
            out_specs=pl.BlockSpec((group, 3 * HD), lambda i, first: (0, 0)),
            scratch_shapes=[
                pltpu.VMEM((steps, HD, BLOCK), LOW),
                pltpu.VMEM((group, HD), F32),
                pltpu.VMEM((group, HD), F32),
            ],
        ),
        out_shape=jax.ShapeDtypeStruct((group, 3 * HD), LOW),
        compiler_params=pltpu.CompilerParams(vmem_limit_bytes=32 * 1024 * 1024),
        cost_estimate=pl.CostEstimate(
            flops=10 * HD * group * group // 4,
            bytes_accessed=group * 2048,
            transcendentals=group * group // 4,
        ),
        name="attend_back",
    )(first, starts.reshape(1, group), mixed, grad, wide, total)


def plane_send(block, mask):
    return lax.ppermute(block, "dp", [(d, d ^ mask) for d in range(lax.axis_size("dp"))])


def plane_gather(block):
    half = block.shape[0] // 2
    one, two = block[:half], block[half:]
    one_x = plane_send(one, 1)
    two_y = plane_send(two, 2)
    one_y = plane_send(one, 2)
    two_x = plane_send(two, 1)
    one_xy = plane_send(one_x, 2)
    two_xy = plane_send(two_y, 1)
    return [one, one_y, one_x, one_xy], [two, two_x, two_y, two_xy]


def plane_scatter(part):
    piece = part.shape[0] // 8

    def at(first, count=1):
        return part[first * piece : (first + count) * piece]

    one = plane_send(at(2, 2), 1)
    two = plane_send(at(6, 2), 2)
    one_sum = (at(0, 2).astype(F32) + one.astype(F32))
    two_sum = (at(4, 2).astype(F32) + two.astype(F32))
    one_last = plane_send(one_sum[piece:].astype(LOW), 2)
    two_last = plane_send(two_sum[piece:].astype(LOW), 1)
    return jnp.concatenate(
        [one_sum[:piece] + one_last.astype(F32), two_sum[:piece] + two_last.astype(F32)], axis=0
    )


def plane_order(first, second, axis):
    me = lax.axis_index("dp")
    blocks = jnp.stack(
        [
            jnp.concatenate([first[0], second[0]], axis=0),
            jnp.concatenate([first[2], second[1]], axis=0),
            jnp.concatenate([first[1], second[2]], axis=0),
            jnp.concatenate([first[3], second[3]], axis=0),
        ],
        axis=0,
    )
    return jnp.concatenate(
        [lax.dynamic_index_in_dim(blocks, me ^ d, 0, keepdims=False) for d in range(4)], axis=axis
    )


def chips():
    return lax.axis_size("mp") // 2


def line_send(block, step, senders):
    count = chips()
    pairs = []
    for z in senders:
        if 0 <= z < count and 0 <= z + step < count:
            pairs += [(2 * z + c, 2 * (z + step) + c) for c in range(2)]
    return lax.ppermute(block, "mp", pairs)


def core_swap(block):
    return lax.ppermute(block, "mp", [(i, i ^ 1) for i in range(lax.axis_size("mp"))])


def line_gather(block):
    count = chips()
    z = lax.axis_index("mp") // 2
    from_below, from_above = [block], [block]
    for step in range(1, count):
        from_below.append(line_send(from_below[-1], 1, range(step - 1, count)))
        from_above.append(line_send(from_above[-1], -1, range(0, count - step + 1)))
    return [block] + [
        jnp.where(z + k < count, from_above[k], from_below[count - k]) for k in range(1, count)
    ]


def line_scatter(parts):
    count = chips()

    def add(left, right):
        return (left.astype(F32) + right.astype(F32)).astype(LOW)

    up, down = parts[count - 1], parts[1]
    for step in range(1, count):
        up_in = line_send(up, 1, range(0, step))
        down_in = line_send(down, -1, range(count - step, count))
        if step < count - 1:
            up = add(up_in, parts[count - step - 1])
            down = add(down_in, parts[step + 1])
    return (parts[0].astype(F32) + up_in.astype(F32) + down_in.astype(F32)).astype(LOW)


def per_device(
    inputs,
    cotangent,
    short_lengths,
    long_lengths,
    norm1_gain,
    norm1_bias,
    query_weight,
    key_weight,
    value_weight,
    query_kernel,
    key_kernel,
    value_kernel,
    out_weight,
    norm2_gain,
    norm2_bias,
    up_weight,
    down_weight,
):
    rows_here = inputs.shape[1]
    width = inputs.shape[2]
    mp = lax.axis_size("mp")
    dp = lax.axis_size("dp")
    me_dp = lax.axis_index("dp")
    me_mp = lax.axis_index("mp")
    group = rows_here * mp
    hidden_here = up_weight.shape[1]
    share = hidden_here // dp

    joined_own = jnp.concatenate([query_weight, key_weight, value_weight], axis=1)
    joined = lax.all_gather(joined_own, "mp", axis=1, tiled=True)
    out_all = lax.all_gather(out_weight, "mp", axis=0, tiled=True)
    kernels = lax.all_gather(
        jnp.concatenate([query_kernel, key_kernel, value_kernel], axis=1), "mp", axis=1, tiled=True
    )
    up_share = lax.dynamic_slice_in_dim(up_weight, me_dp * share, share, 1)
    down_share = lax.dynamic_slice_in_dim(down_weight, me_dp * share, share, 0)
    up_line = jnp.concatenate(line_gather(up_share), axis=1)
    up_all = jnp.concatenate([up_line, core_swap(up_line)], axis=1)
    down_line = jnp.concatenate(line_gather(down_share), axis=0)
    down_all = jnp.concatenate([down_line, core_swap(down_line)], axis=0)

    starts = [document_starts(short_lengths[0], group), document_starts(long_lengths[0], group)]
    places = jnp.arange(group, dtype=jnp.int32)
    halo = 8
    before = lax.ppermute(
        inputs[:, rows_here - halo :], "mp", [(i, i + 1) for i in range(mp - 1)]
    )
    rows = inputs.astype(F32)
    normed_all = layer_norm(
        jnp.concatenate([before, inputs], axis=1).astype(F32), norm1_gain, norm1_bias
    ).astype(LOW)
    normed = normed_all[:, halo:]

    cot_pieces = []
    for index in range(2):
        first, second = plane_gather(cotangent[index])
        cot_pieces.append(jnp.concatenate(first + second, axis=0))

    saved = []
    for index in range(2):
        offsets = lax.dynamic_slice_in_dim(
            jnp.pad(places - starts[index], (0, halo)), me_mp * rows_here, rows_here + halo, 0
        )[:, None]
        raw = dot(normed_all[index], joined)
        here = offsets[:rows_here]
        mixed = (
            kernels[0] * raw[halo:]
            + jnp.where(here >= 1, kernels[1] * raw[halo - 1 : -1], 0.0)
            + jnp.where(here >= 2, kernels[2] * raw[halo - 2 : -2], 0.0)
        ).astype(LOW)
        by_head = mixed.reshape(rows_here, mp, 3 * HD).transpose(1, 0, 2)
        mixed_head = lax.all_to_all(by_head, "mp", 0, 0, tiled=True).reshape(group, 3 * HD)
        attended_head, wide, total = attend(mixed_head, starts[index])
        attended = (
            lax.all_to_all(attended_head.reshape(mp, rows_here, HD), "mp", 0, 0, tiled=True)
            .transpose(1, 0, 2)
            .reshape(rows_here, mp * HD)
        )
        middle = rows[index] + dot(attended, out_all)
        second_norm = layer_norm(middle, norm2_gain, norm2_bias).astype(LOW)
        one, two = plane_gather(second_norm)
        second_all = jnp.concatenate(one + two, axis=0)
        saved.append(
            dict(offsets=offsets, raw=raw, mixed_head=mixed_head, wide=wide, total=total, attended=attended, middle=middle, second_all=second_all)
        )

    results = []
    hiddens, grad_pres = [], []
    for index in range(2):
        keep = saved[index]
        pre = dot(keep["second_all"], up_all)
        hidden = jnp.square(jnp.maximum(pre, 0.0)).astype(LOW)
        grad_hidden = jnp.einsum(
            "gd,fd->gf", cot_pieces[index], down_all, preferred_element_type=F32
        )
        grad_pre = (grad_hidden * 2.0 * jnp.maximum(pre, 0.0)).astype(LOW)
        grad_second = plane_scatter(
            jnp.einsum("gf,df->gd", grad_pre, up_all, preferred_element_type=F32).astype(LOW)
        )
        feed = plane_scatter(dot(hidden, down_all).astype(LOW))
        results.append((keep["middle"] + feed).astype(LOW))
        keep["grad_second"] = grad_second
        hiddens.append(hidden)
        grad_pres.append(grad_pre)

    hidden_both = jnp.concatenate(hiddens, axis=0)
    grad_pre_both = jnp.concatenate(grad_pres, axis=0)
    second_both = jnp.concatenate([saved[0]["second_all"], saved[1]["second_all"]], axis=0)
    cot_both = jnp.concatenate(cot_pieces, axis=0)
    up_part = jnp.einsum("gd,gf->df", second_both, grad_pre_both, preferred_element_type=F32).astype(LOW)
    down_part = jnp.einsum("gf,gd->fd", hidden_both, cot_both, preferred_element_type=F32).astype(LOW)

    def add_low(left, right):
        return (left.astype(F32) + right.astype(F32)).astype(LOW)

    mine = share * (mp // 2)
    up_sum = add_low(up_part[:, :mine], core_swap(up_part[:, mine:]))
    down_sum = add_low(down_part[:mine], core_swap(down_part[mine:]))
    up_mine = line_scatter([up_sum[:, k * share : (k + 1) * share] for k in range(mp // 2)])
    down_mine = line_scatter([down_sum[k * share : (k + 1) * share] for k in range(mp // 2)])
    up_grad = plane_order(*plane_gather(up_mine), axis=1).astype(F32)
    down_grad = plane_order(*plane_gather(down_mine), axis=0).astype(F32)

    out_acc = jnp.zeros((mp * HD, width), F32)
    joined_acc = jnp.zeros(joined.shape, F32)
    kernel_acc = jnp.zeros(kernels.shape, F32)
    norm_acc = [jnp.zeros(norm1_gain.shape, F32) for _ in range(4)]
    input_grads = []
    for index in range(2):
        keep = saved[index]
        unused, pull_two = jax.vjp(layer_norm, keep["middle"], norm2_gain, norm2_bias)
        grad_middle, grad_gain_two, grad_shift_two = pull_two(keep["grad_second"])
        grad_middle = grad_middle + cotangent[index].astype(F32)
        branch = grad_middle.astype(LOW)
        out_acc = out_acc + jnp.einsum(
            "gh,gd->hd", keep["attended"], branch, preferred_element_type=F32
        )
        grad_attended = jnp.einsum(
            "gd,hd->gh", branch, out_all, preferred_element_type=F32
        ).astype(LOW)
        grad_head = lax.all_to_all(
            grad_attended.reshape(rows_here, mp, HD).transpose(1, 0, 2), "mp", 0, 0, tiled=True
        ).reshape(group, HD)
        grad_mixed_head = attend_back(
            keep["mixed_head"], grad_head, keep["wide"], keep["total"], starts[index]
        )
        padded = jnp.pad(grad_mixed_head, ((0, halo), (0, 0)))
        with_halo = jnp.stack(
            [padded[i * rows_here : (i + 1) * rows_here + halo] for i in range(mp)], axis=0
        )
        grad_mixed = (
            lax.all_to_all(with_halo, "mp", 0, 0, tiled=True)
            .transpose(1, 0, 2)
            .reshape(rows_here + halo, mp * 3 * HD)
            .astype(F32)
        )
        offsets, raw = keep["offsets"], keep["raw"]
        here = grad_mixed[:rows_here]
        after_one = jnp.where(offsets[1 : rows_here + 1] >= 1, grad_mixed[1 : rows_here + 1], 0.0)
        after_two = jnp.where(offsets[2 : rows_here + 2] >= 2, grad_mixed[2 : rows_here + 2], 0.0)
        grad_raw = (kernels[0] * here + kernels[1] * after_one + kernels[2] * after_two).astype(LOW)
        own_one = jnp.where(offsets[:rows_here] >= 1, here, 0.0)
        own_two = jnp.where(offsets[:rows_here] >= 2, here, 0.0)
        kernel_acc = kernel_acc + jnp.stack(
            [
                jnp.sum(here * raw[halo:], axis=0),
                jnp.sum(own_one * raw[halo - 1 : -1], axis=0),
                jnp.sum(own_two * raw[halo - 2 : -2], axis=0),
            ],
            axis=0,
        )
        joined_acc = joined_acc + jnp.einsum(
            "gd,gc->dc", normed[index], grad_raw, preferred_element_type=F32
        )
        grad_normed = jnp.einsum("gc,dc->gd", grad_raw, joined, preferred_element_type=F32)
        unused_one, pull_one = jax.vjp(layer_norm, rows[index], norm1_gain, norm1_bias)
        grad_input, grad_gain_one, grad_shift_one = pull_one(grad_normed)
        input_grads.append(grad_middle + grad_input)
        norm_acc = [
            norm_acc[0] + grad_gain_one,
            norm_acc[1] + grad_shift_one,
            norm_acc[2] + grad_gain_two,
            norm_acc[3] + grad_shift_two,
        ]
    joined_grad = lax.psum(
        lax.psum_scatter(joined_acc.astype(LOW), "mp", scatter_dimension=1, tiled=True), "dp"
    ).astype(F32)
    out_grad = lax.psum(
        lax.psum_scatter(out_acc.astype(LOW), "mp", scatter_dimension=0, tiled=True), "dp"
    ).astype(F32)
    kernel_sum, norm_totals = lax.psum((kernel_acc, jnp.stack(norm_acc, axis=0)), ("dp", "mp"))
    kernel_grad = lax.dynamic_slice_in_dim(kernel_sum, me_mp * 3 * HD, 3 * HD, 1)
    return (
        jnp.stack(results, axis=0),
        jnp.stack(input_grads, axis=0),
        norm_totals[0],
        norm_totals[1],
        joined_grad[:, :HD],
        joined_grad[:, HD : 2 * HD],
        joined_grad[:, 2 * HD :],
        kernel_grad[:, :HD],
        kernel_grad[:, HD : 2 * HD],
        kernel_grad[:, 2 * HD :],
        out_grad,
        norm_totals[2],
        norm_totals[3],
        up_grad,
        down_grad,
    )


def solution(mesh):
    return jax.shard_map(
        per_device,
        mesh=mesh,
        in_specs=(
            P(None, ("dp", "mp"), None),
            P(None, ("dp", "mp"), None),
            P("dp", None),
            P("dp", None),
            P(),
            P(),
            P(None, "mp"),
            P(None, "mp"),
            P(None, "mp"),
            P(None, "mp"),
            P(None, "mp"),
            P(None, "mp"),
            P("mp", None),
            P(),
            P(),
            P(None, "mp"),
            P("mp", None),
        ),
        out_specs=(
            P(None, ("dp", "mp"), None),
            P(None, ("dp", "mp"), None),
            P(),
            P(),
            P(None, "mp"),
            P(None, "mp"),
            P(None, "mp"),
            P(None, "mp"),
            P(None, "mp"),
            P(None, "mp"),
            P("mp", None),
            P(),
            P(),
            P(None, "mp"),
            P("mp", None),
        ),
        check_vma=False,
    )
```

time: 2500 us -> 1280 us (0.51)
  waiting for transfers between devices: 1950 us -> 369 us
  starting transfers between devices: 2.62 us -> 192 us
  local copies, waits for them, and re-layouts: 25 us -> 164 us
  matrix products: 361 us -> 232 us
  Pallas kernels: 0 us -> 67.6 us
  other arithmetic: 86.8 us -> 148 us
  blocking collectives: 49 us -> 86.9 us
    reduce_scatter x8 -> x2, waiting for transfers between devices: 1160 us -> 0.01 us  [the longest x1 0.01 us: per_device(): lax.psum_scatter(out_acc.astype(LOW), 'mp', scatter_dimension=0, tiled=True)]
    all_gather x8 -> x2, waiting for transfers between devices: 626 us -> 0.01 us  [the longest x1 0.01 us: per_device(): out_all = lax.all_gather(out_weight, 'mp', axis=0, tiled=True)]
    ppermute x0 -> x81, waiting for transfers between devices: none -> 299 us  [the longest x52 202 us: plane_send(): lax.ppermute(block, 'dp', [(d, d ^ mask) for d in range(lax.axis_size('dp...]
    dot_general x84 -> x22, matrix products: 361 us -> 232 us  [the longest x8 76.4 us: dot(): return jnp.dot(left, right, preferred_element_type=F32)]
    ppermute x0 -> x81, starting transfers between devices: none -> 123 us  [the longest x52 61.6 us: plane_send(): lax.ppermute(block, 'dp', [(d, d ^ mask) for d in range(lax.axis_size('dp...]
    psum x1, waiting for transfers between devices: 161 us -> 40.7 us  [per_device(): lax.psum(lax.psum_scatter(joined_acc.astype(LOW), 'mp', scatter_dimension...]
    all_to_all x0 -> x8, starting transfers between devices: none -> 68.9 us  [the longest x2 29.5 us: per_device(): lax.all_to_all(by_head, 'mp', 0, 0, tiled=True).reshape(group, 3 * HD)]
    pallas_call x0 -> x4, Pallas kernels: none -> 67.6 us  [the longest x2 35 us: attend_back(): pl.pallas_call(attend_back_kernel, grid_spec=pltpu.PrefetchScalarGridSpec...]
  transfers between devices with their start and end apart: 17 -> 94, of which waited for: 17 -> 35; matrix products, arithmetic and copies ran while one was open for 11% -> 36% of each run, Pallas kernels for 0% -> 5%
where the time goes in v1:
time: 1280 us
  waiting for transfers between devices  369 us (29%)
  matrix products  232 us (18%)
  starting transfers between devices  192 us (15%)
  local copies, waits for them, and re-layouts  164 us (13%)
  other arithmetic  148 us (12%)
  blocking collectives  86.9 us (7%)
  Pallas kernels  67.6 us (5%)
  between operations  16.5 us (1%)
    ppermute x52, waiting for transfers between devices, plane_send(): lax.ppermute(block, 'dp', [(d, d ^ mask) for d in range(lax.axis_size('dp...  202 us
    ppermute x24, waiting for transfers between devices, line_send(): return lax.ppermute(block, 'mp', pairs)  96.6 us
    unnamed x352, local copies, waits for them, and re-layouts  77.4 us
    dot_general x8, matrix products, dot(): return jnp.dot(left, right, preferred_element_type=F32)  76.4 us
    psum x1, blocking collectives, per_device(): lax.psum((kernel_acc, jnp.stack(norm_acc, axis=0)), ('dp', 'mp'))  71.5 us
    ppermute x52, starting transfers between devices, plane_send(): lax.ppermute(block, 'dp', [(d, d ^ mask) for d in range(lax.axis_size('dp...  61.6 us
    ppermute x24, starting transfers between devices, line_send(): return lax.ppermute(block, 'mp', pairs)  59 us
    psum x1, waiting for transfers between devices, per_device(): lax.psum(lax.psum_scatter(joined_acc.astype(LOW), 'mp', scatter_dimension...  40.7 us
  transfers between devices with their start and end apart: 94, of which 35 were waited for; matrix products, arithmetic and copies ran while one was open for 36% of the time, Pallas kernels for 5%

profile of v1, /device:TPU:0, one launch (start us, length us, event | category | flops | bytes accessed | tf_op | source)
XLA Modules:
  0.0 1276.2 jit_solution(4545907897902478901)
XLA Ops:
  29.4 15.4 %all-gather = f32[8,192,3]{1,2,0:T(4,128)S(1)} all-gather(f32[1,192,3]{1,2,0:T(4,128)S(1)} %maximum_bitcast_fusion.6), channel_id=1, replica_groups=mesh['dp'=4,'mp'=8] {'mp'}, dimensions={0}, use_global_device_ids=true | all-gather | bytes 20736 | tf_op jit(solution)/shard_map/all_gather | solution.py:323
  78.5 9.0 collective-permute-done.37
  127.9 5.6 fusion.28
  140.4 10.8 collective-permute-done.14
  158.2 17.9 %all-to-all-start.2 = ((bf16[8,320,192]{1,2,0:T(8,128)(2,1)}), bf16[8,320,192]{1,2,0:T(8,128)(2,1)S(1)}, u32[]{:S(2)}, u32[]{:S(2)}) async-start(bf16[8,320,192]{1,2,0:T(8,128)(2,1)} %bitcast.21), calls=%async_computation.2 | async-start | bytes 2359296 | tf_op jit(solution)/shard_map/all_to_all | solution.py:363
  186.4 16.0 %collective-permute-done.18 = bf16[256,2048]{1,0:T(8,128)(2,1)} collective-permute-done((bf16[256,2048]{1,0:T(8,128)(2,1)}, bf16[256,2048]{1,0:T(8,128)(2,1)}, u32[]{:S(2)}, u32[]{:S(2)}) %collective-permute-start.18) | collective-permute-done | bytes 1048608 | tf_op jit(solution)/shard_map/ppermute | solution.py:256
  211.3 10.9 all-to-all-done.2
  222.1 11.6 all-to-all-start
  249.1 19.5 %attend.3 = (bf16[2560,64]{1,0:T(8,128)(2,1)S(1)}, f32[64,2560]{1,0:T(8,128)S(1)}, f32[1,2560]{1,0:T(1,128)S(1)}) custom-call(s32[10]{0:T(128)S(1)} %and_select_fusion.first_ref, s32[1,2560]{1,0:T(1,128)S(1)} %reshape.362.start_ref, bf16[2560,192]{1,0:T(8,128)(2,1)S(1)} %bitcast.259), custom_call_target="tpu_custom_call" | custom-call | flops 419430400 | bytes 5242880 | tf_op jit(solution)/shard_map/attend/pallas_call | solution.py:89
  270.5 8.2 all-to-all-done
  278.7 17.2 %all-to-all-start.3 = ((bf16[8,320,64]{1,2,0:T(8,128)(2,1)}), bf16[8,320,64]{1,2,0:T(8,128)(2,1)}, u32[]{:S(2)}, u32[]{:S(2)}) async-start(bf16[8,320,64]{1,2,0:T(8,128)(2,1)} %copy.104), calls=%async_computation.3 | async-start | bytes 786432 | tf_op jit(solution)/shard_map/all_to_all | solution.py:366
  304.3 13.1 %attend.2 = (bf16[2560,64]{1,0:T(8,128)(2,1)S(1)}, f32[64,2560]{1,0:T(8,128)S(1)}, f32[1,2560]{1,0:T(1,128)S(1)}) custom-call(s32[10]{0:T(128)S(1)} %and_select_fusion.1.first_ref, s32[1,2560]{1,0:T(1,128)S(1)} %reshape.355.start_ref, bf16[2560,192]{1,0:T(8,128)(2,1)S(1)} %bitcast.261), custom_call_target="tpu_custom_call" | custom-call | flops 419430400 | bytes 5242880 | tf_op jit(solution)/shard_map/attend/pallas_call | solution.py:89
  330.0 6.6 all-to-all-done.1
  344.8 5.8 collective-permute-start.2
  358.5 6.7 collective-permute-done.2
  373.3 10.5 collective-permute-done.3
  387.1 13.8 %collective-permute-done.5 = bf16[160,2048]{1,0:T(8,128)(2,1)S(1)} collective-permute-done((bf16[160,2048]{1,0:T(8,128)(2,1)S(1)}, bf16[160,2048]{1,0:T(8,128)(2,1)S(1)}, u32[]{:S(2)}, u32[]{:S(2)}) %collective-permute-start.5) | collective-permute-done | bytes 655392 | tf_op jit(solution)/shard_map/ppermute | solution.py:198
  404.0 11.3 collective-permute-done.6
  419.9 18.1 %multiply_convert_fusion.3 = (bf16[1280,2048]{1,0:T(8,128)(2,1)}, f32[1280,2048]{1,0:T(8,128)}) fusion(bf16[1280,2048]{1,0:T(8,128)(2,1)} %copy-done.77, bf16[2048,2048]{1,0:T(8,128)(2,1)} %constant_dynamic-update-slice_fusion.8), kind=kOutput, calls=%fused_computation.12 | convolution fusion | flops 10745282560 | bytes 29360128 | tf_op jit(solution)/shard_map/dot_general | solution.py:17
  438.0 13.7 %convolution_convert_fusion.3 = bf16[1280,2048]{1,0:T(8,128)(2,1)S(1)} fusion(bf16[1280,2048]{1,0:T(8,128)(2,1)} %get-tuple-element.221, bf16[2048,2048]{1,0:T(8,128)(2,1)S(1)} %constant_dynamic-update-slice_fusion.13), kind=kOutput, calls=%fused_computation.20 | convolution fusion | flops 10740039680 | bytes 18874368 | tf_op jit(solution)/shard_map/dot_general | solution.py:17
  451.7 20.2 %multiply_convert_fusion.1 = bf16[1280,2048]{1,0:T(8,128)(2,1)} fusion(f32[1280,2048]{1,0:T(8,128)} %get-tuple-element.222, bf16[1280,2048]{1,0:T(8,128)(2,1)} %constant_dynamic-update-slice_fusion.26, bf16[2048,2048]{1,0:T(8,128)(2,1)} %copy-done.69), kind=kOutput, calls=%fused_computation.10 | convolution fusion | flops 10747904000 | bytes 29360128 | tf_op jit(solution)/shard_map/gd,fd->gf/dot_general | solution.py:384
  471.9 15.2 %convolution_convert_fusion.1 = bf16[1280,2048]{1,0:T(8,128)(2,1)S(1)} fusion(bf16[1280,2048]{1,0:T(8,128)(2,1)} %multiply_convert_fusion.1, bf16[2048,2048]{1,0:T(8,128)(2,1)} %constant_dynamic-update-slice_fusion.8), kind=kOutput, calls=%fused_computation.18 | convolution fusion | flops 10740039680 | bytes 18874368 | tf_op jit(solution)/shard_map/gf,df->gd/dot_general | solution.py:389
  494.3 39.9 %collective-permute-done.27 = bf16[160,2048]{1,0:T(8,128)(2,1)S(1)} collective-permute-done((bf16[160,2048]{1,0:T(8,128)(2,1)S(1)}, bf16[160,2048]{1,0:T(8,128)(2,1)S(1)}, u32[]{:S(2)}, u32[]{:S(2)}) %collective-permute-start.27) | collective-permute-done | bytes 655392 | tf_op jit(solution)/shard_map/ppermute | solution.py:198
  540.3 7.0 collective-permute-done.21
  547.2 15.0 %collective-permute-done.23 = bf16[320,2048]{1,0:T(8,128)(2,1)S(1)} collective-permute-done((bf16[320,2048]{1,0:T(8,128)(2,1)S(1)}, bf16[320,2048]{1,0:T(8,128)(2,1)S(1)}, u32[]{:S(2)}, u32[]{:S(2)}) %collective-permute-start.23) | collective-permute-done | bytes 1310752 | tf_op jit(solution)/shard_map/ppermute | solution.py:198
  568.9 7.3 collective-permute-done.29
  576.9 9.8 collective-permute-done.24
  602.6 16.3 %multiply_convert_fusion.2 = (bf16[1280,2048]{1,0:T(8,128)(2,1)}, f32[1280,2048]{1,0:T(8,128)}) fusion(bf16[1280,2048]{1,0:T(8,128)(2,1)} %get-tuple-element.180, bf16[2048,2048]{1,0:T(8,128)(2,1)S(1)} %bitcast.293), kind=kOutput, calls=%fused_computation.11 | convolution fusion | flops 10745282560 | bytes 29360128 | tf_op jit(solution)/shard_map/dot_general | solution.py:17
  618.9 17.1 %multiply_convert_fusion = bf16[1280,2048]{1,0:T(8,128)(2,1)} fusion(f32[1280,2048]{1,0:T(8,128)} %get-tuple-element.220, bf16[1280,2048]{1,0:T(8,128)(2,1)S(1)} %bitcast.295, bf16[2048,2048]{1,0:T(8,128)(2,1)} %copy-done.69), kind=kOutput, calls=%fused_computation.9 | convolution fusion | flops 10747904000 | bytes 29360128 | tf_op jit(solution)/shard_map/gd,fd->gf/dot_general | solution.py:384
  636.1 15.4 %convolution_convert_fusion = bf16[1280,2048]{1,0:T(8,128)(2,1)S(1)} fusion(bf16[1280,2048]{1,0:T(8,128)(2,1)} %multiply_convert_fusion, bf16[2048,2048]{1,0:T(8,128)(2,1)} %constant_dynamic-update-slice_fusion.8), kind=kOutput, calls=%fused_computation.17 | convolution fusion | flops 10740039680 | bytes 18874368 | tf_op jit(solution)/shard_map/gf,df->gd/dot_general | solution.py:389
  656.5 13.4 %convolution_convert_fusion.2 = bf16[1280,2048]{1,0:T(8,128)(2,1)S(1)} fusion(bf16[1280,2048]{1,0:T(8,128)(2,1)} %get-tuple-element.219, bf16[2048,2048]{1,0:T(8,128)(2,1)S(1)} %bitcast.291), kind=kOutput, calls=%fused_computation.19 | convolution fusion | flops 10740039680 | bytes 18874368 | tf_op jit(solution)/shard_map/dot_general | solution.py:17
  675.2 28.1 %fusion.11 = bf16[2048,2048]{0,1:T(8,128)(2,1)S(1)} fusion(bf16[2560,2048]{1,0:T(8,128)(2,1)} %get-tuple-element.179, bf16[1280,2048]{1,0:T(8,128)(2,1)} %multiply_convert_fusion, bf16[1280,2048]{1,0:T(8,128)(2,1)} %multiply_convert_fusion.1), kind=kOutput, calls=%fused_computation.16 | convolution fusion | flops 21500002304 | bytes 29360128 | tf_op jit(solution)/shard_map/gd,gf->df/dot_general | solution.py:401
  703.2 30.7 %fusion.8 = bf16[2048,2048]{1,0:T(8,128)(2,1)S(1)} fusion(bf16[2560,2048]{1,0:T(8,128)(2,1)} %get-tuple-element.167, bf16[1280,2048]{1,0:T(8,128)(2,1)} %get-tuple-element.219, bf16[1280,2048]{1,0:T(8,128)(2,1)} %get-tuple-element.221), kind=kOutput, calls=%fused_computation.15 | convolution fusion | flops 21500002304 | bytes 29360128 | tf_op jit(solution)/shard_map/gf,gd->fd/dot_general | solution.py:402
  752.3 11.7 collective-permute-done.54
  767.5 9.5 collective-permute-done.34
  817.1 20.6 %attend_back.3 = bf16[2560,192]{1,0:T(8,128)(2,1)S(1)} custom-call(s32[10]{0:T(128)S(1)} %copy-done.9, s32[1,2560]{1,0:T(1,128)S(1)} %copy-done.5, bf16[2560,192]{1,0:T(8,128)(2,1)S(1)} %bitcast.260, bf16[2560,64]{1,0:T(8,128)(2,1)S(1)} %bitcast.263, f32[64,2560]{1,0:T(8,128)S(1)} %copy-done.1, f32[1,2560]{1,0:T(1,128)S(1)} %get-tuple-element.26.total_ref), custom_call_target="tpu_custom_call" | custom-call | flops 1048576000 | bytes 5242880 | tf_op jit(solution)/shard_map/attend_back/pallas_call | solution.py:167
  852.1 14.4 %attend_back.2 = bf16[2560,192]{1,0:T(8,128)(2,1)S(1)} custom-call(s32[10]{0:T(128)S(1)} %copy-done.7, s32[1,2560]{1,0:T(1,128)S(1)} %reshape.355.start_ref, bf16[2560,192]{1,0:T(8,128)(2,1)S(1)} %bitcast.262, bf16[2560,64]{1,0:T(8,128)(2,1)S(1)} %bitcast.264, f32[64,2560]{1,0:T(8,128)S(1)} %copy-done.3, f32[1,2560]{1,0:T(1,128)S(1)} %get-tuple-element.24.total_ref), custom_call_target="tpu_custom_call" | custom-call | flops 1048576000 | bytes 5242880 | tf_op jit(solution)/shard_map/attend_back/pallas_call | solution.py:167
  868.2 7.7 add_convert_fusion.1
  893.4 7.8 add_convert_fusion.2
  935.8 5.7 add_convert_fusion
  949.1 5.8 fusion.64
  968.9 22.5 %collective-permute-done.56 = bf16[2048,256]{0,1:T(8,128)(2,1)} collective-permute-done((bf16[2048,256]{0,1:T(8,128)(2,1)}, bf16[2048,256]{0,1:T(8,128)(2,1)}, u32[]{:S(2)}, u32[]{:S(2)}) %collective-permute-start.56) | collective-permute-done | bytes 1048608 | tf_op jit(solution)/shard_map/ppermute | solution.py:256
  1006.9 29.5 %collective-permute-done.70 = bf16[256,2048]{1,0:T(8,128)(2,1)} collective-permute-done((bf16[256,2048]{1,0:T(8,128)(2,1)}, bf16[256,2048]{1,0:T(8,128)(2,1)}, u32[]{:S(2)}, u32[]{:S(2)}) %collective-permute-start.70) | collective-permute-done | bytes 1048608 | tf_op jit(solution)/shard_map/ppermute | solution.py:256
  1046.6 71.5 %all-reduce.4 = (f32[4,2048]{1,0:T(4,128)S(1)}, f32[3,1536]{1,0:T(4,128)S(1)}) all-reduce(f32[4,2048]{1,0:T(4,128)S(1)} %pad_maximum_fusion.10, f32[3,1536]{1,0:T(4,128)S(1)} %maximum_add_fusion.2), channel_id=1, replica_groups=mesh['dp'=4,'mp'=8] {'dp','mp'}, use_global_device_ids=true, to_apply=%region_32.33 | all-reduce | flops 12800 | bytes 102400 | tf_op jit(solution)/shard_map/psum | solution.py:482
  1134.7 12.5 collective-permute-done.58
  1167.0 7.0 collective-permute-done.62
  1185.3 16.4 %collective-permute-done.66 = bf16[1024,256]{0,1:T(8,128)(2,1)S(1)} collective-permute-done((bf16[1024,256]{0,1:T(8,128)(2,1)S(1)}, bf16[1024,256]{0,1:T(8,128)(2,1)S(1)}, u32[]{:S(2)}, u32[]{:S(2)}) %collective-permute-start.66) | collective-permute-done | bytes 524320 | tf_op jit(solution)/shard_map/ppermute | solution.py:198
  1224.7 40.7 %all-reduce.8.cloned.1.call-done = (bf16[2048,192]{0,1:T(8,128)(2,1)}, bf16[64,2048]{1,0:T(8,128)(2,1)}) async-done(((bf16[2048,192]{0,1:T(8,128)(2,1)}, bf16[64,2048]{1,0:T(8,128)(2,1)}), (bf16[2048,192]{0,1:T(8,128)(2,1)}, bf16[64,2048]{1,0:T(8,128)(2,1)})) %all-reduce.8.cloned.1.call-update) | async-done | bytes 1048592 | tf_op jit(solution)/shard_map/psum | solution.py:476
  (697 shorter events, 499.4 us)
Async XLA Ops:
  7.2 120.7 %all-gather.4.cloned.1.call-start = ((), (), s32[]{:S(2)}) async-start(), calls=%async_computation.10 | async-start | bytes 7077888 | tf_op jit(solution)/shard_map/all_gather | solution.py:321
  9.3 314.7 %all-gather.6.cloned.1.call-start = ((), (), s32[]{:S(2)}) async-start(), calls=%async_computation.11 | async-start | bytes 2359296 | tf_op jit(solution)/shard_map/all_gather | solution.py:322
  12.6 81.2 %collective-permute-start.46 = (bf16[160,2048]{1,0:T(8,128)(2,1)}, bf16[160,2048]{1,0:T(8,128)(2,1)}, u32[]{:S(2)}, u32[]{:S(2)}) collective-permute-start(bf16[160,2048]{1,0:T(8,128)(2,1)} %get-tuple-element.138), channel_id=1, source_target_pairs={{0,8},{8,0},{16,24},{24,16},{1,9},{9,1},{17,25},{25,17},{2,10},{10... | collective-permute-start | bytes 1966088 | tf_op jit(solution)/shard_map/ppermute | solution.py:198
  15.5 95.7 %collective-permute-start.45 = (bf16[160,2048]{1,0:T(8,128)(2,1)}, bf16[160,2048]{1,0:T(8,128)(2,1)}, u32[]{:S(2)}, u32[]{:S(2)}) collective-permute-start(bf16[160,2048]{1,0:T(8,128)(2,1)} %get-tuple-element.138), channel_id=1, source_target_pairs={{0,16},{8,24},{16,0},{24,8},{1,17},{9,25},{17,1},{25,9},{2,18},{10... | collective-permute-start | bytes 1966088 | tf_op jit(solution)/shard_map/ppermute | solution.py:198
  17.1 45.5 %collective-permute-start.36 = (bf16[160,2048]{1,0:T(8,128)(2,1)}, bf16[160,2048]{1,0:T(8,128)(2,1)S(1)}, u32[]{:S(2)}, u32[]{:S(2)}) collective-permute-start(bf16[160,2048]{1,0:T(8,128)(2,1)} %get-tuple-element.140), channel_id=1, source_target_pairs={{0,8},{8,0},{16,24},{24,16},{1,9},{9,1},{17,25},{25,17},{2,10},{10... | collective-permute-start | bytes 1966088 | tf_op jit(solution)/shard_map/ppermute | solution.py:198
  17.6 48.4 %collective-permute-start.35 = (bf16[160,2048]{1,0:T(8,128)(2,1)}, bf16[160,2048]{1,0:T(8,128)(2,1)}, u32[]{:S(2)}, u32[]{:S(2)}) collective-permute-start(bf16[160,2048]{1,0:T(8,128)(2,1)} %get-tuple-element.140), channel_id=1, source_target_pairs={{0,16},{8,24},{16,0},{24,8},{1,17},{9,25},{17,1},{25,9},{2,18},{10... | collective-permute-start | bytes 1966088 | tf_op jit(solution)/shard_map/ppermute | solution.py:198
  90.7 46.7 %collective-permute-start.7 = (bf16[2048,256]{1,0:T(8,128)(2,1)S(1)}, bf16[2048,256]{1,0:T(8,128)(2,1)}, u32[]{:S(2)}, u32[]{:S(2)}) collective-permute-start(bf16[2048,256]{1,0:T(8,128)(2,1)S(1)} %get-tuple-element.87), channel_id=1, source_target_pairs={{2,0},{3,1},{4,2},{5,3},{6,4},{7,5},{10,8},{11,9},{12,10},{13,11},... | collective-permute-start | bytes 3145736 | tf_op jit(solution)/shard_map/ppermute | solution.py:256
  93.8 44.9 %collective-permute-start.15 = (bf16[256,2048]{1,0:T(8,128)(2,1)S(1)}, bf16[256,2048]{1,0:T(8,128)(2,1)}, u32[]{:S(2)}, u32[]{:S(2)}) collective-permute-start(bf16[256,2048]{1,0:T(8,128)(2,1)S(1)} %get-tuple-element.79), channel_id=1, source_target_pairs={{0,2},{1,3},{2,4},{3,5},{4,6},{5,7},{8,10},{9,11},{10,12},{11,13},... | collective-permute-start | bytes 3145736 | tf_op jit(solution)/shard_map/ppermute | solution.py:256
  137.4 46.1 %collective-permute-start.11 = (bf16[2048,256]{1,0:T(8,128)(2,1)}, bf16[2048,256]{1,0:T(8,128)(2,1)}, u32[]{:S(2)}, u32[]{:S(2)}) collective-permute-start(bf16[2048,256]{1,0:T(8,128)(2,1)} %collective-permute-done.7), channel_id=1, source_target_pairs={{2,0},{3,1},{4,2},{5,3},{10,8},{11,9},{12,10},{13,11},{18,16},{19,... | collective-permute-start | bytes 3145736 | tf_op jit(solution)/shard_map/ppermute | solution.py:256
  138.7 46.0 %collective-permute-start.16 = (bf16[256,2048]{1,0:T(8,128)(2,1)}, bf16[256,2048]{1,0:T(8,128)(2,1)}, u32[]{:S(2)}, u32[]{:S(2)}) collective-permute-start(bf16[256,2048]{1,0:T(8,128)(2,1)} %collective-permute-done.15), channel_id=1, source_target_pairs={{2,4},{3,5},{4,6},{5,7},{10,12},{11,13},{12,14},{13,15},{18,20},{1... | collective-permute-start | bytes 3145736 | tf_op jit(solution)/shard_map/ppermute | solution.py:256
  151.1 51.3 %collective-permute-start.18 = (bf16[256,2048]{1,0:T(8,128)(2,1)}, bf16[256,2048]{1,0:T(8,128)(2,1)}, u32[]{:S(2)}, u32[]{:S(2)}) collective-permute-start(bf16[256,2048]{1,0:T(8,128)(2,1)} %collective-permute-done.14), channel_id=1, source_target_pairs={{2,0},{3,1},{4,2},{5,3},{10,8},{11,9},{12,10},{13,11},{18,16},{19,... | collective-permute-start | bytes 3145736 | tf_op jit(solution)/shard_map/ppermute | solution.py:256
  152.4 51.3 %collective-permute-start.10 = (bf16[2048,256]{1,0:T(8,128)(2,1)}, bf16[2048,256]{1,0:T(8,128)(2,1)}, u32[]{:S(2)}, u32[]{:S(2)}) collective-permute-start(bf16[2048,256]{1,0:T(8,128)(2,1)} %collective-permute-done.9), channel_id=1, source_target_pairs={{4,6},{5,7},{12,14},{13,15},{20,22},{21,23},{28,30},{29,31}} | collective-permute-start | bytes 3145736 | tf_op jit(solution)/shard_map/ppermute | solution.py:256
  158.2 63.9 %all-to-all-start.2 = ((bf16[8,320,192]{1,2,0:T(8,128)(2,1)}), bf16[8,320,192]{1,2,0:T(8,128)(2,1)S(1)}, u32[]{:S(2)}, u32[]{:S(2)}) async-start(bf16[8,320,192]{1,2,0:T(8,128)(2,1)} %bitcast.21), calls=%async_computation.2 | async-start | bytes 2359296 | tf_op jit(solution)/shard_map/all_to_all | solution.py:363
  177.1 174.5 %collective-permute-start.50 = (bf16[160,2048]{1,0:T(8,128)(2,1)}, bf16[160,2048]{1,0:T(8,128)(2,1)}, u32[]{:S(2)}, u32[]{:S(2)}) collective-permute-start(bf16[160,2048]{1,0:T(8,128)(2,1)} %collective-permute-done.49), channel_id=1, source_target_pairs={{0,8},{8,0},{16,24},{24,16},{1,9},{9,1},{17,25},{25,17},{2,10},{10... | collective-permute-start | bytes 1966088 | tf_op jit(solution)/shard_map/ppermute | solution.py:198
  183.4 54.1 %collective-permute-start.12 = (bf16[2048,256]{1,0:T(8,128)(2,1)}, bf16[2048,256]{1,0:T(8,128)(2,1)}, u32[]{:S(2)}, u32[]{:S(2)}) collective-permute-start(bf16[2048,256]{1,0:T(8,128)(2,1)} %collective-permute-done.11), channel_id=1, source_target_pairs={{2,0},{3,1},{10,8},{11,9},{18,16},{19,17},{26,24},{27,25}} | collective-permute-start | bytes 3145736 | tf_op jit(solution)/shard_map/ppermute | solution.py:256
  184.7 57.6 %collective-permute-start.17 = (bf16[256,2048]{1,0:T(8,128)(2,1)}, bf16[256,2048]{1,0:T(8,128)(2,1)}, u32[]{:S(2)}, u32[]{:S(2)}) collective-permute-start(bf16[256,2048]{1,0:T(8,128)(2,1)} %collective-permute-done.16), channel_id=1, source_target_pairs={{4,6},{5,7},{12,14},{13,15},{20,22},{21,23},{28,30},{29,31}} | collective-permute-start | bytes 3145736 | tf_op jit(solution)/shard_map/ppermute | solution.py:256
  202.4 93.5 %collective-permute-start.19 = (bf16[256,2048]{1,0:T(8,128)(2,1)}, bf16[256,2048]{1,0:T(8,128)(2,1)}, u32[]{:S(2)}, u32[]{:S(2)}) collective-permute-start(bf16[256,2048]{1,0:T(8,128)(2,1)} %collective-permute-done.18), channel_id=1, source_target_pairs={{2,0},{3,1},{10,8},{11,9},{18,16},{19,17},{26,24},{27,25}} | collective-permute-start | bytes 3145736 | tf_op jit(solution)/shard_map/ppermute | solution.py:256
  222.1 56.5 %all-to-all-start = ((bf16[8,320,192]{1,2,0:T(8,128)(2,1)}), bf16[8,320,192]{1,2,0:T(8,128)(2,1)}, u32[]{:S(2)}, u32[]{:S(2)}) async-start(bf16[8,320,192]{1,2,0:T(8,128)(2,1)} %bitcast.9), calls=%async_computation | async-start | bytes 2359296 | tf_op jit(solution)/shard_map/all_to_all | solution.py:363
  242.3 111.5 %collective-permute-start.13 = (bf16[2048,1024]{1,0:T(8,128)(2,1)}, bf16[2048,1024]{1,0:T(8,128)(2,1)}, u32[]{:S(2)}, u32[]{:S(2)}) collective-permute-start(bf16[2048,1024]{1,0:T(8,128)(2,1)} %pad_maximum_fusion.1), channel_id=1, source_target_pairs={{0,1},{1,0},{2,3},{3,2},{4,5},{5,4},{6,7},{7,6},{8,9},{9,8},{10,11... | collective-permute-start | bytes 12582920 | tf_op jit(solution)/shard_map/ppermute | solution.py:260
  302.1 63.0 %collective-permute-start.20 = (bf16[1024,2048]{1,0:T(8,128)(2,1)}, bf16[1024,2048]{1,0:T(8,128)(2,1)}, u32[]{:S(2)}, u32[]{:S(2)}) collective-permute-start(bf16[1024,2048]{1,0:T(8,128)(2,1)} %pad_maximum_fusion.2), channel_id=1, source_target_pairs={{0,1},{1,0},{2,3},{3,2},{4,5},{5,4},{6,7},{7,6},{8,9},{9,8},{10,11... | collective-permute-start | bytes 12582920 | tf_op jit(solution)/shard_map/ppermute | solution.py:260
  417.3 71.7 %collective-permute-start.26 = (bf16[160,2048]{1,0:T(8,128)(2,1)S(1)}, bf16[160,2048]{1,0:T(8,128)(2,1)S(1)}, u32[]{:S(2)}, u32[]{:S(2)}) collective-permute-start(bf16[160,2048]{1,0:T(8,128)(2,1)S(1)} %get-tuple-element.154), channel_id=1, source_target_pairs={{0,8},{8,0},{16,24},{24,16},{1,9},{9,1},{17,25},{25,17},{2,10},{10... | collective-permute-start | bytes 1966088 | tf_op jit(solution)/shard_map/ppermute | solution.py:198
  418.5 73.2 %collective-permute-start.25 = (bf16[160,2048]{1,0:T(8,128)(2,1)S(1)}, bf16[160,2048]{1,0:T(8,128)(2,1)S(1)}, u32[]{:S(2)}, u32[]{:S(2)}) collective-permute-start(bf16[160,2048]{1,0:T(8,128)(2,1)S(1)} %get-tuple-element.154), channel_id=1, source_target_pairs={{0,16},{8,24},{16,0},{24,8},{1,17},{9,25},{17,1},{25,9},{2,18},{10... | collective-permute-start | bytes 1966088 | tf_op jit(solution)/shard_map/ppermute | solution.py:198
  487.4 49.7 %collective-permute-start.41 = (bf16[320,2048]{1,0:T(8,128)(2,1)S(1)}, bf16[320,2048]{1,0:T(8,128)(2,1)S(1)}, u32[]{:S(2)}, u32[]{:S(2)}) collective-permute-start(bf16[320,2048]{1,0:T(8,128)(2,1)S(1)} %get-tuple-element.96), channel_id=1, source_target_pairs={{0,8},{8,0},{16,24},{24,16},{1,9},{9,1},{17,25},{25,17},{2,10},{10... | collective-permute-start | bytes 3932168 | tf_op jit(solution)/shard_map/ppermute | solution.py:198
  488.4 49.9 %collective-permute-start.43 = (bf16[320,2048]{1,0:T(8,128)(2,1)S(1)}, bf16[320,2048]{1,0:T(8,128)(2,1)S(1)}, u32[]{:S(2)}, u32[]{:S(2)}) collective-permute-start(bf16[320,2048]{1,0:T(8,128)(2,1)S(1)} %get-tuple-element.97), channel_id=1, source_target_pairs={{0,16},{8,24},{16,0},{24,8},{1,17},{9,25},{17,1},{25,9},{2,18},{10... | collective-permute-start | bytes 3932168 | tf_op jit(solution)/shard_map/ppermute | solution.py:198
  489.0 45.2 %collective-permute-start.27 = (bf16[160,2048]{1,0:T(8,128)(2,1)S(1)}, bf16[160,2048]{1,0:T(8,128)(2,1)S(1)}, u32[]{:S(2)}, u32[]{:S(2)}) collective-permute-start(bf16[160,2048]{1,0:T(8,128)(2,1)S(1)} %collective-permute-done.26), channel_id=1, source_target_pairs={{0,16},{8,24},{16,0},{24,8},{1,17},{9,25},{17,1},{25,9},{2,18},{10... | collective-permute-start | bytes 1966088 | tf_op jit(solution)/shard_map/ppermute | solution.py:198
  490.6 56.7 %collective-permute-start.21 = (bf16[320,2048]{1,0:T(8,128)(2,1)S(1)}, bf16[320,2048]{1,0:T(8,128)(2,1)S(1)}, u32[]{:S(2)}, u32[]{:S(2)}) collective-permute-start(bf16[320,2048]{1,0:T(8,128)(2,1)S(1)} %get-tuple-element.100), channel_id=1, source_target_pairs={{0,8},{8,0},{16,24},{24,16},{1,9},{9,1},{17,25},{25,17},{2,10},{10... | collective-permute-start | bytes 3932168 | tf_op jit(solution)/shard_map/ppermute | solution.py:198
  491.8 70.5 %collective-permute-start.23 = (bf16[320,2048]{1,0:T(8,128)(2,1)S(1)}, bf16[320,2048]{1,0:T(8,128)(2,1)S(1)}, u32[]{:S(2)}, u32[]{:S(2)}) collective-permute-start(bf16[320,2048]{1,0:T(8,128)(2,1)S(1)} %get-tuple-element.101), channel_id=1, source_target_pairs={{0,16},{8,24},{16,0},{24,8},{1,17},{9,25},{17,1},{25,9},{2,18},{10... | collective-permute-start | bytes 3932168 | tf_op jit(solution)/shard_map/ppermute | solution.py:198
  537.1 53.6 %collective-permute-start.28 = (bf16[160,2048]{1,0:T(8,128)(2,1)}, bf16[160,2048]{1,0:T(8,128)(2,1)}, u32[]{:S(2)}, u32[]{:S(2)}) collective-permute-start(bf16[160,2048]{1,0:T(8,128)(2,1)} %get-tuple-element.152), channel_id=1, source_target_pairs={{0,8},{8,0},{16,24},{24,16},{1,9},{9,1},{17,25},{25,17},{2,10},{10... | collective-permute-start | bytes 1966088 | tf_op jit(solution)/shard_map/ppermute | solution.py:198
  539.4 49.5 %collective-permute-start.44 = (bf16[160,2048]{1,0:T(8,128)(2,1)S(1)}, bf16[160,2048]{1,0:T(8,128)(2,1)S(1)}, u32[]{:S(2)}, u32[]{:S(2)}) collective-permute-start(bf16[160,2048]{1,0:T(8,128)(2,1)S(1)} %slice.827), channel_id=1, source_target_pairs={{0,8},{8,0},{16,24},{24,16},{1,9},{9,1},{17,25},{25,17},{2,10},{10... | collective-permute-start | bytes 1966088 | tf_op jit(solution)/shard_map/ppermute | solution.py:198
  654.6 86.3 %collective-permute-start.51 = (bf16[320,2048]{1,0:T(8,128)(2,1)}, bf16[320,2048]{1,0:T(8,128)(2,1)S(1)}, u32[]{:S(2)}, u32[]{:S(2)}) collective-permute-start(bf16[320,2048]{1,0:T(8,128)(2,1)} %get-tuple-element.92), channel_id=1, source_target_pairs={{0,8},{8,0},{16,24},{24,16},{1,9},{9,1},{17,25},{25,17},{2,10},{10... | collective-permute-start | bytes 3932168 | tf_op jit(solution)/shard_map/ppermute | solution.py:198
  655.7 86.3 %collective-permute-start.53 = (bf16[320,2048]{1,0:T(8,128)(2,1)}, bf16[320,2048]{1,0:T(8,128)(2,1)}, u32[]{:S(2)}, u32[]{:S(2)}) collective-permute-start(bf16[320,2048]{1,0:T(8,128)(2,1)} %get-tuple-element.93), channel_id=1, source_target_pairs={{0,16},{8,24},{16,0},{24,8},{1,17},{9,25},{17,1},{25,9},{2,18},{10... | collective-permute-start | bytes 3932168 | tf_op jit(solution)/shard_map/ppermute | solution.py:198
  673.0 74.5 %collective-permute-start.31 = (bf16[320,2048]{1,0:T(8,128)(2,1)}, bf16[320,2048]{1,0:T(8,128)(2,1)}, u32[]{:S(2)}, u32[]{:S(2)}) collective-permute-start(bf16[320,2048]{1,0:T(8,128)(2,1)} %get-tuple-element.104), channel_id=1, source_target_pairs={{0,8},{8,0},{16,24},{24,16},{1,9},{9,1},{17,25},{25,17},{2,10},{10... | collective-permute-start | bytes 3932168 | tf_op jit(solution)/shard_map/ppermute | solution.py:198
  674.1 74.2 %collective-permute-start.33 = (bf16[320,2048]{1,0:T(8,128)(2,1)}, bf16[320,2048]{1,0:T(8,128)(2,1)}, u32[]{:S(2)}, u32[]{:S(2)}) collective-permute-start(bf16[320,2048]{1,0:T(8,128)(2,1)} %get-tuple-element.105), channel_id=1, source_target_pairs={{0,16},{8,24},{16,0},{24,8},{1,17},{9,25},{17,1},{25,9},{2,18},{10... | collective-permute-start | bytes 3932168 | tf_op jit(solution)/shard_map/ppermute | solution.py:198
  740.9 127.3 %collective-permute-start.68 = (bf16[1024,2048]{1,0:T(8,128)(2,1)}, bf16[1024,2048]{1,0:T(8,128)(2,1)}, u32[]{:S(2)}, u32[]{:S(2)}) collective-permute-start(bf16[1024,2048]{1,0:T(8,128)(2,1)} %slice.645), channel_id=1, source_target_pairs={{0,1},{1,0},{2,3},{3,2},{4,5},{5,4},{6,7},{7,6},{8,9},{9,8},{10,11... | collective-permute-start | bytes 12582920 | tf_op jit(solution)/shard_map/ppermute | solution.py:260
  740.9 152.5 %collective-permute-start.55 = (bf16[2048,1024]{0,1:T(8,128)(2,1)}, bf16[2048,1024]{0,1:T(8,128)(2,1)}, u32[]{:S(2)}, u32[]{:S(2)}) collective-permute-start(bf16[2048,1024]{0,1:T(8,128)(2,1)} %slice.637), channel_id=1, source_target_pairs={{0,1},{1,0},{2,3},{3,2},{4,5},{5,4},{6,7},{7,6},{8,9},{9,8},{10,11... | collective-permute-start | bytes 12582920 | tf_op jit(solution)/shard_map/ppermute | solution.py:260
  793.7 420.4 %reduce-scatter.5.cloned.1.call-start = ((), (), s32[]{:S(2)}) async-start(), calls=%async_computation.13 | async-start | bytes 2359296 | tf_op jit(solution)/shard_map/reduce_scatter | solution.py:480
  883.8 330.2 %reduce-scatter.3.cloned.1.call-start = ((), (), s32[]{:S(2)}) async-start(), calls=%async_computation.12 | async-start | bytes 7077888 | tf_op jit(solution)/shard_map/reduce_scatter | solution.py:477
  887.0 74.7 %collective-permute-start.69 = (bf16[256,2048]{1,0:T(8,128)(2,1)}, bf16[256,2048]{1,0:T(8,128)(2,1)}, u32[]{:S(2)}, u32[]{:S(2)}) collective-permute-start(bf16[256,2048]{1,0:T(8,128)(2,1)} %get-tuple-element.114), channel_id=1, source_target_pairs={{0,2},{1,3},{8,10},{9,11},{16,18},{17,19},{24,26},{25,27}} | collective-permute-start | bytes 3145736 | tf_op jit(solution)/shard_map/ppermute | solution.py:256
  891.8 69.9 %collective-permute-start.72 = (bf16[256,2048]{1,0:T(8,128)(2,1)}, bf16[256,2048]{1,0:T(8,128)(2,1)}, u32[]{:S(2)}, u32[]{:S(2)}) collective-permute-start(bf16[256,2048]{1,0:T(8,128)(2,1)} %get-tuple-element.115), channel_id=1, source_target_pairs={{6,4},{7,5},{14,12},{15,13},{22,20},{23,21},{30,28},{31,29}} | collective-permute-start | bytes 3145736 | tf_op jit(solution)/shard_map/ppermute | solution.py:256
  941.5 323.9 %all-reduce.8.cloned.1.call-start = ((), (), s32[]{:S(2)}) async-start(), calls=%async_computation.14 | async-start | bytes 2097152 | tf_op jit(solution)/shard_map/psum | solution.py:476
  944.7 46.7 %collective-permute-start.56 = (bf16[2048,256]{0,1:T(8,128)(2,1)}, bf16[2048,256]{0,1:T(8,128)(2,1)}, u32[]{:S(2)}, u32[]{:S(2)}) collective-permute-start(bf16[2048,256]{0,1:T(8,128)(2,1)} %get-tuple-element.124), channel_id=1, source_target_pairs={{0,2},{1,3},{8,10},{9,11},{16,18},{17,19},{24,26},{25,27}} | collective-permute-start | bytes 3145736 | tf_op jit(solution)/shard_map/ppermute | solution.py:256
  947.1 44.3 %collective-permute-start.59 = (bf16[2048,256]{0,1:T(8,128)(2,1)}, bf16[2048,256]{0,1:T(8,128)(2,1)}, u32[]{:S(2)}, u32[]{:S(2)}) collective-permute-start(bf16[2048,256]{0,1:T(8,128)(2,1)} %get-tuple-element.125), channel_id=1, source_target_pairs={{6,4},{7,5},{14,12},{15,13},{22,20},{23,21},{30,28},{31,29}} | collective-permute-start | bytes 3145736 | tf_op jit(solution)/shard_map/ppermute | solution.py:256
  964.8 71.5 %collective-permute-start.70 = (bf16[256,2048]{1,0:T(8,128)(2,1)}, bf16[256,2048]{1,0:T(8,128)(2,1)}, u32[]{:S(2)}, u32[]{:S(2)}) collective-permute-start(bf16[256,2048]{1,0:T(8,128)(2,1)} %get-tuple-element.112), channel_id=1, source_target_pairs={{0,2},{1,3},{2,4},{3,5},{8,10},{9,11},{10,12},{11,13},{16,18},{17,... | collective-permute-start | bytes 3145736 | tf_op jit(solution)/shard_map/ppermute | solution.py:256
  967.1 69.2 %collective-permute-start.73 = (bf16[256,2048]{1,0:T(8,128)(2,1)S(1)}, bf16[256,2048]{1,0:T(8,128)(2,1)}, u32[]{:S(2)}, u32[]{:S(2)}) collective-permute-start(bf16[256,2048]{1,0:T(8,128)(2,1)S(1)} %get-tuple-element.113), channel_id=1, source_target_pairs={{4,2},{5,3},{6,4},{7,5},{12,10},{13,11},{14,12},{15,13},{20,18},{2... | collective-permute-start | bytes 3145736 | tf_op jit(solution)/shard_map/ppermute | solution.py:256
  995.3 122.8 %collective-permute-start.57 = (bf16[2048,256]{0,1:T(8,128)(2,1)}, bf16[2048,256]{0,1:T(8,128)(2,1)}, u32[]{:S(2)}, u32[]{:S(2)}) collective-permute-start(bf16[2048,256]{0,1:T(8,128)(2,1)} %get-tuple-element.122), channel_id=1, source_target_pairs={{0,2},{1,3},{2,4},{3,5},{8,10},{9,11},{10,12},{11,13},{16,18},{17,... | collective-permute-start | bytes 3145736 | tf_op jit(solution)/shard_map/ppermute | solution.py:256
  1000.8 117.4 %collective-permute-start.60 = (bf16[2048,256]{0,1:T(8,128)(2,1)}, bf16[2048,256]{0,1:T(8,128)(2,1)}, u32[]{:S(2)}, u32[]{:S(2)}) collective-permute-start(bf16[2048,256]{0,1:T(8,128)(2,1)} %get-tuple-element.123), channel_id=1, source_target_pairs={{4,2},{5,3},{6,4},{7,5},{12,10},{13,11},{14,12},{15,13},{20,18},{2... | collective-permute-start | bytes 3145736 | tf_op jit(solution)/shard_map/ppermute | solution.py:256
  1039.9 87.8 %collective-permute-start.71 = (bf16[256,2048]{1,0:T(8,128)(2,1)}, bf16[256,2048]{1,0:T(8,128)(2,1)}, u32[]{:S(2)}, u32[]{:S(2)}) collective-permute-start(bf16[256,2048]{1,0:T(8,128)(2,1)} %get-tuple-element.110), channel_id=1, source_target_pairs={{0,2},{1,3},{2,4},{3,5},{4,6},{5,7},{8,10},{9,11},{10,12},{11,13},... | collective-permute-start | bytes 3145736 | tf_op jit(solution)/shard_map/ppermute | solution.py:256
  1045.3 82.4 %collective-permute-start.74 = (bf16[256,2048]{1,0:T(8,128)(2,1)}, bf16[256,2048]{1,0:T(8,128)(2,1)}, u32[]{:S(2)}, u32[]{:S(2)}) collective-permute-start(bf16[256,2048]{1,0:T(8,128)(2,1)} %get-tuple-element.111), channel_id=1, source_target_pairs={{2,0},{3,1},{4,2},{5,3},{6,4},{7,5},{10,8},{11,9},{12,10},{13,11},... | collective-permute-start | bytes 3145736 | tf_op jit(solution)/shard_map/ppermute | solution.py:256
  (192 other events, 4127.4 us)
Sparse Core Ops, SparseCore 0:
  10.2 67.6 all-gather.3
  79.5 41.1 all-gather.5
  804.1 40.1 reduce-scatter.4
  941.7 129.5 reduce-scatter.2
  1214.2 51.2 all-reduce.7

commit v2 on v1

v2 whole, which is shorter than its diff:
```python
from functools import partial

import jax
import jax.numpy as jnp
from jax import lax
from jax.experimental import pallas as pl
from jax.experimental.pallas import tpu as pltpu
from jax.sharding import PartitionSpec as P

HD = 64
BLOCK = 256
CHUNK = 512
VMEM_LIMIT = 62 * 1024 * 1024
MESH = pl.DeviceIdType.MESH
LOW = jnp.bfloat16
F32 = jnp.float32


def dot(left, right):
    return jnp.dot(left, right, preferred_element_type=F32)


def layer_norm(rows, gain, shift):
    row_mean = jnp.mean(rows, axis=-1, keepdims=True)
    centered = rows - row_mean
    variance = jnp.mean(centered * centered, axis=-1, keepdims=True)
    return centered * lax.rsqrt(variance + 1e-05) * gain + shift


def document_starts(lengths, count):
    ends = jnp.cumsum(lengths)
    places = jnp.arange(count, dtype=jnp.int32)
    passed = (places[:, None] >= ends[None, :]).astype(jnp.int32)
    return jnp.sum(passed * lengths[None, :], axis=1)


def allowed_pairs(start_row, key_block, query_block):
    keys = key_block * BLOCK + lax.broadcasted_iota(jnp.int32, (BLOCK, BLOCK), 0)
    queries = query_block * BLOCK + lax.broadcasted_iota(jnp.int32, (BLOCK, BLOCK), 1)
    return (keys <= queries) & (keys >= start_row)


def attend_kernel(
    first_ref, start_ref, qk_ref, v_ref, out_ref, wide_ref, total_ref, values_t
):
    s, step = pl.program_id(0), pl.program_id(1)

    @pl.when(step == 0)
    def _():
        def turn(at, carry):
            rows = pl.ds(pl.multiple_of(at * BLOCK, BLOCK), BLOCK)
            both = v_ref[0, rows, :].T
            values_t[at] = jnp.where(s == 0, both[:HD], both[HD:])
            return carry

        lax.fori_loop(0, values_t.shape[0], turn, 0)

    here = pl.ds(pl.multiple_of(step * BLOCK, BLOCK), BLOCK)
    query_t = (qk_ref[0, here, 0:HD] * HD ** (-0.5)).astype(LOW).T
    start_row = start_ref[0]

    def one(at, carry):
        top, summed, acc = carry
        rows = pl.ds(pl.multiple_of(at * BLOCK, BLOCK), BLOCK)
        scores = dot(qk_ref[0, rows, HD : 2 * HD], query_t)
        scores = jnp.where(allowed_pairs(start_row, at, step), scores, -1e30)
        new_top = jnp.maximum(top, jnp.max(scores, axis=0, keepdims=True))
        powered = jnp.exp(scores - new_top)
        shrink = jnp.exp(top - new_top)
        summed = summed * shrink + jnp.sum(powered, axis=0, keepdims=True)
        acc = acc * shrink + dot(values_t[at], powered.astype(LOW))
        return new_top, summed, acc

    top, summed, acc = lax.fori_loop(
        first_ref[s, step],
        step + 1,
        one,
        (
            jnp.full((1, BLOCK), -1e30, F32),
            jnp.zeros((1, BLOCK), F32),
            jnp.zeros((HD, BLOCK), F32),
        ),
    )
    result = acc / summed
    wide_ref[0] = result
    total_ref[0] = top + jnp.log(summed)
    low = result.T.astype(LOW)

    @pl.when(s == 0)
    def _():
        out_ref[0, here, 0:HD] = low

    @pl.when(s == 1)
    def _():
        out_ref[0, here, HD : 2 * HD] = low


def attend(mixed, starts):
    group = mixed.shape[1]
    steps = group // BLOCK
    row = pl.BlockSpec((1, 1, BLOCK), lambda s, i, first: (s, 0, i))
    return pl.pallas_call(
        attend_kernel,
        grid_spec=pltpu.PrefetchScalarGridSpec(
            num_scalar_prefetch=1,
            grid=(2, steps),
            in_specs=[
                row,
                pl.BlockSpec((1, group, 2 * HD), lambda s, i, first: (s, 0, 0)),
                pl.BlockSpec((1, group, 2 * HD), lambda s, i, first: (2, 0, 0)),
            ],
            out_specs=[
                pl.BlockSpec((1, group, 2 * HD), lambda s, i, first: (0, 0, 0)),
                pl.BlockSpec((1, HD, BLOCK), lambda s, i, first: (s, 0, i)),
                row,
            ],
            scratch_shapes=[pltpu.VMEM((steps, HD, BLOCK), LOW)],
        ),
        out_shape=[
            jax.ShapeDtypeStruct((1, group, 2 * HD), LOW),
            jax.ShapeDtypeStruct((2, HD, group), F32),
            jax.ShapeDtypeStruct((2, 1, group), F32),
        ],
        compiler_params=pltpu.CompilerParams(vmem_limit_bytes=32 * 1024 * 1024),
        cost_estimate=pl.CostEstimate(
            flops=2**34, bytes_accessed=group * 2048, transcendentals=group * group // 4
        ),
        name="attend",
    )(starts[:, ::BLOCK] // BLOCK, starts[:, None, :], mixed, mixed)


def attend_back_kernel(
    first_ref, start_ref, qk_ref, v_ref, grad_ref, wide_ref, total_ref, out_ref,
    keys_t, values, grad_keys, grad_values,
):
    s, step = pl.program_id(0), pl.program_id(1)
    group = qk_ref.shape[1]

    @pl.when(step == 0)
    def _():
        def turn(at, carry):
            rows = pl.ds(pl.multiple_of(at * BLOCK, BLOCK), BLOCK)
            keys_t[at] = qk_ref[0, rows, HD : 2 * HD].T
            both = v_ref[0, rows, :]
            values[rows, :] = jnp.where(s == 0, both[:, :HD], both[:, HD:])
            return carry

        lax.fori_loop(0, keys_t.shape[0], turn, 0)
        grad_keys[...] = jnp.zeros(grad_keys.shape, F32)
        grad_values[...] = jnp.zeros(grad_values.shape, F32)

    here = pl.ds(pl.multiple_of(step * BLOCK, BLOCK), BLOCK)
    query = (qk_ref[0, here, 0:HD] * HD ** (-0.5)).astype(LOW)
    query_t = query.T
    both = grad_ref[0]
    grad = jnp.where(s == 0, both[:, :HD], both[:, HD:])
    grad_t = grad.T
    start_row = start_ref[0]
    total = total_ref[0]
    inner = jnp.sum(grad_t.astype(F32) * wide_ref[0], axis=0, keepdims=True)

    def one(at, acc):
        rows = pl.ds(pl.multiple_of(at * BLOCK, BLOCK), BLOCK)
        scores = dot(qk_ref[0, rows, HD : 2 * HD], query_t)
        scores = jnp.where(allowed_pairs(start_row, at, step), scores, -1e30)
        probs = jnp.exp(scores - total)
        grad_probs = dot(values[rows, :], grad_t)
        grad_scores = (probs * (grad_probs - inner)).astype(LOW)
        grad_values[rows, :] += dot(probs.astype(LOW), grad)
        grad_keys[rows, :] += dot(grad_scores, query)
        return acc + dot(keys_t[at], grad_scores)

    acc = lax.fori_loop(first_ref[s, step], step + 1, one, jnp.zeros((HD, BLOCK), F32))
    out_ref[s, here, 0:HD] = (acc * HD ** (-0.5)).T.astype(out_ref.dtype)

    @pl.when(step == pl.num_programs(1) - 1)
    def _():
        out_ref[s, 0:group, HD : 2 * HD] = grad_keys[...].astype(out_ref.dtype)
        out_ref[s, group:, :] = jnp.zeros((out_ref.shape[1] - group, 2 * HD), out_ref.dtype)

        @pl.when(s == 0)
        def _():
            out_ref[2, 0:group, 0:HD] = grad_values[...].astype(out_ref.dtype)

        @pl.when(s == 1)
        def _():
            out_ref[2, 0:group, HD : 2 * HD] = grad_values[...].astype(out_ref.dtype)
            out_ref[2, group:, :] = jnp.zeros((out_ref.shape[1] - group, 2 * HD), out_ref.dtype)


def attend_back(mixed, grad, wide, total, starts, halo):
    group = mixed.shape[1]
    steps = group // BLOCK
    row = pl.BlockSpec((1, 1, BLOCK), lambda s, i, first: (s, 0, i))
    return pl.pallas_call(
        attend_back_kernel,
        grid_spec=pltpu.PrefetchScalarGridSpec(
            num_scalar_prefetch=1,
            grid=(2, steps),
            in_specs=[
                row,
                pl.BlockSpec((1, group, 2 * HD), lambda s, i, first: (s, 0, 0)),
                pl.BlockSpec((1, group, 2 * HD), lambda s, i, first: (2, 0, 0)),
                pl.BlockSpec((1, BLOCK, 2 * HD), lambda s, i, first: (0, i, 0)),
                pl.BlockSpec((1, HD, BLOCK), lambda s, i, first: (s, 0, i)),
                row,
            ],
            out_specs=pl.BlockSpec((3, group + halo, 2 * HD), lambda s, i, first: (0, 0, 0)),
            scratch_shapes=[
                pltpu.VMEM((steps, HD, BLOCK), LOW),
                pltpu.VMEM((group, HD), LOW),
                pltpu.VMEM((group, HD), F32),
                pltpu.VMEM((group, HD), F32),
            ],
        ),
        out_shape=jax.ShapeDtypeStruct((3, group + halo, 2 * HD), LOW),
        compiler_params=pltpu.CompilerParams(vmem_limit_bytes=32 * 1024 * 1024),
        cost_estimate=pl.CostEstimate(
            flops=2**35, bytes_accessed=group * 2048, transcendentals=group * group // 4
        ),
        name="attend_back",
    )(starts[:, ::BLOCK] // BLOCK, starts[:, None, :], mixed, mixed, grad, wide, total)


def plane_partners():
    me = lax.axis_index("dp")
    return {"dp": me + 1 - 2 * lax.rem(me, 2)}, {"dp": me + 2 - 4 * (me // 2)}


def dot_nt(left, right):
    return lax.dot_general(left, right, (((1,), (1,)), ((), ())), preferred_element_type=F32)


def mesh_place():
    me = lax.axis_index("mp")
    return me // 2, lax.rem(me, 2)


def wire(source, target, send, recv, partner):
    return pltpu.make_async_remote_copy(
        src_ref=source,
        dst_ref=target,
        send_sem=send,
        recv_sem=recv,
        device_id=partner,
        device_id_type=MESH,
    )


def line_partner(z, step):
    _, core = mesh_place()
    return {"mp": 2 * (z + step) + core}


def other_core():
    z, core = mesh_place()
    return {"mp": 2 * z + 1 - core}


def greet(partners):
    barrier = pltpu.get_barrier_semaphore()
    for partner in partners:
        pl.semaphore_signal(barrier, inc=1, device_id=partner, device_id_type=MESH)
    pl.semaphore_wait(barrier, len(partners))


def greet_line(with_plane):
    z, _ = mesh_place()
    count = lax.axis_size("mp") // 2
    barrier = pltpu.get_barrier_semaphore()
    partners = [other_core()]
    if with_plane:
        partners += list(plane_partners())
    for partner in partners:
        pl.semaphore_signal(barrier, inc=1, device_id=partner, device_id_type=MESH)
    for turn in (1, -1):

        @pl.when((z + turn >= 0) & (z + turn < count))
        def _(turn=turn):
            pl.semaphore_signal(barrier, inc=1, device_id=line_partner(z, turn), device_id_type=MESH)

    near = jnp.where(z > 0, 1, 0) + jnp.where(z < count - 1, 1, 0)
    pl.semaphore_wait(barrier, near + len(partners))


class LineGather:
    def __init__(self, place, send, recv, swap_send, swap_recv):
        self.z, self.core = mesh_place()
        self.count = lax.axis_size("mp") // 2
        self.place, self.send, self.recv = place, send, recv
        self.swap_send, self.swap_recv = swap_send, swap_recv

    def copies(self, step):
        z, count = self.z, self.count
        out = []
        for way, turn in enumerate((1, -1)):
            leaves = z - turn * (step - 1)
            lands = z - turn * step
            far = z + turn
            sends = (leaves >= 0) & (leaves < count) & (far >= 0) & (far < count)
            receives = (lands >= 0) & (lands < count)
            at = jnp.clip(leaves, 0, count - 1)
            to = jnp.clip(lands, 0, count - 1)
            sems = (self.send.at[way, step - 1], self.recv.at[way, step - 1], line_partner(z, turn))
            leaving = wire(self.place(at, self.core), self.place(at, self.core), *sems)
            landing = wire(self.place(to, self.core), self.place(to, self.core), *sems)
            out.append((sends, leaving, receives, landing, to))
        return out

    def start(self, step):
        for sends, leaving, _, _, _ in self.copies(step):
            pl.when(sends)(leaving.start)

    def swap(self, at, number):
        sems = (self.swap_send.at[number], self.swap_recv.at[number], other_core())
        leaving = wire(self.place(at, self.core), self.place(at, self.core), *sems)
        landing = wire(self.place(at, 1 - self.core), self.place(at, 1 - self.core), *sems)
        return leaving, landing

    def swap_own(self):
        self.swap(self.z, 0)[0].start()

    def arrive(self, step):
        for way, (_, _, receives, landing, at) in enumerate(self.copies(step)):

            @pl.when(receives)
            def _(landing=landing, at=at, way=way):
                landing.wait_recv()
                self.swap(at, 1 + 2 * (step - 1) + way)[0].start()

    def swapped(self, at, number):
        leaving, landing = self.swap(at, number)
        leaving.wait_send()
        landing.wait_recv()

    def finish(self, steps, own):
        if own:
            self.swapped(self.z, 0)
        for step in steps:
            for way, (sends, leaving, receives, _, at) in enumerate(self.copies(step)):
                pl.when(sends)(leaving.wait_send)
                pl.when(receives)(
                    lambda at=at, way=way, step=step: self.swapped(at, 1 + 2 * (step - 1) + way)
                )


def line_semaphores(count):
    return [
        pltpu.SemaphoreType.DMA((2, count)),
        pltpu.SemaphoreType.DMA((2, count)),
        pltpu.SemaphoreType.DMA((2 * count,)),
        pltpu.SemaphoreType.DMA((2 * count,)),
    ]


def early_steps(count):
    return range(1, count // 2 + 1)


def prepare_kernel(
    inputs_ref, gain_ref, shift_ref, qk_ref, v_ref, out_ref, taps_ref, up_ref,
    all_qk_ref, all_v_ref, all_out_ref, all_taps_ref, normed_ref, halo_ref, up_all_ref,
    rows, normed, local, *sems,
):
    mp = lax.axis_size("mp")
    dp = lax.axis_index("dp")
    me = lax.axis_index("mp")
    z, core = mesh_place()
    count = mp // 2
    rows_here, depth = rows.shape[1:]
    to_x, to_y = plane_partners()
    share = up_ref.shape[0]
    owned = (qk_ref, v_ref, out_ref)
    whole = (all_qk_ref, all_v_ref, all_out_ref)
    (plane_send_sem, plane_recv_sem, plane_swap_send, plane_swap_recv) = sems[:4]
    taps_send, taps_recv, halo_send, halo_recv = sems[4:8]
    line_sems = [sems[8 + 4 * part : 12 + 4 * part] for part in range(4)]

    def up_place(at, at_core):
        start = pl.multiple_of((at_core * count + at) * share, 16)
        return up_all_ref.at[pl.ds(start, share), :]

    loads = [
        pltpu.make_async_copy(inputs_ref, rows, local.at[0]),
        pltpu.make_async_copy(taps_ref, all_taps_ref.at[me], local.at[1]),
        pltpu.make_async_copy(up_ref, up_place(z, core), local.at[2]),
    ] + [
        pltpu.make_async_copy(
            owned[part].at[dp], whole[part].at[z, core, dp], local.at[3 + part]
        )
        for part in range(3)
    ]
    for copy in loads:
        copy.start()

    barrier = pltpu.get_barrier_semaphore()
    for step in range(1, mp):
        pl.semaphore_signal(
            barrier, inc=1, device_id={"mp": lax.rem(me + step, mp)}, device_id_type=MESH
        )
    for partner in (to_x, to_y):
        pl.semaphore_signal(barrier, inc=1, device_id=partner, device_id_type=MESH)
    pl.semaphore_wait(barrier, mp + 1)
    for copy in loads[1:]:
        copy.wait()

    lines = [
        LineGather(lambda at, at_core, part=part: whole[part].at[at, at_core, dp], *line_sems[part])
        for part in range(3)
    ]
    up_line = LineGather(up_place, *line_sems[3])
    for line in lines:
        line.start(1)
    tap_copies = [
        (
            wire(
                taps_ref, all_taps_ref.at[me], taps_send.at[step], taps_recv.at[step],
                {"mp": lax.rem(me + step, mp)},
            ),
            wire(
                taps_ref, all_taps_ref.at[lax.rem(me + mp - step, mp)], taps_send.at[step],
                taps_recv.at[step], {"mp": lax.rem(me + step, mp)},
            ),
        )
        for step in range(1, mp)
    ]
    for copy, _ in tap_copies:
        copy.start()
    for line in lines:
        line.swap_own()

    loads[0].wait()
    tall = 16

    def norm(s):
        def some(at, carry):
            here = pl.ds(pl.multiple_of(at * tall, tall), tall)
            values = rows[s, here, :].astype(F32)
            centered = values - jnp.mean(values, axis=1, keepdims=True)
            variance = jnp.mean(centered * centered, axis=1, keepdims=True)
            normed[s, here, :] = (
                centered * lax.rsqrt(variance + 1e-05) * gain_ref[...] + shift_ref[...]
            ).astype(LOW)
            return carry

        lax.fori_loop(0, rows_here // tall, some, 0)

    norm(0)
    for step in range(1, count):
        for line in lines:
            line.arrive(step)
        if step + 1 < count:
            for line in lines:
                line.start(step + 1)

    half = depth // 2
    lanes = (pl.ds(0, half), pl.ds(half, half))
    dp_x = dp + 1 - 2 * lax.rem(dp, 2)
    dp_y = dp + 2 - 4 * (dp // 2)
    dp_xy = dp_x + 2 - 4 * (dp_x // 2)
    legs = ((0, to_x), (1, to_y), (0, to_y), (1, to_x), (0, to_y), (1, to_x))

    def plane(number, quarter):
        side, partner = legs[number]
        out = []
        for part in range(3):
            block = whole[part].at[:, core, quarter, :, lanes[side]]
            out.append(
                wire(
                    block, block, plane_send_sem.at[part, number], plane_recv_sem.at[part, number], partner
                )
            )
        return out

    leaving = [plane(number, quarter) for number, quarter in enumerate((dp, dp, dp, dp, dp_x, dp_y))]
    landing = [
        plane(number, quarter) for number, quarter in enumerate((dp_x, dp_y, dp_y, dp_x, dp_xy, dp_xy))
    ]

    def pass_on(number, at_core):
        quarter = (dp_x, dp_y, dp_xy)[number]
        out = []
        for part in range(3):
            block = whole[part].at[:, at_core, quarter]
            out.append(
                wire(
                    block, block, plane_swap_send.at[part, number], plane_swap_recv.at[part, number],
                    other_core(),
                )
            )
        return out

    def each(copies, what):
        for copy in copies:
            getattr(copy, what)()

    for number in range(4):
        each(leaving[number], "start")
    up_line.start(1)
    up_line.swap_own()
    norm(1)
    save = pltpu.make_async_copy(normed, normed_ref, local.at[0])
    save.start()
    halo = halo_ref.shape[1]
    halo_copy = wire(
        normed.at[:, pl.ds(rows_here - halo, halo), :], halo_ref, halo_send, halo_recv,
        {"mp": lax.rem(me + 1, mp)},
    )
    halo_copy.start()
    each(landing[0], "wait_recv")
    each(leaving[4], "start")
    each(landing[1], "wait_recv")
    each(leaving[5], "start")
    early = early_steps(count)
    up_line.arrive(1)
    up_line.start(2)
    each(landing[3], "wait_recv")
    each(pass_on(0, core), "start")
    each(landing[2], "wait_recv")
    each(pass_on(1, core), "start")
    each(landing[4], "wait_recv")
    each(landing[5], "wait_recv")
    each(pass_on(2, core), "start")
    for step in early[1:]:
        up_line.arrive(step)
        if step != early[-1]:
            up_line.start(step + 1)
    for line in lines:
        line.finish(range(1, count), True)
    up_line.finish(early, True)
    for number in range(6):
        each(leaving[number], "wait_send")
    for number in range(3):
        each(pass_on(number, core), "wait_send")
        each(pass_on(number, 1 - core), "wait_recv")
    for copy, landed in tap_copies:
        copy.wait_send()
        landed.wait_recv()
    halo_copy.wait()
    save.wait()


HALO = 16


def prepare(inputs, gain, shift, qk, v, out, taps, up):
    mp = lax.axis_size("mp")
    count = mp // 2
    rows_here, depth = inputs.shape[1:]
    anywhere = pl.BlockSpec(memory_space=pl.ANY)
    vmem = pl.BlockSpec(memory_space=pltpu.VMEM)
    dma = pltpu.SemaphoreType.DMA
    return pl.pallas_call(
        prepare_kernel,
        in_specs=[anywhere, vmem, vmem] + [anywhere] * 5,
        out_specs=[anywhere] * 7,
        out_shape=[
            jax.ShapeDtypeStruct((count, 2) + qk.shape, LOW),
            jax.ShapeDtypeStruct((count, 2) + v.shape, LOW),
            jax.ShapeDtypeStruct((count, 2) + out.shape, LOW),
            jax.ShapeDtypeStruct((mp,) + taps.shape, F32),
            jax.ShapeDtypeStruct(inputs.shape, LOW),
            jax.ShapeDtypeStruct((2, HALO, depth), LOW),
            jax.ShapeDtypeStruct((mp * up.shape[0], depth), LOW),
        ],
        scratch_shapes=[
            pltpu.VMEM(inputs.shape, LOW),
            pltpu.VMEM(inputs.shape, LOW),
            dma((6,)),
            dma((3, 6)),
            dma((3, 6)),
            dma((3, 3)),
            dma((3, 3)),
            dma((mp,)),
            dma((mp,)),
            dma,
            dma,
        ]
        + line_semaphores(count) * 4,
        compiler_params=pltpu.CompilerParams(
            collective_id=3, has_side_effects=True, vmem_limit_bytes=32 * 2**20
        ),
        cost_estimate=pl.CostEstimate(flops=2**36, bytes_accessed=2**26, transcendentals=0),
        name="prepare",
    )(inputs, gain.reshape(1, depth), shift.reshape(1, depth), qk, v, out, taps, up)


def exchange_kernel(halo, x_ref, o_ref, local, send, recv):
    mp = lax.axis_size("mp")
    me = lax.axis_index("mp")
    if halo is None:

        def source(at):
            return x_ref.at[:, :, pl.ds(pl.multiple_of(at * 128, 128), 128)]

        def target(at):
            return o_ref.at[:, at]
    else:
        tall = o_ref.shape[1]

        def source(at):
            return x_ref.at[:, pl.ds(pl.multiple_of(at * (tall - halo), 16), tall), :]

        def target(at):
            return o_ref.at[:, :, pl.ds(pl.multiple_of(at * 128, 128), 128)]

    barrier = pltpu.get_barrier_semaphore()
    for step in range(1, mp):
        pl.semaphore_signal(
            barrier, inc=1, device_id={"mp": lax.rem(me + step, mp)}, device_id_type=MESH
        )
    own = pltpu.make_async_copy(source(me), target(me), local)
    own.start()
    pl.semaphore_wait(barrier, mp - 1)
    copies = []
    for step in range(1, mp):
        to = lax.rem(me + step, mp)
        sems = (send.at[step], recv.at[step], {"mp": to})
        leaving = wire(source(to), target(me), *sems)
        landing = wire(source(to), target(lax.rem(me + mp - step, mp)), *sems)
        leaving.start()
        copies.append((leaving, landing))
    own.wait()
    for leaving, landing in copies:
        leaving.wait_send()
        landing.wait_recv()


def exchange(x, shape, halo, number, name):
    mp = lax.axis_size("mp")
    anywhere = pl.BlockSpec(memory_space=pl.ANY)
    return pl.pallas_call(
        partial(exchange_kernel, halo),
        in_specs=[anywhere],
        out_specs=anywhere,
        out_shape=jax.ShapeDtypeStruct(shape, x.dtype),
        scratch_shapes=[
            pltpu.SemaphoreType.DMA,
            pltpu.SemaphoreType.DMA((mp,)),
            pltpu.SemaphoreType.DMA((mp,)),
        ],
        compiler_params=pltpu.CompilerParams(collective_id=number, has_side_effects=True),
        cost_estimate=pl.CostEstimate(flops=2**34, bytes_accessed=2**24, transcendentals=0),
        name=name,
    )(x)


def heads_out(x, number, name):
    parts, rows_here, width = x.shape
    mp = lax.axis_size("mp")
    out = exchange(x, (parts, mp, rows_here, 128), None, number, name)
    return out.reshape(parts, mp * rows_here, 128)


def heads_back(x, rows_here, halo, number, name):
    mp = lax.axis_size("mp")
    return exchange(x, (x.shape[0], rows_here + halo, mp * 128), halo, number, name)


def feed_in_kernel(
    second_ref, up_ref, down_ref, all_ref, relu_ref, hidden_ref, down_all_ref, up_all_ref,
    rows, up, relu, hidden, local, outs, send, recv, *line_sems,
):
    depth = rows.shape[3]
    units = up.shape[0]
    share = down_ref.shape[0]
    count = lax.axis_size("mp") // 2
    z, core = mesh_place()
    lanes = (pl.ds(0, depth // 2), pl.ds(depth // 2, depth // 2))
    to_x, to_y = plane_partners()

    def line_place(ref):
        return lambda at, at_core: ref.at[
            pl.ds(pl.multiple_of((at_core * count + at) * share, 16), share), :
        ]

    own = [pltpu.make_async_copy(second_ref.at[s], rows.at[s, 0], local.at[s]) for s in range(2)]
    own.append(pltpu.make_async_copy(up_ref, up, local.at[2]))
    own.append(pltpu.make_async_copy(down_ref, line_place(down_all_ref)(z, core), local.at[4]))
    for copy in own:
        copy.start()
    for copy in own:
        copy.wait()
    greet_line(True)
    up_line = LineGather(line_place(up), *line_sems[:4])
    down_line = LineGather(line_place(down_all_ref), *line_sems[4:])

    def remote(s, source, target, half, partner, number):
        return wire(
            rows.at[s, source, :, lanes[half]], rows.at[s, target, :, lanes[half]],
            send.at[s, number], recv.at[s, number], partner,
        )

    copies = [
        [
            remote(s, 0, 1, 0, to_x, 0),
            remote(s, 0, 2, 1, to_y, 1),
            remote(s, 0, 2, 0, to_y, 2),
            remote(s, 0, 1, 1, to_x, 3),
            remote(s, 1, 3, 0, to_y, 4),
            remote(s, 2, 3, 1, to_x, 5),
        ]
        for s in range(2)
    ]
    pending = [None, None]
    done = [0]

    def tile(s, m):
        slot = done[0] % 2
        done[0] += 1
        if pending[slot] is not None:
            for copy in pending[slot]:
                copy.wait()

        def one(at, carry):
            columns = pl.ds(pl.multiple_of(at * CHUNK, CHUNK), CHUNK)
            kept = jnp.maximum(dot_nt(rows[s, m], up[columns, :]), 0.0)
            relu[slot, :, columns] = kept
            hidden[slot, :, columns] = (kept * kept).astype(LOW)
            return carry

        lax.fori_loop(0, units // CHUNK, one, 0)
        pending[slot] = [
            pltpu.make_async_copy(relu.at[slot], relu_ref.at[s, m], outs.at[slot, 0]),
            pltpu.make_async_copy(hidden.at[slot], hidden_ref.at[s, m], outs.at[slot, 1]),
        ]
        for copy in pending[slot]:
            copy.start()

    for number in range(4):
        copies[0][number].start()
    late = range(early_steps(count)[-1] + 1, count)
    for step in late:
        up_line.start(step)
        if step != late[-1]:
            up_line.arrive(step)
    copies[0][0].wait_recv()
    copies[0][4].start()
    copies[0][1].wait_recv()
    copies[0][5].start()
    copies[1][0].start()
    copies[1][1].start()
    up_line.arrive(late[-1])
    down_line.start(1)
    down_line.swap_own()
    up_line.finish(late, False)
    whole_up = pltpu.make_async_copy(up, up_all_ref, local.at[0])
    whole_up.start()
    tile(0, 0)
    tile(1, 0)
    copies[0][3].wait_recv()
    tile(0, 1)
    copies[0][2].wait_recv()
    copies[1][2].start()
    copies[1][3].start()
    tile(0, 2)
    down_line.arrive(1)
    down_line.start(2)
    copies[1][0].wait_recv()
    copies[1][4].start()
    copies[1][1].wait_recv()
    copies[1][5].start()
    copies[0][4].wait_recv()
    copies[0][5].wait_recv()
    tile(0, 3)
    down_line.arrive(2)
    for step in range(3, count):
        down_line.start(step)
        if step != count - 1:
            down_line.arrive(step)
    copies[1][3].wait_recv()
    tile(1, 1)
    copies[1][2].wait_recv()
    tile(1, 2)
    copies[1][4].wait_recv()
    copies[1][5].wait_recv()
    gathered = pltpu.make_async_copy(rows, all_ref, local.at[3])
    gathered.start()
    tile(1, 3)
    down_line.arrive(count - 1)
    down_line.finish(range(1, count), True)
    for slot in pending:
        for copy in slot:
            copy.wait()
    for s in range(2):
        for copy in copies[s]:
            copy.wait_send()
    gathered.wait()
    whole_up.wait()


def feed_in(second, up_all, down):
    rows_here, depth = second.shape[1:]
    units = up_all.shape[0]
    count = lax.axis_size("mp") // 2
    anywhere = pl.BlockSpec(memory_space=pl.ANY)
    return pl.pallas_call(
        feed_in_kernel,
        in_specs=[anywhere] * 3,
        out_specs=[anywhere] * 5,
        out_shape=[
            jax.ShapeDtypeStruct((2, 4, rows_here, depth), LOW),
            jax.ShapeDtypeStruct((2, 4, rows_here, units), F32),
            jax.ShapeDtypeStruct((2, 4, rows_here, units), LOW),
            jax.ShapeDtypeStruct((units, depth), LOW),
            jax.ShapeDtypeStruct((units, depth), LOW),
        ],
        scratch_shapes=[
            pltpu.VMEM((2, 4, rows_here, depth), LOW),
            pltpu.VMEM((units, depth), LOW),
            pltpu.VMEM((2, rows_here, units), F32),
            pltpu.VMEM((2, rows_here, units), LOW),
            pltpu.SemaphoreType.DMA((5,)),
            pltpu.SemaphoreType.DMA((2, 2)),
            pltpu.SemaphoreType.DMA((2, 6)),
            pltpu.SemaphoreType.DMA((2, 6)),
        ]
        + line_semaphores(count) * 2,
        compiler_params=pltpu.CompilerParams(
            collective_id=1, has_side_effects=True, vmem_limit_bytes=VMEM_LIMIT
        ),
        cost_estimate=pl.CostEstimate(
            flops=2 * 8 * rows_here * depth * units * 3,
            bytes_accessed=60 * 2**20,
            transcendentals=0,
        ),
        name="feed_in",
    )(second, up_all, down)


def feed_out_kernel(
    cot_ref, relu_ref, hidden_ref, up_ref, down_ref, grad_ref, feed_ref, back_ref,
    up, down, cot, relu, grad, part, arrived, feed, result, local, loads, outs, send, recv,
):
    units, depth = up.shape
    half = depth // 2
    lanes = (pl.ds(0, half), pl.ds(half, half))
    to_x, to_y = plane_partners()
    weights = [
        pltpu.make_async_copy(down_ref, down, local.at[0]),
        pltpu.make_async_copy(up_ref, up, local.at[1]),
    ]
    order = [(s, m) for s in range(2) for m in (3, 1, 2, 0)]

    def load(at):
        s, m = order[at]
        slot = at % 2
        return [
            pltpu.make_async_copy(cot_ref.at[s, m], cot.at[slot], loads.at[slot, 0]),
            pltpu.make_async_copy(relu_ref.at[s, m], relu.at[slot], loads.at[slot, 1]),
        ]

    for copy in load(0) + weights:
        copy.start()
    greet([to_x, to_y])
    for copy in weights:
        copy.wait()

    def remote(s, source, number, side, partner):
        return pltpu.make_async_remote_copy(
            src_ref=part.at[s, source, :, lanes[side]],
            dst_ref=arrived.at[s, number],
            send_sem=send.at[s, number],
            recv_sem=recv.at[s, number],
            device_id=partner,
            device_id_type=MESH,
        )

    copies = [
        [
            remote(s, 1, 0, 0, to_x),
            remote(s, 3, 1, 0, to_x),
            remote(s, 2, 2, 1, to_y),
            remote(s, 3, 3, 1, to_y),
            remote(s, 2, 4, 0, to_y),
            remote(s, 1, 5, 1, to_x),
        ]
        for s in range(2)
    ]
    saving = [None, None]

    def tile(at):
        s, m = order[at]
        slot = at % 2
        for copy in load(at):
            copy.wait()
        if at + 1 < len(order):
            for copy in load(at + 1):
                copy.start()
        if saving[slot] is not None:
            saving[slot].wait()

        def back(step, carry):
            columns = pl.ds(pl.multiple_of(step * CHUNK, CHUNK), CHUNK)
            product = dot_nt(cot[slot], down[columns, :])
            grad[slot, :, columns] = (product * 2.0 * relu[slot, :, columns]).astype(LOW)
            return carry

        lax.fori_loop(0, units // CHUNK, back, 0)
        saving[slot] = pltpu.make_async_copy(grad.at[slot], grad_ref.at[s, m], outs.at[slot])
        saving[slot].start()

        def through(step, carry):
            columns = pl.ds(pl.multiple_of(step * CHUNK, CHUNK), CHUNK)
            part[s, m, :, columns] = dot(grad[slot], up[:, columns]).astype(LOW)
            return carry

        lax.fori_loop(0, depth // CHUNK, through, 0)

    def second_leg(s):
        copies[s][1].wait_recv()
        part[s, 2, :, lanes[0]] = (
            part[s, 2, :, lanes[0]].astype(F32) + arrived[s, 1].astype(F32)
        ).astype(LOW)
        copies[s][4].start()
        copies[s][3].wait_recv()
        part[s, 1, :, lanes[1]] = (
            part[s, 1, :, lanes[1]].astype(F32) + arrived[s, 3].astype(F32)
        ).astype(LOW)
        copies[s][5].start()

    def finish(s):
        for side, near, last in ((0, 0, 4), (1, 2, 5)):
            copies[s][near].wait_recv()
            copies[s][last].wait_recv()
            result[:, lanes[side]] = (
                part[s, 0, :, lanes[side]].astype(F32)
                + arrived[s, near].astype(F32)
                + arrived[s, last].astype(F32)
            )
        done = pltpu.make_async_copy(result, back_ref.at[s], local.at[2])
        done.start()
        return done

    def send_after(at):
        s, m = order[at]
        for number in {3: (1, 3), 1: (0,), 2: (2,), 0: ()}[m]:
            copies[s][number].start()

    for at in range(5):
        tile(at)
        send_after(at)
    second_leg(0)
    for at in range(5, 8):
        tile(at)
        send_after(at)
    done = finish(0)

    feeding = [None, None]

    def feed_load(at):
        s, m = order[at]
        return pltpu.make_async_copy(hidden_ref.at[s, m], cot.at[at % 2], loads.at[at % 2, 0])

    def feed_tile(at):
        s, m = order[at]
        slot = at % 2
        feed_load(at).wait()
        if at + 1 < len(order):
            feed_load(at + 1).start()
        if feeding[slot] is not None:
            feeding[slot].wait()

        def one(step, carry):
            columns = pl.ds(pl.multiple_of(step * CHUNK, CHUNK), CHUNK)
            feed[slot, :, columns] = dot(cot[slot], down[:, columns]).astype(LOW)
            return carry

        lax.fori_loop(0, depth // CHUNK, one, 0)
        feeding[slot] = pltpu.make_async_copy(feed.at[slot], feed_ref.at[s, m], outs.at[2 + slot])
        feeding[slot].start()

    feed_load(0).start()
    for at in range(2):
        feed_tile(at)
    second_leg(1)
    for at in range(2, 8):
        feed_tile(at)
    done.wait()
    finish(1).wait()
    for slot in range(2):
        saving[slot].wait()
        feeding[slot].wait()
    for s in range(2):
        for number in range(6):
            copies[s][number].wait_send()


def feed_out(cot_all, relu, hidden, up_all, down_all):
    rows_here, depth = cot_all.shape[2:]
    units = up_all.shape[0]
    anywhere = pl.BlockSpec(memory_space=pl.ANY)
    return pl.pallas_call(
        feed_out_kernel,
        in_specs=[anywhere] * 5,
        out_specs=[anywhere] * 3,
        out_shape=[
            jax.ShapeDtypeStruct((2, 4, rows_here, units), LOW),
            jax.ShapeDtypeStruct((2, 4, rows_here, depth), LOW),
            jax.ShapeDtypeStruct((2, rows_here, depth), F32),
        ],
        scratch_shapes=[
            pltpu.VMEM((units, depth), LOW),
            pltpu.VMEM((units, depth), LOW),
            pltpu.VMEM((2, rows_here, depth), LOW),
            pltpu.VMEM((2, rows_here, units), F32),
            pltpu.VMEM((2, rows_here, units), LOW),
            pltpu.VMEM((2, 4, rows_here, depth), LOW),
            pltpu.VMEM((2, 6, rows_here, depth // 2), LOW),
            pltpu.VMEM((2, rows_here, depth), LOW),
            pltpu.VMEM((rows_here, depth), F32),
            pltpu.SemaphoreType.DMA((3,)),
            pltpu.SemaphoreType.DMA((2, 2)),
            pltpu.SemaphoreType.DMA((4,)),
            pltpu.SemaphoreType.DMA((2, 6)),
            pltpu.SemaphoreType.DMA((2, 6)),
        ],
        compiler_params=pltpu.CompilerParams(
            collective_id=2, has_side_effects=True, vmem_limit_bytes=VMEM_LIMIT
        ),
        cost_estimate=pl.CostEstimate(
            flops=2 * 8 * rows_here * depth * units * 4,
            bytes_accessed=60 * 2**20,
            transcendentals=0,
        ),
        name="feed_out",
    )(cot_all, relu, hidden, up_all, down_all)


def plane_send(block, mask):
    return lax.ppermute(block, "dp", [(d, d ^ mask) for d in range(lax.axis_size("dp"))])


def plane_gather(block):
    half = block.shape[1] // 2
    one, two = block[:, :half], block[:, half:]
    one_x = plane_send(one, 1)
    two_y = plane_send(two, 2)
    one_y = plane_send(one, 2)
    two_x = plane_send(two, 1)
    one_xy = plane_send(one_x, 2)
    two_xy = plane_send(two_y, 1)
    return [
        block,
        jnp.concatenate([one_x, two_x], axis=1),
        jnp.concatenate([one_y, two_y], axis=1),
        jnp.concatenate([one_xy, two_xy], axis=1),
    ]


def plane_scatter(part):
    half = part.shape[2] // 2
    wide = lambda block: block.astype(F32)
    one, two = part[:, :, :half], part[:, :, half:]
    one_in = plane_send(one[1::2], 1)
    two_in = plane_send(two[2:], 2)
    one_sum = (wide(one[2]) + wide(one_in[1])).astype(LOW)
    two_sum = (wide(two[1]) + wide(two_in[1])).astype(LOW)
    one_last = plane_send(one_sum, 2)
    two_last = plane_send(two_sum, 1)
    return jnp.concatenate(
        [
            wide(one[0]) + wide(one_in[0]) + wide(one_last),
            wide(two[0]) + wide(two_in[0]) + wide(two_last),
        ],
        axis=1,
    )


def plane_order(blocks, axis):
    me = lax.axis_index("dp")
    stacked = jnp.stack(blocks, axis=0)
    return jnp.concatenate(
        [lax.dynamic_index_in_dim(stacked, me ^ d, 0, keepdims=False) for d in range(4)], axis=axis
    )


def chips():
    return lax.axis_size("mp") // 2


def line_send(block, step, senders):
    count = chips()
    pairs = []
    for z in senders:
        if 0 <= z < count and 0 <= z + step < count:
            pairs += [(2 * z + c, 2 * (z + step) + c) for c in range(2)]
    return lax.ppermute(block, "mp", pairs)


def core_swap(block):
    return lax.ppermute(block, "mp", [(i, i ^ 1) for i in range(lax.axis_size("mp"))])


def line_scatter(parts):
    count = chips()

    def add(left, right):
        return (left.astype(F32) + right.astype(F32)).astype(LOW)

    up, down = parts[count - 1], parts[1]
    for step in range(1, count):
        up_in = line_send(up, 1, range(0, step))
        down_in = line_send(down, -1, range(count - step, count))
        if step < count - 1:
            up = add(up_in, parts[count - step - 1])
            down = add(down_in, parts[step + 1])
    return (parts[0].astype(F32) + up_in.astype(F32) + down_in.astype(F32)).astype(LOW)


def per_device(
    inputs,
    cotangent,
    short_lengths,
    long_lengths,
    norm1_gain,
    norm1_bias,
    query_weight,
    key_weight,
    value_weight,
    query_kernel,
    key_kernel,
    value_kernel,
    out_weight,
    norm2_gain,
    norm2_bias,
    up_weight,
    down_weight,
):
    rows_here = inputs.shape[1]
    width = inputs.shape[2]
    mp = lax.axis_size("mp")
    dp = lax.axis_size("dp")
    me_dp = lax.axis_index("dp")
    me_mp = lax.axis_index("mp")
    group = rows_here * mp
    hidden_here = up_weight.shape[1]
    share = hidden_here // dp

    starts = jnp.stack(
        [document_starts(short_lengths[0], group), document_starts(long_lengths[0], group)]
    )
    rows = inputs.astype(F32)

    def quarters(weight):
        return weight.reshape(4, weight.shape[0] // 4, width)

    qk_own = jnp.concatenate([query_weight, key_weight], axis=1).T
    up_own = lax.dynamic_slice_in_dim(up_weight, me_dp * share, share, 1).T
    down_own = lax.dynamic_slice_in_dim(down_weight, me_dp * share, share, 0)
    taps_own = jnp.pad(
        jnp.concatenate([query_kernel, key_kernel, value_kernel], axis=1), ((0, 5), (0, HD))
    )
    qk_all, v_all, out_all, taps_all, normed, halo_rows, up_early = prepare(
        inputs, norm1_gain, norm1_bias, quarters(qk_own), quarters(value_weight.T), quarters(out_weight), taps_own, up_own,
    )
    qk_all = qk_all.reshape(mp * 2 * HD, width)
    v_all = v_all.reshape(mp * HD, width)
    out_all = out_all.reshape(mp * HD, width)
    taps = taps_all[:, :3].transpose(1, 0, 2)
    qk_taps = taps[:, :, : 2 * HD].reshape(3, mp * 2 * HD)
    v_taps = taps[:, :, 2 * HD : 3 * HD].reshape(3, mp * HD)

    cot_all = jnp.stack([jnp.stack(plane_gather(cotangent[index])) for index in range(2)])

    normed_ext = jnp.concatenate([halo_rows, normed], axis=1)
    raw_qk = jnp.einsum("srd,cd->src", normed_ext, qk_all, preferred_element_type=F32)
    raw_v = jnp.einsum("srd,cd->src", normed_ext, v_all, preferred_element_type=F32)
    places = jnp.arange(group, dtype=jnp.int32)
    offsets = lax.dynamic_slice_in_dim(
        jnp.pad(places[None, :] - starts, ((0, 0), (0, HALO))), me_mp * rows_here, rows_here + HALO, 1
    )[:, :, None]
    here = offsets[:, :rows_here]

    def conv(raw, tap):
        return (
            tap[0] * raw[:, HALO:]
            + jnp.where(here >= 1, tap[1] * raw[:, HALO - 1 : -1], 0.0)
            + jnp.where(here >= 2, tap[2] * raw[:, HALO - 2 : -2], 0.0)
        ).astype(LOW)

    mixed_qk = conv(raw_qk, qk_taps)
    mixed_v = conv(raw_v, v_taps)

    def side_by_side(pair):
        split = pair.reshape(2, rows_here, mp, HD)
        return split.transpose(1, 2, 0, 3).reshape(1, rows_here, mp * 2 * HD)

    def apart(joint):
        split = joint.reshape(joint.shape[1], mp, 2, HD)
        return split.transpose(2, 0, 1, 3).reshape(2, joint.shape[1], mp * HD)

    mixed = heads_out(jnp.concatenate([mixed_qk, side_by_side(mixed_v)], axis=0), 4, "mixed_out")
    attended_head, wide, total = attend(mixed, starts)
    attended = apart(heads_back(attended_head, rows_here, 0, 5, "attended_back"))
    middle = rows + dot(attended, out_all)
    second = layer_norm(middle, norm2_gain, norm2_bias).astype(LOW)

    second_all, relu, hidden, down_all, up_all = feed_in(second, up_early, down_own)
    grad_pre, feed_part, grad_second = feed_out(cot_all, relu, hidden, up_all, down_all)
    down_part = jnp.einsum(
        "gf,gd->fd",
        hidden.reshape(-1, hidden.shape[3]),
        cot_all.reshape(-1, width),
        preferred_element_type=F32,
    ).astype(LOW)
    up_part = jnp.einsum(
        "gf,gd->fd",
        grad_pre.reshape(-1, hidden.shape[3]),
        second_all.reshape(-1, width),
        preferred_element_type=F32,
    ).astype(LOW)
    results = jnp.stack(
        [(middle[index] + plane_scatter(feed_part[index])).astype(LOW) for index in range(2)]
    )

    def add_low(left, right):
        return (left.astype(F32) + right.astype(F32)).astype(LOW)

    core = me_mp % 2
    mine = share * (mp // 2)

    def reduce_units(part):
        own = lax.dynamic_slice_in_dim(part, core * mine, mine, 0)
        other = lax.dynamic_slice_in_dim(part, (1 - core) * mine, mine, 0)
        total = add_low(own, core_swap(other)).reshape(mp // 2, share, width)
        z = me_mp // 2
        return line_scatter(
            [
                lax.dynamic_index_in_dim(total, (z + k) % (mp // 2), 0, keepdims=False)
                for k in range(mp // 2)
            ]
        )

    up_mine = reduce_units(up_part).T
    down_mine = reduce_units(down_part)
    up_grad = plane_order(plane_gather(up_mine), axis=1).astype(F32)
    down_grad = plane_order(plane_gather(down_mine), axis=0).astype(F32)

    def norm_back(values, gain, grad):
        flat = values.reshape(-1, width)
        unused, pull = jax.vjp(layer_norm, flat, gain, norm1_bias)
        grad_rows, grad_gain, grad_shift = pull(grad.reshape(-1, width))
        return grad_rows.reshape(values.shape), grad_gain, grad_shift

    grad_middle, gain_two, shift_two = norm_back(middle, norm2_gain, grad_second)
    grad_middle = grad_middle + cotangent.astype(F32)
    branch = grad_middle.astype(LOW)
    out_part = jnp.einsum("srh,srd->hd", attended, branch, preferred_element_type=F32).astype(LOW)
    grad_attended = jnp.einsum("srd,hd->srh", branch, out_all, preferred_element_type=F32).astype(LOW)
    grad_head = heads_out(side_by_side(grad_attended), 6, "attended_grad_out")
    grad_mixed_head = attend_back(mixed, grad_head, wide, total, starts, HALO)
    grad_mixed = heads_back(grad_mixed_head, rows_here, HALO, 7, "mixed_grad_back")
    grad_qk = grad_mixed[:2].astype(F32)
    grad_v = apart(grad_mixed[2:]).astype(F32)

    def conv_back(grad, raw, tap):
        after_one = jnp.where(offsets[:, 1 : rows_here + 1] >= 1, grad[:, 1 : rows_here + 1], 0.0)
        after_two = jnp.where(offsets[:, 2 : rows_here + 2] >= 2, grad[:, 2 : rows_here + 2], 0.0)
        own = grad[:, :rows_here]
        grad_raw = (tap[0] * own + tap[1] * after_one + tap[2] * after_two).astype(LOW)
        grad_tap = jnp.stack(
            [
                jnp.sum(own * raw[:, HALO:], axis=(0, 1)),
                jnp.sum(jnp.where(here >= 1, own, 0.0) * raw[:, HALO - 1 : -1], axis=(0, 1)),
                jnp.sum(jnp.where(here >= 2, own, 0.0) * raw[:, HALO - 2 : -2], axis=(0, 1)),
            ]
        )
        return grad_raw, grad_tap

    grad_raw_qk, grad_tap_qk = conv_back(grad_qk, raw_qk, qk_taps)
    grad_raw_v, grad_tap_v = conv_back(grad_v, raw_v, v_taps)
    qk_part = jnp.einsum("src,srd->cd", grad_raw_qk, normed, preferred_element_type=F32).astype(LOW)
    v_part = jnp.einsum("src,srd->cd", grad_raw_v, normed, preferred_element_type=F32).astype(LOW)
    grad_normed = dot(grad_raw_qk, qk_all) + dot(grad_raw_v, v_all)
    grad_input, gain_one, shift_one = norm_back(rows, norm1_gain, grad_normed)
    input_grads = grad_middle + grad_input

    joint = jnp.concatenate(
        [
            qk_part.reshape(mp, 2 * HD, width),
            v_part.reshape(mp, HD, width),
            out_part.reshape(mp, HD, width),
        ],
        axis=1,
    ).reshape(mp * 4 * HD, width)
    joint_grad = lax.psum(
        lax.psum_scatter(joint, "mp", scatter_dimension=0, tiled=True), "dp"
    ).astype(F32)
    small_sum, tap_sum = lax.psum(
        (
            jnp.stack([gain_one, shift_one, gain_two, shift_two]),
            jnp.concatenate([grad_tap_qk, grad_tap_v], axis=1),
        ),
        ("dp", "mp"),
    )
    qk_tap_grad = lax.dynamic_slice_in_dim(tap_sum, me_mp * 2 * HD, 2 * HD, 1)
    v_tap_grad = lax.dynamic_slice_in_dim(tap_sum, mp * 2 * HD + me_mp * HD, HD, 1)
    return (
        results,
        input_grads,
        small_sum[0],
        small_sum[1],
        joint_grad[:HD].T,
        joint_grad[HD : 2 * HD].T,
        joint_grad[2 * HD : 3 * HD].T,
        qk_tap_grad[:, :HD],
        qk_tap_grad[:, HD:],
        v_tap_grad,
        joint_grad[3 * HD :],
        small_sum[2],
        small_sum[3],
        up_grad,
        down_grad,
    )


def solution(mesh):
    return jax.shard_map(
        per_device,
        mesh=mesh,
        in_specs=(
            P(None, ("dp", "mp"), None),
            P(None, ("dp", "mp"), None),
            P("dp", None),
            P("dp", None),
            P(),
            P(),
            P(None, "mp"),
            P(None, "mp"),
            P(None, "mp"),
            P(None, "mp"),
            P(None, "mp"),
            P(None, "mp"),
            P("mp", None),
            P(),
            P(),
            P(None, "mp"),
            P("mp", None),
        ),
        out_specs=(
            P(None, ("dp", "mp"), None),
            P(None, ("dp", "mp"), None),
            P(),
            P(),
            P(None, "mp"),
            P(None, "mp"),
            P(None, "mp"),
            P(None, "mp"),
            P(None, "mp"),
            P(None, "mp"),
            P("mp", None),
            P(),
            P(),
            P(None, "mp"),
            P("mp", None),
        ),
        check_vma=False,
    )
```

time: 1280 us -> 1240 us (0.969)
  Pallas kernels: 67.6 us -> 507 us
  matrix products: 232 us -> 84.7 us
  starting transfers between devices: 192 us -> 72.9 us
  waiting for transfers between devices: 369 us -> 287 us
  local copies, waits for them, and re-layouts: 164 us -> 108 us
  other arithmetic: 148 us -> 109 us
  blocking collectives: 86.9 us -> 51.4 us
    pallas_call x0 -> x7, Pallas kernels: none -> 436 us  [the longest x1 142 us: feed_in(): pl.pallas_call(feed_in_kernel, in_specs=[anywhere] * 3, out_specs=[anywhe...]
    ppermute x52 -> x32, waiting for transfers between devices: 202 us -> 91.1 us  [plane_send(): lax.ppermute(block, 'dp', [(d, d ^ mask) for d in range(lax.axis_size('dp...]
    dot_general x14 -> x8, matrix products: 155 us -> 73.1 us  [the longest x1 29 us: per_device(): jnp.einsum('gf,gd->fd', hidden.reshape(-1, hidden.shape[3]), cot_all.resh...]
    all_to_all x8 -> x0, starting transfers between devices: 68.9 us -> none  [the longest x2 29.5 us: per_device(): lax.all_to_all(by_head, 'mp', 0, 0, tiled=True).reshape(group, 3 * HD)]
    dot_general x8 -> x3, matrix products: 76.4 us -> 11.5 us  [dot(): return jnp.dot(left, right, preferred_element_type=F32)]
    unnamed x352 -> x207, local copies, waits for them, and re-layouts: 77.4 us -> 35.3 us
    ppermute x24 -> x12, waiting for transfers between devices: 96.6 us -> 134 us  [line_send(): return lax.ppermute(block, 'mp', pairs)]
    ppermute x24 -> x12, starting transfers between devices: 59 us -> 28.1 us  [line_send(): return lax.ppermute(block, 'mp', pairs)]
  transfers between devices with their start and end apart: 94 -> 48, of which waited for: 35 -> 22; matrix products, arithmetic and copies ran while one was open for 36% -> 16% of each run, Pallas kernels for 5% -> 25%
where the time goes in v2:
time: 1240 us
  Pallas kernels  507 us (41%)
  waiting for transfers between devices  287 us (23%)
  other arithmetic  109 us (9%)
  local copies, waits for them, and re-layouts  108 us (9%)
  matrix products  84.7 us (7%)
  starting transfers between devices  72.9 us (6%)
  blocking collectives  51.4 us (4%)
  between operations  16.3 us (1%)
    pallas_call x1, Pallas kernels, feed_in(): pl.pallas_call(feed_in_kernel, in_specs=[anywhere] * 3, out_specs=[anywhe...  142 us
    ppermute x12, waiting for transfers between devices, line_send(): return lax.ppermute(block, 'mp', pairs)  134 us
    pallas_call x4, Pallas kernels, exchange(): pl.pallas_call(partial(exchange_kernel, halo), in_specs=[anywhere], out_s...  113 us
    pallas_call x1, Pallas kernels, feed_out(): pl.pallas_call(feed_out_kernel, in_specs=[anywhere] * 5, out_specs=[anywh...  105 us
    ppermute x32, waiting for transfers between devices, plane_send(): lax.ppermute(block, 'dp', [(d, d ^ mask) for d in range(lax.axis_size('dp...  91.1 us
    pallas_call x1, Pallas kernels, prepare(): pl.pallas_call(prepare_kernel, in_specs=[anywhere, vmem, vmem] + [anywher...  75.9 us
    psum x1, waiting for transfers between devices, per_device(): lax.psum(lax.psum_scatter(joint, 'mp', scatter_dimension=0, tiled=True),...  62.5 us
    psum x1, blocking collectives, per_device(): lax.psum((jnp.stack([gain_one, shift_one, gain_two, shift_two]), jnp.conc...  51.4 us
  transfers between devices with their start and end apart: 48, of which 22 were waited for; matrix products, arithmetic and copies ran while one was open for 16% of the time, Pallas kernels for 25%

profile of v2, /device:TPU:0, one launch (start us, length us, event | category | flops | bytes accessed | tf_op | source)
XLA Modules:
  0.0 1237.1 jit_solution(11082380318734433627)
XLA Ops:
  7.2 3.9 fusion.38
  28.6 75.9 %prepare.1 = (bf16[4,2,4,32,2048]{4,3,2,1,0:T(8,128)(2,1)S(1)}, bf16[4,2,4,16,2048]{4,3,2,1,0:T(8,128)(2,1)S(1)}, bf16[4,2,4,16,2048]{4,3,2,1,0:T(8,128)(2,1)S(1...) custom-call(bf16[2,320,2048]{2,1,0:T(8,128)(2,1)S(1)} %copy-done, ...), custom_call_target="tpu_custom_call" | custom-call | flops 68719476736 | bytes 67108864 | tf_op jit(solution)/shard_map/prepare/pallas_call | solution.py:553
  118.7 4.6 fusion.48
  128.6 4.6 add_convert_fusion.3
  134.6 34.9 %mixed_out.1 = bf16[3,8,320,128]{3,2,1,0:T(8,128)(2,1)} custom-call(bf16[3,320,1024]{2,1,0:T(8,128)(2,1)} %pad_maximum_fusion.5.x_ref), custom_call_target="tpu_custom_call" | custom-call | flops 17179869184 | bytes 16777216 | tf_op jit(solution)/shard_map/mixed_out/pallas_call | solution.py:632
  171.1 33.6 %attend.1 = (bf16[1,2560,128]{2,1,0:T(8,128)(2,1)S(1)}, f32[2,64,2560]{2,1,0:T(8,128)S(1)}, f32[2,1,2560]{2,1,0:T(1,128)S(1)}) custom-call(s32[2,10]{1,0:T(2,128)S(1)} %and_select_fusion.first_ref, s32[2,1,2560]{2,1,0:T(1,128)S(1)} %broadcast_in_dim.118.start_ref, bf16[3,2560,128]{2,1,0:T(8,128)(2,1)S(1)} %bitcast.243, bf16[3,2560,128]{2,1,0:T(8,128)(2,1)S(1)} %bitcast.244), custom_call_target="tpu_custom_call" | custom-call | flops 17179869184 | bytes 5242880 | tf_op jit(solution)/shard_map/attend/pallas_call | solution.py:102
  206.6 24.9 %attended_back.1 = bf16[1,320,1024]{2,1,0:T(8,128)(2,1)} custom-call(bf16[1,2560,128]{2,1,0:T(8,128)(2,1)} %copy-done.22), custom_call_target="tpu_custom_call" | custom-call | flops 17179869184 | bytes 16777216 | tf_op jit(solution)/shard_map/attended_back/pallas_call | solution.py:632
  243.5 142.5 %feed_in.1 = (bf16[2,4,320,2048]{3,2,1,0:T(8,128)(2,1)}, f32[2,4,320,2048]{3,2,1,0:T(8,128)}, bf16[2,4,320,2048]{3,2,1,0:T(8,128)(2,1)}, bf16[2048,2048]{1,0:T(8,128)(2,1)}, bf16[2048,2048]{1,0:T(8,128)(2,1)}) custom-call(bf16[2,320,2048]{2,1,0:T(8,128)(2,1)} %add_convert_fusion.2.second_ref, bf16[2048,2048]{1,0:T(8,128)(2,1)} %get-tuple-element.40.up_ref, ...), custom_call_target="tpu_custom_call" | custom-call | flops 64424509440 | bytes 62914560 | tf_op jit(solution)/shard_map/feed_in/pallas_call | solution.py:797
  388.3 4.2 collective-permute-start.6
  400.0 8.3 collective-permute-done.6
  411.5 10.9 collective-permute-done.7
  424.2 12.2 collective-permute-done.5
  439.5 10.6 collective-permute-done.11
  453.3 8.8 pad_maximum_fusion.cot_ref
  462.1 29.0 %bitcast_convert_fusion = bf16[2048,2048]{1,0:T(8,128)(2,1)} fusion(bf16[2,4,320,2048]{3,2,1,0:T(8,128)(2,1)} %get-tuple-element.42.hidden_ref, bf16[1,4,320,2048]{3,2,1,0:T(8,128)(2,1)} %maximum_bitcast_fusion.1, bf16[1,4,320,2048]{3,2,1,0:T(8,128)(2,1)} %maximum_bitcast_fusion), kind=kOutput, calls=%fused_computation | convolution fusion | flops 21484273664 | bytes 29360128 | tf_op jit(solution)/shard_map/gf,gd->fd/dot_general | solution.py:1201
  491.1 104.5 %feed_out.1 = (bf16[2,4,320,2048]{3,2,1,0:T(8,128)(2,1)}, bf16[2,4,320,2048]{3,2,1,0:T(8,128)(2,1)}, f32[2,320,2048]{2,1,0:T(8,128)}) custom-call(bf16[2,4,320,2048]{3,2,1,0:T(8,128)(2,1)} %pad_maximum_fusion.cot_ref, f32[2,4,320,2048]{3,2,1,0:T(8,128)} %get-tuple-element.41.relu_ref, bf16[2,4,320,2048]{3,2,1,0:T(8,128)(2,1)} %get-tuple-element.42.hidden_ref, ...), custom_call_target="tpu_custom_call" | custom-call | flops 85899345920 | bytes 62914560 | tf_op jit(solution)/shard_map/feed_out/pallas_call | solution.py:993
  595.7 6.3 multiply_reduce_fusion
  611.7 13.7 %attended_grad_out.1 = bf16[1,8,320,128]{3,2,1,0:T(8,128)(2,1)} custom-call(bf16[1,320,1024]{2,1,0:T(8,128)(2,1)} %copy.70.x_ref), custom_call_target="tpu_custom_call" | custom-call | flops 17179869184 | bytes 16777216 | tf_op jit(solution)/shard_map/attended_grad_out/pallas_call | solution.py:632
  627.8 37.3 %attend_back.1.x_ref = bf16[3,2576,128]{2,1,0:T(8,128)(2,1)S(1)} custom-call(s32[2,10]{1,0:T(2,128)S(1)} %and_select_fusion.first_ref, s32[2,1,2560]{2,1,0:T(1,128)S(1)} %broadcast_in_dim.118.start_ref, bf16[3,2560,128]{2,1,0:T(8,128)(2,1)S(1)} %bitcast.245, bf16[3,2560,128]{2,1,0:T(8,128)(2,1)S(1)} %bitcast.246, bf16[1,2560,128]{2,1,0:T(8,128)(2,1)S(1)} %bitcast.247, ...), custom_call_target="tpu_custom_call" | custom-call | flops 34359738368 | bytes 5242880 | tf_op jit(solution)/shard_map/attend_back/pallas_call | solution.py:195
  666.4 39.9 %mixed_grad_back.1 = bf16[3,336,1024]{2,1,0:T(8,128)(2,1)} custom-call(bf16[3,2576,128]{2,1,0:T(8,128)(2,1)} %copy-done.19), custom_call_target="tpu_custom_call" | custom-call | flops 17179869184 | bytes 16777216 | tf_op jit(solution)/shard_map/mixed_grad_back/pallas_call | solution.py:632
  710.7 10.2 slice_bitcast_fusion.1
  736.1 5.5 collective-permute-start.12
  744.1 5.0 bitcast_convert_fusion.2
  761.0 27.7 %bitcast_convert_fusion.1 = bf16[2048,2048]{1,0:T(8,128)(2,1)S(1)} fusion(bf16[2,4,320,2048]{3,2,1,0:T(8,128)(2,1)} %get-tuple-element.49, bf16[2,4,320,2048]{3,2,1,0:T(8,128)(2,1)} %get-tuple-element.50), kind=kOutput, calls=%fused_computation.1 | convolution fusion | flops 21479030784 | bytes 29360128 | tf_op jit(solution)/shard_map/gf,gd->fd/dot_general | solution.py:1207
  793.3 5.0 constant_dynamic-slice_fusion
  804.1 3.8 pad_maximum_fusion.1
  808.1 5.7 fusion.50
  818.6 51.4 %all-reduce.2 = (f32[4,2048]{1,0:T(4,128)S(1)}, f32[3,1536]{1,0:T(4,128)S(1)}) all-reduce(f32[4,2048]{1,0:T(4,128)S(1)} %pad_maximum_fusion.7, f32[3,1536]{1,0:T(4,128)S(1)} %maximum_maximum_fusion), channel_id=1, replica_groups=mesh['dp'=4,'mp'=8] {'dp','mp'}, use_global_device_ids=true, to_apply=%region_16.17 | all-reduce | flops 12800 | bytes 102400 | tf_op jit(solution)/shard_map/psum | solution.py:1290
  870.1 8.5 add_convert_fusion
  884.0 3.8 add_add_fusion.2
  887.8 37.7 %collective-permute-done.34 = bf16[256,2048]{1,0:T(8,128)(2,1)S(1)} collective-permute-done((bf16[256,2048]{1,0:T(8,128)(2,1)S(1)}, bf16[256,2048]{1,0:T(8,128)(2,1)S(1)}, u32[]{:S(2)}, u32[]{:S(2)}) %collective-permute-start.34) | collective-permute-done | bytes 1048608 | tf_op jit(solution)/shard_map/ppermute | solution.py:1088
  926.0 4.5 collective-permute-start.35
  930.5 17.5 %collective-permute-done.21 = bf16[256,2048]{1,0:T(8,128)(2,1)S(1)} collective-permute-done((bf16[256,2048]{1,0:T(8,128)(2,1)S(1)}, bf16[256,2048]{1,0:T(8,128)(2,1)S(1)}, u32[]{:S(2)}, u32[]{:S(2)}) %collective-permute-start.21) | collective-permute-done | bytes 1048608 | tf_op jit(solution)/shard_map/ppermute | solution.py:1088
  948.4 4.5 collective-permute-start.22
  954.5 15.9 %collective-permute-done.35 = bf16[256,2048]{1,0:T(8,128)(2,1)S(1)} collective-permute-done((bf16[256,2048]{1,0:T(8,128)(2,1)S(1)}, bf16[256,2048]{1,0:T(8,128)(2,1)S(1)}, u32[]{:S(2)}, u32[]{:S(2)}) %collective-permute-start.35) | collective-permute-done | bytes 1048608 | tf_op jit(solution)/shard_map/ppermute | solution.py:1088
  974.0 18.6 %collective-permute-done.22 = bf16[256,2048]{1,0:T(8,128)(2,1)S(1)} collective-permute-done((bf16[256,2048]{1,0:T(8,128)(2,1)S(1)}, bf16[256,2048]{1,0:T(8,128)(2,1)S(1)}, u32[]{:S(2)}, u32[]{:S(2)}) %collective-permute-start.22) | collective-permute-done | bytes 1048608 | tf_op jit(solution)/shard_map/ppermute | solution.py:1088
  1007.0 8.2 collective-permute-done.13
  1019.2 8.8 collective-permute-done.17
  1030.8 5.4 collective-permute-start.36
  1046.1 13.0 %collective-permute-done.36 = bf16[256,2048]{1,0:T(8,128)(2,1)} collective-permute-done((bf16[256,2048]{1,0:T(8,128)(2,1)}, bf16[256,2048]{1,0:T(8,128)(2,1)}, u32[]{:S(2)}, u32[]{:S(2)}) %collective-permute-start.36) | collective-permute-done | bytes 1048608 | tf_op jit(solution)/shard_map/ppermute | solution.py:1088
  1059.1 14.4 %collective-permute-done.39 = bf16[256,2048]{1,0:T(8,128)(2,1)} collective-permute-done((bf16[256,2048]{1,0:T(8,128)(2,1)}, bf16[256,2048]{1,0:T(8,128)(2,1)}, u32[]{:S(2)}, u32[]{:S(2)}) %collective-permute-start.39) | collective-permute-done | bytes 1048608 | tf_op jit(solution)/shard_map/ppermute | solution.py:1088
  1080.2 15.8 %collective-permute-done.26 = bf16[256,2048]{1,0:T(8,128)(2,1)} collective-permute-done((bf16[256,2048]{1,0:T(8,128)(2,1)}, bf16[256,2048]{1,0:T(8,128)(2,1)}, u32[]{:S(2)}, u32[]{:S(2)}) %collective-permute-start.26) | collective-permute-done | bytes 1048608 | tf_op jit(solution)/shard_map/ppermute | solution.py:1088
  1106.3 5.8 collective-permute-done.27
  1114.9 9.5 collective-permute-done.30
  1128.7 11.1 collective-permute-done.31
  1156.0 4.0 maximum_convert_fusion
  1160.0 3.9 maximum_convert_fusion.1
  1163.9 62.5 %all-reduce.5.cloned.1.call-done = bf16[256,2048]{1,0:T(8,128)(2,1)} async-done(((bf16[256,2048]{1,0:T(8,128)(2,1)}), bf16[256,2048]{1,0:T(8,128)(2,1)}) %all-reduce.5.cloned.1.call-update) | async-done | bytes 1048592 | tf_op jit(solution)/shard_map/psum | solution.py:1287
  (407 shorter events, 222.3 us)
Async XLA Ops:
  7.2 1145.9 %reduce-scatter.2.cloned.1.call-start = ((), (), s32[]{:S(2)}) async-start(), calls=%async_computation.1 | async-start | bytes 9437184 | tf_op jit(solution)/shard_map/reduce_scatter | solution.py:1288
  12.4 376.0 %collective-permute-start.2 = (bf16[320,1024]{1,0:T(8,128)(2,1)}, bf16[320,1024]{1,0:T(8,128)(2,1)}, u32[]{:S(2)}, u32[]{:S(2)}) collective-permute-start(bf16[320,1024]{1,0:T(8,128)(2,1)} %get-tuple-element.108), channel_id=1, source_target_pairs={{0,16},{8,24},{16,0},{24,8},{1,17},{9,25},{17,1},{25,9},{2,18},{10... | collective-permute-start | bytes 1966088 | tf_op jit(solution)/shard_map/ppermute | solution.py:1031
  15.3 377.2 %collective-permute-start = (bf16[320,1024]{1,0:T(8,128)(2,1)}, bf16[320,1024]{1,0:T(8,128)(2,1)}, u32[]{:S(2)}, u32[]{:S(2)}) collective-permute-start(bf16[320,1024]{1,0:T(8,128)(2,1)} %get-tuple-element.108), channel_id=1, source_target_pairs={{0,8},{8,0},{16,24},{24,16},{1,9},{9,1},{17,25},{25,17},{2,10},{10... | collective-permute-start | bytes 1966088 | tf_op jit(solution)/shard_map/ppermute | solution.py:1031
  16.8 376.3 %collective-permute-start.3 = (bf16[320,1024]{1,0:T(8,128)(2,1)}, bf16[320,1024]{1,0:T(8,128)(2,1)}, u32[]{:S(2)}, u32[]{:S(2)}) collective-permute-start(bf16[320,1024]{1,0:T(8,128)(2,1)} %get-tuple-element.109), channel_id=1, source_target_pairs={{0,16},{8,24},{16,0},{24,8},{1,17},{9,25},{17,1},{25,9},{2,18},{10... | collective-permute-start | bytes 1966088 | tf_op jit(solution)/shard_map/ppermute | solution.py:1031
  17.3 377.3 %collective-permute-start.1 = (bf16[320,1024]{1,0:T(8,128)(2,1)}, bf16[320,1024]{1,0:T(8,128)(2,1)}, u32[]{:S(2)}, u32[]{:S(2)}) collective-permute-start(bf16[320,1024]{1,0:T(8,128)(2,1)} %get-tuple-element.109), channel_id=1, source_target_pairs={{0,8},{8,0},{16,24},{24,16},{1,9},{9,1},{17,25},{25,17},{2,10},{10... | collective-permute-start | bytes 1966088 | tf_op jit(solution)/shard_map/ppermute | solution.py:1031
  18.6 378.0 %collective-permute-start.8 = (bf16[320,1024]{1,0:T(8,128)(2,1)}, bf16[320,1024]{1,0:T(8,128)(2,1)}, u32[]{:S(2)}, u32[]{:S(2)}) collective-permute-start(bf16[320,1024]{1,0:T(8,128)(2,1)} %get-tuple-element.110), channel_id=1, source_target_pairs={{0,16},{8,24},{16,0},{24,8},{1,17},{9,25},{17,1},{25,9},{2,18},{10... | collective-permute-start | bytes 1966088 | tf_op jit(solution)/shard_map/ppermute | solution.py:1031
  388.3 20.0 %collective-permute-start.6 = (bf16[320,1024]{1,0:T(8,128)(2,1)}, bf16[320,1024]{1,0:T(8,128)(2,1)S(1)}, u32[]{:S(2)}, u32[]{:S(2)}) collective-permute-start(bf16[320,1024]{1,0:T(8,128)(2,1)} %get-tuple-element.110), channel_id=1, source_target_pairs={{0,8},{8,0},{16,24},{24,16},{1,9},{9,1},{17,25},{25,17},{2,10},{10... | collective-permute-start | bytes 1966088 | tf_op jit(solution)/shard_map/ppermute | solution.py:1031
  392.5 17.6 %collective-permute-start.9 = (bf16[320,1024]{1,0:T(8,128)(2,1)S(1)}, bf16[320,1024]{1,0:T(8,128)(2,1)S(1)}, u32[]{:S(2)}, u32[]{:S(2)}) collective-permute-start(bf16[320,1024]{1,0:T(8,128)(2,1)S(1)} %copy-done.51), channel_id=1, source_target_pairs={{0,16},{8,24},{16,0},{24,8},{1,17},{9,25},{17,1},{25,9},{2,18},{10... | collective-permute-start | bytes 1966088 | tf_op jit(solution)/shard_map/ppermute | solution.py:1031
  393.1 29.2 %collective-permute-start.7 = (bf16[320,1024]{1,0:T(8,128)(2,1)S(1)}, bf16[320,1024]{1,0:T(8,128)(2,1)S(1)}, u32[]{:S(2)}, u32[]{:S(2)}) collective-permute-start(bf16[320,1024]{1,0:T(8,128)(2,1)S(1)} %copy-done.51), channel_id=1, source_target_pairs={{0,8},{8,0},{16,24},{24,16},{1,9},{9,1},{17,25},{25,17},{2,10},{10... | collective-permute-start | bytes 1966088 | tf_op jit(solution)/shard_map/ppermute | solution.py:1031
  394.6 41.8 %collective-permute-start.5 = (bf16[320,1024]{1,0:T(8,128)(2,1)}, bf16[320,1024]{1,0:T(8,128)(2,1)S(1)}, u32[]{:S(2)}, u32[]{:S(2)}) collective-permute-start(bf16[320,1024]{1,0:T(8,128)(2,1)} %collective-permute-done.3), channel_id=1, source_target_pairs={{0,8},{8,0},{16,24},{24,16},{1,9},{9,1},{17,25},{25,17},{2,10},{10... | collective-permute-start | bytes 1966088 | tf_op jit(solution)/shard_map/ppermute | solution.py:1031
  396.6 27.6 %collective-permute-start.4 = (bf16[320,1024]{1,0:T(8,128)(2,1)}, bf16[320,1024]{1,0:T(8,128)(2,1)S(1)}, u32[]{:S(2)}, u32[]{:S(2)}) collective-permute-start(bf16[320,1024]{1,0:T(8,128)(2,1)} %collective-permute-done), channel_id=1, source_target_pairs={{0,16},{8,24},{16,0},{24,8},{1,17},{9,25},{17,1},{25,9},{2,18},{10... | collective-permute-start | bytes 1966088 | tf_op jit(solution)/shard_map/ppermute | solution.py:1031
  408.3 31.2 %collective-permute-start.10 = (bf16[320,1024]{1,0:T(8,128)(2,1)S(1)}, bf16[320,1024]{1,0:T(8,128)(2,1)S(1)}, u32[]{:S(2)}, u32[]{:S(2)}) collective-permute-start(bf16[320,1024]{1,0:T(8,128)(2,1)S(1)} %collective-permute-done.6), channel_id=1, source_target_pairs={{0,16},{8,24},{16,0},{24,8},{1,17},{9,25},{17,1},{25,9},{2,18},{10... | collective-permute-start | bytes 1966088 | tf_op jit(solution)/shard_map/ppermute | solution.py:1031
  410.1 40.0 %collective-permute-start.11 = (bf16[320,1024]{1,0:T(8,128)(2,1)S(1)}, bf16[320,1024]{1,0:T(8,128)(2,1)S(1)}, u32[]{:S(2)}, u32[]{:S(2)}) collective-permute-start(bf16[320,1024]{1,0:T(8,128)(2,1)S(1)} %collective-permute-done.9), channel_id=1, source_target_pairs={{0,8},{8,0},{16,24},{24,16},{1,9},{9,1},{17,25},{25,17},{2,10},{10... | collective-permute-start | bytes 1966088 | tf_op jit(solution)/shard_map/ppermute | solution.py:1031
  729.4 269.9 %collective-permute-start.18 = (bf16[2,320,1024]{2,1,0:T(8,128)(2,1)}, bf16[2,320,1024]{2,1,0:T(8,128)(2,1)}, u32[]{:S(2)}, u32[]{:S(2)}) collective-permute-start(bf16[2,320,1024]{2,1,0:T(8,128)(2,1)} %slice.360), channel_id=1, source_target_pairs={{0,16},{8,24},{16,0},{24,8},{1,17},{9,25},{17,1},{25,9},{2,18},{10... | collective-permute-start | bytes 3932168 | tf_op jit(solution)/shard_map/ppermute | solution.py:1031
  730.7 264.0 %collective-permute-start.14 = (bf16[2,320,1024]{2,1,0:T(8,128)(2,1)}, bf16[2,320,1024]{2,1,0:T(8,128)(2,1)}, u32[]{:S(2)}, u32[]{:S(2)}) collective-permute-start(bf16[2,320,1024]{2,1,0:T(8,128)(2,1)} %slice.349), channel_id=1, source_target_pairs={{0,16},{8,24},{16,0},{24,8},{1,17},{9,25},{17,1},{25,9},{2,18},{10... | collective-permute-start | bytes 3932168 | tf_op jit(solution)/shard_map/ppermute | solution.py:1031
  736.1 259.6 %collective-permute-start.12 = (bf16[2,320,1024]{2,1,0:T(8,128)(2,1)}, bf16[2,320,1024]{2,1,0:T(8,128)(2,1)}, u32[]{:S(2)}, u32[]{:S(2)}) collective-permute-start(bf16[2,320,1024]{2,1,0:T(8,128)(2,1)} %slice.279), channel_id=1, source_target_pairs={{0,8},{8,0},{16,24},{24,16},{1,9},{9,1},{17,25},{25,17},{2,10},{10... | collective-permute-start | bytes 3932168 | tf_op jit(solution)/shard_map/ppermute | solution.py:1031
  798.3 71.9 %collective-permute-start.33 = (bf16[1024,2048]{1,0:T(8,128)(2,1)}, bf16[1024,2048]{1,0:T(8,128)(2,1)}, u32[]{:S(2)}, u32[]{:S(2)}) collective-permute-start(bf16[1024,2048]{1,0:T(8,128)(2,1)} %constant_dynamic-slice_fusion), channel_id=1, source_target_pairs={{0,1},{1,0},{2,3},{3,2},{4,5},{5,4},{6,7},{7,6},{8,9},{9,8},{10,11... | collective-permute-start | bytes 12582920 | tf_op jit(solution)/shard_map/ppermute | solution.py:1092
  798.8 71.3 %collective-permute-start.20 = (bf16[1024,2048]{1,0:T(8,128)(2,1)}, bf16[1024,2048]{1,0:T(8,128)(2,1)}, u32[]{:S(2)}, u32[]{:S(2)}) collective-permute-start(bf16[1024,2048]{1,0:T(8,128)(2,1)} %constant_dynamic-slice_fusion.5), channel_id=1, source_target_pairs={{0,1},{1,0},{2,3},{3,2},{4,5},{5,4},{6,7},{7,6},{8,9},{9,8},{10,11... | collective-permute-start | bytes 12582920 | tf_op jit(solution)/shard_map/ppermute | solution.py:1092
  808.0 418.5 %all-reduce.5.cloned.1.call-start = ((), (), s32[]{:S(2)}) async-start(), calls=%async_computation.2 | async-start | bytes 2097152 | tf_op jit(solution)/shard_map/psum | solution.py:1287
  878.8 46.7 %collective-permute-start.34 = (bf16[256,2048]{1,0:T(8,128)(2,1)S(1)}, bf16[256,2048]{1,0:T(8,128)(2,1)S(1)}, u32[]{:S(2)}, u32[]{:S(2)}) collective-permute-start(bf16[256,2048]{1,0:T(8,128)(2,1)S(1)} %dynamic-slice_bitcast_fusion.5), channel_id=1, source_target_pairs={{0,2},{1,3},{8,10},{9,11},{16,18},{17,19},{24,26},{25,27}} | collective-permute-start | bytes 3145736 | tf_op jit(solution)/shard_map/ppermute | solution.py:1088
  882.2 65.8 %collective-permute-start.21 = (bf16[256,2048]{1,0:T(8,128)(2,1)S(1)}, bf16[256,2048]{1,0:T(8,128)(2,1)S(1)}, u32[]{:S(2)}, u32[]{:S(2)}) collective-permute-start(bf16[256,2048]{1,0:T(8,128)(2,1)S(1)} %dynamic-slice_bitcast_fusion.7), channel_id=1, source_target_pairs={{0,2},{1,3},{8,10},{9,11},{16,18},{17,19},{24,26},{25,27}} | collective-permute-start | bytes 3145736 | tf_op jit(solution)/shard_map/ppermute | solution.py:1088
  926.0 44.5 %collective-permute-start.35 = (bf16[256,2048]{1,0:T(8,128)(2,1)S(1)}, bf16[256,2048]{1,0:T(8,128)(2,1)S(1)}, u32[]{:S(2)}, u32[]{:S(2)}) collective-permute-start(bf16[256,2048]{1,0:T(8,128)(2,1)S(1)} %fusion.18), channel_id=1, source_target_pairs={{0,2},{1,3},{2,4},{3,5},{8,10},{9,11},{10,12},{11,13},{16,18},{17,... | collective-permute-start | bytes 3145736 | tf_op jit(solution)/shard_map/ppermute | solution.py:1088
  948.4 44.2 %collective-permute-start.22 = (bf16[256,2048]{1,0:T(8,128)(2,1)S(1)}, bf16[256,2048]{1,0:T(8,128)(2,1)S(1)}, u32[]{:S(2)}, u32[]{:S(2)}) collective-permute-start(bf16[256,2048]{1,0:T(8,128)(2,1)S(1)} %fusion.16), channel_id=1, source_target_pairs={{0,2},{1,3},{2,4},{3,5},{8,10},{9,11},{10,12},{11,13},{16,18},{17,... | collective-permute-start | bytes 3145736 | tf_op jit(solution)/shard_map/ppermute | solution.py:1088
  970.5 30.3 %collective-permute-start.16 = (bf16[2,320,1024]{2,1,0:T(8,128)(2,1)S(1)}, bf16[2,320,1024]{2,1,0:T(8,128)(2,1)S(1)}, u32[]{:S(2)}, u32[]{:S(2)}) collective-permute-start(bf16[2,320,1024]{2,1,0:T(8,128)(2,1)S(1)} %slice.292), channel_id=1, source_target_pairs={{0,8},{8,0},{16,24},{24,16},{1,9},{9,1},{17,25},{25,17},{2,10},{10... | collective-permute-start | bytes 3932168 | tf_op jit(solution)/shard_map/ppermute | solution.py:1031
  992.6 11.0 collective-permute-start.37
  994.7 11.1 collective-permute-start.24
  997.5 17.7 %collective-permute-start.13 = (bf16[320,1024]{1,0:T(8,128)(2,1)S(1)}, bf16[320,1024]{1,0:T(8,128)(2,1)S(1)}, u32[]{:S(2)}, u32[]{:S(2)}) collective-permute-start(bf16[320,1024]{1,0:T(8,128)(2,1)S(1)} %get-tuple-element.82), channel_id=1, source_target_pairs={{0,16},{8,24},{16,0},{24,8},{1,17},{9,25},{17,1},{25,9},{2,18},{10... | collective-permute-start | bytes 1966088 | tf_op jit(solution)/shard_map/ppermute | solution.py:1031
  999.3 17.7 %collective-permute-start.15 = (bf16[320,1024]{1,0:T(8,128)(2,1)S(1)}, bf16[320,1024]{1,0:T(8,128)(2,1)S(1)}, u32[]{:S(2)}, u32[]{:S(2)}) collective-permute-start(bf16[320,1024]{1,0:T(8,128)(2,1)S(1)} %get-tuple-element.83), channel_id=1, source_target_pairs={{0,8},{8,0},{16,24},{24,16},{1,9},{9,1},{17,25},{25,17},{2,10},{10... | collective-permute-start | bytes 1966088 | tf_op jit(solution)/shard_map/ppermute | solution.py:1031
  1002.4 25.6 %collective-permute-start.17 = (bf16[320,1024]{1,0:T(8,128)(2,1)S(1)}, bf16[320,1024]{1,0:T(8,128)(2,1)S(1)}, u32[]{:S(2)}, u32[]{:S(2)}) collective-permute-start(bf16[320,1024]{1,0:T(8,128)(2,1)S(1)} %get-tuple-element.86), channel_id=1, source_target_pairs={{0,16},{8,24},{16,0},{24,8},{1,17},{9,25},{17,1},{25,9},{2,18},{10... | collective-permute-start | bytes 1966088 | tf_op jit(solution)/shard_map/ppermute | solution.py:1031
  1003.6 25.4 %collective-permute-start.19 = (bf16[320,1024]{1,0:T(8,128)(2,1)S(1)}, bf16[320,1024]{1,0:T(8,128)(2,1)S(1)}, u32[]{:S(2)}, u32[]{:S(2)}) collective-permute-start(bf16[320,1024]{1,0:T(8,128)(2,1)S(1)} %get-tuple-element.87), channel_id=1, source_target_pairs={{0,8},{8,0},{16,24},{24,16},{1,9},{9,1},{17,25},{25,17},{2,10},{10... | collective-permute-start | bytes 1966088 | tf_op jit(solution)/shard_map/ppermute | solution.py:1031
  1005.8 33.5 %collective-permute-start.38 = (bf16[256,2048]{1,0:T(8,128)(2,1)S(1)}, bf16[256,2048]{1,0:T(8,128)(2,1)S(1)}, u32[]{:S(2)}, u32[]{:S(2)}) collective-permute-start(bf16[256,2048]{1,0:T(8,128)(2,1)S(1)} %fusion.19), channel_id=1, source_target_pairs={{4,2},{5,3},{6,4},{7,5},{12,10},{13,11},{14,12},{15,13},{20,18},{2... | collective-permute-start | bytes 3145736 | tf_op jit(solution)/shard_map/ppermute | solution.py:1088
  1015.2 26.8 %collective-permute-start.25 = (bf16[256,2048]{1,0:T(8,128)(2,1)S(1)}, bf16[256,2048]{1,0:T(8,128)(2,1)S(1)}, u32[]{:S(2)}, u32[]{:S(2)}) collective-permute-start(bf16[256,2048]{1,0:T(8,128)(2,1)S(1)} %fusion.17), channel_id=1, source_target_pairs={{4,2},{5,3},{6,4},{7,5},{12,10},{13,11},{14,12},{15,13},{20,18},{2... | collective-permute-start | bytes 3145736 | tf_op jit(solution)/shard_map/ppermute | solution.py:1088
  1030.8 28.3 %collective-permute-start.36 = (bf16[256,2048]{1,0:T(8,128)(2,1)}, bf16[256,2048]{1,0:T(8,128)(2,1)}, u32[]{:S(2)}, u32[]{:S(2)}) collective-permute-start(bf16[256,2048]{1,0:T(8,128)(2,1)} %get-tuple-element.70), channel_id=1, source_target_pairs={{0,2},{1,3},{2,4},{3,5},{4,6},{5,7},{8,10},{9,11},{10,12},{11,13},... | collective-permute-start | bytes 3145736 | tf_op jit(solution)/shard_map/ppermute | solution.py:1088
  1036.2 42.4 %collective-permute-start.23 = (bf16[256,2048]{1,0:T(8,128)(2,1)}, bf16[256,2048]{1,0:T(8,128)(2,1)}, u32[]{:S(2)}, u32[]{:S(2)}) collective-permute-start(bf16[256,2048]{1,0:T(8,128)(2,1)} %get-tuple-element.72), channel_id=1, source_target_pairs={{0,2},{1,3},{2,4},{3,5},{4,6},{5,7},{8,10},{9,11},{10,12},{11,13},... | collective-permute-start | bytes 3145736 | tf_op jit(solution)/shard_map/ppermute | solution.py:1088
  1040.6 32.8 %collective-permute-start.39 = (bf16[256,2048]{1,0:T(8,128)(2,1)}, bf16[256,2048]{1,0:T(8,128)(2,1)}, u32[]{:S(2)}, u32[]{:S(2)}) collective-permute-start(bf16[256,2048]{1,0:T(8,128)(2,1)} %add_convert_fusion.4), channel_id=1, source_target_pairs={{2,0},{3,1},{4,2},{5,3},{6,4},{7,5},{10,8},{11,9},{12,10},{13,11},... | collective-permute-start | bytes 3145736 | tf_op jit(solution)/shard_map/ppermute | solution.py:1088
  1043.3 52.7 %collective-permute-start.26 = (bf16[256,2048]{1,0:T(8,128)(2,1)}, bf16[256,2048]{1,0:T(8,128)(2,1)}, u32[]{:S(2)}, u32[]{:S(2)}) collective-permute-start(bf16[256,2048]{1,0:T(8,128)(2,1)} %add_convert_fusion.6), channel_id=1, source_target_pairs={{2,0},{3,1},{4,2},{5,3},{6,4},{7,5},{10,8},{11,9},{12,10},{13,11},... | collective-permute-start | bytes 3145736 | tf_op jit(solution)/shard_map/ppermute | solution.py:1088
  1075.6 22.7 %collective-permute-start.42 = (bf16[256,1024]{1,0:T(8,128)(2,1)S(1)}, bf16[256,1024]{1,0:T(8,128)(2,1)S(1)}, u32[]{:S(2)}, u32[]{:S(2)}) collective-permute-start(bf16[256,1024]{1,0:T(8,128)(2,1)S(1)} %get-tuple-element.112), channel_id=1, source_target_pairs={{0,16},{8,24},{16,0},{24,8},{1,17},{9,25},{17,1},{25,9},{2,18},{10... | collective-permute-start | bytes 1572872 | tf_op jit(solution)/shard_map/ppermute | solution.py:1031
  1075.7 22.7 %collective-permute-start.40 = (bf16[256,1024]{1,0:T(8,128)(2,1)S(1)}, bf16[256,1024]{1,0:T(8,128)(2,1)}, u32[]{:S(2)}, u32[]{:S(2)}) collective-permute-start(bf16[256,1024]{1,0:T(8,128)(2,1)S(1)} %get-tuple-element.112), channel_id=1, source_target_pairs={{0,8},{8,0},{16,24},{24,16},{1,9},{9,1},{17,25},{25,17},{2,10},{10... | collective-permute-start | bytes 1572872 | tf_op jit(solution)/shard_map/ppermute | solution.py:1031
  1075.8 30.4 %collective-permute-start.43 = (bf16[256,1024]{1,0:T(8,128)(2,1)S(1)}, bf16[256,1024]{1,0:T(8,128)(2,1)}, u32[]{:S(2)}, u32[]{:S(2)}) collective-permute-start(bf16[256,1024]{1,0:T(8,128)(2,1)S(1)} %get-tuple-element.113), channel_id=1, source_target_pairs={{0,16},{8,24},{16,0},{24,8},{1,17},{9,25},{17,1},{25,9},{2,18},{10... | collective-permute-start | bytes 1572872 | tf_op jit(solution)/shard_map/ppermute | solution.py:1031
  1078.7 23.5 %collective-permute-start.41 = (bf16[256,1024]{1,0:T(8,128)(2,1)S(1)}, bf16[256,1024]{1,0:T(8,128)(2,1)S(1)}, u32[]{:S(2)}, u32[]{:S(2)}) collective-permute-start(bf16[256,1024]{1,0:T(8,128)(2,1)S(1)} %get-tuple-element.113), channel_id=1, source_target_pairs={{0,8},{8,0},{16,24},{24,16},{1,9},{9,1},{17,25},{25,17},{2,10},{10... | collective-permute-start | bytes 1572872 | tf_op jit(solution)/shard_map/ppermute | solution.py:1031
  1098.2 28.3 %collective-permute-start.29 = (bf16[2048,128]{0,1:T(8,128)(2,1)S(1)}, bf16[2048,128]{0,1:T(8,128)(2,1)S(1)}, u32[]{:S(2)}, u32[]{:S(2)}) collective-permute-start(bf16[2048,128]{0,1:T(8,128)(2,1)S(1)} %get-tuple-element.114), channel_id=1, source_target_pairs={{0,16},{8,24},{16,0},{24,8},{1,17},{9,25},{17,1},{25,9},{2,18},{10... | collective-permute-start | bytes 1572872 | tf_op jit(solution)/shard_map/ppermute | solution.py:1031
  1098.3 13.8 %collective-permute-start.27 = (bf16[2048,128]{0,1:T(8,128)(2,1)S(1)}, bf16[2048,128]{0,1:T(8,128)(2,1)S(1)}, u32[]{:S(2)}, u32[]{:S(2)}) collective-permute-start(bf16[2048,128]{0,1:T(8,128)(2,1)S(1)} %get-tuple-element.114), channel_id=1, source_target_pairs={{0,8},{8,0},{16,24},{24,16},{1,9},{9,1},{17,25},{25,17},{2,10},{10... | collective-permute-start | bytes 1572872 | tf_op jit(solution)/shard_map/ppermute | solution.py:1031
  1098.4 26.0 %collective-permute-start.30 = (bf16[2048,128]{0,1:T(8,128)(2,1)S(1)}, bf16[2048,128]{0,1:T(8,128)(2,1)S(1)}, u32[]{:S(2)}, u32[]{:S(2)}) collective-permute-start(bf16[2048,128]{0,1:T(8,128)(2,1)S(1)} %get-tuple-element.115), channel_id=1, source_target_pairs={{0,16},{8,24},{16,0},{24,8},{1,17},{9,25},{17,1},{25,9},{2,18},{10... | collective-permute-start | bytes 1572872 | tf_op jit(solution)/shard_map/ppermute | solution.py:1031
  1102.1 26.5 %collective-permute-start.28 = (bf16[2048,128]{0,1:T(8,128)(2,1)S(1)}, bf16[2048,128]{0,1:T(8,128)(2,1)S(1)}, u32[]{:S(2)}, u32[]{:S(2)}) collective-permute-start(bf16[2048,128]{0,1:T(8,128)(2,1)S(1)} %get-tuple-element.115), channel_id=1, source_target_pairs={{0,8},{8,0},{16,24},{24,16},{1,9},{9,1},{17,25},{25,17},{2,10},{10... | collective-permute-start | bytes 1572872 | tf_op jit(solution)/shard_map/ppermute | solution.py:1031
  1106.2 42.7 %collective-permute-start.44 = (bf16[256,1024]{1,0:T(8,128)(2,1)}, bf16[256,1024]{1,0:T(8,128)(2,1)}, u32[]{:S(2)}, u32[]{:S(2)}) collective-permute-start(bf16[256,1024]{1,0:T(8,128)(2,1)} %collective-permute-done.40), channel_id=1, source_target_pairs={{0,16},{8,24},{16,0},{24,8},{1,17},{9,25},{17,1},{25,9},{2,18},{10... | collective-permute-start | bytes 1572872 | tf_op jit(solution)/shard_map/ppermute | solution.py:1031
  1112.1 27.8 %collective-permute-start.31 = (bf16[2048,128]{0,1:T(8,128)(2,1)S(1)}, bf16[2048,128]{0,1:T(8,128)(2,1)S(1)}, u32[]{:S(2)}, u32[]{:S(2)}) collective-permute-start(bf16[2048,128]{0,1:T(8,128)(2,1)S(1)} %collective-permute-done.27), channel_id=1, source_target_pairs={{0,16},{8,24},{16,0},{24,8},{1,17},{9,25},{17,1},{25,9},{2,18},{10... | collective-permute-start | bytes 1572872 | tf_op jit(solution)/shard_map/ppermute | solution.py:1031
  1124.4 15.5 %collective-permute-start.32 = (bf16[2048,128]{0,1:T(8,128)(2,1)S(1)}, bf16[2048,128]{0,1:T(8,128)(2,1)S(1)}, u32[]{:S(2)}, u32[]{:S(2)}) collective-permute-start(bf16[2048,128]{0,1:T(8,128)(2,1)S(1)} %collective-permute-done.30), channel_id=1, source_target_pairs={{0,8},{8,0},{16,24},{24,16},{1,9},{9,1},{17,25},{25,17},{2,10},{10... | collective-permute-start | bytes 1572872 | tf_op jit(solution)/shard_map/ppermute | solution.py:1031
  1126.5 22.4 %collective-permute-start.45 = (bf16[256,1024]{1,0:T(8,128)(2,1)}, bf16[256,1024]{1,0:T(8,128)(2,1)}, u32[]{:S(2)}, u32[]{:S(2)}) collective-permute-start(bf16[256,1024]{1,0:T(8,128)(2,1)} %collective-permute-done.43), channel_id=1, source_target_pairs={{0,8},{8,0},{16,24},{24,16},{1,9},{9,1},{17,25},{25,17},{2,10},{10... | collective-permute-start | bytes 1572872 | tf_op jit(solution)/shard_map/ppermute | solution.py:1031
  (101 other events, 1150.7 us)
Sparse Core Ops, SparseCore 0:
  808.1 116.3 reduce-scatter.1
  1153.2 73.2 all-reduce.4

commit v3 on v2

--- a/solution.py
+++ b/solution.py
@@ -360,7 +360,7 @@
 def prepare_kernel(
     inputs_ref, gain_ref, shift_ref, qk_ref, v_ref, out_ref, taps_ref, up_ref,
     all_qk_ref, all_v_ref, all_out_ref, all_taps_ref, normed_ref, halo_ref, up_all_ref,
-    rows, normed, local, *sems,
+    rows, normed, all_qk, all_v, all_out, up_all, local, *sems,
 ):
     mp = lax.axis_size("mp")
     dp = lax.axis_index("dp")
@@ -371,14 +371,14 @@
     to_x, to_y = plane_partners()
     share = up_ref.shape[0]
     owned = (qk_ref, v_ref, out_ref)
-    whole = (all_qk_ref, all_v_ref, all_out_ref)
+    whole = (all_qk, all_v, all_out)
     (plane_send_sem, plane_recv_sem, plane_swap_send, plane_swap_recv) = sems[:4]
     taps_send, taps_recv, halo_send, halo_recv = sems[4:8]
     line_sems = [sems[8 + 4 * part : 12 + 4 * part] for part in range(4)]
 
     def up_place(at, at_core):
-        start = pl.multiple_of((at_core * count + at) * share, 16)
-        return up_all_ref.at[pl.ds(start, share), :]
+        start = pl.multiple_of((2 * at + at_core) * share, 16)
+        return up_all.at[pl.ds(start, share), :]
 
     loads = [
         pltpu.make_async_copy(inputs_ref, rows, local.at[0]),
@@ -538,6 +538,16 @@
         landed.wait_recv()
     halo_copy.wait()
     save.wait()
+    saves = [
+        pltpu.make_async_copy(here, there, local.at[2 + at])
+        for at, (here, there) in enumerate(
+            ((all_qk, all_qk_ref), (all_v, all_v_ref), (all_out, all_out_ref), (up_all, up_all_ref))
+        )
+    ]
+    for copy in saves:
+        copy.start()
+    for copy in saves:
+        copy.wait()
 
 
 HALO = 16
@@ -566,6 +576,10 @@
         scratch_shapes=[
             pltpu.VMEM(inputs.shape, LOW),
             pltpu.VMEM(inputs.shape, LOW),
+            pltpu.VMEM((count, 2) + qk.shape, LOW),
+            pltpu.VMEM((count, 2) + v.shape, LOW),
+            pltpu.VMEM((count, 2) + out.shape, LOW),
+            pltpu.VMEM((mp * up.shape[0], depth), LOW),
             dma((6,)),
             dma((3, 6)),
             dma((3, 6)),
@@ -578,14 +592,117 @@
         ]
         + line_semaphores(count) * 4,
         compiler_params=pltpu.CompilerParams(
-            collective_id=3, has_side_effects=True, vmem_limit_bytes=32 * 2**20
+            collective_id=3, has_side_effects=True, vmem_limit_bytes=VMEM_LIMIT
         ),
         cost_estimate=pl.CostEstimate(flops=2**36, bytes_accessed=2**26, transcendentals=0),
         name="prepare",
     )(inputs, gain.reshape(1, depth), shift.reshape(1, depth), qk, v, out, taps, up)
 
 
-def exchange_kernel(halo, x_ref, o_ref, local, send, recv):
+def weight_grad(left_ref, pieces, whole, tiles, outs, out_ref, load, tile_sem, out_sem):
+    wide = tiles.shape[2]
+    steps = left_ref.shape[1] // wide
+    if len(pieces) == 1:
+        loading = [pltpu.make_async_copy(pieces[0], whole, load.at[0])]
+    else:
+        tall = whole.shape[0] // 8
+        loading = []
+        for s in range(2):
+            for m in range(4):
+                target = whole.at[pl.ds((4 * s + m) * tall, tall), :]
+                loading += piece_copies(pieces, s, m, target, load.at[s, m])
+
+    def tile(at, slot):
+        columns = pl.ds(pl.multiple_of(at * wide, wide), wide)
+        return pltpu.make_async_copy(left_ref.at[:, columns], tiles.at[slot], tile_sem.at[slot])
+
+    def out(at, slot):
+        rows = pl.ds(pl.multiple_of(at * wide, wide), wide)
+        return pltpu.make_async_copy(outs.at[slot], out_ref.at[rows, :], out_sem.at[slot])
+
+    for copy in loading:
+        copy.start()
+    tile(0, 0).start()
+    for copy in loading:
+        copy.wait()
+
+    def one(at, carry):
+        slot = lax.rem(at, 2)
+        tile(at, slot).wait()
+
+        @pl.when(at + 1 < steps)
+        def _():
+            tile(at + 1, 1 - slot).start()
+
+        @pl.when(at >= 2)
+        def _():
+            out(at - 2, slot).wait()
+
+        outs[slot] = lax.dot_general(
+            tiles[slot], whole[...], (((0,), (0,)), ((), ())), preferred_element_type=F32
+        ).astype(LOW)
+        out(at, slot).start()
+        return carry
+
+    lax.fori_loop(0, steps, one, 0)
+    out(steps - 2, lax.rem(steps - 2, 2)).wait()
+    out(steps - 1, lax.rem(steps - 1, 2)).wait()
+
+
+def weight_grad_scratch(rows, depth, pieces):
+    dma = pltpu.SemaphoreType.DMA
+    return [
+        pltpu.VMEM((rows, depth), LOW),
+        pltpu.VMEM((2, rows, 256), LOW),
+        pltpu.VMEM((2, 256, depth), LOW),
+        dma((1,)) if pieces == 1 else dma((2, 4, 2)),
+        dma((2,)),
+        dma((2,)),
+    ]
+
+
+def whole_weight_grad(left, right):
+    rows, units = left.shape
+    depth = right[0].shape[-1]
+    anywhere = pl.BlockSpec(memory_space=pl.ANY)
+
+    def kernel(left_ref, *refs):
+        pieces, out_ref, scratch = refs[: len(right)], refs[len(right)], refs[len(right) + 1 :]
+        weight_grad(left_ref, pieces, *scratch[:3], out_ref, *scratch[3:])
+
+    return pl.pallas_call(
+        kernel,
+        in_specs=[anywhere] * (1 + len(right)),
+        out_specs=anywhere,
+        out_shape=jax.ShapeDtypeStruct((units, depth), LOW),
+        scratch_shapes=weight_grad_scratch(rows, depth, len(right)),
+        compiler_params=pltpu.CompilerParams(vmem_limit_bytes=48 * 2**20),
+        cost_estimate=pl.CostEstimate(
+            flops=2 * rows * units * depth, bytes_accessed=2**25, transcendentals=0
+        ),
+        name="weight_grad",
+    )(left, *right)
+
+
+def carry_copies(carried, targets, send, recv):
+    partners = plane_partners()
+    return [
+        wire(ref, target, send.at[at], recv.at[at], partners[way])
+        for at, ((way, ref), target) in enumerate(zip(carried, targets))
+    ]
+
+
+def exchange_kernel(halo, pieces, ways, x_ref, *refs):
+    count = 1 + pieces if pieces else 0
+    left_ref, right_refs = (refs[0], refs[1:count]) if pieces else (None, ())
+    carried = list(zip(ways, refs[count : count + len(ways)]))
+    refs = refs[count + len(ways) :]
+    o_ref, refs = refs[0], refs[1:]
+    if pieces:
+        grad_ref, refs = refs[0], refs[1:]
+    targets, refs = refs[: len(ways)], refs[len(ways) :]
+    landed, local, send, recv = refs[:4]
+    refs = refs[4:]
     mp = lax.axis_size("mp")
     me = lax.axis_index("mp")
     if halo is None:
@@ -594,7 +711,7 @@
             return x_ref.at[:, :, pl.ds(pl.multiple_of(at * 128, 128), 128)]
 
         def target(at):
-            return o_ref.at[:, at]
+            return landed.at[:, at]
     else:
         tall = o_ref.shape[1]
 
@@ -602,16 +719,19 @@
             return x_ref.at[:, pl.ds(pl.multiple_of(at * (tall - halo), 16), tall), :]
 
         def target(at):
-            return o_ref.at[:, :, pl.ds(pl.multiple_of(at * 128, 128), 128)]
+            return landed.at[:, :, pl.ds(pl.multiple_of(at * 128, 128), 128)]
 
     barrier = pltpu.get_barrier_semaphore()
     for step in range(1, mp):
         pl.semaphore_signal(
             barrier, inc=1, device_id={"mp": lax.rem(me + step, mp)}, device_id_type=MESH
         )
-    own = pltpu.make_async_copy(source(me), target(me), local)
+    partners = plane_partners() if ways else ()
+    for partner in partners:
+        pl.semaphore_signal(barrier, inc=1, device_id=partner, device_id_type=MESH)
+    own = pltpu.make_async_copy(source(me), target(me), local.at[0])
     own.start()
-    pl.semaphore_wait(barrier, mp - 1)
+    pl.semaphore_wait(barrier, mp - 1 + len(partners))
     copies = []
     for step in range(1, mp):
         to = lax.rem(me + step, mp)
@@ -620,70 +740,144 @@
         landing = wire(source(to), target(lax.rem(me + mp - step, mp)), *sems)
         leaving.start()
         copies.append((leaving, landing))
+    carries = []
+    if ways:
+        carries = carry_copies(carried, targets, refs[0], refs[1])
+        refs = refs[2:]
+    for copy in carries:
+        copy.start()
+    if pieces:
+        weight_grad(left_ref, right_refs, *refs[:3], grad_ref, *refs[3:])
     own.wait()
     for leaving, landing in copies:
+        landing.wait_recv()
+    save = pltpu.make_async_copy(landed, o_ref, local.at[1])
+    save.start()
+    for leaving, landing in copies:
         leaving.wait_send()
-        landing.wait_recv()
-
-
-def exchange(x, shape, halo, number, name):
+    for copy in carries:
+        copy.wait()
+    save.wait()
+
+
+def exchange(x, shape, halo, number, name, left=None, right=(), carried=()):
     mp = lax.axis_size("mp")
     anywhere = pl.BlockSpec(memory_space=pl.ANY)
+    dma = pltpu.SemaphoreType.DMA
+    scratch = [pltpu.VMEM(shape, x.dtype), dma((2,)), dma((mp,)), dma((mp,))]
+    if carried:
+        scratch += [dma((len(carried),)), dma((len(carried),))]
+    outs = [jax.ShapeDtypeStruct(shape, x.dtype)]
+    extra = ()
+    if left is not None:
+        rows, units = left.shape
+        depth = right[0].shape[-1]
+        outs.append(jax.ShapeDtypeStruct((units, depth), LOW))
+        scratch += weight_grad_scratch(rows, depth, len(right))
+        extra = (left,) + tuple(right)
+    ways = tuple(way for way, _ in carried)
+    extra += tuple(block for _, block in carried)
+    outs += [jax.ShapeDtypeStruct(block.shape, block.dtype) for _, block in carried]
     return pl.pallas_call(
-        partial(exchange_kernel, halo),
-        in_specs=[anywhere],
-        out_specs=anywhere,
-        out_shape=jax.ShapeDtypeStruct(shape, x.dtype),
-        scratch_shapes=[
-            pltpu.SemaphoreType.DMA,
-            pltpu.SemaphoreType.DMA((mp,)),
-            pltpu.SemaphoreType.DMA((mp,)),
-        ],
-        compiler_params=pltpu.CompilerParams(collective_id=number, has_side_effects=True),
-        cost_estimate=pl.CostEstimate(flops=2**34, bytes_accessed=2**24, transcendentals=0),
+        partial(exchange_kernel, halo, len(right), ways),
+        in_specs=[pl.BlockSpec(memory_space=pltpu.VMEM)] + [anywhere] * len(extra),
+        out_specs=[anywhere] * len(outs),
+        out_shape=outs,
+        scratch_shapes=scratch,
+        compiler_params=pltpu.CompilerParams(
+            collective_id=number, has_side_effects=True, vmem_limit_bytes=48 * 2**20
+        ),
+        cost_estimate=pl.CostEstimate(flops=2**35, bytes_accessed=2**24, transcendentals=0),
         name=name,
-    )(x)
-
-
-def heads_out(x, number, name):
+    )(x, *extra)
+
+
+def heads_out(x, number, name, left=None, right=(), carried=()):
     parts, rows_here, width = x.shape
     mp = lax.axis_size("mp")
-    out = exchange(x, (parts, mp, rows_here, 128), None, number, name)
-    return out.reshape(parts, mp * rows_here, 128)
-
-
-def heads_back(x, rows_here, halo, number, name):
+    shape = (parts, mp, rows_here, 128)
+    out, *more = exchange(x, shape, None, number, name, left, right, carried)
+    return [out.reshape(parts, mp * rows_here, 128)] + more
+
+
+def heads_back(x, rows_here, halo, number, name, left=None, right=(), carried=()):
     mp = lax.axis_size("mp")
-    return exchange(x, (x.shape[0], rows_here + halo, mp * 128), halo, number, name)
-
-
-def feed_in_kernel(
-    second_ref, up_ref, down_ref, all_ref, relu_ref, hidden_ref, down_all_ref, up_all_ref,
-    rows, up, relu, hidden, local, outs, send, recv, *line_sems,
-):
+    shape = (x.shape[0], rows_here + halo, mp * 128)
+    return exchange(x, shape, halo, number, name, left, right, carried)
+
+
+def line_blocks(place, sources, local, send, recv):
+    z, core = mesh_place()
+    count = lax.axis_size("mp") // 2
+    out = []
+    for number, (step, way, ref) in enumerate(sources):
+        at = z - way * step
+        there = (at >= 0) & (at < count)
+        at = jnp.clip(at, 0, count - 1)
+        sems = (send.at[number], recv.at[number], other_core())
+        out.append(
+            (
+                there,
+                pltpu.make_async_copy(ref, place(at, core), local.at[number]),
+                wire(ref, place(at, core), *sems),
+                wire(ref, place(at, 1 - core), *sems),
+            )
+        )
+    return out
+
+
+def blocks_start(blocks):
+    for there, here, leaving, _ in blocks:
+
+        @pl.when(there)
+        def _(here=here, leaving=leaving):
+            here.start()
+            leaving.start()
+
+
+def blocks_wait(blocks, local=True):
+    for there, here, leaving, landing in blocks:
+
+        @pl.when(there)
+        def _(here=here, leaving=leaving, landing=landing):
+            if local:
+                here.wait()
+            leaving.wait_send()
+            landing.wait_recv()
+
+
+def feed_in_kernel(up_steps, down_steps, *refs):
+    second_ref, up_ref = refs[:2]
+    up_sources = [(step, way, ref) for (step, way), ref in zip(up_steps, refs[2:])]
+    refs = refs[2 + len(up_steps) :]
+    down_sources = [(step, way, ref) for (step, way), ref in zip(down_steps, refs)]
+    (
+        all_ref, relu_ref, hidden_ref, down_all_ref, up_all_ref,
+        rows, up, relu, hidden, down, local, outs, send, recv,
+        up_local, up_send, up_recv, down_local, down_send, down_recv, *line_sems,
+    ) = refs[len(down_steps) :]
+    count = lax.axis_size("mp") // 2
     depth = rows.shape[3]
     units = up.shape[0]
-    share = down_ref.shape[0]
-    count = lax.axis_size("mp") // 2
-    z, core = mesh_place()
+    share = units // lax.axis_size("mp")
     lanes = (pl.ds(0, depth // 2), pl.ds(depth // 2, depth // 2))
     to_x, to_y = plane_partners()
 
     def line_place(ref):
         return lambda at, at_core: ref.at[
-            pl.ds(pl.multiple_of((at_core * count + at) * share, 16), share), :
+            pl.ds(pl.multiple_of((2 * at + at_core) * share, 16), share), :
         ]
 
     own = [pltpu.make_async_copy(second_ref.at[s], rows.at[s, 0], local.at[s]) for s in range(2)]
-    own.append(pltpu.make_async_copy(up_ref, up, local.at[2]))
-    own.append(pltpu.make_async_copy(down_ref, line_place(down_all_ref)(z, core), local.at[4]))
-    for copy in own:
+    weights = pltpu.make_async_copy(up_ref, up, local.at[2])
+    for copy in own + [weights]:
         copy.start()
-    for copy in own:
+    for copy in own + [weights]:
         copy.wait()
     greet_line(True)
-    up_line = LineGather(line_place(up), *line_sems[:4])
-    down_line = LineGather(line_place(down_all_ref), *line_sems[4:])
+    up_blocks = line_blocks(line_place(up), up_sources, up_local, up_send, up_recv)
+    down_blocks = line_blocks(line_place(down), down_sources, down_local, down_send, down_recv)
+    down_line = LineGather(line_place(down), *line_sems)
 
     def remote(s, source, target, half, partner, number):
         return wire(
@@ -729,24 +923,21 @@
 
     for number in range(4):
         copies[0][number].start()
-    late = range(early_steps(count)[-1] + 1, count)
-    for step in late:
-        up_line.start(step)
-        if step != late[-1]:
-            up_line.arrive(step)
+    blocks_start(up_blocks)
+    blocks_start(down_blocks)
+    blocks_wait(up_blocks)
+    for there, here, _, _ in down_blocks:
+        pl.when(there)(here.wait)
+    down_line.start(1)
+    whole_up = pltpu.make_async_copy(up, up_all_ref, local.at[2])
+    whole_up.start()
+    tile(0, 0)
     copies[0][0].wait_recv()
     copies[0][4].start()
     copies[0][1].wait_recv()
     copies[0][5].start()
     copies[1][0].start()
     copies[1][1].start()
-    up_line.arrive(late[-1])
-    down_line.start(1)
-    down_line.swap_own()
-    up_line.finish(late, False)
-    whole_up = pltpu.make_async_copy(up, up_all_ref, local.at[0])
-    whole_up.start()
-    tile(0, 0)
     tile(1, 0)
     copies[0][3].wait_recv()
     tile(0, 1)
@@ -755,7 +946,8 @@
     copies[1][3].start()
     tile(0, 2)
     down_line.arrive(1)
-    down_line.start(2)
+    if count > 2:
+        down_line.start(2)
     copies[1][0].wait_recv()
     copies[1][4].start()
     copies[1][1].wait_recv()
@@ -763,11 +955,10 @@
     copies[0][4].wait_recv()
     copies[0][5].wait_recv()
     tile(0, 3)
-    down_line.arrive(2)
+    blocks_wait(down_blocks, local=False)
     for step in range(3, count):
+        down_line.arrive(step - 1)
         down_line.start(step)
-        if step != count - 1:
-            down_line.arrive(step)
     copies[1][3].wait_recv()
     tile(1, 1)
     copies[1][2].wait_recv()
@@ -777,8 +968,11 @@
     gathered = pltpu.make_async_copy(rows, all_ref, local.at[3])
     gathered.start()
     tile(1, 3)
-    down_line.arrive(count - 1)
-    down_line.finish(range(1, count), True)
+    if count > 2:
+        down_line.arrive(count - 1)
+    down_line.finish(range(1, count), False)
+    whole_down = pltpu.make_async_copy(down, down_all_ref, local.at[0])
+    whole_down.start()
     for slot in pending:
         for copy in slot:
             copy.wait()
@@ -787,16 +981,17 @@
             copy.wait_send()
     gathered.wait()
     whole_up.wait()
-
-
-def feed_in(second, up_all, down):
+    whole_down.wait()
+
+
+def feed_in(second, up_early, up_late, down_blocks):
     rows_here, depth = second.shape[1:]
-    units = up_all.shape[0]
-    count = lax.axis_size("mp") // 2
+    units = up_early.shape[0]
     anywhere = pl.BlockSpec(memory_space=pl.ANY)
+    dma = pltpu.SemaphoreType.DMA
     return pl.pallas_call(
-        feed_in_kernel,
-        in_specs=[anywhere] * 3,
+        partial(feed_in_kernel, tuple(up_late), tuple(down_blocks)),
+        in_specs=[anywhere] * (2 + len(up_late) + len(down_blocks)),
         out_specs=[anywhere] * 5,
         out_shape=[
             jax.ShapeDtypeStruct((2, 4, rows_here, depth), LOW),
@@ -810,12 +1005,15 @@
             pltpu.VMEM((units, depth), LOW),
             pltpu.VMEM((2, rows_here, units), F32),
             pltpu.VMEM((2, rows_here, units), LOW),
-            pltpu.SemaphoreType.DMA((5,)),
-            pltpu.SemaphoreType.DMA((2, 2)),
-            pltpu.SemaphoreType.DMA((2, 6)),
-            pltpu.SemaphoreType.DMA((2, 6)),
+            pltpu.VMEM((units, depth), LOW),
+            dma((4,)),
+            dma((2, 2)),
+            dma((2, 6)),
+            dma((2, 6)),
         ]
-        + line_semaphores(count) * 2,
+        + [dma((len(up_late),))] * 3
+        + [dma((len(down_blocks),))] * 3
+        + line_semaphores(lax.axis_size("mp") // 2),
         compiler_params=pltpu.CompilerParams(
             collective_id=1, has_side_effects=True, vmem_limit_bytes=VMEM_LIMIT
         ),
@@ -825,11 +1023,24 @@
             transcendentals=0,
         ),
         name="feed_in",
-    )(second, up_all, down)
+    )(second, up_early, *up_late.values(), *down_blocks.values())
+
+
+def piece_copies(pieces, s, m, target, sems):
+    half = target.shape[-1] // 2
+    if m == 0:
+        return [pltpu.make_async_copy(pieces[0].at[s], target, sems.at[0])]
+    return [
+        pltpu.make_async_copy(
+            pieces[2 * m - 1 + side].at[s], target.at[:, pl.ds(side * half, half)], sems.at[side]
+        )
+        for side in range(2)
+    ]
 
 
 def feed_out_kernel(
-    cot_ref, relu_ref, hidden_ref, up_ref, down_ref, grad_ref, feed_ref, back_ref,
+    cot_0, cot_1, cot_2, cot_3, cot_4, cot_5, cot_6, relu_ref, hidden_ref, up_ref, down_ref,
+    grad_ref, feed_x0_ref, feed_x1_ref, feed_y0_ref, feed_y1_ref, keep_a_ref, keep_b_ref, back_ref,
     up, down, cot, relu, grad, part, arrived, feed, result, local, loads, outs, send, recv,
 ):
     units, depth = up.shape
@@ -841,13 +1052,14 @@
         pltpu.make_async_copy(up_ref, up, local.at[1]),
     ]
     order = [(s, m) for s in range(2) for m in (3, 1, 2, 0)]
+    feed_x_refs, feed_y_refs = (feed_x0_ref, feed_x1_ref), (feed_y0_ref, feed_y1_ref)
+    pieces = (cot_0, cot_1, cot_2, cot_3, cot_4, cot_5, cot_6)
 
     def load(at):
         s, m = order[at]
         slot = at % 2
-        return [
-            pltpu.make_async_copy(cot_ref.at[s, m], cot.at[slot], loads.at[slot, 0]),
-            pltpu.make_async_copy(relu_ref.at[s, m], relu.at[slot], loads.at[slot, 1]),
+        return piece_copies(pieces, s, m, cot.at[slot], loads.at[slot]) + [
+            pltpu.make_async_copy(relu_ref.at[s, m], relu.at[slot], loads.at[slot, 2]),
         ]
 
     for copy in load(0) + weights:
@@ -959,7 +1171,8 @@
         if at + 1 < len(order):
             feed_load(at + 1).start()
         if feeding[slot] is not None:
-            feeding[slot].wait()
+            for copy in feeding[slot]:
+                copy.wait()
 
         def one(step, carry):
             columns = pl.ds(pl.multiple_of(step * CHUNK, CHUNK), CHUNK)
@@ -967,8 +1180,16 @@
             return carry
 
         lax.fori_loop(0, depth // CHUNK, one, 0)
-        feeding[slot] = pltpu.make_async_copy(feed.at[slot], feed_ref.at[s, m], outs.at[2 + slot])
-        feeding[slot].start()
+        targets = (
+            (keep_a_ref.at[s, 0], feed_x_refs[s].at[0], keep_a_ref.at[s, 1], feed_x_refs[s].at[1])[m],
+            (keep_b_ref.at[s, 0], keep_b_ref.at[s, 1], feed_y_refs[s].at[0], feed_y_refs[s].at[1])[m],
+        )
+        feeding[slot] = [
+            pltpu.make_async_copy(feed.at[slot, :, lanes[side]], target, outs.at[2 + 2 * slot + side])
+            for side, target in enumerate(targets)
+        ]
+        for copy in feeding[slot]:
+            copy.start()
 
     feed_load(0).start()
     for at in range(2):
@@ -980,23 +1201,27 @@
     finish(1).wait()
     for slot in range(2):
         saving[slot].wait()
-        feeding[slot].wait()
+        for copy in feeding[slot]:
+            copy.wait()
     for s in range(2):
         for number in range(6):
             copies[s][number].wait_send()
 
 
-def feed_out(cot_all, relu, hidden, up_all, down_all):
-    rows_here, depth = cot_all.shape[2:]
-    units = up_all.shape[0]
+def feed_out(cot_pieces, relu, hidden, up_all, down_all):
+    rows_here, units = relu.shape[2:]
+    depth = up_all.shape[1]
     anywhere = pl.BlockSpec(memory_space=pl.ANY)
     return pl.pallas_call(
         feed_out_kernel,
-        in_specs=[anywhere] * 5,
-        out_specs=[anywhere] * 3,
+        in_specs=[anywhere] * 11,
+        out_specs=[anywhere] * 8,
         out_shape=[
             jax.ShapeDtypeStruct((2, 4, rows_here, units), LOW),
-            jax.ShapeDtypeStruct((2, 4, rows_here, depth), LOW),
+        ]
+        + [jax.ShapeDtypeStruct((2, rows_here, depth // 2), LOW)] * 4
+        + [jax.ShapeDtypeStruct((2, 2, rows_here, depth // 2), LOW)] * 2
+        + [
             jax.ShapeDtypeStruct((2, rows_here, depth), F32),
         ],
         scratch_shapes=[
@@ -1010,8 +1235,8 @@
             pltpu.VMEM((2, rows_here, depth), LOW),
             pltpu.VMEM((rows_here, depth), F32),
             pltpu.SemaphoreType.DMA((3,)),
-            pltpu.SemaphoreType.DMA((2, 2)),
-            pltpu.SemaphoreType.DMA((4,)),
+            pltpu.SemaphoreType.DMA((2, 3)),
+            pltpu.SemaphoreType.DMA((6,)),
             pltpu.SemaphoreType.DMA((2, 6)),
             pltpu.SemaphoreType.DMA((2, 6)),
         ],
@@ -1024,47 +1249,299 @@
             transcendentals=0,
         ),
         name="feed_out",
-    )(cot_all, relu, hidden, up_all, down_all)
+    )(*cot_pieces, relu, hidden, up_all, down_all)
+
+
+def finish_kernel(
+    ways, qk_ref, v_ref, out_ref, norms_ref, taps_ref, *refs
+):
+    carried, refs = list(zip(ways, refs[: len(ways)])), refs[len(ways) :]
+    joint_ref, norms_sum_ref, taps_sum_ref = refs[:3]
+    targets, refs = refs[3 : 3 + len(ways)], refs[3 + len(ways) :]
+    (
+    acc, got, plane_in, line_in, gathered, norms_all, taps_all, norms_dp, taps_dp,
+    local, swap_send, swap_recv, plane_send_sem, plane_recv_sem, line_send_sem, line_recv_sem,
+    gather_send, gather_recv, small_send, small_recv, carry_send, carry_recv,
+    ) = refs
+    mp = lax.axis_size("mp")
+    dp = lax.axis_index("dp")
+    me = lax.axis_index("mp")
+    z, core = mesh_place()
+    count = mp // 2
+    depth = acc.shape[3]
+    half = depth // 2
+    lanes = (pl.ds(0, half), pl.ds(half, half))
+    to_x, to_y = plane_partners()
+    dp_x = dp + 1 - 2 * lax.rem(dp, 2)
+    dp_y = dp + 2 - 4 * (dp // 2)
+    dp_xy = dp_x + 2 - 4 * (dp_x // 2)
+    parts = (qk_ref, v_ref, out_ref)
+    spans = (pl.ds(0, HD // 2), pl.ds(HD // 2, HD // 4), pl.ds(3 * HD // 4, HD // 4))
+    loads = [
+        pltpu.make_async_copy(part.at[:, core], acc.at[:, :, span, :], local.at[at])
+        for at, (part, span) in enumerate(zip(parts, spans))
+    ]
+    for copy in loads:
+        copy.start()
+
+    barrier = pltpu.get_barrier_semaphore()
+    for step in range(1, mp):
+        pl.semaphore_signal(
+            barrier, inc=1, device_id={"mp": lax.rem(me + step, mp)}, device_id_type=MESH
+        )
+    for step in range(1, 4):
+        pl.semaphore_signal(
+            barrier, inc=1, device_id={"dp": lax.rem(dp + step, 4)}, device_id_type=MESH
+        )
+    pl.semaphore_wait(barrier, mp + 2)
+
+    swaps = [
+        [
+            wire(
+                part.at[:, 1 - core, quarter], got.at[:, quarter, span, :],
+                swap_send.at[at, number], swap_recv.at[at, number], other_core(),
+            )
+            for at, (part, span) in enumerate(zip(parts, spans))
+        ]
+        for number, quarter in enumerate((dp_xy, dp_x, dp_y, dp))
+    ]
+    for group in swaps:
+        for copy in group:
+            copy.start()
+
+    def small(axis, at, others, source, target, number, first):
+        out = []
+        for step in range(1, others):
+            to = lax.rem(at + step, others)
+            frm = lax.rem(at + others - step, others)
+            sems = (small_send.at[number, step], small_recv.at[number, step], {axis: to})
+            out.append((wire(source(to), target.at[at], *sems), wire(source(to), target.at[frm], *sems)))
+        return out
+
+    own_small = [
+        pltpu.make_async_copy(norms_ref, norms_all.at[me], local.at[3]),
+        pltpu.make_async_copy(taps_ref.at[me], taps_all.at[me], local.at[4]),
+    ]
+    for copy in own_small:
+        copy.start()
+    over_mp = small("mp", me, mp, lambda to: norms_ref, norms_all, 0, None) + small(
+        "mp", me, mp, lambda to: taps_ref.at[to], taps_all, 1, None
+    )
+    for leaving, _ in over_mp:
+        leaving.start()
+
+    def add(quarter, side, number):
+        acc[:, quarter, :, lanes[side]] = (
+            acc[:, quarter, :, lanes[side]].astype(F32) + plane_in[number].astype(F32)
+        ).astype(LOW)
+
+    def add_core(number, quarter):
+        for copy in swaps[number]:
+            copy.wait_recv()
+        acc[:, quarter] = (acc[:, quarter].astype(F32) + got[:, quarter].astype(F32)).astype(LOW)
+
+    def plane(quarter, side, partner, number):
+        return wire(
+            acc.at[:, quarter, :, lanes[side]], plane_in.at[number],
+            plane_send_sem.at[number], plane_recv_sem.at[number], partner,
+        )
+
+    sends = [
+        plane(dp_x, 0, to_x, 0),
+        plane(dp_xy, 0, to_x, 1),
+        plane(dp_y, 1, to_y, 2),
+        plane(dp_xy, 1, to_y, 3),
+        plane(dp_y, 0, to_y, 4),
+        plane(dp_x, 1, to_x, 5),
+    ]
+    for copy in loads:
+        copy.wait()
+    add_core(0, dp_xy)
+    sends[1].start()
+    sends[3].start()
+    add_core(1, dp_x)
+    sends[0].start()
+    add_core(2, dp_y)
+    sends[2].start()
+    add_core(3, dp)
+    for _, landing in over_mp:
+        landing.wait_recv()
+    for copy in own_small:
+        copy.wait()
+    norms_dp[dp] = jnp.sum(norms_all[...], axis=0)
+    taps_dp[dp] = jnp.sum(taps_all[...], axis=0)
+    over_dp = small("dp", dp, 4, lambda to: norms_dp.at[dp], norms_dp, 2, None) + small(
+        "dp", dp, 4, lambda to: taps_dp.at[dp], taps_dp, 3, None
+    )
+    for leaving, _ in over_dp:
+        leaving.start()
+    sends[1].wait_recv()
+    add(dp_y, 0, 1)
+    sends[4].start()
+    sends[3].wait_recv()
+    add(dp_x, 1, 3)
+    sends[5].start()
+    sends[0].wait_recv()
+    add(dp, 0, 0)
+    sends[2].wait_recv()
+    add(dp, 1, 2)
+    sends[4].wait_recv()
+    add(dp, 0, 4)
+    sends[5].wait_recv()
+    add(dp, 1, 5)
+
+    carries = carry_copies(carried, targets, carry_send, carry_recv)
+    for copy in carries:
+        copy.start()
+
+    def line(step):
+        out = []
+        for way, turn in enumerate((1, -1)):
+            target = z + turn * (count - step)
+            far = z + turn
+            lands = far - 2 * turn + turn * (count - step)
+            sends = (target >= 0) & (target < count)
+            receives = (lands >= 0) & (lands < count) & (z - turn >= 0) & (z - turn < count)
+            at = jnp.clip(target, 0, count - 1)
+            to = jnp.clip(lands, 0, count - 1)
+            copy = wire(
+                acc.at[at, dp], line_in.at[way, step - 1],
+                line_send_sem.at[way, step - 1], line_recv_sem.at[way, step - 1],
+                line_partner(z, turn),
+            )
+            out.append((sends, receives, to, copy))
+        return out
+
+    for step in range(1, count):
+        legs = line(step)
+        for sends_now, _, _, copy in legs:
+            pl.when(sends_now)(copy.start)
+        for way, (_, receives, to, copy) in enumerate(legs):
+
+            @pl.when(receives)
+            def _(to=to, copy=copy, way=way):
+                copy.wait_recv()
+                acc[to, dp] = (
+                    acc[to, dp].astype(F32) + line_in[way, step - 1].astype(F32)
+                ).astype(LOW)
+
+    gathered[dp] = acc[z, dp]
+
+    def gather(quarter, side, partner, number):
+        block = gathered.at[quarter, :, lanes[side]]
+        return wire(block, block, gather_send.at[number], gather_recv.at[number], partner)
+
+    leaving = [
+        gather(dp, 0, to_x, 0), gather(dp, 1, to_y, 1), gather(dp, 0, to_y, 2), gather(dp, 1, to_x, 3),
+        gather(dp_x, 0, to_y, 4), gather(dp_y, 1, to_x, 5),
+    ]
+    landing = [
+        gather(dp_x, 0, to_x, 0), gather(dp_y, 1, to_y, 1), gather(dp_y, 0, to_y, 2), gather(dp_x, 1, to_x, 3),
+        gather(dp_xy, 0, to_y, 4), gather(dp_xy, 1, to_x, 5),
+    ]
+    for number in range(4):
+        leaving[number].start()
+    for _, landed in over_dp:
+        landed.wait_recv()
+    norms_sum_ref[...] = jnp.sum(norms_dp[...], axis=0)
+    taps_sum_ref[...] = jnp.sum(taps_dp[...], axis=0)
+    landing[0].wait_recv()
+    leaving[4].start()
+    landing[1].wait_recv()
+    leaving[5].start()
+    for number in range(2, 6):
+        landing[number].wait_recv()
+    save = pltpu.make_async_copy(gathered, joint_ref, local.at[5])
+    save.start()
+    for group in swaps:
+        for copy in group:
+            copy.wait_send()
+    for copy in sends:
+        copy.wait_send()
+    for step in range(1, count):
+        for sends_now, _, _, copy in line(step):
+            pl.when(sends_now)(copy.wait_send)
+    for copy in leaving:
+        copy.wait_send()
+    for copy, _ in over_mp + over_dp:
+        copy.wait_send()
+    for copy in carries:
+        copy.wait()
+    save.wait()
+
+
+def finish(qk, v, out, norms, taps, carried):
+    mp = lax.axis_size("mp")
+    count = mp // 2
+    depth = qk.shape[-1]
+    anywhere = pl.BlockSpec(memory_space=pl.ANY)
+    vmem = pl.BlockSpec(memory_space=pltpu.VMEM)
+    dma = pltpu.SemaphoreType.DMA
+    return pl.pallas_call(
+        partial(finish_kernel, tuple(way for way, _ in carried)),
+        in_specs=[anywhere] * 3 + [vmem] * 2 + [anywhere] * len(carried),
+        out_specs=[anywhere, vmem, vmem] + [anywhere] * len(carried),
+        out_shape=[
+            jax.ShapeDtypeStruct((4, HD, depth), LOW),
+            jax.ShapeDtypeStruct(norms.shape, F32),
+            jax.ShapeDtypeStruct(taps.shape[1:], F32),
+        ]
+        + [jax.ShapeDtypeStruct(block.shape, block.dtype) for _, block in carried],
+        scratch_shapes=[
+            pltpu.VMEM((count, 4, HD, depth), LOW),
+            pltpu.VMEM((count, 4, HD, depth), LOW),
+            pltpu.VMEM((6, count, HD, depth // 2), LOW),
+            pltpu.VMEM((2, count, HD, depth), LOW),
+            pltpu.VMEM((4, HD, depth), LOW),
+            pltpu.VMEM((mp,) + norms.shape, F32),
+            pltpu.VMEM(taps.shape, F32),
+            pltpu.VMEM((4,) + norms.shape, F32),
+            pltpu.VMEM((4,) + taps.shape[1:], F32),
+            dma((6,)),
+            dma((3, 4)),
+            dma((3, 4)),
+            dma((6,)),
+            dma((6,)),
+            dma((2, count)),
+            dma((2, count)),
+            dma((6,)),
+            dma((6,)),
+            dma((4, mp)),
+            dma((4, mp)),
+            dma((len(carried),)),
+            dma((len(carried),)),
+        ],
+        compiler_params=pltpu.CompilerParams(
+            collective_id=8, has_side_effects=True, vmem_limit_bytes=VMEM_LIMIT
+        ),
+        cost_estimate=pl.CostEstimate(flops=2**36, bytes_accessed=2**26, transcendentals=0),
+        name="finish",
+    )(qk, v, out, norms, taps, *(block for _, block in carried))
 
 
 def plane_send(block, mask):
     return lax.ppermute(block, "dp", [(d, d ^ mask) for d in range(lax.axis_size("dp"))])
 
 
-def plane_gather(block):
-    half = block.shape[1] // 2
-    one, two = block[:, :half], block[:, half:]
-    one_x = plane_send(one, 1)
-    two_y = plane_send(two, 2)
-    one_y = plane_send(one, 2)
-    two_x = plane_send(two, 1)
-    one_xy = plane_send(one_x, 2)
-    two_xy = plane_send(two_y, 1)
+def plane_gather_begin(block):
+    half = block.shape[-1] // 2
+    one, two = block[..., :half], block[..., half:]
+    return plane_send(one, 1), plane_send(two, 2), plane_send(one, 2), plane_send(two, 1)
+
+
+def plane_gather_end(block, legs):
+    one_x, two_y, one_y, two_x = legs
+    return plane_send(one_x, 2), plane_send(two_y, 1)
+
+
+def plane_blocks(block, legs, last):
+    one_x, two_y, one_y, two_x = legs
     return [
         block,
-        jnp.concatenate([one_x, two_x], axis=1),
-        jnp.concatenate([one_y, two_y], axis=1),
-        jnp.concatenate([one_xy, two_xy], axis=1),
+        jnp.concatenate([one_x, two_x], axis=-1),
+        jnp.concatenate([one_y, two_y], axis=-1),
+        jnp.concatenate(last, axis=-1),
     ]
-
-
-def plane_scatter(part):
-    half = part.shape[2] // 2
-    wide = lambda block: block.astype(F32)
-    one, two = part[:, :, :half], part[:, :, half:]
-    one_in = plane_send(one[1::2], 1)
-    two_in = plane_send(two[2:], 2)
-    one_sum = (wide(one[2]) + wide(one_in[1])).astype(LOW)
-    two_sum = (wide(two[1]) + wide(two_in[1])).astype(LOW)
-    one_last = plane_send(one_sum, 2)
-    two_last = plane_send(two_sum, 1)
-    return jnp.concatenate(
-        [
-            wide(one[0]) + wide(one_in[0]) + wide(one_last),
-            wide(two[0]) + wide(two_in[0]) + wide(two_last),
-        ],
-        axis=1,
-    )
 
 
 def plane_order(blocks, axis):
@@ -1075,37 +1552,11 @@
     )
 
 
-def chips():
-    return lax.axis_size("mp") // 2
-
-
-def line_send(block, step, senders):
-    count = chips()
-    pairs = []
-    for z in senders:
-        if 0 <= z < count and 0 <= z + step < count:
-            pairs += [(2 * z + c, 2 * (z + step) + c) for c in range(2)]
-    return lax.ppermute(block, "mp", pairs)
-
-
-def core_swap(block):
-    return lax.ppermute(block, "mp", [(i, i ^ 1) for i in range(lax.axis_size("mp"))])
-
-
-def line_scatter(parts):
-    count = chips()
-
-    def add(left, right):
-        return (left.astype(F32) + right.astype(F32)).astype(LOW)
-
-    up, down = parts[count - 1], parts[1]
-    for step in range(1, count):
-        up_in = line_send(up, 1, range(0, step))
-        down_in = line_send(down, -1, range(count - step, count))
-        if step < count - 1:
-            up = add(up_in, parts[count - step - 1])
-            down = add(down_in, parts[step + 1])
-    return (parts[0].astype(F32) + up_in.astype(F32) + down_in.astype(F32)).astype(LOW)
+def line_step(blocks, step):
+    count = lax.axis_size("mp") // 2
+    up = [(2 * z + c, 2 * z + 2 + c) for z in range(step - 1, count - 1) for c in range(2)]
+    down = [(2 * z + c, 2 * z - 2 + c) for z in range(1, count - step + 1) for c in range(2)]
+    return lax.ppermute(blocks[0], "mp", up), lax.ppermute(blocks[1], "mp", down)
 
 
 def per_device(
@@ -1161,8 +1612,23 @@
     qk_taps = taps[:, :, : 2 * HD].reshape(3, mp * 2 * HD)
     v_taps = taps[:, :, 2 * HD : 3 * HD].reshape(3, mp * HD)
 
-    cot_all = jnp.stack([jnp.stack(plane_gather(cotangent[index])) for index in range(2)])
-
+    cot, qk_all, up_early, down_own = lax.optimization_barrier(
+        (cotangent, qk_all, up_early, down_own)
+    )
+    cot_legs = plane_gather_begin(cot)
+    chips = mp // 2
+    late = list(range(early_steps(chips)[-1] + 1, chips))
+    z = me_mp // 2
+
+    def early_block(at):
+        start = (2 * jnp.clip(at, 0, chips - 1) + me_mp % 2) * share
+        return lax.dynamic_slice_in_dim(up_early, start, share, 0)
+
+    up_late = {}
+    blocks = (early_block(z - late[0] + 1), early_block(z + late[0] - 1))
+    for step in late:
+        blocks = line_step(blocks, step)
+        up_late[step, 1], up_late[step, -1] = blocks
     normed_ext = jnp.concatenate([halo_rows, normed], axis=1)
     raw_qk = jnp.einsum("srd,cd->src", normed_ext, qk_all, preferred_element_type=F32)
     raw_v = jnp.einsum("srd,cd->src", normed_ext, v_all, preferred_element_type=F32)
@@ -1190,53 +1656,27 @@
         split = joint.reshape(joint.shape[1], mp, 2, HD)
         return split.transpose(2, 0, 1, 3).reshape(2, joint.shape[1], mp * HD)
 
-    mixed = heads_out(jnp.concatenate([mixed_qk, side_by_side(mixed_v)], axis=0), 4, "mixed_out")
+    mixed_qk, up_late = lax.optimization_barrier((mixed_qk, up_late))
+    (mixed,) = heads_out(jnp.concatenate([mixed_qk, side_by_side(mixed_v)], axis=0), 4, "mixed_out")
+    mixed, cot_legs = lax.optimization_barrier((mixed, cot_legs))
+    cot_last = plane_gather_end(cot, cot_legs)
+    down_blocks = {(0, 1): down_own}
     attended_head, wide, total = attend(mixed, starts)
-    attended = apart(heads_back(attended_head, rows_here, 0, 5, "attended_back"))
+    attended_head, cot_last = lax.optimization_barrier((attended_head, cot_last))
+    one_x, two_y, one_y, two_x = cot_legs
+    cot_pieces = (cot, one_x, two_x, one_y, two_y) + tuple(cot_last)
+    (attended,) = heads_back(attended_head, rows_here, 0, 5, "attended_back")
+    attended = apart(attended)
     middle = rows + dot(attended, out_all)
     second = layer_norm(middle, norm2_gain, norm2_bias).astype(LOW)
 
-    second_all, relu, hidden, down_all, up_all = feed_in(second, up_early, down_own)
-    grad_pre, feed_part, grad_second = feed_out(cot_all, relu, hidden, up_all, down_all)
-    down_part = jnp.einsum(
-        "gf,gd->fd",
-        hidden.reshape(-1, hidden.shape[3]),
-        cot_all.reshape(-1, width),
-        preferred_element_type=F32,
-    ).astype(LOW)
-    up_part = jnp.einsum(
-        "gf,gd->fd",
-        grad_pre.reshape(-1, hidden.shape[3]),
-        second_all.reshape(-1, width),
-        preferred_element_type=F32,
-    ).astype(LOW)
-    results = jnp.stack(
-        [(middle[index] + plane_scatter(feed_part[index])).astype(LOW) for index in range(2)]
+    second_all, relu, hidden, down_all, up_all = feed_in(second, up_early, up_late, down_blocks)
+    down_part = whole_weight_grad(hidden.reshape(-1, hidden.shape[3]), cot_pieces)
+    down_mine = lax.psum_scatter(down_part, "mp", scatter_dimension=0, tiled=True)
+    down_part, relu = lax.optimization_barrier((down_part, relu))
+    grad_pre, feed_x0, feed_x1, feed_y0, feed_y1, keep_a, keep_b, grad_second = feed_out(
+        cot_pieces, relu, hidden, up_all, down_all
     )
-
-    def add_low(left, right):
-        return (left.astype(F32) + right.astype(F32)).astype(LOW)
-
-    core = me_mp % 2
-    mine = share * (mp // 2)
-
-    def reduce_units(part):
-        own = lax.dynamic_slice_in_dim(part, core * mine, mine, 0)
-        other = lax.dynamic_slice_in_dim(part, (1 - core) * mine, mine, 0)
-        total = add_low(own, core_swap(other)).reshape(mp // 2, share, width)
-        z = me_mp // 2
-        return line_scatter(
-            [
-                lax.dynamic_index_in_dim(total, (z + k) % (mp // 2), 0, keepdims=False)
-                for k in range(mp // 2)
-            ]
-        )
-
-    up_mine = reduce_units(up_part).T
-    down_mine = reduce_units(down_part)
-    up_grad = plane_order(plane_gather(up_mine), axis=1).astype(F32)
-    down_grad = plane_order(plane_gather(down_mine), axis=0).astype(F32)
-
     def norm_back(values, gain, grad):
         flat = values.reshape(-1, width)
         unused, pull = jax.vjp(layer_norm, flat, gain, norm1_bias)
@@ -1248,9 +1688,29 @@
     branch = grad_middle.astype(LOW)
     out_part = jnp.einsum("srh,srd->hd", attended, branch, preferred_element_type=F32).astype(LOW)
     grad_attended = jnp.einsum("srd,hd->srh", branch, out_all, preferred_element_type=F32).astype(LOW)
-    grad_head = heads_out(side_by_side(grad_attended), 6, "attended_grad_out")
+    grad_head, up_part, x_first, y_first = heads_out(
+        side_by_side(grad_attended), 6, "attended_grad_out", grad_pre.reshape(-1, hidden.shape[3]),
+        (second_all.reshape(-1, width),), ((0, feed_x0), (1, feed_y0)),
+    )
+    up_mine = lax.psum_scatter(up_part, "mp", scatter_dimension=0, tiled=True)
+    grad_head, down_mine = lax.optimization_barrier((grad_head, down_mine))
+    down_legs = plane_gather_begin(down_mine)
     grad_mixed_head = attend_back(mixed, grad_head, wide, total, starts, HALO)
-    grad_mixed = heads_back(grad_mixed_head, rows_here, HALO, 7, "mixed_grad_back")
+    grad_mixed_head, down_legs = lax.optimization_barrier((grad_mixed_head, down_legs))
+    down_last = plane_gather_end(down_mine, down_legs)
+    grad_mixed, x_second, y_second = heads_back(
+        grad_mixed_head, rows_here, HALO, 7, "mixed_grad_back",
+        carried=((0, feed_x1), (1, feed_y1)),
+    )
+    grad_mixed, down_last = lax.optimization_barrier((grad_mixed, down_last))
+    down_grad = plane_order(plane_blocks(down_mine, down_legs, down_last), axis=0).astype(F32)
+    x_in, y_in = jnp.stack([x_first, x_second]), jnp.stack([y_first, y_second])
+
+    def add(left, right):
+        return left.astype(F32) + right.astype(F32)
+
+    feed_a = add(keep_a[:, 1], x_in[:, 1]).astype(LOW)
+    feed_b = add(keep_b[:, 1], y_in[:, 1]).astype(LOW)
     grad_qk = grad_mixed[:2].astype(F32)
     grad_v = apart(grad_mixed[2:]).astype(F32)
 
@@ -1270,44 +1730,58 @@
 
     grad_raw_qk, grad_tap_qk = conv_back(grad_qk, raw_qk, qk_taps)
     grad_raw_v, grad_tap_v = conv_back(grad_v, raw_v, v_taps)
+    grad_raw_qk, up_mine = lax.optimization_barrier((grad_raw_qk, up_mine))
+    up_legs = plane_gather_begin(up_mine)
     qk_part = jnp.einsum("src,srd->cd", grad_raw_qk, normed, preferred_element_type=F32).astype(LOW)
     v_part = jnp.einsum("src,srd->cd", grad_raw_v, normed, preferred_element_type=F32).astype(LOW)
     grad_normed = dot(grad_raw_qk, qk_all) + dot(grad_raw_v, v_all)
     grad_input, gain_one, shift_one = norm_back(rows, norm1_gain, grad_normed)
     input_grads = grad_middle + grad_input
 
-    joint = jnp.concatenate(
-        [
-            qk_part.reshape(mp, 2 * HD, width),
-            v_part.reshape(mp, HD, width),
-            out_part.reshape(mp, HD, width),
-        ],
-        axis=1,
-    ).reshape(mp * 4 * HD, width)
-    joint_grad = lax.psum(
-        lax.psum_scatter(joint, "mp", scatter_dimension=0, tiled=True), "dp"
-    ).astype(F32)
-    small_sum, tap_sum = lax.psum(
-        (
-            jnp.stack([gain_one, shift_one, gain_two, shift_two]),
-            jnp.concatenate([grad_tap_qk, grad_tap_v], axis=1),
-        ),
-        ("dp", "mp"),
+    def split_parts(part):
+        return part.reshape(mp // 2, 2, 4, part.shape[0] // (4 * mp), width)
+
+    norms = jnp.stack([gain_one, shift_one, gain_two, shift_two]).reshape(8, width // 2)
+    taps_part = jnp.concatenate(
+        [grad_tap_qk.reshape(3, mp, 2 * HD), grad_tap_v.reshape(3, mp, HD)], axis=2
+    ).transpose(1, 0, 2)
+    taps_part = jnp.pad(taps_part, ((0, 0), (0, 5), (0, HD)))
+    norms, up_legs = lax.optimization_barrier((norms, up_legs))
+    up_last = plane_gather_end(up_mine, up_legs)
+    joint_grad, norms_sum, taps_sum, feed_a, feed_b = finish(
+        split_parts(qk_part), split_parts(v_part), split_parts(out_part), norms, taps_part,
+        ((1, feed_a), (0, feed_b)),
     )
-    qk_tap_grad = lax.dynamic_slice_in_dim(tap_sum, me_mp * 2 * HD, 2 * HD, 1)
-    v_tap_grad = lax.dynamic_slice_in_dim(tap_sum, mp * 2 * HD + me_mp * HD, HD, 1)
+    results = (
+        middle
+        + jnp.concatenate(
+            [
+                add(keep_a[:, 0], x_in[:, 0]) + feed_a.astype(F32),
+                add(keep_b[:, 0], y_in[:, 0]) + feed_b.astype(F32),
+            ],
+            axis=2,
+        )
+    ).astype(LOW)
+    joint_grad, up_last = lax.optimization_barrier((joint_grad, up_last))
+    up_grad = plane_order(plane_blocks(up_mine, up_legs, up_last), axis=0).T.astype(F32)
+    joint_grad = joint_grad.astype(F32)
+    small_sum = norms_sum.reshape(4, width)
+    qk_grad = joint_grad[:, : HD // 2].reshape(2 * HD, width).T
+    v_grad = joint_grad[:, HD // 2 : 3 * HD // 4].reshape(HD, width).T
+    out_grad = joint_grad[:, 3 * HD // 4 :].reshape(HD, width)
+    taps_sum = taps_sum[:3]
     return (
         results,
         input_grads,
         small_sum[0],
         small_sum[1],
-        joint_grad[:HD].T,
-        joint_grad[HD : 2 * HD].T,
-        joint_grad[2 * HD : 3 * HD].T,
-        qk_tap_grad[:, :HD],
-        qk_tap_grad[:, HD:],
-        v_tap_grad,
-        joint_grad[3 * HD :],
+        qk_grad[:, :HD],
+        qk_grad[:, HD:],
+        v_grad,
+        taps_sum[:, :HD],
+        taps_sum[:, HD : 2 * HD],
+        taps_sum[:, 2 * HD : 3 * HD],
+        out_grad,
         small_sum[2],
         small_sum[3],
         up_grad,

time: 1240 us -> 880 us (0.71)
  waiting for transfers between devices: 287 us -> 0.09 us
  Pallas kernels: 507 us -> 647 us
  blocking collectives: 51.4 us -> 0 us
  starting transfers between devices: 72.9 us -> 23.1 us
  matrix products: 84.7 us -> 40.6 us
  other arithmetic: 109 us -> 65 us
  local copies, waits for them, and re-layouts: 108 us -> 82.4 us
    ppermute x14 -> x2, waiting for transfers between devices: 134 us -> 0.01 us  [the longest x1 0.01 us: line_step(): lax.ppermute(blocks[0], 'mp', up)]
    pallas_call x6 -> x8, Pallas kernels: 360 us -> 486 us  [the longest x4 151 us: exchange(): pl.pallas_call(partial(exchange_kernel, halo, len(right), ways), in_specs...]
    ppermute x32 -> x18, waiting for transfers between devices: 91.1 us -> 0.05 us  [plane_send(): lax.ppermute(block, 'dp', [(d, d ^ mask) for d in range(lax.axis_size('dp...]
    psum x1 -> x0, waiting for transfers between devices: 62.5 us -> none  [per_device(): lax.psum(lax.psum_scatter(joint, 'mp', scatter_dimension=0, tiled=True),...]
    dot_general x2 -> x0, matrix products: 56.7 us -> none  [the longest x1 29 us: per_device(): jnp.einsum('gf,gd->fd', hidden.reshape(-1, hidden.shape[3]), cot_all.resh...]
    psum x1 -> x0, blocking collectives: 51.4 us -> none  [per_device(): lax.psum((jnp.stack([gain_one, shift_one, gain_two, shift_two]), jnp.conc...]
    ppermute x14 -> x2, starting transfers between devices: 28.7 us -> 3.42 us  [the longest x1 2.14 us: line_step(): lax.ppermute(blocks[0], 'mp', up)]
    ppermute x32 -> x18, starting transfers between devices: 44.1 us -> 19.4 us  [plane_send(): lax.ppermute(block, 'dp', [(d, d ^ mask) for d in range(lax.axis_size('dp...]
  transfers between devices with their start and end apart: 48 -> 22, of which waited for: 22 -> 0; matrix products, arithmetic and copies ran while one was open for 16% -> 14% of each run, Pallas kernels for 25% -> 47%
where the time goes in v3:
time: 880 us; the launch traced here: 874 us
  Pallas kernels  647 us (74%)
  local copies, waits for them, and re-layouts  82.4 us (9%)
  other arithmetic  65 us (7%)
  matrix products  40.6 us (5%)
  starting transfers between devices  23.1 us (3%)
  between operations  15.7 us (2%)
    pallas_call x4, Pallas kernels, exchange(): pl.pallas_call(partial(exchange_kernel, halo, len(right), ways), in_specs...  151 us
    pallas_call x1, Pallas kernels, feed_out(): pl.pallas_call(feed_out_kernel, in_specs=[anywhere] * 11, out_specs=[anyw...  107 us
    pallas_call x1, Pallas kernels, feed_in(): pl.pallas_call(partial(feed_in_kernel, tuple(up_late), tuple(down_blocks)...  103 us
    pallas_call x1, Pallas kernels, finish(): pl.pallas_call(partial(finish_kernel, tuple((way for way, _ in carried)))...  97.2 us
    pallas_call x1, Pallas kernels, prepare(): pl.pallas_call(prepare_kernel, in_specs=[anywhere, vmem, vmem] + [anywher...  82.8 us
    unnamed x213, local copies, waits for them, and re-layouts  44.8 us
    pallas_call x1, Pallas kernels, attend_back(): pl.pallas_call(attend_back_kernel, grid_spec=pltpu.PrefetchScalarGridSpec...  41 us
    pallas_call x1, Pallas kernels, attend(): pl.pallas_call(attend_kernel, grid_spec=pltpu.PrefetchScalarGridSpec(num_...  37 us
  transfers between devices with their start and end apart: 22, of which 0 were waited for; matrix products, arithmetic and copies ran while one was open for 14% of the time, Pallas kernels for 47%

profile of v3, /device:TPU:0, one launch (start us, length us, event | category | flops | bytes accessed | tf_op | source)
XLA Modules:
  0.0 873.7 jit_solution(16852192796645425346)
XLA Ops:
  10.0 2.3 constant_dynamic-slice_fusion.2.refs_4_
  13.8 82.8 %prepare.1 = (bf16[4,2,4,32,2048]{4,3,2,1,0:T(8,128)(2,1)}, bf16[4,2,4,16,2048]{4,3,2,1,0:T(8,128)(2,1)}, bf16[4,2,4,16,2048]{4,3,2,1,0:T(8,128)(2,1)}, f32[8,8,...) custom-call(bf16[2,320,2048]{2,1,0:T(8,128)(2,1)} %inputs_ref.1, ...), custom_call_target="tpu_custom_call" | custom-call | flops 68719476736 | bytes 67108864 | tf_op jit(solution)/shard_map/prepare/pallas_call | solution.py:563
  96.6 3.4 fusion.29
  103.2 3.2 constant_dynamic-slice_fusion
  107.6 2.1 collective-permute-start.1
  112.5 3.7 constant_dynamic-update-slice_fusion
  116.2 6.6 fusion.11
  122.8 2.7 fusion.38
  125.7 2.8 add_convert_fusion.5
  129.9 2.1 copy.64
  133.5 4.7 add_convert_fusion.3
  139.0 37.0 %mixed_out.1 = bf16[3,8,320,128]{3,2,1,0:T(8,128)(2,1)S(1)} custom-call(bf16[3,320,1024]{2,1,0:T(8,128)(2,1)S(1)} %pad_maximum_fusion.2.x_ref), custom_call_target="tpu_custom_call" | custom-call | flops 34359738368 | bytes 16777216 | tf_op jit(solution)/shard_map/mixed_out/pallas_call | solution.py:781
  179.2 37.0 %attend.1 = (bf16[1,2560,128]{2,1,0:T(8,128)(2,1)S(1)}, f32[2,64,2560]{2,1,0:T(8,128)S(1)}, f32[2,1,2560]{2,1,0:T(1,128)S(1)}) custom-call(s32[2,10]{1,0:T(2,128)S(1)} %and_select_fusion.first_ref, s32[2,1,2560]{2,1,0:T(1,128)S(1)} %broadcast_in_dim.118.start_ref, bf16[3,2560,128]{2,1,0:T(8,128)(2,1)S(1)} %bitcast.173, bf16[3,2560,128]{2,1,0:T(8,128)(2,1)S(1)} %bitcast.174), custom_call_target="tpu_custom_call" | custom-call | flops 17179869184 | bytes 5242880 | tf_op jit(solution)/shard_map/attend/pallas_call | solution.py:102
  218.9 24.4 %attended_back.1 = bf16[1,320,1024]{2,1,0:T(8,128)(2,1)S(1)} custom-call(bf16[1,2560,128]{2,1,0:T(8,128)(2,1)S(1)} %get-tuple-element.100.x_ref), custom_call_target="tpu_custom_call" | custom-call | flops 34359738368 | bytes 16777216 | tf_op jit(solution)/shard_map/attended_back/pallas_call | solution.py:781
  243.7 4.5 fusion.37
  251.2 2.4 add_convert_fusion.refs_0_
  253.6 102.9 %feed_in.1 = (bf16[2,4,320,2048]{3,2,1,0:T(8,128)(2,1)}, f32[2,4,320,2048]{3,2,1,0:T(8,128)}, bf16[2,4,320,2048]{3,2,1,0:T(8,128)(2,1)}, bf16[2048,2048]{1,0:T(8,128)(2,1)}, bf16[2048,2048]{1,0:T(8,128)(2,1)}) custom-call(bf16[2,320,2048]{2,1,0:T(8,128)(2,1)} %add_convert_fusion.refs_0_, bf16[2048,2048]{1,0:T(8,128)(2,1)} %get-tuple-element.92.refs_1_, ...), custom_call_target="tpu_custom_call" | custom-call | flops 64424509440 | bytes 62914560 | tf_op jit(solution)/shard_map/feed_in/pallas_call | solution.py:992
  359.1 27.7 %weight_grad.1 = bf16[2048,2048]{1,0:T(8,128)(2,1)} custom-call(bf16[2560,2048]{1,0:T(8,128)(2,1)} %bitcast.228, bf16[2,320,2048]{2,1,0:T(8,128)(2,1)} %cot_0, bf16[2,320,1024]{2,1,0:T(8,128)(2,1)S(1)} %collective-permute-done.2.refs_1_.cot_1, bf16[2,320,1024]{2,1,0:T(8,128)(2,1)S(1)} %copy-done.14, bf16[2,320,1024]{2,1,0:T(8,128)(2,1)S(1)} %copy-done.12, ...), custom_call_target="tpu_custom_call" | custom-call | flops 21474836480 | bytes 33554432 | tf_op jit(solution)/shard_map/weight_grad/pallas_call | solution.py:673
  387.1 107.3 %feed_out.1 = (bf16[2,4,320,2048]{3,2,1,0:T(8,128)(2,1)}, bf16[2,320,1024]{2,1,0:T(8,128)(2,1)}, bf16[2,320,1024]{2,1,0:T(8,128)(2,1)}, bf16[2,320,1024]{2,1,0:T...) custom-call(bf16[2,320,2048]{2,1,0:T(8,128)(2,1)} %cot_0, ...), custom_call_target="tpu_custom_call" | custom-call | flops 85899345920 | bytes 62914560 | tf_op jit(solution)/shard_map/feed_out/pallas_call | solution.py:1215
  494.5 6.5 multiply_reduce_fusion
  510.8 33.3 %attended_grad_out.1 = (bf16[1,8,320,128]{3,2,1,0:T(8,128)(2,1)S(1)}, bf16[2048,2048]{1,0:T(8,128)(2,1)}, bf16[2,320,1024]{2,1,0:T(8,128)(2,1)S(1)}, bf16[2,320,1024]{2,1,0:T(8,128)(2,1)S(1)}) custom-call(bf16[1,320,1024]{2,1,0:T(8,128)(2,1)S(1)} %copy.72.x_ref, bf16[2560,2048]{1,0:T(8,128)(2,1)} %bitcast.227, bf16[2560,2048]{1,0:T(8,128)(2,1)} %bitcast.226, ...), custom_call_target="tpu_custom_call" | custom-call | flops 34359738368 | bytes 16777216 | tf_op jit(solution)/shard_map/attended_grad_out/pallas_call | solution.py:781
  545.0 2.6 convert_reduce_fusion
  547.9 4.5 bitcast_convert_fusion.1
  553.8 1.8 collective-permute-start.8
  555.9 1.9 collective-permute-start.9
  560.8 41.0 %attend_back.1.x_ref = bf16[3,2576,128]{2,1,0:T(8,128)(2,1)S(1)} custom-call(s32[2,10]{1,0:T(2,128)S(1)} %copy-done.9, s32[2,1,2560]{2,1,0:T(1,128)S(1)} %copy-done.7, bf16[3,2560,128]{2,1,0:T(8,128)(2,1)S(1)} %bitcast.175, bf16[3,2560,128]{2,1,0:T(8,128)(2,1)S(1)} %bitcast.176, bf16[1,2560,128]{2,1,0:T(8,128)(2,1)S(1)} %bitcast.177, ...), custom_call_target="tpu_custom_call" | custom-call | flops 34359738368 | bytes 5242880 | tf_op jit(solution)/shard_map/attend_back/pallas_call | solution.py:195
  604.0 56.3 %mixed_grad_back.1 = (bf16[3,336,1024]{2,1,0:T(8,128)(2,1)}, bf16[2,320,1024]{2,1,0:T(8,128)(2,1)S(1)}, bf16[2,320,1024]{2,1,0:T(8,128)(2,1)S(1)}) custom-call(bf16[3,2576,128]{2,1,0:T(8,128)(2,1)} %copy-done.21, bf16[2,320,1024]{2,1,0:T(8,128)(2,1)S(1)} %copy-done.23, bf16[2,320,1024]{2,1,0:T(8,128)(2,1)S(1)} %copy-done.24), custom_call_target="tpu_custom_call" | custom-call | flops 34359738368 | bytes 16777216 | tf_op jit(solution)/shard_map/mixed_grad_back/pallas_call | solution.py:781
  660.4 1.8 fusion.20.refs_0_
  668.5 3.2 multiply_reduce_fusion.5
  671.7 2.2 fusion.33
  673.9 1.7 collective-permute-start.14
  678.0 8.1 fusion.9
  686.1 5.3 bitcast_convert_fusion
  694.6 3.1 fusion.30
  697.7 2.9 copy.86
  700.6 3.0 copy.87
  703.6 2.9 copy.88
  706.6 2.8 multiply_reduce_fusion.8
  710.1 4.2 fusion.7
  714.4 2.5 fusion.19
  717.9 8.5 add_add_fusion.2
  729.2 3.9 maximum_convert_fusion
  733.8 3.1 bitcast_convert_fusion.2
  739.9 97.2 %finish.1 = (bf16[4,64,2048]{2,1,0:T(8,128)(2,1)}, f32[8,1024]{1,0:T(8,128)}, f32[8,256]{1,0:T(8,128)}, bf16[2,320,1024]{2,1,0:T(8,128)(2,1)}, bf16[2,320,1024]{2,1,0:T(8,128)(2,1)}) custom-call(bf16[4,2,4,32,2048]{4,3,2,1,0:T(8,128)(2,1)} %bitcast.231, bf16[4,2,4,16,2048]{4,3,2,1,0:T(8,128)(2,1)} %bitcast.198, bf16[4,2,4,16,2048]{4,3,2,1,0:T(8,128)(2,1)} %bitcast.232, ...), custom_call_target="tpu_custom_call" | custom-call | flops 68719476736 | bytes 67108864 | tf_op jit(solution)/shard_map/finish/pallas_call | solution.py:1480
  842.6 3.4 bitcast_add_fusion
  846.7 2.3 fusion.8
  852.5 3.9 convert_bitcast_fusion
  856.3 9.2 %copy.82 = f32[2048,1024]{1,0:T(8,128)} copy(f32[2048,1024]{0,1:T(8,128)} %convert_bitcast_fusion) | data formatting | bytes 16777216
  (320 shorter events, 75.0 us)
Async XLA Ops:
  7.2 545.3 %reduce-scatter.3.cloned.1.call-start = ((), (), s32[]{:S(2)}) async-start(), calls=%async_computation.2 | async-start | bytes 9437184 | tf_op jit(solution)/shard_map/reduce_scatter | solution.py:1675
  100.1 10.3 %copy-start.57 = (bf16[2,16,2048]{2,1,0:T(8,128)(2,1)S(1)}, bf16[2,16,2048]{2,1,0:T(8,128)(2,1)}, u32[]{:S(2)}) copy-start(bf16[2,16,2048]{2,1,0:T(8,128)(2,1)} %get-tuple-element.87) | copy-start | bytes 393220
  100.1 11.0 %copy-start.86 = (f32[8,8,256]{2,1,0:T(8,128)S(1)}, f32[8,8,256]{2,1,0:T(8,128)}, u32[]{:S(2)}) copy-start(f32[8,8,256]{2,1,0:T(8,128)} %get-tuple-element.86) | copy-start | bytes 196612
  100.1 11.0 %copy-start.94 = (s32[1,4]{1,0:T(1,128)S(1)}, s32[1,4]{1,0:T(1,128)}, u32[]{:S(2)}) copy-start(s32[1,4]{1,0:T(1,128)} %param.19) | copy-start | bytes 52
  100.1 11.3 %copy-start.95 = (s32[1,2]{1,0:T(1,128)S(1)}, s32[1,2]{1,0:T(1,128)}, u32[]{:S(2)}) copy-start(s32[1,2]{1,0:T(1,128)} %param.20) | copy-start | bytes 28
  100.1 75.9 %collective-permute-start.2 = (bf16[2,320,1024]{2,1,0:T(8,128)(2,1)}, bf16[2,320,1024]{2,1,0:T(8,128)(2,1)S(1)}, u32[]{:S(2)}, u32[]{:S(2)}) collective-permute-start(bf16[2,320,1024]{2,1,0:T(8,128)(2,1)} %get-tuple-element.218), channel_id=1, source_target_pairs={{0,8},{8,0},{16,24},{24,16},{1,9},{9,1},{17,25},{25,17},{2,10},{10... | collective-permute-start | bytes 3932168 | tf_op jit(solution)/shard_map/ppermute | solution.py:1523
  101.7 74.4 %collective-permute-start.4 = (bf16[2,320,1024]{2,1,0:T(8,128)(2,1)}, bf16[2,320,1024]{2,1,0:T(8,128)(2,1)S(1)}, u32[]{:S(2)}, u32[]{:S(2)}) collective-permute-start(bf16[2,320,1024]{2,1,0:T(8,128)(2,1)} %get-tuple-element.218), channel_id=1, source_target_pairs={{0,16},{8,24},{16,0},{24,8},{1,17},{9,25},{17,1},{25,9},{2,18},{10... | collective-permute-start | bytes 3932168 | tf_op jit(solution)/shard_map/ppermute | solution.py:1523
  106.3 31.9 %collective-permute-start = (bf16[256,2048]{1,0:T(8,128)(2,1)}, bf16[256,2048]{1,0:T(8,128)(2,1)}, u32[]{:S(2)}, u32[]{:S(2)}) collective-permute-start(bf16[256,2048]{1,0:T(8,128)(2,1)} %get-tuple-element.207), channel_id=1, source_target_pairs={{2,0},{3,1},{10,8},{11,9},{18,16},{19,17},{26,24},{27,25}} | collective-permute-start | bytes 3145736 | tf_op jit(solution)/shard_map/ppermute | solution.py:1559
  107.6 31.2 %collective-permute-start.1 = (bf16[256,2048]{1,0:T(8,128)(2,1)}, bf16[256,2048]{1,0:T(8,128)(2,1)}, u32[]{:S(2)}, u32[]{:S(2)}) collective-permute-start(bf16[256,2048]{1,0:T(8,128)(2,1)} %get-tuple-element.206), channel_id=1, source_target_pairs={{4,6},{5,7},{12,14},{13,15},{20,22},{21,23},{28,30},{29,31}} | collective-permute-start | bytes 3145736 | tf_op jit(solution)/shard_map/ppermute | solution.py:1559
  109.8 66.2 %collective-permute-start.3 = (bf16[2,320,1024]{2,1,0:T(8,128)(2,1)}, bf16[2,320,1024]{2,1,0:T(8,128)(2,1)}, u32[]{:S(2)}, u32[]{:S(2)}) collective-permute-start(bf16[2,320,1024]{2,1,0:T(8,128)(2,1)} %get-tuple-element.217), channel_id=1, source_target_pairs={{0,16},{8,24},{16,0},{24,8},{1,17},{9,25},{17,1},{25,9},{2,18},{10... | collective-permute-start | bytes 3932168 | tf_op jit(solution)/shard_map/ppermute | solution.py:1523
  112.4 21.0 %copy-start.64 = (pred[2,320]{1,0:T(4,128)(4,1)}, pred[2,320]{1,0:T(4,128)(4,1)S(1)}, u32[]{:S(2)}) copy-start(pred[2,320]{1,0:T(4,128)(4,1)S(1)} %get-tuple-element.246) | copy-start | bytes 1924
  112.5 21.0 %copy-start.66 = (pred[2,320]{1,0:T(4,128)(4,1)}, pred[2,320]{1,0:T(4,128)(4,1)S(1)}, u32[]{:S(2)}) copy-start(pred[2,320]{1,0:T(4,128)(4,1)S(1)} %get-tuple-element.248) | copy-start | bytes 1924
  128.6 50.6 %copy-start.6 = (s32[2,1,2560]{2,1,0:T(1,128)}, s32[2,1,2560]{2,1,0:T(1,128)S(1)}, u32[]{:S(2)}) copy-start(s32[2,1,2560]{2,1,0:T(1,128)S(1)} %broadcast_in_dim.118.start_ref) | copy-start | bytes 61444
  133.4 45.8 %copy-start.8 = (s32[2,10]{1,0:T(2,128)}, s32[2,10]{1,0:T(2,128)S(1)}, u32[]{:S(2)}) copy-start(s32[2,10]{1,0:T(2,128)S(1)} %and_select_fusion.first_ref) | copy-start | bytes 244
  138.2 37.8 %collective-permute-start.5 = (bf16[2,320,1024]{2,1,0:T(8,128)(2,1)}, bf16[2,320,1024]{2,1,0:T(8,128)(2,1)S(1)}, u32[]{:S(2)}, u32[]{:S(2)}) collective-permute-start(bf16[2,320,1024]{2,1,0:T(8,128)(2,1)} %get-tuple-element.217), channel_id=1, source_target_pairs={{0,8},{8,0},{16,24},{24,16},{1,9},{9,1},{17,25},{25,17},{2,10},{10... | collective-permute-start | bytes 3932168 | tf_op jit(solution)/shard_map/ppermute | solution.py:1523
  176.0 40.2 %copy-start.15 = (bf16[3,8,320,128]{3,2,1,0:T(8,128)(2,1)}, bf16[3,8,320,128]{3,2,1,0:T(8,128)(2,1)S(1)}, u32[]{:S(2)}) copy-start(bf16[3,8,320,128]{3,2,1,0:T(8,128)(2,1)S(1)} %mixed_out.1) | copy-start | bytes 5898244
  176.0 180.4 %copy-start.10 = (bf16[2,320,1024]{2,1,0:T(8,128)(2,1)}, bf16[2,320,1024]{2,1,0:T(8,128)(2,1)S(1)}, u32[]{:S(2)}) copy-start(bf16[2,320,1024]{2,1,0:T(8,128)(2,1)S(1)} %collective-permute-done.2.refs_1_.cot_1) | copy-start | bytes 3932164
  176.1 40.2 %copy-start.11 = (bf16[2,320,1024]{2,1,0:T(8,128)(2,1)}, bf16[2,320,1024]{2,1,0:T(8,128)(2,1)S(1)}, u32[]{:S(2)}) copy-start(bf16[2,320,1024]{2,1,0:T(8,128)(2,1)S(1)} %collective-permute-done.4.refs_3_.cot_3) | copy-start | bytes 3932164
  176.1 40.2 %copy-start.13 = (bf16[2,320,1024]{2,1,0:T(8,128)(2,1)}, bf16[2,320,1024]{2,1,0:T(8,128)(2,1)S(1)}, u32[]{:S(2)}) copy-start(bf16[2,320,1024]{2,1,0:T(8,128)(2,1)S(1)} %collective-permute-done.5.refs_2_.cot_2) | copy-start | bytes 3932164
  176.1 41.3 %collective-permute-start.6 = (bf16[2,320,1024]{2,1,0:T(8,128)(2,1)S(1)}, bf16[2,320,1024]{2,1,0:T(8,128)(2,1)S(1)}, u32[]{:S(2)}, u32[]{:S(2)}) collective-permute-start(bf16[2,320,1024]{2,1,0:T(8,128)(2,1)S(1)} %collective-permute-done.2.refs_1_.cot_1), channel_id=1, source_target_pairs={{0,16},{8,24},{16,0},{24,8},{1,17},{9,25},{17,1},{25,9},{2,18},{10... | collective-permute-start | bytes 3932168 | tf_op jit(solution)/shard_map/ppermute | solution.py:1523
  177.7 39.8 %collective-permute-start.7 = (bf16[2,320,1024]{2,1,0:T(8,128)(2,1)}, bf16[2,320,1024]{2,1,0:T(8,128)(2,1)S(1)}, u32[]{:S(2)}, u32[]{:S(2)}) collective-permute-start(bf16[2,320,1024]{2,1,0:T(8,128)(2,1)} %collective-permute-done.3.refs_4_.cot_4), channel_id=1, source_target_pairs={{0,8},{8,0},{16,24},{24,16},{1,9},{9,1},{17,25},{25,17},{2,10},{10... | collective-permute-start | bytes 3932168 | tf_op jit(solution)/shard_map/ppermute | solution.py:1523
  386.8 284.9 %reduce-scatter.5.cloned.1.call-start = ((), (), s32[]{:S(2)}) async-start(), calls=%async_computation.3 | async-start | bytes 9437184 | tf_op jit(solution)/shard_map/reduce_scatter | solution.py:1695
  387.1 107.3 %copy-start.59 = (f32[2,320]{1,0:T(2,128)S(1)}, f32[2,320]{1,0:T(2,128)}, u32[]{:S(2)}) copy-start(f32[2,320]{1,0:T(2,128)} %copy-done.58) | copy-start | bytes 7684
  387.1 107.3 %copy-start.61 = (f32[2048]{0:T(1024)S(1)}, f32[2048]{0:T(1024)}, u32[]{:S(2)}) copy-start(f32[2048]{0:T(1024)} %param.30) | copy-start | bytes 24580
  387.1 107.3 %copy-start.63 = (f32[2,320]{1,0:T(2,128)S(1)}, f32[2,320]{1,0:T(2,128)}, u32[]{:S(2)}) copy-start(f32[2,320]{1,0:T(2,128)} %copy-done.62) | copy-start | bytes 7684
  544.9 118.8 %copy-start = (bf16[2,320,1024]{2,1,0:T(8,128)(2,1)}, bf16[2,320,1024]{2,1,0:T(8,128)(2,1)S(1)}, u32[]{:S(2)}) copy-start(bf16[2,320,1024]{2,1,0:T(8,128)(2,1)S(1)} %get-tuple-element.139) | copy-start | bytes 3932164
  547.9 9.9 %copy-start.7 = (s32[2,1,2560]{2,1,0:T(1,128)S(1)}, s32[2,1,2560]{2,1,0:T(1,128)}, u32[]{:S(2)}) copy-start(s32[2,1,2560]{2,1,0:T(1,128)} %copy-done.6) | copy-start | bytes 61444
  547.9 9.9 %copy-start.9 = (s32[2,10]{1,0:T(2,128)S(1)}, s32[2,10]{1,0:T(2,128)}, u32[]{:S(2)}) copy-start(s32[2,10]{1,0:T(2,128)} %copy-done.8) | copy-start | bytes 244
  547.9 9.9 %copy-start.18 = (bf16[1,8,320,128]{3,2,1,0:T(8,128)(2,1)S(1)}, bf16[1,8,320,128]{3,2,1,0:T(8,128)(2,1)}, u32[]{:S(2)}) copy-start(bf16[1,8,320,128]{3,2,1,0:T(8,128)(2,1)} %copy-done.17) | copy-start | bytes 1966084
  553.7 49.3 %collective-permute-start.10 = (bf16[256,1024]{1,0:T(8,128)(2,1)S(1)}, bf16[256,1024]{1,0:T(8,128)(2,1)S(1)}, u32[]{:S(2)}, u32[]{:S(2)}) collective-permute-start(bf16[256,1024]{1,0:T(8,128)(2,1)S(1)} %get-tuple-element.230), channel_id=1, source_target_pairs={{0,16},{8,24},{16,0},{24,8},{1,17},{9,25},{17,1},{25,9},{2,18},{10... | collective-permute-start | bytes 1572872 | tf_op jit(solution)/shard_map/ppermute | solution.py:1523
  553.8 49.2 %collective-permute-start.8 = (bf16[256,1024]{1,0:T(8,128)(2,1)S(1)}, bf16[256,1024]{1,0:T(8,128)(2,1)S(1)}, u32[]{:S(2)}, u32[]{:S(2)}) collective-permute-start(bf16[256,1024]{1,0:T(8,128)(2,1)S(1)} %get-tuple-element.230), channel_id=1, source_target_pairs={{0,8},{8,0},{16,24},{24,16},{1,9},{9,1},{17,25},{25,17},{2,10},{10... | collective-permute-start | bytes 1572872 | tf_op jit(solution)/shard_map/ppermute | solution.py:1523
  555.6 47.4 %collective-permute-start.11 = (bf16[256,1024]{1,0:T(8,128)(2,1)S(1)}, bf16[256,1024]{1,0:T(8,128)(2,1)S(1)}, u32[]{:S(2)}, u32[]{:S(2)}) collective-permute-start(bf16[256,1024]{1,0:T(8,128)(2,1)S(1)} %get-tuple-element.229), channel_id=1, source_target_pairs={{0,8},{8,0},{16,24},{24,16},{1,9},{9,1},{17,25},{25,17},{2,10},{10... | collective-permute-start | bytes 1572872 | tf_op jit(solution)/shard_map/ppermute | solution.py:1523
  555.9 47.1 %collective-permute-start.9 = (bf16[256,1024]{1,0:T(8,128)(2,1)S(1)}, bf16[256,1024]{1,0:T(8,128)(2,1)S(1)}, u32[]{:S(2)}, u32[]{:S(2)}) collective-permute-start(bf16[256,1024]{1,0:T(8,128)(2,1)S(1)} %get-tuple-element.229), channel_id=1, source_target_pairs={{0,16},{8,24},{16,0},{24,8},{1,17},{9,25},{17,1},{25,9},{2,18},{10... | collective-permute-start | bytes 1572872 | tf_op jit(solution)/shard_map/ppermute | solution.py:1523
  560.8 43.2 %copy-start.23 = (bf16[2,320,1024]{2,1,0:T(8,128)(2,1)S(1)}, bf16[2,320,1024]{2,1,0:T(8,128)(2,1)}, u32[]{:S(2)}) copy-start(bf16[2,320,1024]{2,1,0:T(8,128)(2,1)} %get-tuple-element.127.refs_0_) | copy-start | bytes 3932164
  560.8 43.2 %copy-start.24 = (bf16[2,320,1024]{2,1,0:T(8,128)(2,1)S(1)}, bf16[2,320,1024]{2,1,0:T(8,128)(2,1)}, u32[]{:S(2)}) copy-start(bf16[2,320,1024]{2,1,0:T(8,128)(2,1)} %get-tuple-element.128.refs_1_) | copy-start | bytes 3932164
  603.0 63.2 %collective-permute-start.12 = (bf16[256,1024]{1,0:T(8,128)(2,1)S(1)}, bf16[256,1024]{1,0:T(8,128)(2,1)S(1)}, u32[]{:S(2)}, u32[]{:S(2)}) collective-permute-start(bf16[256,1024]{1,0:T(8,128)(2,1)S(1)} %collective-permute-done.8), channel_id=1, source_target_pairs={{0,16},{8,24},{16,0},{24,8},{1,17},{9,25},{17,1},{25,9},{2,18},{10... | collective-permute-start | bytes 1572872 | tf_op jit(solution)/shard_map/ppermute | solution.py:1523
  603.1 63.1 %collective-permute-start.13 = (bf16[256,1024]{1,0:T(8,128)(2,1)S(1)}, bf16[256,1024]{1,0:T(8,128)(2,1)S(1)}, u32[]{:S(2)}, u32[]{:S(2)}) collective-permute-start(bf16[256,1024]{1,0:T(8,128)(2,1)S(1)} %collective-permute-done.9), channel_id=1, source_target_pairs={{0,8},{8,0},{16,24},{24,16},{1,9},{9,1},{17,25},{25,17},{2,10},{10... | collective-permute-start | bytes 1572872 | tf_op jit(solution)/shard_map/ppermute | solution.py:1523
  604.0 56.4 %copy-start.41 = (bf16[2,2,320,1024]{3,2,1,0:T(8,128)(2,1)S(1)}, bf16[2,2,320,1024]{3,2,1,0:T(8,128)(2,1)}, u32[]{:S(2)}) copy-start(bf16[2,2,320,1024]{3,2,1,0:T(8,128)(2,1)} %get-tuple-element.114) | copy-start | bytes 7864324
  673.9 63.0 %collective-permute-start.14 = (bf16[256,1024]{1,0:T(8,128)(2,1)}, bf16[256,1024]{1,0:T(8,128)(2,1)}, u32[]{:S(2)}, u32[]{:S(2)}) collective-permute-start(bf16[256,1024]{1,0:T(8,128)(2,1)} %get-tuple-element.228), channel_id=1, source_target_pairs={{0,8},{8,0},{16,24},{24,16},{1,9},{9,1},{17,25},{25,17},{2,10},{10... | collective-permute-start | bytes 1572872 | tf_op jit(solution)/shard_map/ppermute | solution.py:1523
  675.6 61.3 %collective-permute-start.16 = (bf16[256,1024]{1,0:T(8,128)(2,1)}, bf16[256,1024]{1,0:T(8,128)(2,1)}, u32[]{:S(2)}, u32[]{:S(2)}) collective-permute-start(bf16[256,1024]{1,0:T(8,128)(2,1)} %get-tuple-element.228), channel_id=1, source_target_pairs={{0,16},{8,24},{16,0},{24,8},{1,17},{9,25},{17,1},{25,9},{2,18},{10... | collective-permute-start | bytes 1572872 | tf_op jit(solution)/shard_map/ppermute | solution.py:1523
  677.1 9.0 %copy-start.33 = (bf16[2,320,2048]{2,1,0:T(8,128)(2,1)S(1)}, bf16[2,320,2048]{2,1,0:T(8,128)(2,1)}, u32[]{:S(2)}) copy-start(bf16[2,320,2048]{2,1,0:T(8,128)(2,1)} %get-tuple-element.88) | copy-start | bytes 7864324
  677.1 9.0 %copy-start.49 = (bf16[2,320,1024]{2,1,0:T(8,128)(2,1)S(1)}, bf16[2,320,1024]{2,1,0:T(8,128)(2,1)}, u32[]{:S(2)}) copy-start(bf16[2,320,1024]{2,1,0:T(8,128)(2,1)} %get-tuple-element.135) | copy-start | bytes 3932164
  677.1 59.8 %collective-permute-start.15 = (bf16[256,1024]{1,0:T(8,128)(2,1)}, bf16[256,1024]{1,0:T(8,128)(2,1)}, u32[]{:S(2)}, u32[]{:S(2)}) collective-permute-start(bf16[256,1024]{1,0:T(8,128)(2,1)} %get-tuple-element.227), channel_id=1, source_target_pairs={{0,16},{8,24},{16,0},{24,8},{1,17},{9,25},{17,1},{25,9},{2,18},{10... | collective-permute-start | bytes 1572872 | tf_op jit(solution)/shard_map/ppermute | solution.py:1523
  677.7 59.3 %collective-permute-start.17 = (bf16[256,1024]{1,0:T(8,128)(2,1)}, bf16[256,1024]{1,0:T(8,128)(2,1)}, u32[]{:S(2)}, u32[]{:S(2)}) collective-permute-start(bf16[256,1024]{1,0:T(8,128)(2,1)} %get-tuple-element.227), channel_id=1, source_target_pairs={{0,8},{8,0},{16,24},{24,16},{1,9},{9,1},{17,25},{25,17},{2,10},{10... | collective-permute-start | bytes 1572872 | tf_op jit(solution)/shard_map/ppermute | solution.py:1523
  717.9 8.6 copy-start.51
  717.9 8.7 copy-start.39
  736.9 112.0 %collective-permute-start.18 = (bf16[256,1024]{1,0:T(8,128)(2,1)}, bf16[256,1024]{1,0:T(8,128)(2,1)S(1)}, u32[]{:S(2)}, u32[]{:S(2)}) collective-permute-start(bf16[256,1024]{1,0:T(8,128)(2,1)} %collective-permute-done.14), channel_id=1, source_target_pairs={{0,16},{8,24},{16,0},{24,8},{1,17},{9,25},{17,1},{25,9},{2,18},{10... | collective-permute-start | bytes 1572872 | tf_op jit(solution)/shard_map/ppermute | solution.py:1523
  738.4 110.6 %collective-permute-start.19 = (bf16[256,1024]{1,0:T(8,128)(2,1)}, bf16[256,1024]{1,0:T(8,128)(2,1)}, u32[]{:S(2)}, u32[]{:S(2)}) collective-permute-start(bf16[256,1024]{1,0:T(8,128)(2,1)} %collective-permute-done.15), channel_id=1, source_target_pairs={{0,8},{8,0},{16,24},{24,16},{1,9},{9,1},{17,25},{25,17},{2,10},{10... | collective-permute-start | bytes 1572872 | tf_op jit(solution)/shard_map/ppermute | solution.py:1523
  (77 other events, 249.1 us)
Sparse Core Ops, SparseCore 0:
  387.0 90.8 reduce-scatter.2
  545.1 107.1 reduce-scatter.4

commit v4 on v3

--- a/solution.py
+++ b/solution.py
@@ -8,7 +8,8 @@
 from jax.sharding import PartitionSpec as P
 
 HD = 64
-BLOCK = 256
+QUERIES, KEYS = 512, 512
+WIDE = 256
 CHUNK = 512
 VMEM_LIMIT = 62 * 1024 * 1024
 MESH = pl.DeviceIdType.MESH
@@ -35,9 +36,14 @@
 
 
 def allowed_pairs(start_row, key_block, query_block):
-    keys = key_block * BLOCK + lax.broadcasted_iota(jnp.int32, (BLOCK, BLOCK), 0)
-    queries = query_block * BLOCK + lax.broadcasted_iota(jnp.int32, (BLOCK, BLOCK), 1)
+    shape = (KEYS, QUERIES)
+    keys = key_block * KEYS + lax.broadcasted_iota(jnp.int32, shape, 0)
+    queries = query_block * QUERIES + lax.broadcasted_iota(jnp.int32, (1, QUERIES), 1)
     return (keys <= queries) & (keys >= start_row)
+
+
+def key_blocks(first_ref, s, step):
+    return first_ref[s, step], ((step + 1) * QUERIES + KEYS - 1) // KEYS
 
 
 def attend_kernel(
@@ -48,20 +54,20 @@
     @pl.when(step == 0)
     def _():
         def turn(at, carry):
-            rows = pl.ds(pl.multiple_of(at * BLOCK, BLOCK), BLOCK)
+            rows = pl.ds(pl.multiple_of(at * KEYS, KEYS), KEYS)
             both = v_ref[0, rows, :].T
             values_t[at] = jnp.where(s == 0, both[:HD], both[HD:])
             return carry
 
         lax.fori_loop(0, values_t.shape[0], turn, 0)
 
-    here = pl.ds(pl.multiple_of(step * BLOCK, BLOCK), BLOCK)
+    here = pl.ds(pl.multiple_of(step * QUERIES, QUERIES), QUERIES)
     query_t = (qk_ref[0, here, 0:HD] * HD ** (-0.5)).astype(LOW).T
     start_row = start_ref[0]
 
     def one(at, carry):
         top, summed, acc = carry
-        rows = pl.ds(pl.multiple_of(at * BLOCK, BLOCK), BLOCK)
+        rows = pl.ds(pl.multiple_of(at * KEYS, KEYS), KEYS)
         scores = dot(qk_ref[0, rows, HD : 2 * HD], query_t)
         scores = jnp.where(allowed_pairs(start_row, at, step), scores, -1e30)
         new_top = jnp.maximum(top, jnp.max(scores, axis=0, keepdims=True))
@@ -72,13 +78,12 @@
         return new_top, summed, acc
 
     top, summed, acc = lax.fori_loop(
-        first_ref[s, step],
-        step + 1,
+        *key_blocks(first_ref, s, step),
         one,
         (
-            jnp.full((1, BLOCK), -1e30, F32),
-            jnp.zeros((1, BLOCK), F32),
-            jnp.zeros((HD, BLOCK), F32),
+            jnp.full((1, QUERIES), -1e30, F32),
+            jnp.zeros((1, QUERIES), F32),
+            jnp.zeros((HD, QUERIES), F32),
         ),
     )
     result = acc / summed
@@ -97,8 +102,8 @@
 
 def attend(mixed, starts):
     group = mixed.shape[1]
-    steps = group // BLOCK
-    row = pl.BlockSpec((1, 1, BLOCK), lambda s, i, first: (s, 0, i))
+    steps = group // QUERIES
+    row = pl.BlockSpec((1, 1, QUERIES), lambda s, i, first: (s, 0, i))
     return pl.pallas_call(
         attend_kernel,
         grid_spec=pltpu.PrefetchScalarGridSpec(
@@ -111,10 +116,10 @@
             ],
             out_specs=[
                 pl.BlockSpec((1, group, 2 * HD), lambda s, i, first: (0, 0, 0)),
-                pl.BlockSpec((1, HD, BLOCK), lambda s, i, first: (s, 0, i)),
+                pl.BlockSpec((1, HD, QUERIES), lambda s, i, first: (s, 0, i)),
                 row,
             ],
-            scratch_shapes=[pltpu.VMEM((steps, HD, BLOCK), LOW)],
+            scratch_shapes=[pltpu.VMEM((group // KEYS, HD, KEYS), LOW)],
         ),
         out_shape=[
             jax.ShapeDtypeStruct((1, group, 2 * HD), LOW),
@@ -126,7 +131,7 @@
             flops=2**34, bytes_accessed=group * 2048, transcendentals=group * group // 4
         ),
         name="attend",
-    )(starts[:, ::BLOCK] // BLOCK, starts[:, None, :], mixed, mixed)
+    )(starts[:, ::QUERIES] // KEYS, starts[:, None, :], mixed, mixed)
 
 
 def attend_back_kernel(
@@ -139,7 +144,7 @@
     @pl.when(step == 0)
     def _():
         def turn(at, carry):
-            rows = pl.ds(pl.multiple_of(at * BLOCK, BLOCK), BLOCK)
+            rows = pl.ds(pl.multiple_of(at * KEYS, KEYS), KEYS)
             keys_t[at] = qk_ref[0, rows, HD : 2 * HD].T
             both = v_ref[0, rows, :]
             values[rows, :] = jnp.where(s == 0, both[:, :HD], both[:, HD:])
@@ -149,7 +154,7 @@
         grad_keys[...] = jnp.zeros(grad_keys.shape, F32)
         grad_values[...] = jnp.zeros(grad_values.shape, F32)
 
-    here = pl.ds(pl.multiple_of(step * BLOCK, BLOCK), BLOCK)
+    here = pl.ds(pl.multiple_of(step * QUERIES, QUERIES), QUERIES)
     query = (qk_ref[0, here, 0:HD] * HD ** (-0.5)).astype(LOW)
     query_t = query.T
     both = grad_ref[0]
@@ -160,7 +165,7 @@
     inner = jnp.sum(grad_t.astype(F32) * wide_ref[0], axis=0, keepdims=True)
 
     def one(at, acc):
-        rows = pl.ds(pl.multiple_of(at * BLOCK, BLOCK), BLOCK)
+        rows = pl.ds(pl.multiple_of(at * KEYS, KEYS), KEYS)
         scores = dot(qk_ref[0, rows, HD : 2 * HD], query_t)
         scores = jnp.where(allowed_pairs(start_row, at, step), scores, -1e30)
         probs = jnp.exp(scores - total)
@@ -170,7 +175,9 @@
         grad_keys[rows, :] += dot(grad_scores, query)
         return acc + dot(keys_t[at], grad_scores)
 
-    acc = lax.fori_loop(first_ref[s, step], step + 1, one, jnp.zeros((HD, BLOCK), F32))
+    acc = lax.fori_loop(
+        *key_blocks(first_ref, s, step), one, jnp.zeros((HD, QUERIES), F32)
+    )
     out_ref[s, here, 0:HD] = (acc * HD ** (-0.5)).T.astype(out_ref.dtype)
 
     @pl.when(step == pl.num_programs(1) - 1)
@@ -190,8 +197,8 @@
 
 def attend_back(mixed, grad, wide, total, starts, halo):
     group = mixed.shape[1]
-    steps = group // BLOCK
-    row = pl.BlockSpec((1, 1, BLOCK), lambda s, i, first: (s, 0, i))
+    steps = group // QUERIES
+    row = pl.BlockSpec((1, 1, QUERIES), lambda s, i, first: (s, 0, i))
     return pl.pallas_call(
         attend_back_kernel,
         grid_spec=pltpu.PrefetchScalarGridSpec(
@@ -201,13 +208,13 @@
                 row,
                 pl.BlockSpec((1, group, 2 * HD), lambda s, i, first: (s, 0, 0)),
                 pl.BlockSpec((1, group, 2 * HD), lambda s, i, first: (2, 0, 0)),
-                pl.BlockSpec((1, BLOCK, 2 * HD), lambda s, i, first: (0, i, 0)),
-                pl.BlockSpec((1, HD, BLOCK), lambda s, i, first: (s, 0, i)),
+                pl.BlockSpec((1, QUERIES, 2 * HD), lambda s, i, first: (0, i, 0)),
+                pl.BlockSpec((1, HD, QUERIES), lambda s, i, first: (s, 0, i)),
                 row,
             ],
             out_specs=pl.BlockSpec((3, group + halo, 2 * HD), lambda s, i, first: (0, 0, 0)),
             scratch_shapes=[
-                pltpu.VMEM((steps, HD, BLOCK), LOW),
+                pltpu.VMEM((group // KEYS, HD, KEYS), LOW),
                 pltpu.VMEM((group, HD), LOW),
                 pltpu.VMEM((group, HD), F32),
                 pltpu.VMEM((group, HD), F32),
@@ -219,7 +226,7 @@
             flops=2**35, bytes_accessed=group * 2048, transcendentals=group * group // 4
         ),
         name="attend_back",
-    )(starts[:, ::BLOCK] // BLOCK, starts[:, None, :], mixed, mixed, grad, wide, total)
+    )(starts[:, ::QUERIES] // KEYS, starts[:, None, :], mixed, mixed, grad, wide, total)
 
 
 def plane_partners():
@@ -357,246 +364,7 @@
     return range(1, count // 2 + 1)
 
 
-def prepare_kernel(
-    inputs_ref, gain_ref, shift_ref, qk_ref, v_ref, out_ref, taps_ref, up_ref,
-    all_qk_ref, all_v_ref, all_out_ref, all_taps_ref, normed_ref, halo_ref, up_all_ref,
-    rows, normed, all_qk, all_v, all_out, up_all, local, *sems,
-):
-    mp = lax.axis_size("mp")
-    dp = lax.axis_index("dp")
-    me = lax.axis_index("mp")
-    z, core = mesh_place()
-    count = mp // 2
-    rows_here, depth = rows.shape[1:]
-    to_x, to_y = plane_partners()
-    share = up_ref.shape[0]
-    owned = (qk_ref, v_ref, out_ref)
-    whole = (all_qk, all_v, all_out)
-    (plane_send_sem, plane_recv_sem, plane_swap_send, plane_swap_recv) = sems[:4]
-    taps_send, taps_recv, halo_send, halo_recv = sems[4:8]
-    line_sems = [sems[8 + 4 * part : 12 + 4 * part] for part in range(4)]
-
-    def up_place(at, at_core):
-        start = pl.multiple_of((2 * at + at_core) * share, 16)
-        return up_all.at[pl.ds(start, share), :]
-
-    loads = [
-        pltpu.make_async_copy(inputs_ref, rows, local.at[0]),
-        pltpu.make_async_copy(taps_ref, all_taps_ref.at[me], local.at[1]),
-        pltpu.make_async_copy(up_ref, up_place(z, core), local.at[2]),
-    ] + [
-        pltpu.make_async_copy(
-            owned[part].at[dp], whole[part].at[z, core, dp], local.at[3 + part]
-        )
-        for part in range(3)
-    ]
-    for copy in loads:
-        copy.start()
-
-    barrier = pltpu.get_barrier_semaphore()
-    for step in range(1, mp):
-        pl.semaphore_signal(
-            barrier, inc=1, device_id={"mp": lax.rem(me + step, mp)}, device_id_type=MESH
-        )
-    for partner in (to_x, to_y):
-        pl.semaphore_signal(barrier, inc=1, device_id=partner, device_id_type=MESH)
-    pl.semaphore_wait(barrier, mp + 1)
-    for copy in loads[1:]:
-        copy.wait()
-
-    lines = [
-        LineGather(lambda at, at_core, part=part: whole[part].at[at, at_core, dp], *line_sems[part])
-        for part in range(3)
-    ]
-    up_line = LineGather(up_place, *line_sems[3])
-    for line in lines:
-        line.start(1)
-    tap_copies = [
-        (
-            wire(
-                taps_ref, all_taps_ref.at[me], taps_send.at[step], taps_recv.at[step],
-                {"mp": lax.rem(me + step, mp)},
-            ),
-            wire(
-                taps_ref, all_taps_ref.at[lax.rem(me + mp - step, mp)], taps_send.at[step],
-                taps_recv.at[step], {"mp": lax.rem(me + step, mp)},
-            ),
-        )
-        for step in range(1, mp)
-    ]
-    for copy, _ in tap_copies:
-        copy.start()
-    for line in lines:
-        line.swap_own()
-
-    loads[0].wait()
-    tall = 16
-
-    def norm(s):
-        def some(at, carry):
-            here = pl.ds(pl.multiple_of(at * tall, tall), tall)
-            values = rows[s, here, :].astype(F32)
-            centered = values - jnp.mean(values, axis=1, keepdims=True)
-            variance = jnp.mean(centered * centered, axis=1, keepdims=True)
-            normed[s, here, :] = (
-                centered * lax.rsqrt(variance + 1e-05) * gain_ref[...] + shift_ref[...]
-            ).astype(LOW)
-            return carry
-
-        lax.fori_loop(0, rows_here // tall, some, 0)
-
-    norm(0)
-    for step in range(1, count):
-        for line in lines:
-            line.arrive(step)
-        if step + 1 < count:
-            for line in lines:
-                line.start(step + 1)
-
-    half = depth // 2
-    lanes = (pl.ds(0, half), pl.ds(half, half))
-    dp_x = dp + 1 - 2 * lax.rem(dp, 2)
-    dp_y = dp + 2 - 4 * (dp // 2)
-    dp_xy = dp_x + 2 - 4 * (dp_x // 2)
-    legs = ((0, to_x), (1, to_y), (0, to_y), (1, to_x), (0, to_y), (1, to_x))
-
-    def plane(number, quarter):
-        side, partner = legs[number]
-        out = []
-        for part in range(3):
-            block = whole[part].at[:, core, quarter, :, lanes[side]]
-            out.append(
-                wire(
-                    block, block, plane_send_sem.at[part, number], plane_recv_sem.at[part, number], partner
-                )
-            )
-        return out
-
-    leaving = [plane(number, quarter) for number, quarter in enumerate((dp, dp, dp, dp, dp_x, dp_y))]
-    landing = [
-        plane(number, quarter) for number, quarter in enumerate((dp_x, dp_y, dp_y, dp_x, dp_xy, dp_xy))
-    ]
-
-    def pass_on(number, at_core):
-        quarter = (dp_x, dp_y, dp_xy)[number]
-        out = []
-        for part in range(3):
-            block = whole[part].at[:, at_core, quarter]
-            out.append(
-                wire(
-                    block, block, plane_swap_send.at[part, number], plane_swap_recv.at[part, number],
-                    other_core(),
-                )
-            )
-        return out
-
-    def each(copies, what):
-        for copy in copies:
-            getattr(copy, what)()
-
-    for number in range(4):
-        each(leaving[number], "start")
-    up_line.start(1)
-    up_line.swap_own()
-    norm(1)
-    save = pltpu.make_async_copy(normed, normed_ref, local.at[0])
-    save.start()
-    halo = halo_ref.shape[1]
-    halo_copy = wire(
-        normed.at[:, pl.ds(rows_here - halo, halo), :], halo_ref, halo_send, halo_recv,
-        {"mp": lax.rem(me + 1, mp)},
-    )
-    halo_copy.start()
-    each(landing[0], "wait_recv")
-    each(leaving[4], "start")
-    each(landing[1], "wait_recv")
-    each(leaving[5], "start")
-    early = early_steps(count)
-    up_line.arrive(1)
-    up_line.start(2)
-    each(landing[3], "wait_recv")
-    each(pass_on(0, core), "start")
-    each(landing[2], "wait_recv")
-    each(pass_on(1, core), "start")
-    each(landing[4], "wait_recv")
-    each(landing[5], "wait_recv")
-    each(pass_on(2, core), "start")
-    for step in early[1:]:
-        up_line.arrive(step)
-        if step != early[-1]:
-            up_line.start(step + 1)
-    for line in lines:
-        line.finish(range(1, count), True)
-    up_line.finish(early, True)
-    for number in range(6):
-        each(leaving[number], "wait_send")
-    for number in range(3):
-        each(pass_on(number, core), "wait_send")
-        each(pass_on(number, 1 - core), "wait_recv")
-    for copy, landed in tap_copies:
-        copy.wait_send()
-        landed.wait_recv()
-    halo_copy.wait()
-    save.wait()
-    saves = [
-        pltpu.make_async_copy(here, there, local.at[2 + at])
-        for at, (here, there) in enumerate(
-            ((all_qk, all_qk_ref), (all_v, all_v_ref), (all_out, all_out_ref), (up_all, up_all_ref))
-        )
-    ]
-    for copy in saves:
-        copy.start()
-    for copy in saves:
-        copy.wait()
-
-
 HALO = 16
-
-
-def prepare(inputs, gain, shift, qk, v, out, taps, up):
-    mp = lax.axis_size("mp")
-    count = mp // 2
-    rows_here, depth = inputs.shape[1:]
-    anywhere = pl.BlockSpec(memory_space=pl.ANY)
-    vmem = pl.BlockSpec(memory_space=pltpu.VMEM)
-    dma = pltpu.SemaphoreType.DMA
-    return pl.pallas_call(
-        prepare_kernel,
-        in_specs=[anywhere, vmem, vmem] + [anywhere] * 5,
-        out_specs=[anywhere] * 7,
-        out_shape=[
-            jax.ShapeDtypeStruct((count, 2) + qk.shape, LOW),
-            jax.ShapeDtypeStruct((count, 2) + v.shape, LOW),
-            jax.ShapeDtypeStruct((count, 2) + out.shape, LOW),
-            jax.ShapeDtypeStruct((mp,) + taps.shape, F32),
-            jax.ShapeDtypeStruct(inputs.shape, LOW),
-            jax.ShapeDtypeStruct((2, HALO, depth), LOW),
-            jax.ShapeDtypeStruct((mp * up.shape[0], depth), LOW),
-        ],
-        scratch_shapes=[
-            pltpu.VMEM(inputs.shape, LOW),
-            pltpu.VMEM(inputs.shape, LOW),
-            pltpu.VMEM((count, 2) + qk.shape, LOW),
-            pltpu.VMEM((count, 2) + v.shape, LOW),
-            pltpu.VMEM((count, 2) + out.shape, LOW),
-            pltpu.VMEM((mp * up.shape[0], depth), LOW),
-            dma((6,)),
-            dma((3, 6)),
-            dma((3, 6)),
-            dma((3, 3)),
-            dma((3, 3)),
-            dma((mp,)),
-            dma((mp,)),
-            dma,
-            dma,
-        ]
-        + line_semaphores(count) * 4,
-        compiler_params=pltpu.CompilerParams(
-            collective_id=3, has_side_effects=True, vmem_limit_bytes=VMEM_LIMIT
-        ),
-        cost_estimate=pl.CostEstimate(flops=2**36, bytes_accessed=2**26, transcendentals=0),
-        name="prepare",
-    )(inputs, gain.reshape(1, depth), shift.reshape(1, depth), qk, v, out, taps, up)
 
 
 def weight_grad(left_ref, pieces, whole, tiles, outs, out_ref, load, tile_sem, out_sem):
@@ -661,35 +429,46 @@
     ]
 
 
-def whole_weight_grad(left, right):
-    rows, units = left.shape
-    depth = right[0].shape[-1]
-    anywhere = pl.BlockSpec(memory_space=pl.ANY)
-
-    def kernel(left_ref, *refs):
-        pieces, out_ref, scratch = refs[: len(right)], refs[len(right)], refs[len(right) + 1 :]
-        weight_grad(left_ref, pieces, *scratch[:3], out_ref, *scratch[3:])
-
-    return pl.pallas_call(
-        kernel,
-        in_specs=[anywhere] * (1 + len(right)),
-        out_specs=anywhere,
-        out_shape=jax.ShapeDtypeStruct((units, depth), LOW),
-        scratch_shapes=weight_grad_scratch(rows, depth, len(right)),
-        compiler_params=pltpu.CompilerParams(vmem_limit_bytes=48 * 2**20),
-        cost_estimate=pl.CostEstimate(
-            flops=2 * rows * units * depth, bytes_accessed=2**25, transcendentals=0
-        ),
-        name="weight_grad",
-    )(left, *right)
-
-
 def carry_copies(carried, targets, send, recv):
     partners = plane_partners()
     return [
         wire(ref, target, send.at[at], recv.at[at], partners[way])
         for at, ((way, ref), target) in enumerate(zip(carried, targets))
     ]
+
+
+def greet_members(ways):
+    mp = lax.axis_size("mp")
+    me = lax.axis_index("mp")
+    barrier = pltpu.get_barrier_semaphore()
+    for step in range(1, mp):
+        pl.semaphore_signal(
+            barrier, inc=1, device_id={"mp": lax.rem(me + step, mp)}, device_id_type=MESH
+        )
+    partners = plane_partners() if ways else ()
+    for partner in partners:
+        pl.semaphore_signal(barrier, inc=1, device_id=partner, device_id_type=MESH)
+    pl.semaphore_wait(barrier, mp - 1 + len(partners))
+
+
+def member_copies(source, target, send, recv):
+    mp = lax.axis_size("mp")
+    me = lax.axis_index("mp")
+    copies = []
+    for step in range(1, mp):
+        to = lax.rem(me + step, mp)
+        sems = (send.at[step], recv.at[step], {"mp": to})
+        copies.append(
+            (
+                wire(source(to), target(me), *sems),
+                wire(source(to), target(lax.rem(me + mp - step, mp)), *sems),
+            )
+        )
+    return copies
+
+
+def head_lanes(at):
+    return pl.ds(pl.multiple_of(at * 128, 128), 128)
 
 
 def exchange_kernel(halo, pieces, ways, x_ref, *refs):
@@ -703,12 +482,11 @@
     targets, refs = refs[: len(ways)], refs[len(ways) :]
     landed, local, send, recv = refs[:4]
     refs = refs[4:]
-    mp = lax.axis_size("mp")
     me = lax.axis_index("mp")
     if halo is None:
 
         def source(at):
-            return x_ref.at[:, :, pl.ds(pl.multiple_of(at * 128, 128), 128)]
+            return x_ref.at[:, :, head_lanes(at)]
 
         def target(at):
             return landed.at[:, at]
@@ -719,27 +497,14 @@
             return x_ref.at[:, pl.ds(pl.multiple_of(at * (tall - halo), 16), tall), :]
 
         def target(at):
-            return landed.at[:, :, pl.ds(pl.multiple_of(at * 128, 128), 128)]
-
-    barrier = pltpu.get_barrier_semaphore()
-    for step in range(1, mp):
-        pl.semaphore_signal(
-            barrier, inc=1, device_id={"mp": lax.rem(me + step, mp)}, device_id_type=MESH
-        )
-    partners = plane_partners() if ways else ()
-    for partner in partners:
-        pl.semaphore_signal(barrier, inc=1, device_id=partner, device_id_type=MESH)
+            return landed.at[:, :, head_lanes(at)]
+
     own = pltpu.make_async_copy(source(me), target(me), local.at[0])
     own.start()
-    pl.semaphore_wait(barrier, mp - 1 + len(partners))
-    copies = []
-    for step in range(1, mp):
-        to = lax.rem(me + step, mp)
-        sems = (send.at[step], recv.at[step], {"mp": to})
-        leaving = wire(source(to), target(me), *sems)
-        landing = wire(source(to), target(lax.rem(me + mp - step, mp)), *sems)
+    greet_members(ways)
+    copies = member_copies(source, target, send, recv)
+    for leaving, _ in copies:
         leaving.start()
-        copies.append((leaving, landing))
     carries = []
     if ways:
         carries = carry_copies(carried, targets, refs[0], refs[1])
@@ -758,6 +523,411 @@
     for copy in carries:
         copy.wait()
     save.wait()
+
+
+def front_kernel(
+    inputs_ref, gain_ref, shift_ref, qk_ref, v_ref, out_ref, taps_ref, up_ref, masks_ref, cot_ref,
+    all_qk_ref, all_v_ref, all_out_ref, all_taps_ref, normed_ref, up_all_ref, raw_ref, o_ref, cot_x_ref, cot_y_ref,
+    inputs, rows, all_qk, all_v, all_out, all_taps, up_all, raw, mixed, landed, local, *sems,
+):
+    mp = lax.axis_size("mp")
+    dp = lax.axis_index("dp")
+    me = lax.axis_index("mp")
+    z, core = mesh_place()
+    count = mp // 2
+    rows_here, depth = inputs.shape[1:]
+    halo = rows.shape[1] - rows_here
+    to_x, to_y = plane_partners()
+    share = up_ref.shape[0]
+    owned = (qk_ref, v_ref, out_ref)
+    whole = (all_qk, all_v, all_out)
+    (plane_send_sem, plane_recv_sem, plane_swap_send, plane_swap_recv) = sems[:4]
+    taps_send, taps_recv, halo_send, halo_recv, carry_send, carry_recv, head_send, head_recv = sems[4:12]
+    line_sems = [sems[12 + 4 * part : 16 + 4 * part] for part in range(4)]
+
+    def up_place(at, at_core):
+        start = pl.multiple_of((2 * at + at_core) * share, 16)
+        return up_all.at[pl.ds(start, share), :]
+
+    def taps_place(at):
+        return all_taps.at[:, :, head_lanes(at)]
+
+    loads = [
+        pltpu.make_async_copy(inputs_ref, inputs, local.at[0]),
+        pltpu.make_async_copy(taps_ref, taps_place(me), local.at[1]),
+        pltpu.make_async_copy(up_ref, up_place(z, core), local.at[2]),
+    ] + [
+        pltpu.make_async_copy(
+            owned[part].at[dp], whole[part].at[z, core, dp], local.at[3 + part]
+        )
+        for part in range(3)
+    ]
+    for copy in loads:
+        copy.start()
+    greet_members((0, 1))
+    for copy in loads[1:]:
+        copy.wait()
+
+    lines = [
+        LineGather(lambda at, at_core, part=part: whole[part].at[at, at_core, dp], *line_sems[part])
+        for part in range(3)
+    ]
+    up_line = LineGather(up_place, *line_sems[3])
+    for line in lines:
+        line.start(1)
+    tap_copies = member_copies(lambda to: taps_ref, taps_place, taps_send, taps_recv)
+    for copy, _ in tap_copies:
+        copy.start()
+    for line in lines:
+        line.swap_own()
+
+    loads[0].wait()
+    tall = 16
+
+    def norm(s):
+        def some(at, carry):
+            here = pl.ds(pl.multiple_of(at * tall, tall), tall)
+            there = pl.ds(pl.multiple_of(halo + at * tall, tall), tall)
+            values = inputs[s, here, :].astype(F32)
+            centered = values - jnp.mean(values, axis=1, keepdims=True)
+            variance = jnp.mean(centered * centered, axis=1, keepdims=True)
+            rows[s, there, :] = (
+                centered * lax.rsqrt(variance + 1e-05) * gain_ref[...] + shift_ref[...]
+            ).astype(LOW)
+            return carry
+
+        lax.fori_loop(0, rows_here // tall, some, 0)
+
+    norm(0)
+    for step in range(1, count):
+        for line in lines:
+            line.arrive(step)
+        if step + 1 < count:
+            for line in lines:
+                line.start(step + 1)
+
+    half = depth // 2
+    lanes = (pl.ds(0, half), pl.ds(half, half))
+    dp_x = dp + 1 - 2 * lax.rem(dp, 2)
+    dp_y = dp + 2 - 4 * (dp // 2)
+    dp_xy = dp_x + 2 - 4 * (dp_x // 2)
+    legs = ((0, to_x), (1, to_y), (0, to_y), (1, to_x), (0, to_y), (1, to_x))
+
+    def plane(number, quarter):
+        side, partner = legs[number]
+        out = []
+        for part in range(3):
+            block = whole[part].at[:, core, quarter, :, lanes[side]]
+            out.append(
+                wire(
+                    block, block, plane_send_sem.at[part, number], plane_recv_sem.at[part, number], partner
+                )
+            )
+        return out
+
+    leaving = [plane(number, quarter) for number, quarter in enumerate((dp, dp, dp, dp, dp_x, dp_y))]
+    landing = [
+        plane(number, quarter) for number, quarter in enumerate((dp_x, dp_y, dp_y, dp_x, dp_xy, dp_xy))
+    ]
+
+    def pass_on(number, at_core):
+        quarter = (dp_x, dp_y, dp_xy)[number]
+        out = []
+        for part in range(3):
+            block = whole[part].at[:, at_core, quarter]
+            out.append(
+                wire(
+                    block, block, plane_swap_send.at[part, number], plane_swap_recv.at[part, number],
+                    other_core(),
+                )
+            )
+        return out
+
+    def each(copies, what):
+        for copy in copies:
+            getattr(copy, what)()
+
+    for number in range(4):
+        each(leaving[number], "start")
+    early = early_steps(count)
+    up_line.start(1)
+    up_line.swap_own()
+    norm(1)
+    own_rows = rows.at[:, pl.ds(halo, rows_here), :]
+    save = pltpu.make_async_copy(own_rows, normed_ref, local.at[0])
+    save.start()
+    halo_copy = wire(
+        rows.at[:, pl.ds(rows_here, halo), :], rows.at[:, pl.ds(0, halo), :], halo_send, halo_recv,
+        {"mp": lax.rem(me + 1, mp)},
+    )
+    halo_copy.start()
+    each(landing[0], "wait_recv")
+    each(leaving[4], "start")
+    each(landing[1], "wait_recv")
+    each(leaving[5], "start")
+    each(landing[3], "wait_recv")
+    each(pass_on(0, core), "start")
+    each(landing[2], "wait_recv")
+    each(pass_on(1, core), "start")
+    up_line.arrive(1)
+    up_line.start(2)
+    each(landing[4], "wait_recv")
+    each(landing[5], "wait_recv")
+    each(pass_on(2, core), "start")
+    for step in early[1:-1]:
+        up_line.arrive(step)
+        up_line.start(step + 1)
+    carries = [
+        wire(cot_ref.at[:, :, lanes[0]], cot_x_ref, carry_send.at[0], carry_recv.at[0], to_x),
+        wire(cot_ref.at[:, :, lanes[1]], cot_y_ref, carry_send.at[1], carry_recv.at[1], to_y),
+    ]
+    for copy in carries:
+        copy.start()
+    for line in lines:
+        line.finish(range(1, count), True)
+    for number in range(3):
+        each(pass_on(number, 1 - core), "wait_recv")
+    for _, landed_taps in tap_copies:
+        landed_taps.wait_recv()
+    halo_copy.wait_recv()
+    saves = [
+        pltpu.make_async_copy(here, there, local.at[2 + at])
+        for at, (here, there) in enumerate(
+            ((all_qk, all_qk_ref), (all_v, all_v_ref), (all_out, all_out_ref), (all_taps, all_taps_ref))
+        )
+    ]
+    for copy in saves:
+        copy.start()
+
+    def chip(at, carry):
+        weights = all_qk[at].reshape(4 * HD, depth)
+        columns = pl.ds(pl.multiple_of(at * 4 * HD, 4 * HD), 4 * HD)
+        for s in range(2):
+            raw[s, :, columns] = dot_nt(rows[s], weights)
+        return carry
+
+    lax.fori_loop(0, count, chip, 0)
+    lane = lax.broadcasted_iota(jnp.int32, (rows.shape[1], 128), 1)
+
+    def two_heads(at, carry):
+        weights = all_v[at].reshape(2 * HD, depth)
+        zero, one = dot_nt(rows[0], weights), dot_nt(rows[1], weights)
+        raw[2, :, head_lanes(2 * at)] = jnp.where(lane < HD, zero, pltpu.roll(one, HD, 1))
+        raw[2, :, head_lanes(2 * at + 1)] = jnp.where(lane < HD, pltpu.roll(zero, HD, 1), one)
+        return carry
+
+    lax.fori_loop(0, count, two_heads, 0)
+    save_raw = pltpu.make_async_copy(raw, raw_ref, local.at[6])
+    save_raw.start()
+    for plane_at in range(3):
+        tap = all_taps.at[plane_at]
+
+        def conv(at, carry, plane_at=plane_at, tap=tap):
+            lanes_at = head_lanes(at)
+            values = raw[plane_at, :, lanes_at]
+            one = pltpu.roll(values, 1, 0)[halo:]
+            two = pltpu.roll(values, 2, 0)[halo:]
+            mixed[plane_at, :, lanes_at] = (
+                tap[0:1, lanes_at] * values[halo:]
+                + jnp.where(masks_ref[plane_at, 0] > 0.5, tap[1:2, lanes_at] * one, 0.0)
+                + jnp.where(masks_ref[plane_at, 1] > 0.5, tap[2:3, lanes_at] * two, 0.0)
+            ).astype(LOW)
+            return carry
+
+        lax.fori_loop(0, mp, conv, 0)
+
+    def source(at):
+        return mixed.at[:, :, head_lanes(at)]
+
+    def target(at):
+        return landed.at[:, at]
+
+    own = pltpu.make_async_copy(source(me), target(me), local.at[7])
+    own.start()
+    copies = member_copies(source, target, head_send, head_recv)
+    for copy, _ in copies:
+        copy.start()
+    up_line.arrive(early[-1])
+    up_line.finish(early, True)
+    save_up = pltpu.make_async_copy(up_all, up_all_ref, local.at[8])
+    save_up.start()
+    own.wait()
+    for _, copy in copies:
+        copy.wait_recv()
+    save_heads = pltpu.make_async_copy(landed, o_ref, local.at[9])
+    save_heads.start()
+    for number in range(6):
+        each(leaving[number], "wait_send")
+    for number in range(3):
+        each(pass_on(number, core), "wait_send")
+    for copy, _ in tap_copies + copies:
+        copy.wait_send()
+    halo_copy.wait_send()
+    for copy in carries:
+        copy.wait()
+    save.wait()
+    for copy in saves:
+        copy.wait()
+    save_raw.wait()
+    save_up.wait()
+    save_heads.wait()
+
+
+def front(inputs, gain, shift, qk, v, out, taps, up, masks, cot):
+    mp = lax.axis_size("mp")
+    count = mp // 2
+    rows_here, depth = inputs.shape[1:]
+    tall = rows_here + HALO
+    anywhere = pl.BlockSpec(memory_space=pl.ANY)
+    vmem = pl.BlockSpec(memory_space=pltpu.VMEM)
+    dma = pltpu.SemaphoreType.DMA
+    whole = [((count, 2) + part.shape, LOW) for part in (qk, v, out)]
+    whole.append(((3, 8, mp * 128), F32))
+    kept = [
+        ((2, rows_here, depth), LOW),
+        ((mp * up.shape[0], depth), LOW),
+        ((3, tall, mp * 128), F32),
+        ((3, mp, rows_here, 128), LOW),
+        ((2, rows_here, depth // 2), LOW),
+        ((2, rows_here, depth // 2), LOW),
+    ]
+    return pl.pallas_call(
+        front_kernel,
+        in_specs=[anywhere, vmem, vmem] + [anywhere] * 5 + [vmem, anywhere],
+        out_specs=[anywhere] * 10,
+        out_shape=[jax.ShapeDtypeStruct(*shape) for shape in whole + kept],
+        scratch_shapes=[
+            pltpu.VMEM(inputs.shape, LOW),
+            pltpu.VMEM((2, tall, depth), LOW),
+        ]
+        + [pltpu.VMEM(*shape) for shape in whole]
+        + [
+            pltpu.VMEM(*kept[1]),
+            pltpu.VMEM(*kept[2]),
+            pltpu.VMEM((3, rows_here, mp * 128), LOW),
+            pltpu.VMEM(*kept[3]),
+            dma((10,)),
+            dma((3, 6)),
+            dma((3, 6)),
+            dma((3, 3)),
+            dma((3, 3)),
+            dma((mp,)),
+            dma((mp,)),
+            dma,
+            dma,
+            dma((2,)),
+            dma((2,)),
+            dma((mp,)),
+            dma((mp,)),
+        ]
+        + line_semaphores(count) * 4,
+        compiler_params=pltpu.CompilerParams(
+            collective_id=3, has_side_effects=True, vmem_limit_bytes=VMEM_LIMIT
+        ),
+        cost_estimate=pl.CostEstimate(flops=2**36, bytes_accessed=2**26, transcendentals=0),
+        name="front",
+    )(inputs, gain.reshape(1, depth), shift.reshape(1, depth), qk, v, out, taps, up, masks, cot)
+
+
+def project_back_kernel(
+    ways, x_ref, raw_ref, taps_ref, masks_ref, *refs
+):
+    carried, refs = list(zip(ways, refs[: len(ways)])), refs[len(ways) :]
+    grad_ref, sums_ref = refs[:2]
+    targets, refs = refs[2 : 2 + len(ways)], refs[2 + len(ways) :]
+    landed, raw, local, send, recv, carry_send, carry_recv = refs
+    me = lax.axis_index("mp")
+    tall = landed.shape[1]
+    rows_here = grad_ref.shape[1]
+    halo = tall - rows_here
+    heads = landed.shape[2] // 128
+
+    def source(at):
+        return x_ref.at[:, pl.ds(pl.multiple_of(at * rows_here, 16), tall), :]
+
+    def target(at):
+        return landed.at[:, :, head_lanes(at)]
+
+    own = pltpu.make_async_copy(source(me), target(me), local.at[0])
+    own.start()
+    load = pltpu.make_async_copy(raw_ref, raw, local.at[1])
+    load.start()
+    greet_members(ways)
+    copies = member_copies(source, target, send, recv)
+    for leaving, _ in copies:
+        leaving.start()
+    carries = carry_copies(carried, targets, carry_send, carry_recv)
+    for copy in carries:
+        copy.start()
+    own.wait()
+    load.wait()
+    for _, landing in copies:
+        landing.wait_recv()
+    for plane in range(3):
+        tap = taps_ref.at[plane]
+
+        def back(at, carry, plane=plane, tap=tap):
+            lanes = head_lanes(at)
+            grad = landed[plane, :, lanes].astype(F32)
+            one = pltpu.roll(grad, tall - 1, 0)[:rows_here]
+            two = pltpu.roll(grad, tall - 2, 0)[:rows_here]
+            here = grad[:rows_here]
+            grad_ref[plane, :, lanes] = (
+                tap[0:1, lanes] * here
+                + jnp.where(masks_ref[plane, 2] > 0.5, tap[1:2, lanes] * one, 0.0)
+                + jnp.where(masks_ref[plane, 3] > 0.5, tap[2:3, lanes] * two, 0.0)
+            ).astype(LOW)
+            values = raw[plane, :, lanes]
+            before = pltpu.roll(values, 1, 0)[halo:]
+            before_two = pltpu.roll(values, 2, 0)[halo:]
+            products = (
+                here * values[halo:],
+                jnp.where(masks_ref[plane, 0] > 0.5, here * before, 0.0),
+                jnp.where(masks_ref[plane, 1] > 0.5, here * before_two, 0.0),
+            )
+            for row, product in enumerate(products):
+                sums_ref[plane, row : row + 1, lanes] = jnp.sum(product, axis=0, keepdims=True)
+            sums_ref[plane, 3:8, lanes] = jnp.zeros((5, 128), F32)
+            return carry
+
+        lax.fori_loop(0, heads, back, 0)
+    for leaving, _ in copies:
+        leaving.wait_send()
+    for copy in carries:
+        copy.wait()
+
+
+def project_back(x, raw, taps, masks, carried):
+    mp = lax.axis_size("mp")
+    rows_here = masks.shape[2]
+    tall = raw.shape[1]
+    anywhere = pl.BlockSpec(memory_space=pl.ANY)
+    dma = pltpu.SemaphoreType.DMA
+    vmem = pl.BlockSpec(memory_space=pltpu.VMEM)
+    return pl.pallas_call(
+        partial(project_back_kernel, tuple(way for way, _ in carried)),
+        in_specs=[vmem, anywhere, vmem, vmem] + [anywhere] * len(carried),
+        out_specs=[vmem] * 2 + [anywhere] * len(carried),
+        out_shape=[
+            jax.ShapeDtypeStruct((3, rows_here, mp * 128), LOW),
+            jax.ShapeDtypeStruct((3, 8, mp * 128), F32),
+        ]
+        + [jax.ShapeDtypeStruct(block.shape, block.dtype) for _, block in carried],
+        scratch_shapes=[
+            pltpu.VMEM((3, tall, mp * 128), LOW),
+            pltpu.VMEM((3, tall, mp * 128), F32),
+            dma((2,)),
+            dma((mp,)),
+            dma((mp,)),
+            dma((len(carried),)),
+            dma((len(carried),)),
+        ],
+        compiler_params=pltpu.CompilerParams(
+            collective_id=7, has_side_effects=True, vmem_limit_bytes=VMEM_LIMIT
+        ),
+        cost_estimate=pl.CostEstimate(flops=2**35, bytes_accessed=2**24, transcendentals=0),
+        name="project_back",
+    )(x, raw, taps, masks, *(block for _, block in carried))
 
 
 def exchange(x, shape, halo, number, name, left=None, right=(), carried=()):
@@ -806,62 +976,19 @@
     return exchange(x, shape, halo, number, name, left, right, carried)
 
 
-def line_blocks(place, sources, local, send, recv):
-    z, core = mesh_place()
-    count = lax.axis_size("mp") // 2
-    out = []
-    for number, (step, way, ref) in enumerate(sources):
-        at = z - way * step
-        there = (at >= 0) & (at < count)
-        at = jnp.clip(at, 0, count - 1)
-        sems = (send.at[number], recv.at[number], other_core())
-        out.append(
-            (
-                there,
-                pltpu.make_async_copy(ref, place(at, core), local.at[number]),
-                wire(ref, place(at, core), *sems),
-                wire(ref, place(at, 1 - core), *sems),
-            )
-        )
-    return out
-
-
-def blocks_start(blocks):
-    for there, here, leaving, _ in blocks:
-
-        @pl.when(there)
-        def _(here=here, leaving=leaving):
-            here.start()
-            leaving.start()
-
-
-def blocks_wait(blocks, local=True):
-    for there, here, leaving, landing in blocks:
-
-        @pl.when(there)
-        def _(here=here, leaving=leaving, landing=landing):
-            if local:
-                here.wait()
-            leaving.wait_send()
-            landing.wait_recv()
-
-
-def feed_in_kernel(up_steps, down_steps, *refs):
-    second_ref, up_ref = refs[:2]
-    up_sources = [(step, way, ref) for (step, way), ref in zip(up_steps, refs[2:])]
-    refs = refs[2 + len(up_steps) :]
-    down_sources = [(step, way, ref) for (step, way), ref in zip(down_steps, refs)]
-    (
-        all_ref, relu_ref, hidden_ref, down_all_ref, up_all_ref,
-        rows, up, relu, hidden, down, local, outs, send, recv,
-        up_local, up_send, up_recv, down_local, down_send, down_recv, *line_sems,
-    ) = refs[len(down_steps) :]
+def feed_in_kernel(
+    second_ref, up_ref, down_ref, cot_0, cot_1, cot_2, cot_3, cot_4, cot_5, cot_6,
+    all_ref, relu_ref, hidden_ref, down_all_ref, up_all_ref, first_ref,
+    rows, up, relu, hidden, down, cot, tiles, sums, local, outs, send, recv, cot_sem, tile_sem, sum_sem, *line_sems,
+):
     count = lax.axis_size("mp") // 2
     depth = rows.shape[3]
     units = up.shape[0]
-    share = units // lax.axis_size("mp")
+    share = down_ref.shape[0]
+    z, core = mesh_place()
     lanes = (pl.ds(0, depth // 2), pl.ds(depth // 2, depth // 2))
     to_x, to_y = plane_partners()
+    pieces = (cot_0, cot_1, cot_2, cot_3, cot_4, cot_5, cot_6)
 
     def line_place(ref):
         return lambda at, at_core: ref.at[
@@ -869,15 +996,15 @@
         ]
 
     own = [pltpu.make_async_copy(second_ref.at[s], rows.at[s, 0], local.at[s]) for s in range(2)]
-    weights = pltpu.make_async_copy(up_ref, up, local.at[2])
-    for copy in own + [weights]:
+    own.append(pltpu.make_async_copy(up_ref, up, local.at[2]))
+    own.append(pltpu.make_async_copy(down_ref, line_place(down)(z, core), local.at[3]))
+    for copy in own:
         copy.start()
-    for copy in own + [weights]:
+    for copy in own:
         copy.wait()
     greet_line(True)
-    up_blocks = line_blocks(line_place(up), up_sources, up_local, up_send, up_recv)
-    down_blocks = line_blocks(line_place(down), down_sources, down_local, down_send, down_recv)
-    down_line = LineGather(line_place(down), *line_sems)
+    up_line = LineGather(line_place(up), *line_sems[:4])
+    down_line = LineGather(line_place(down), *line_sems[4:])
 
     def remote(s, source, target, half, partner, number):
         return wire(
@@ -899,12 +1026,16 @@
     pending = [None, None]
     done = [0]
 
+    def settle(slot):
+        if pending[slot] is not None:
+            for copy in pending[slot]:
+                copy.wait()
+        pending[slot] = None
+
     def tile(s, m):
         slot = done[0] % 2
         done[0] += 1
-        if pending[slot] is not None:
-            for copy in pending[slot]:
-                copy.wait()
+        settle(slot)
 
         def one(at, carry):
             columns = pl.ds(pl.multiple_of(at * CHUNK, CHUNK), CHUNK)
@@ -923,22 +1054,29 @@
 
     for number in range(4):
         copies[0][number].start()
-    blocks_start(up_blocks)
-    blocks_start(down_blocks)
-    blocks_wait(up_blocks)
-    for there, here, _, _ in down_blocks:
-        pl.when(there)(here.wait)
-    down_line.start(1)
-    whole_up = pltpu.make_async_copy(up, up_all_ref, local.at[2])
-    whole_up.start()
-    tile(0, 0)
+    late = range(early_steps(count)[-1] + 1, count)
+    for step in late:
+        up_line.start(step)
+        if step != late[-1]:
+            up_line.arrive(step)
+    cot_loads = []
+    for m in range(4):
+        cot_loads += piece_copies(pieces, 0, m, cot.at[m], cot_sem.at[m])
+    for copy in cot_loads:
+        copy.start()
     copies[0][0].wait_recv()
     copies[0][4].start()
     copies[0][1].wait_recv()
     copies[0][5].start()
     copies[1][0].start()
     copies[1][1].start()
-    tile(1, 0)
+    up_line.arrive(late[-1])
+    down_line.start(1)
+    down_line.swap_own()
+    up_line.finish(late, False)
+    whole_up = pltpu.make_async_copy(up, up_all_ref, local.at[2])
+    whole_up.start()
+    tile(0, 0)
     copies[0][3].wait_recv()
     tile(0, 1)
     copies[0][2].wait_recv()
@@ -955,7 +1093,16 @@
     copies[0][4].wait_recv()
     copies[0][5].wait_recv()
     tile(0, 3)
-    blocks_wait(down_blocks, local=False)
+    tile(1, 0)
+    settle(0)
+    settle(1)
+    for copy in cot_loads:
+        copy.wait()
+
+    def first_half():
+        gradient_tiles(hidden_ref.at[0], cot, tiles, sums, first_ref, tile_sem, sum_sem)
+
+    first_half()
     for step in range(3, count):
         down_line.arrive(step - 1)
         down_line.start(step)
@@ -965,17 +1112,16 @@
     tile(1, 2)
     copies[1][4].wait_recv()
     copies[1][5].wait_recv()
-    gathered = pltpu.make_async_copy(rows, all_ref, local.at[3])
+    gathered = pltpu.make_async_copy(rows, all_ref, local.at[0])
     gathered.start()
     tile(1, 3)
     if count > 2:
         down_line.arrive(count - 1)
-    down_line.finish(range(1, count), False)
-    whole_down = pltpu.make_async_copy(down, down_all_ref, local.at[0])
+    down_line.finish(range(1, count), True)
+    whole_down = pltpu.make_async_copy(down, down_all_ref, local.at[1])
     whole_down.start()
-    for slot in pending:
-        for copy in slot:
-            copy.wait()
+    settle(0)
+    settle(1)
     for s in range(2):
         for copy in copies[s]:
             copy.wait_send()
@@ -984,19 +1130,120 @@
     whole_down.wait()
 
 
-def feed_in(second, up_early, up_late, down_blocks):
+def gradient_tiles(left_ref, right, tiles, sums, out_ref, tile_sem, sum_sem, before=None):
+    wide = tiles.shape[3]
+    steps = left_ref.shape[2] // wide
+
+    def load(at, slot):
+        columns = pl.ds(pl.multiple_of(at * wide, wide), wide)
+        return pltpu.make_async_copy(left_ref.at[:, :, columns], tiles.at[slot], tile_sem.at[slot])
+
+    def rows_of(at):
+        return pl.ds(pl.multiple_of(at * wide, wide), wide)
+
+    def save(at, slot):
+        return pltpu.make_async_copy(sums.at[slot], out_ref.at[rows_of(at), :], sum_sem.at[slot])
+
+    def load_before(at, slot):
+        before_ref, buffer, sem = before
+        return pltpu.make_async_copy(before_ref.at[rows_of(at), :], buffer.at[slot], sem.at[slot])
+
+    load(0, 0).start()
+    if before is not None:
+        load_before(0, 0).start()
+
+    def one(at, carry):
+        slot = lax.rem(at, 2)
+        load(at, slot).wait()
+        if before is not None:
+            load_before(at, slot).wait()
+
+        @pl.when(at + 1 < steps)
+        def _():
+            load(at + 1, 1 - slot).start()
+            if before is not None:
+                load_before(at + 1, 1 - slot).start()
+
+        @pl.when(at >= 2)
+        def _():
+            save(at - 2, slot).wait()
+
+        blocks, tall = right.shape[:2]
+        result = lax.dot_general(
+            tiles[slot].reshape(blocks * tall, wide),
+            right[...].reshape(blocks * tall, right.shape[2]),
+            (((0,), (0,)), ((), ())),
+            preferred_element_type=F32,
+        )
+        if before is not None:
+            result = result + before[1][slot].astype(F32)
+        sums[slot] = result.astype(LOW)
+        save(at, slot).start()
+        return carry
+
+    lax.fori_loop(0, steps, one, 0)
+    save(steps - 2, (steps - 2) % 2).wait()
+    save(steps - 1, (steps - 1) % 2).wait()
+
+
+def down_grad_rest(hidden, cot_pieces, first):
+    rows_here, units = hidden.shape[2:]
+    depth = first.shape[1]
+    anywhere = pl.BlockSpec(memory_space=pl.ANY)
+    dma = pltpu.SemaphoreType.DMA
+
+    def kernel(hidden_ref, first_ref, *refs):
+        pieces, out_ref = refs[:7], refs[7]
+        cot, tiles, sums, buffer, cot_sem, tile_sem, sum_sem, first_sem = refs[8:]
+        loads = []
+        for m in range(4):
+            loads += piece_copies(pieces, 1, m, cot.at[m], cot_sem.at[m])
+        for copy in loads:
+            copy.start()
+        for copy in loads:
+            copy.wait()
+        gradient_tiles(
+            hidden_ref.at[1], cot, tiles, sums, out_ref, tile_sem, sum_sem, (first_ref, buffer, first_sem)
+        )
+
+    return pl.pallas_call(
+        kernel,
+        in_specs=[anywhere] * 9,
+        out_specs=anywhere,
+        out_shape=jax.ShapeDtypeStruct((units, depth), LOW),
+        scratch_shapes=[
+            pltpu.VMEM((4, rows_here, depth), LOW),
+            pltpu.VMEM((2, 4, rows_here, WIDE), LOW),
+            pltpu.VMEM((2, WIDE, depth), LOW),
+            pltpu.VMEM((2, WIDE, depth), LOW),
+            dma((4, 2)),
+            dma((2,)),
+            dma((2,)),
+            dma((2,)),
+        ],
+        compiler_params=pltpu.CompilerParams(vmem_limit_bytes=48 * 2**20),
+        cost_estimate=pl.CostEstimate(
+            flops=2 * 4 * rows_here * units * depth, bytes_accessed=2**25, transcendentals=0
+        ),
+        name="down_grad_rest",
+    )(hidden, first, *cot_pieces)
+
+
+def feed_in(second, up_early, down, cot_pieces):
     rows_here, depth = second.shape[1:]
     units = up_early.shape[0]
+    count = lax.axis_size("mp") // 2
     anywhere = pl.BlockSpec(memory_space=pl.ANY)
     dma = pltpu.SemaphoreType.DMA
     return pl.pallas_call(
-        partial(feed_in_kernel, tuple(up_late), tuple(down_blocks)),
-        in_specs=[anywhere] * (2 + len(up_late) + len(down_blocks)),
-        out_specs=[anywhere] * 5,
+        feed_in_kernel,
+        in_specs=[anywhere] * 10,
+        out_specs=[anywhere] * 6,
         out_shape=[
             jax.ShapeDtypeStruct((2, 4, rows_here, depth), LOW),
             jax.ShapeDtypeStruct((2, 4, rows_here, units), F32),
             jax.ShapeDtypeStruct((2, 4, rows_here, units), LOW),
+            jax.ShapeDtypeStruct((units, depth), LOW),
             jax.ShapeDtypeStruct((units, depth), LOW),
             jax.ShapeDtypeStruct((units, depth), LOW),
         ],
@@ -1006,14 +1253,18 @@
             pltpu.VMEM((2, rows_here, units), F32),
             pltpu.VMEM((2, rows_here, units), LOW),
             pltpu.VMEM((units, depth), LOW),
+            pltpu.VMEM((4, rows_here, depth), LOW),
+            pltpu.VMEM((2, 4, rows_here, WIDE), LOW),
+            pltpu.VMEM((2, WIDE, depth), LOW),
             dma((4,)),
             dma((2, 2)),
             dma((2, 6)),
             dma((2, 6)),
+            dma((4, 2)),
+            dma((2,)),
+            dma((2,)),
         ]
-        + [dma((len(up_late),))] * 3
-        + [dma((len(down_blocks),))] * 3
-        + line_semaphores(lax.axis_size("mp") // 2),
+        + line_semaphores(count) * 2,
         compiler_params=pltpu.CompilerParams(
             collective_id=1, has_side_effects=True, vmem_limit_bytes=VMEM_LIMIT
         ),
@@ -1023,7 +1274,7 @@
             transcendentals=0,
         ),
         name="feed_in",
-    )(second, up_early, *up_late.values(), *down_blocks.values())
+    )(second, up_early, down, *cot_pieces)
 
 
 def piece_copies(pieces, s, m, target, sems):
@@ -1523,24 +1774,24 @@
     return lax.ppermute(block, "dp", [(d, d ^ mask) for d in range(lax.axis_size("dp"))])
 
 
-def plane_gather_begin(block):
-    half = block.shape[-1] // 2
-    one, two = block[..., :half], block[..., half:]
+def plane_gather_begin(block, axis=-1):
+    half = block.shape[axis] // 2
+    one, two = jnp.split(block, [half], axis=axis)
     return plane_send(one, 1), plane_send(two, 2), plane_send(one, 2), plane_send(two, 1)
 
 
-def plane_gather_end(block, legs):
+def plane_gather_end(legs):
     one_x, two_y, one_y, two_x = legs
     return plane_send(one_x, 2), plane_send(two_y, 1)
 
 
-def plane_blocks(block, legs, last):
+def plane_blocks(block, legs, last, axis=-1):
     one_x, two_y, one_y, two_x = legs
     return [
         block,
-        jnp.concatenate([one_x, two_x], axis=-1),
-        jnp.concatenate([one_y, two_y], axis=-1),
-        jnp.concatenate(last, axis=-1),
+        jnp.concatenate([one_x, two_x], axis=axis),
+        jnp.concatenate([one_y, two_y], axis=axis),
+        jnp.concatenate(last, axis=axis),
     ]
 
 
@@ -1550,13 +1801,6 @@
     return jnp.concatenate(
         [lax.dynamic_index_in_dim(stacked, me ^ d, 0, keepdims=False) for d in range(4)], axis=axis
     )
-
-
-def line_step(blocks, step):
-    count = lax.axis_size("mp") // 2
-    up = [(2 * z + c, 2 * z + 2 + c) for z in range(step - 1, count - 1) for c in range(2)]
-    down = [(2 * z + c, 2 * z - 2 + c) for z in range(1, count - step + 1) for c in range(2)]
-    return lax.ppermute(blocks[0], "mp", up), lax.ppermute(blocks[1], "mp", down)
 
 
 def per_device(
@@ -1599,54 +1843,41 @@
     qk_own = jnp.concatenate([query_weight, key_weight], axis=1).T
     up_own = lax.dynamic_slice_in_dim(up_weight, me_dp * share, share, 1).T
     down_own = lax.dynamic_slice_in_dim(down_weight, me_dp * share, share, 0)
-    taps_own = jnp.pad(
-        jnp.concatenate([query_kernel, key_kernel, value_kernel], axis=1), ((0, 5), (0, HD))
+    qk_taps = jnp.concatenate([query_kernel, key_kernel], axis=1)
+    v_taps = jnp.concatenate([value_kernel, value_kernel], axis=1)
+    taps_own = jnp.pad(jnp.stack([qk_taps, qk_taps, v_taps]), ((0, 0), (0, 5), (0, 0)))
+    places = jnp.arange(group, dtype=jnp.int32)
+    offsets = lax.dynamic_slice_in_dim(
+        jnp.pad(places[None, :] - starts, ((0, 0), (0, HALO))), me_mp * rows_here, rows_here + HALO, 1
     )
-    qk_all, v_all, out_all, taps_all, normed, halo_rows, up_early = prepare(
+    masks = jnp.stack(
+        [
+            offsets[:, :rows_here] >= 1,
+            offsets[:, :rows_here] >= 2,
+            offsets[:, 1 : rows_here + 1] >= 1,
+            offsets[:, 2 : rows_here + 2] >= 2,
+        ],
+        axis=1,
+    ).astype(F32)[..., None]
+    wide_masks = jnp.broadcast_to(masks, masks.shape[:3] + (HD,))
+    masks = jnp.stack(
+        [
+            jnp.concatenate([wide_masks[left], wide_masks[right]], axis=2)
+            for left, right in ((0, 0), (1, 1), (0, 1))
+        ]
+    )
+
+    qk_all, v_all, out_all, taps, normed, up_early, raw, mixed, one_x, two_y = front(
         inputs, norm1_gain, norm1_bias, quarters(qk_own), quarters(value_weight.T), quarters(out_weight), taps_own, up_own,
+        masks, cotangent,
     )
     qk_all = qk_all.reshape(mp * 2 * HD, width)
     v_all = v_all.reshape(mp * HD, width)
     out_all = out_all.reshape(mp * HD, width)
-    taps = taps_all[:, :3].transpose(1, 0, 2)
-    qk_taps = taps[:, :, : 2 * HD].reshape(3, mp * 2 * HD)
-    v_taps = taps[:, :, 2 * HD : 3 * HD].reshape(3, mp * HD)
-
-    cot, qk_all, up_early, down_own = lax.optimization_barrier(
-        (cotangent, qk_all, up_early, down_own)
-    )
-    cot_legs = plane_gather_begin(cot)
-    chips = mp // 2
-    late = list(range(early_steps(chips)[-1] + 1, chips))
-    z = me_mp // 2
-
-    def early_block(at):
-        start = (2 * jnp.clip(at, 0, chips - 1) + me_mp % 2) * share
-        return lax.dynamic_slice_in_dim(up_early, start, share, 0)
-
-    up_late = {}
-    blocks = (early_block(z - late[0] + 1), early_block(z + late[0] - 1))
-    for step in late:
-        blocks = line_step(blocks, step)
-        up_late[step, 1], up_late[step, -1] = blocks
-    normed_ext = jnp.concatenate([halo_rows, normed], axis=1)
-    raw_qk = jnp.einsum("srd,cd->src", normed_ext, qk_all, preferred_element_type=F32)
-    raw_v = jnp.einsum("srd,cd->src", normed_ext, v_all, preferred_element_type=F32)
-    places = jnp.arange(group, dtype=jnp.int32)
-    offsets = lax.dynamic_slice_in_dim(
-        jnp.pad(places[None, :] - starts, ((0, 0), (0, HALO))), me_mp * rows_here, rows_here + HALO, 1
-    )[:, :, None]
-    here = offsets[:, :rows_here]
-
-    def conv(raw, tap):
-        return (
-            tap[0] * raw[:, HALO:]
-            + jnp.where(here >= 1, tap[1] * raw[:, HALO - 1 : -1], 0.0)
-            + jnp.where(here >= 2, tap[2] * raw[:, HALO - 2 : -2], 0.0)
-        ).astype(LOW)
-
-    mixed_qk = conv(raw_qk, qk_taps)
-    mixed_v = conv(raw_v, v_taps)
+    mixed = mixed.reshape(3, group, 128)
+    cot, mixed = lax.optimization_barrier((cotangent, mixed))
+    one_y, two_x = plane_send(cot[:, :, : width // 2], 2), plane_send(cot[:, :, width // 2 :], 1)
+    one_xy, two_xy = plane_send(one_x, 2), plane_send(two_y, 1)
 
     def side_by_side(pair):
         split = pair.reshape(2, rows_here, mp, HD)
@@ -1656,22 +1887,20 @@
         split = joint.reshape(joint.shape[1], mp, 2, HD)
         return split.transpose(2, 0, 1, 3).reshape(2, joint.shape[1], mp * HD)
 
-    mixed_qk, up_late = lax.optimization_barrier((mixed_qk, up_late))
-    (mixed,) = heads_out(jnp.concatenate([mixed_qk, side_by_side(mixed_v)], axis=0), 4, "mixed_out")
-    mixed, cot_legs = lax.optimization_barrier((mixed, cot_legs))
-    cot_last = plane_gather_end(cot, cot_legs)
-    down_blocks = {(0, 1): down_own}
     attended_head, wide, total = attend(mixed, starts)
-    attended_head, cot_last = lax.optimization_barrier((attended_head, cot_last))
-    one_x, two_y, one_y, two_x = cot_legs
-    cot_pieces = (cot, one_x, two_x, one_y, two_y) + tuple(cot_last)
     (attended,) = heads_back(attended_head, rows_here, 0, 5, "attended_back")
     attended = apart(attended)
     middle = rows + dot(attended, out_all)
     second = layer_norm(middle, norm2_gain, norm2_bias).astype(LOW)
 
-    second_all, relu, hidden, down_all, up_all = feed_in(second, up_early, up_late, down_blocks)
-    down_part = whole_weight_grad(hidden.reshape(-1, hidden.shape[3]), cot_pieces)
+    second, one_y, two_x, one_xy, two_xy = lax.optimization_barrier(
+        (second, one_y, two_x, one_xy, two_xy)
+    )
+    cot_pieces = (cot, one_x, two_x, one_y, two_y, one_xy, two_xy)
+    second_all, relu, hidden, down_all, up_all, down_first = feed_in(
+        second, up_early, down_own, cot_pieces
+    )
+    down_part = down_grad_rest(hidden, cot_pieces, down_first)
     down_mine = lax.psum_scatter(down_part, "mp", scatter_dimension=0, tiled=True)
     down_part, relu = lax.optimization_barrier((down_part, relu))
     grad_pre, feed_x0, feed_x1, feed_y0, feed_y1, keep_a, keep_b, grad_second = feed_out(
@@ -1697,12 +1926,11 @@
     down_legs = plane_gather_begin(down_mine)
     grad_mixed_head = attend_back(mixed, grad_head, wide, total, starts, HALO)
     grad_mixed_head, down_legs = lax.optimization_barrier((grad_mixed_head, down_legs))
-    down_last = plane_gather_end(down_mine, down_legs)
-    grad_mixed, x_second, y_second = heads_back(
-        grad_mixed_head, rows_here, HALO, 7, "mixed_grad_back",
-        carried=((0, feed_x1), (1, feed_y1)),
+    down_last = plane_gather_end(down_legs)
+    grad_raw, tap_sums, x_second, y_second = project_back(
+        grad_mixed_head, raw, taps, masks, ((0, feed_x1), (1, feed_y1))
     )
-    grad_mixed, down_last = lax.optimization_barrier((grad_mixed, down_last))
+    grad_raw, down_last = lax.optimization_barrier((grad_raw, down_last))
     down_grad = plane_order(plane_blocks(down_mine, down_legs, down_last), axis=0).astype(F32)
     x_in, y_in = jnp.stack([x_first, x_second]), jnp.stack([y_first, y_second])
 
@@ -1711,27 +1939,10 @@
 
     feed_a = add(keep_a[:, 1], x_in[:, 1]).astype(LOW)
     feed_b = add(keep_b[:, 1], y_in[:, 1]).astype(LOW)
-    grad_qk = grad_mixed[:2].astype(F32)
-    grad_v = apart(grad_mixed[2:]).astype(F32)
-
-    def conv_back(grad, raw, tap):
-        after_one = jnp.where(offsets[:, 1 : rows_here + 1] >= 1, grad[:, 1 : rows_here + 1], 0.0)
-        after_two = jnp.where(offsets[:, 2 : rows_here + 2] >= 2, grad[:, 2 : rows_here + 2], 0.0)
-        own = grad[:, :rows_here]
-        grad_raw = (tap[0] * own + tap[1] * after_one + tap[2] * after_two).astype(LOW)
-        grad_tap = jnp.stack(
-            [
-                jnp.sum(own * raw[:, HALO:], axis=(0, 1)),
-                jnp.sum(jnp.where(here >= 1, own, 0.0) * raw[:, HALO - 1 : -1], axis=(0, 1)),
-                jnp.sum(jnp.where(here >= 2, own, 0.0) * raw[:, HALO - 2 : -2], axis=(0, 1)),
-            ]
-        )
-        return grad_raw, grad_tap
-
-    grad_raw_qk, grad_tap_qk = conv_back(grad_qk, raw_qk, qk_taps)
-    grad_raw_v, grad_tap_v = conv_back(grad_v, raw_v, v_taps)
+    grad_raw_qk, grad_raw_v = grad_raw[:2], apart(grad_raw[2:])
     grad_raw_qk, up_mine = lax.optimization_barrier((grad_raw_qk, up_mine))
-    up_legs = plane_gather_begin(up_mine)
+    up_mine = up_mine.T
+    up_legs = plane_gather_begin(up_mine, 0)
     qk_part = jnp.einsum("src,srd->cd", grad_raw_qk, normed, preferred_element_type=F32).astype(LOW)
     v_part = jnp.einsum("src,srd->cd", grad_raw_v, normed, preferred_element_type=F32).astype(LOW)
     grad_normed = dot(grad_raw_qk, qk_all) + dot(grad_raw_v, v_all)
@@ -1742,12 +1953,12 @@
         return part.reshape(mp // 2, 2, 4, part.shape[0] // (4 * mp), width)
 
     norms = jnp.stack([gain_one, shift_one, gain_two, shift_two]).reshape(8, width // 2)
-    taps_part = jnp.concatenate(
-        [grad_tap_qk.reshape(3, mp, 2 * HD), grad_tap_v.reshape(3, mp, HD)], axis=2
-    ).transpose(1, 0, 2)
-    taps_part = jnp.pad(taps_part, ((0, 0), (0, 5), (0, HD)))
+    qk_sums = (tap_sums[0] + tap_sums[1]).reshape(8, mp, 2 * HD)
+    v_sums = tap_sums[2].reshape(8, mp, 2, HD).sum(axis=2)
+    taps_part = jnp.concatenate([qk_sums, v_sums, jnp.zeros_like(v_sums)], axis=2)
+    taps_part = taps_part.transpose(1, 0, 2)
     norms, up_legs = lax.optimization_barrier((norms, up_legs))
-    up_last = plane_gather_end(up_mine, up_legs)
+    up_last = plane_gather_end(up_legs)
     joint_grad, norms_sum, taps_sum, feed_a, feed_b = finish(
         split_parts(qk_part), split_parts(v_part), split_parts(out_part), norms, taps_part,
         ((1, feed_a), (0, feed_b)),
@@ -1763,7 +1974,7 @@
         )
     ).astype(LOW)
     joint_grad, up_last = lax.optimization_barrier((joint_grad, up_last))
-    up_grad = plane_order(plane_blocks(up_mine, up_legs, up_last), axis=0).T.astype(F32)
+    up_grad = plane_order(plane_blocks(up_mine, up_legs, up_last, 0), axis=1).astype(F32)
     joint_grad = joint_grad.astype(F32)
     small_sum = norms_sum.reshape(4, width)
     qk_grad = joint_grad[:, : HD // 2].reshape(2 * HD, width).T

time: 880 us -> 807 us (0.917)
  local copies, waits for them, and re-layouts: 82.4 us -> 51.3 us
  Pallas kernels: 647 us -> 618 us
  matrix products: 40.6 us -> 29.5 us
    pallas_call x3 -> x4, Pallas kernels: 213 us -> 314 us  [the longest x1 125 us: feed_in(): pl.pallas_call(feed_in_kernel, in_specs=[anywhere] * 10, out_specs=[anywh...]
    pallas_call x4 -> x2, Pallas kernels: 151 us -> 55.4 us  [exchange(): pl.pallas_call(partial(exchange_kernel, halo, len(right), ways), in_specs...]
    unnamed x213 -> x143, local copies, waits for them, and re-layouts: 44.8 us -> 17.8 us
    pallas_call x1, Pallas kernels: 37 us -> 17.9 us  [attend(): pl.pallas_call(attend_kernel, grid_spec=pltpu.PrefetchScalarGridSpec(num_...]
    pallas_call x1, Pallas kernels: 41 us -> 26.4 us  [attend_back(): pl.pallas_call(attend_back_kernel, grid_spec=pltpu.PrefetchScalarGridSpec...]
    dot_general x2 -> x0, matrix products: 9.29 us -> none  [the longest x1 6.58 us: per_device(): jnp.einsum('srd,cd->src', normed_ext, qk_all, preferred_element_type=F32)]
    ppermute x18 -> x16, starting transfers between devices: 19.4 us -> 19.2 us  [plane_send(): lax.ppermute(block, 'dp', [(d, d ^ mask) for d in range(lax.axis_size('dp...]
  transfers between devices with their start and end apart: 22 -> 18, of which waited for: 0 -> 1; matrix products, arithmetic and copies ran while one was open for 14% -> 12% of each run, Pallas kernels for 47% -> 46%
where the time goes in v4:
time: 807 us; the launch traced here: 797 us
  Pallas kernels  618 us (77%)
  other arithmetic  62.5 us (8%)
  local copies, waits for them, and re-layouts  51.3 us (6%)
  matrix products  29.5 us (4%)
  starting transfers between devices  19.8 us (2%)
  between operations  15.4 us (2%)
    pallas_call x1, Pallas kernels, feed_in(): pl.pallas_call(feed_in_kernel, in_specs=[anywhere] * 10, out_specs=[anywh...  125 us
    pallas_call x1, Pallas kernels, front(): pl.pallas_call(front_kernel, in_specs=[anywhere, vmem, vmem] + [anywhere]...  106 us
    pallas_call x1, Pallas kernels, feed_out(): pl.pallas_call(feed_out_kernel, in_specs=[anywhere] * 11, out_specs=[anyw...  105 us
    pallas_call x1, Pallas kernels, finish(): pl.pallas_call(partial(finish_kernel, tuple((way for way, _ in carried)))...  98.9 us
    pallas_call x1, Pallas kernels, project_back(): pl.pallas_call(partial(project_back_kernel, tuple((way for way, _ in carr...  64.5 us
    pallas_call x2, Pallas kernels, exchange(): pl.pallas_call(partial(exchange_kernel, halo, len(right), ways), in_specs...  55.4 us
    pallas_call x1, Pallas kernels, attend_back(): pl.pallas_call(attend_back_kernel, grid_spec=pltpu.PrefetchScalarGridSpec...  26.4 us
    ppermute x16, starting transfers between devices, plane_send(): lax.ppermute(block, 'dp', [(d, d ^ mask) for d in range(lax.axis_size('dp...  19.2 us
  transfers between devices with their start and end apart: 18, of which 1 were waited for; matrix products, arithmetic and copies ran while one was open for 12% of the time, Pallas kernels for 46%

profile of v4, /device:TPU:0, one launch (start us, length us, event | category | flops | bytes accessed | tf_op | source)
XLA Modules:
  0.0 797.3 jit_solution(10646706520745009200)
XLA Ops:
  17.3 106.3 %front.1 = (bf16[4,2,4,32,2048]{4,3,2,1,0:T(8,128)(2,1)}, bf16[4,2,4,16,2048]{4,3,2,1,0:T(8,128)(2,1)}, bf16[4,2,4,16,2048]{4,3,2,1,0:T(8,128)(2,1)}, f32[3,8,10...) custom-call(bf16[2,320,2048]{2,1,0:T(8,128)(2,1)} %inputs_ref.1, ...), custom_call_target="tpu_custom_call" | custom-call | flops 68719476736 | bytes 67108864 | tf_op jit(solution)/shard_map/front/pallas_call | solution.py:794
  123.7 3.5 fusion.22
  127.2 2.4 collective-permute-start
  129.6 2.0 collective-permute-start.2
  133.3 17.9 %attend.1 = (bf16[1,2560,128]{2,1,0:T(8,128)(2,1)S(1)}, f32[2,64,2560]{2,1,0:T(8,128)S(1)}, f32[2,1,2560]{2,1,0:T(1,128)S(1)}) custom-call(s32[2,5]{1,0:T(2,128)S(1)} %and_select_fusion.first_ref, s32[2,1,2560]{2,1,0:T(1,128)S(1)} %broadcast_in_dim.20.start_ref, bf16[3,2560,128]{2,1,0:T(8,128)(2,1)S(1)} %bitcast.165, bf16[3,2560,128]{2,1,0:T(8,128)(2,1)S(1)} %bitcast.166), custom_call_target="tpu_custom_call" | custom-call | flops 17179869184 | bytes 5242880 | tf_op jit(solution)/shard_map/attend/pallas_call | solution.py:107
  152.3 22.4 %attended_back.1 = bf16[1,320,1024]{2,1,0:T(8,128)(2,1)S(1)} custom-call(bf16[1,2560,128]{2,1,0:T(8,128)(2,1)S(1)} %get-tuple-element.85.x_ref), custom_call_target="tpu_custom_call" | custom-call | flops 34359738368 | bytes 16777216 | tf_op jit(solution)/shard_map/attended_back/pallas_call | solution.py:951
  177.1 4.5 fusion.29
  182.3 3.2 constant_dynamic-slice_fusion.4.down_ref
  185.5 2.4 add_convert_fusion.second_ref
  188.9 124.9 %feed_in.1 = (bf16[2,4,320,2048]{3,2,1,0:T(8,128)(2,1)}, f32[2,4,320,2048]{3,2,1,0:T(8,128)}, bf16[2,4,320,2048]{3,2,1,0:T(8,128)(2,1)}, bf16[2048,2048]{1,0:T(8...) custom-call(bf16[2,320,2048]{2,1,0:T(8,128)(2,1)} %add_convert_fusion.second_ref, ...), custom_call_target="tpu_custom_call" | custom-call | flops 64424509440 | bytes 62914560 | tf_op jit(solution)/shard_map/feed_in/pallas_call | solution.py:1238
  313.8 18.0 %down_grad_rest.1 = bf16[2048,2048]{1,0:T(8,128)(2,1)} custom-call(bf16[2,4,320,2048]{3,2,1,0:T(8,128)(2,1)} %get-tuple-element.96.hidden_ref, bf16[2048,2048]{1,0:T(8,128)(2,1)} %get-tuple-element.97.first_ref, bf16[2,320,2048]{2,1,0:T(8,128)(2,1)} %cot_0.1, bf16[2,320,1024]{2,1,0:T(8,128)(2,1)S(1)} %copy-done.6, ...), custom_call_target="tpu_custom_call" | custom-call | flops 10737418240 | bytes 33554432 | tf_op jit(solution)/shard_map/down_grad_rest/pallas_call | solution.py:1209
  332.5 105.4 %feed_out.1 = (bf16[2,4,320,2048]{3,2,1,0:T(8,128)(2,1)}, bf16[2,320,1024]{2,1,0:T(8,128)(2,1)}, bf16[2,320,1024]{2,1,0:T(8,128)(2,1)}, bf16[2,320,1024]{2,1,0:T...) custom-call(bf16[2,320,2048]{2,1,0:T(8,128)(2,1)} %cot_0.1, ...), custom_call_target="tpu_custom_call" | custom-call | flops 85899345920 | bytes 62914560 | tf_op jit(solution)/shard_map/feed_out/pallas_call | solution.py:1466
  438.0 6.3 multiply_reduce_fusion
  445.1 1.6 fusion.21
  447.5 1.7 copy-done.15
  454.3 33.0 %attended_grad_out.1 = (bf16[1,8,320,128]{3,2,1,0:T(8,128)(2,1)S(1)}, bf16[2048,2048]{1,0:T(8,128)(2,1)}, bf16[2,320,1024]{2,1,0:T(8,128)(2,1)S(1)}, bf16[2,320,1024]{2,1,0:T(8,128)(2,1)S(1)}) custom-call(bf16[1,320,1024]{2,1,0:T(8,128)(2,1)S(1)} %copy.88.x_ref, bf16[2560,2048]{1,0:T(8,128)(2,1)} %bitcast.222, bf16[2560,2048]{1,0:T(8,128)(2,1)} %bitcast.221, ...), custom_call_target="tpu_custom_call" | custom-call | flops 34359738368 | bytes 16777216 | tf_op jit(solution)/shard_map/attended_grad_out/pallas_call | solution.py:951
  488.6 2.2 convert_reduce_fusion
  490.8 5.1 bitcast_convert_fusion.1
  497.3 1.8 collective-permute-start.6
  499.4 1.9 collective-permute-start.7
  504.2 26.4 %attend_back.1.x_ref = bf16[3,2576,128]{2,1,0:T(8,128)(2,1)S(1)} custom-call(s32[2,5]{1,0:T(2,128)S(1)} %copy-done.4, s32[2,1,2560]{2,1,0:T(1,128)S(1)} %copy-done.2, bf16[3,2560,128]{2,1,0:T(8,128)(2,1)S(1)} %bitcast.167, bf16[3,2560,128]{2,1,0:T(8,128)(2,1)S(1)} %bitcast.168, bf16[1,2560,128]{2,1,0:T(8,128)(2,1)S(1)} %bitcast.169, ...), custom_call_target="tpu_custom_call" | custom-call | flops 34359738368 | bytes 5242880 | tf_op jit(solution)/shard_map/attend_back/pallas_call | solution.py:202
  532.0 3.0 collective-permute-start.8
  535.0 2.1 maximum_bitcast_fusion.3
  537.1 2.1 maximum_bitcast_fusion.4
  539.2 64.5 %project_back.1 = (bf16[3,320,1024]{2,1,0:T(8,128)(2,1)}, f32[3,8,1024]{2,1,0:T(8,128)}, bf16[2,320,1024]{2,1,0:T(8,128)(2,1)}, bf16[2,320,1024]{2,1,0:T(8,128)(2,1)}) custom-call(bf16[3,2576,128]{2,1,0:T(8,128)(2,1)} %copy-done.11, f32[3,336,1024]{2,1,0:T(8,128)} %get-tuple-element.115.raw_ref, f32[3,8,1024]{2,1,0:T(8,128)} %get-tuple-element.116.taps_ref, ...), custom_call_target="tpu_custom_call" | custom-call | flops 34359738368 | bytes 16777216 | tf_op jit(solution)/shard_map/project_back/pallas_call | solution.py:907
  603.7 3.5 fusion.11.refs_0_
  608.1 3.1 fusion.12.refs_1_
  612.5 2.2 fusion.25
  614.7 1.8 collective-permute-start.10
  616.5 1.7 collective-permute-start.12
  621.2 5.2 fusion.30
  626.4 5.5 bitcast_convert_fusion
  632.0 2.9 fusion.7
  634.9 2.6 fusion.10
  637.6 3.9 add_add_fusion.2
  644.3 3.9 maximum_convert_fusion.1
  648.9 4.9 bitcast_convert_fusion.2
  655.3 2.1 maximum_bitcast_fusion
  657.4 2.0 collective-permute-start.15
  659.5 2.3 maximum_bitcast_fusion.1
  661.7 98.9 %finish.1 = (bf16[4,64,2048]{2,1,0:T(8,128)(2,1)}, f32[8,1024]{1,0:T(8,128)}, f32[8,256]{1,0:T(8,128)}, bf16[2,320,1024]{2,1,0:T(8,128)(2,1)}, bf16[2,320,1024]{2,1,0:T(8,128)(2,1)}) custom-call(bf16[4,2,4,32,2048]{4,3,2,1,0:T(8,128)(2,1)} %bitcast.224, bf16[4,2,4,16,2048]{4,3,2,1,0:T(8,128)(2,1)} %bitcast.226, bf16[4,2,4,16,2048]{4,3,2,1,0:T(8,128)(2,1)} %bitcast.225, ...), custom_call_target="tpu_custom_call" | custom-call | flops 68719476736 | bytes 67108864 | tf_op jit(solution)/shard_map/finish/pallas_call | solution.py:1731
  760.7 3.1 bitcast_add_fusion.1
  763.8 2.2 bitcast_add_fusion
  769.1 2.3 fusion.8
  775.7 1.8 constant_dynamic-slice_fusion.3
  779.0 2.3 copy.99
  783.9 2.4 fusion.24
  786.3 4.0 maximum_convert_fusion
  (237 shorter events, 52.7 us)
Async XLA Ops:
  7.2 488.8 %reduce-scatter.3.cloned.1.call-start = ((), (), s32[]{:S(2)}) async-start(), calls=%async_computation.2 | async-start | bytes 9437184 | tf_op jit(solution)/shard_map/reduce_scatter | solution.py:1904
  123.6 6.0 copy-start.5
  127.2 60.8 %collective-permute-start = (bf16[2,320,1024]{2,1,0:T(8,128)(2,1)}, bf16[2,320,1024]{2,1,0:T(8,128)(2,1)}, u32[]{:S(2)}, u32[]{:S(2)}) collective-permute-start(bf16[2,320,1024]{2,1,0:T(8,128)(2,1)} %get-tuple-element.172), channel_id=1, source_target_pairs={{0,16},{8,24},{16,0},{24,8},{1,17},{9,25},{17,1},{25,9},{2,18},{10... | collective-permute-start | bytes 3932168 | tf_op jit(solution)/shard_map/ppermute | solution.py:1774
  129.6 58.3 %collective-permute-start.1 = (bf16[2,320,1024]{2,1,0:T(8,128)(2,1)}, bf16[2,320,1024]{2,1,0:T(8,128)(2,1)}, u32[]{:S(2)}, u32[]{:S(2)}) collective-permute-start(bf16[2,320,1024]{2,1,0:T(8,128)(2,1)} %get-tuple-element.171), channel_id=1, source_target_pairs={{0,8},{8,0},{16,24},{24,16},{1,9},{9,1},{17,25},{25,17},{2,10},{10... | collective-permute-start | bytes 3932168 | tf_op jit(solution)/shard_map/ppermute | solution.py:1774
  129.6 58.3 %collective-permute-start.2 = (bf16[2,320,1024]{2,1,0:T(8,128)(2,1)S(1)}, bf16[2,320,1024]{2,1,0:T(8,128)(2,1)}, u32[]{:S(2)}, u32[]{:S(2)}) collective-permute-start(bf16[2,320,1024]{2,1,0:T(8,128)(2,1)S(1)} %copy-done.5), channel_id=1, source_target_pairs={{0,16},{8,24},{16,0},{24,8},{1,17},{9,25},{17,1},{25,9},{2,18},{10... | collective-permute-start | bytes 3932168 | tf_op jit(solution)/shard_map/ppermute | solution.py:1774
  131.7 57.2 %collective-permute-start.3 = (bf16[2,320,1024]{2,1,0:T(8,128)(2,1)}, bf16[2,320,1024]{2,1,0:T(8,128)(2,1)}, u32[]{:S(2)}, u32[]{:S(2)}) collective-permute-start(bf16[2,320,1024]{2,1,0:T(8,128)(2,1)} %get-tuple-element.89.cot_4.refs_4_), channel_id=1, source_target_pairs={{0,8},{8,0},{16,24},{24,16},{1,9},{9,1},{17,25},{25,17},{2,10},{10... | collective-permute-start | bytes 3932168 | tf_op jit(solution)/shard_map/ppermute | solution.py:1774
  131.7 19.6 %copy-start.1 = (s32[2,1,2560]{2,1,0:T(1,128)}, s32[2,1,2560]{2,1,0:T(1,128)S(1)}, u32[]{:S(2)}) copy-start(s32[2,1,2560]{2,1,0:T(1,128)S(1)} %broadcast_in_dim.20.start_ref) | copy-start | bytes 61444
  133.3 17.9 %copy-start.3 = (s32[2,5]{1,0:T(2,128)}, s32[2,5]{1,0:T(2,128)S(1)}, u32[]{:S(2)}) copy-start(s32[2,5]{1,0:T(2,128)S(1)} %and_select_fusion.first_ref) | copy-start | bytes 124
  177.1 4.5 copy-start.31
  182.3 5.7 copy-start.54
  182.3 5.6 copy-start.49
  188.9 124.9 %copy-start.6 = (bf16[2,320,1024]{2,1,0:T(8,128)(2,1)S(1)}, bf16[2,320,1024]{2,1,0:T(8,128)(2,1)}, u32[]{:S(2)}) copy-start(bf16[2,320,1024]{2,1,0:T(8,128)(2,1)} %get-tuple-element.88.cot_1.refs_1_) | copy-start | bytes 3932164
  331.9 280.6 %reduce-scatter.5.cloned.1.call-start = ((), (), s32[]{:S(2)}) async-start(), calls=%async_computation.3 | async-start | bytes 9437184 | tf_op jit(solution)/shard_map/reduce_scatter | solution.py:1924
  332.5 105.4 %copy-start.46 = (f32[2,320]{1,0:T(2,128)S(1)}, f32[2,320]{1,0:T(2,128)}, u32[]{:S(2)}) copy-start(f32[2,320]{1,0:T(2,128)} %copy-done.45) | copy-start | bytes 7684
  332.5 105.4 %copy-start.48 = (f32[2048]{0:T(1024)S(1)}, f32[2048]{0:T(1024)}, u32[]{:S(2)}) copy-start(f32[2048]{0:T(1024)} %param.30) | copy-start | bytes 24580
  332.5 105.4 %copy-start.50 = (f32[2,320]{1,0:T(2,128)S(1)}, f32[2,320]{1,0:T(2,128)}, u32[]{:S(2)}) copy-start(f32[2,320]{1,0:T(2,128)} %copy-done.49) | copy-start | bytes 7684
  437.9 6.4 slice-start
  437.9 6.4 copy-start.55
  437.9 6.4 slice-start.1
  438.0 7.1 copy-start.18
  490.8 10.5 %copy-start.2 = (s32[2,1,2560]{2,1,0:T(1,128)S(1)}, s32[2,1,2560]{2,1,0:T(1,128)}, u32[]{:S(2)}) copy-start(s32[2,1,2560]{2,1,0:T(1,128)} %copy-done.1) | copy-start | bytes 61444
  490.8 10.5 %copy-start.4 = (s32[2,5]{1,0:T(2,128)S(1)}, s32[2,5]{1,0:T(2,128)}, u32[]{:S(2)}) copy-start(s32[2,5]{1,0:T(2,128)} %copy-done.3) | copy-start | bytes 124
  497.2 34.7 %collective-permute-start.4 = (bf16[256,1024]{1,0:T(8,128)(2,1)S(1)}, bf16[256,1024]{1,0:T(8,128)(2,1)}, u32[]{:S(2)}, u32[]{:S(2)}) collective-permute-start(bf16[256,1024]{1,0:T(8,128)(2,1)S(1)} %get-tuple-element.180), channel_id=1, source_target_pairs={{0,8},{8,0},{16,24},{24,16},{1,9},{9,1},{17,25},{25,17},{2,10},{10... | collective-permute-start | bytes 1572872 | tf_op jit(solution)/shard_map/ppermute | solution.py:1774
  497.3 34.7 %collective-permute-start.6 = (bf16[256,1024]{1,0:T(8,128)(2,1)S(1)}, bf16[256,1024]{1,0:T(8,128)(2,1)S(1)}, u32[]{:S(2)}, u32[]{:S(2)}) collective-permute-start(bf16[256,1024]{1,0:T(8,128)(2,1)S(1)} %get-tuple-element.180), channel_id=1, source_target_pairs={{0,16},{8,24},{16,0},{24,8},{1,17},{9,25},{17,1},{25,9},{2,18},{10... | collective-permute-start | bytes 1572872 | tf_op jit(solution)/shard_map/ppermute | solution.py:1774
  499.1 32.9 %collective-permute-start.5 = (bf16[256,1024]{1,0:T(8,128)(2,1)S(1)}, bf16[256,1024]{1,0:T(8,128)(2,1)}, u32[]{:S(2)}, u32[]{:S(2)}) collective-permute-start(bf16[256,1024]{1,0:T(8,128)(2,1)S(1)} %get-tuple-element.179), channel_id=1, source_target_pairs={{0,16},{8,24},{16,0},{24,8},{1,17},{9,25},{17,1},{25,9},{2,18},{10... | collective-permute-start | bytes 1572872 | tf_op jit(solution)/shard_map/ppermute | solution.py:1774
  499.4 32.6 %collective-permute-start.7 = (bf16[256,1024]{1,0:T(8,128)(2,1)S(1)}, bf16[256,1024]{1,0:T(8,128)(2,1)S(1)}, u32[]{:S(2)}, u32[]{:S(2)}) collective-permute-start(bf16[256,1024]{1,0:T(8,128)(2,1)S(1)} %get-tuple-element.179), channel_id=1, source_target_pairs={{0,8},{8,0},{16,24},{24,16},{1,9},{9,1},{17,25},{25,17},{2,10},{10... | collective-permute-start | bytes 1572872 | tf_op jit(solution)/shard_map/ppermute | solution.py:1774
  532.0 79.2 %collective-permute-start.8 = (bf16[256,1024]{1,0:T(8,128)(2,1)}, bf16[256,1024]{1,0:T(8,128)(2,1)S(1)}, u32[]{:S(2)}, u32[]{:S(2)}) collective-permute-start(bf16[256,1024]{1,0:T(8,128)(2,1)} %collective-permute-done.4), channel_id=1, source_target_pairs={{0,16},{8,24},{16,0},{24,8},{1,17},{9,25},{17,1},{25,9},{2,18},{10... | collective-permute-start | bytes 1572872 | tf_op jit(solution)/shard_map/ppermute | solution.py:1774
  535.0 76.2 %collective-permute-start.9 = (bf16[256,1024]{1,0:T(8,128)(2,1)}, bf16[256,1024]{1,0:T(8,128)(2,1)}, u32[]{:S(2)}, u32[]{:S(2)}) collective-permute-start(bf16[256,1024]{1,0:T(8,128)(2,1)} %collective-permute-done.5), channel_id=1, source_target_pairs={{0,8},{8,0},{16,24},{24,16},{1,9},{9,1},{17,25},{25,17},{2,10},{10... | collective-permute-start | bytes 1572872 | tf_op jit(solution)/shard_map/ppermute | solution.py:1774
  603.7 4.3 copy-start.19
  614.7 39.1 %collective-permute-start.10 = (bf16[1024,256]{0,1:T(8,128)(2,1)}, bf16[1024,256]{0,1:T(8,128)(2,1)S(1)}, u32[]{:S(2)}, u32[]{:S(2)}) collective-permute-start(bf16[1024,256]{0,1:T(8,128)(2,1)} %get-tuple-element.178), channel_id=1, source_target_pairs={{0,8},{8,0},{16,24},{24,16},{1,9},{9,1},{17,25},{25,17},{2,10},{10... | collective-permute-start | bytes 1572872 | tf_op jit(solution)/shard_map/ppermute | solution.py:1774
  616.5 37.3 %collective-permute-start.12 = (bf16[1024,256]{0,1:T(8,128)(2,1)}, bf16[1024,256]{0,1:T(8,128)(2,1)}, u32[]{:S(2)}, u32[]{:S(2)}) collective-permute-start(bf16[1024,256]{0,1:T(8,128)(2,1)} %get-tuple-element.178), channel_id=1, source_target_pairs={{0,16},{8,24},{16,0},{24,8},{1,17},{9,25},{17,1},{25,9},{2,18},{10... | collective-permute-start | bytes 1572872 | tf_op jit(solution)/shard_map/ppermute | solution.py:1774
  618.2 35.6 %collective-permute-start.11 = (bf16[1024,256]{0,1:T(8,128)(2,1)}, bf16[1024,256]{0,1:T(8,128)(2,1)}, u32[]{:S(2)}, u32[]{:S(2)}) collective-permute-start(bf16[1024,256]{0,1:T(8,128)(2,1)} %get-tuple-element.177), channel_id=1, source_target_pairs={{0,16},{8,24},{16,0},{24,8},{1,17},{9,25},{17,1},{25,9},{2,18},{10... | collective-permute-start | bytes 1572872 | tf_op jit(solution)/shard_map/ppermute | solution.py:1774
  618.5 35.3 %collective-permute-start.13 = (bf16[1024,256]{0,1:T(8,128)(2,1)}, bf16[1024,256]{0,1:T(8,128)(2,1)}, u32[]{:S(2)}, u32[]{:S(2)}) collective-permute-start(bf16[1024,256]{0,1:T(8,128)(2,1)} %get-tuple-element.177), channel_id=1, source_target_pairs={{0,8},{8,0},{16,24},{24,16},{1,9},{9,1},{17,25},{25,17},{2,10},{10... | collective-permute-start | bytes 1572872 | tf_op jit(solution)/shard_map/ppermute | solution.py:1774
  621.2 5.2 copy-start.37
  621.2 5.2 copy-start.61
  626.4 5.5 copy-start.14
  626.4 5.5 copy-start.34
  626.4 5.5 copy-start.43
  626.4 11.1 %slice-start.4 = ((s8[5242880]{0:T(1024)(128)(4,1)}), s8[4194304]{0:T(1024)(128)(4,1)S(1)}, s32[]{:S(2)}) async-start(s8[5242880]{0:T(1024)(128)(4,1)} %bitcast.174), calls=%async_computation.8 | async-start | bytes 8388608
  631.9 5.6 slice-start.5
  637.5 5.1 copy-start.28
  644.3 4.0 copy-start.52
  644.3 3.9 copy-start.53
  653.8 117.6 %collective-permute-start.14 = (bf16[1024,256]{0,1:T(8,128)(2,1)S(1)}, bf16[1024,256]{0,1:T(8,128)(2,1)}, u32[]{:S(2)}, u32[]{:S(2)}) collective-permute-start(bf16[1024,256]{0,1:T(8,128)(2,1)S(1)} %collective-permute-done.10), channel_id=1, source_target_pairs={{0,16},{8,24},{16,0},{24,8},{1,17},{9,25},{17,1},{25,9},{2,18},{10... | collective-permute-start | bytes 1572872 | tf_op jit(solution)/shard_map/ppermute | solution.py:1774
  657.4 114.0 %collective-permute-start.15 = (bf16[1024,256]{0,1:T(8,128)(2,1)}, bf16[1024,256]{0,1:T(8,128)(2,1)}, u32[]{:S(2)}, u32[]{:S(2)}) collective-permute-start(bf16[1024,256]{0,1:T(8,128)(2,1)} %collective-permute-done.11), channel_id=1, source_target_pairs={{0,8},{8,0},{16,24},{24,16},{1,9},{9,1},{17,25},{25,17},{2,10},{10... | collective-permute-start | bytes 1572872 | tf_op jit(solution)/shard_map/ppermute | solution.py:1774
  760.6 8.4 %slice-start.2 = ((s8[5242880]{0:T(1024)(128)(4,1)}), s8[4194304]{0:T(1024)(128)(4,1)S(1)}, s32[]{:S(2)}) async-start(s8[5242880]{0:T(1024)(128)(4,1)} %bitcast.172), calls=%async_computation.6 | async-start | bytes 8388608
  763.8 4.7 copy-start.57
  763.8 5.3 slice-start.3
  (38 other events, 89.8 us)
Sparse Core Ops, SparseCore 0:
  332.0 88.8 reduce-scatter.2
  488.6 115.3 reduce-scatter.4

commit v5 on v4

--- a/solution.py
+++ b/solution.py
@@ -1,3 +1,4 @@
+import math
 from functools import partial
 
 import jax
@@ -11,7 +12,7 @@
 QUERIES, KEYS = 512, 512
 WIDE = 256
 CHUNK = 512
-VMEM_LIMIT = 62 * 1024 * 1024
+VMEM_LIMIT = 63 * 1024 * 1024
 MESH = pl.DeviceIdType.MESH
 LOW = jnp.bfloat16
 F32 = jnp.float32
@@ -367,68 +368,6 @@
 HALO = 16
 
 
-def weight_grad(left_ref, pieces, whole, tiles, outs, out_ref, load, tile_sem, out_sem):
-    wide = tiles.shape[2]
-    steps = left_ref.shape[1] // wide
-    if len(pieces) == 1:
-        loading = [pltpu.make_async_copy(pieces[0], whole, load.at[0])]
-    else:
-        tall = whole.shape[0] // 8
-        loading = []
-        for s in range(2):
-            for m in range(4):
-                target = whole.at[pl.ds((4 * s + m) * tall, tall), :]
-                loading += piece_copies(pieces, s, m, target, load.at[s, m])
-
-    def tile(at, slot):
-        columns = pl.ds(pl.multiple_of(at * wide, wide), wide)
-        return pltpu.make_async_copy(left_ref.at[:, columns], tiles.at[slot], tile_sem.at[slot])
-
-    def out(at, slot):
-        rows = pl.ds(pl.multiple_of(at * wide, wide), wide)
-        return pltpu.make_async_copy(outs.at[slot], out_ref.at[rows, :], out_sem.at[slot])
-
-    for copy in loading:
-        copy.start()
-    tile(0, 0).start()
-    for copy in loading:
-        copy.wait()
-
-    def one(at, carry):
-        slot = lax.rem(at, 2)
-        tile(at, slot).wait()
-
-        @pl.when(at + 1 < steps)
-        def _():
-            tile(at + 1, 1 - slot).start()
-
-        @pl.when(at >= 2)
-        def _():
-            out(at - 2, slot).wait()
-
-        outs[slot] = lax.dot_general(
-            tiles[slot], whole[...], (((0,), (0,)), ((), ())), preferred_element_type=F32
-        ).astype(LOW)
-        out(at, slot).start()
-        return carry
-
-    lax.fori_loop(0, steps, one, 0)
-    out(steps - 2, lax.rem(steps - 2, 2)).wait()
-    out(steps - 1, lax.rem(steps - 1, 2)).wait()
-
-
-def weight_grad_scratch(rows, depth, pieces):
-    dma = pltpu.SemaphoreType.DMA
-    return [
-        pltpu.VMEM((rows, depth), LOW),
-        pltpu.VMEM((2, rows, 256), LOW),
-        pltpu.VMEM((2, 256, depth), LOW),
-        dma((1,)) if pieces == 1 else dma((2, 4, 2)),
-        dma((2,)),
-        dma((2,)),
-    ]
-
-
 def carry_copies(carried, targets, send, recv):
     partners = plane_partners()
     return [
@@ -469,60 +408,6 @@
 
 def head_lanes(at):
     return pl.ds(pl.multiple_of(at * 128, 128), 128)
-
-
-def exchange_kernel(halo, pieces, ways, x_ref, *refs):
-    count = 1 + pieces if pieces else 0
-    left_ref, right_refs = (refs[0], refs[1:count]) if pieces else (None, ())
-    carried = list(zip(ways, refs[count : count + len(ways)]))
-    refs = refs[count + len(ways) :]
-    o_ref, refs = refs[0], refs[1:]
-    if pieces:
-        grad_ref, refs = refs[0], refs[1:]
-    targets, refs = refs[: len(ways)], refs[len(ways) :]
-    landed, local, send, recv = refs[:4]
-    refs = refs[4:]
-    me = lax.axis_index("mp")
-    if halo is None:
-
-        def source(at):
-            return x_ref.at[:, :, head_lanes(at)]
-
-        def target(at):
-            return landed.at[:, at]
-    else:
-        tall = o_ref.shape[1]
-
-        def source(at):
-            return x_ref.at[:, pl.ds(pl.multiple_of(at * (tall - halo), 16), tall), :]
-
-        def target(at):
-            return landed.at[:, :, head_lanes(at)]
-
-    own = pltpu.make_async_copy(source(me), target(me), local.at[0])
-    own.start()
-    greet_members(ways)
-    copies = member_copies(source, target, send, recv)
-    for leaving, _ in copies:
-        leaving.start()
-    carries = []
-    if ways:
-        carries = carry_copies(carried, targets, refs[0], refs[1])
-        refs = refs[2:]
-    for copy in carries:
-        copy.start()
-    if pieces:
-        weight_grad(left_ref, right_refs, *refs[:3], grad_ref, *refs[3:])
-    own.wait()
-    for leaving, landing in copies:
-        landing.wait_recv()
-    save = pltpu.make_async_copy(landed, o_ref, local.at[1])
-    save.start()
-    for leaving, landing in copies:
-        leaving.wait_send()
-    for copy in carries:
-        copy.wait()
-    save.wait()
 
 
 def front_kernel(
@@ -829,13 +714,37 @@
     )(inputs, gain.reshape(1, depth), shift.reshape(1, depth), qk, v, out, taps, up, masks, cot)
 
 
+def left_t_right(left, right):
+    return lax.dot_general(left, right, (((0,), (0,)), ((), ())), preferred_element_type=F32)
+
+
+def stream_out(steps, compute, buffer, ref, sem):
+    def save(at, slot):
+        return pltpu.make_async_copy(buffer.at[slot], ref.at[at], sem.at[slot])
+
+    def one(at, carry):
+        slot = lax.rem(at, 2)
+
+        @pl.when(at >= 2)
+        def _():
+            save(at - 2, slot).wait()
+
+        buffer[slot] = compute(at)
+        save(at, slot).start()
+        return carry
+
+    lax.fori_loop(0, steps, one, 0)
+    save(steps - 2, (steps - 2) % 2).wait()
+    save(steps - 1, (steps - 1) % 2).wait()
+
+
 def project_back_kernel(
-    ways, x_ref, raw_ref, taps_ref, masks_ref, *refs
+    ways, x_ref, raw_ref, taps_ref, masks_ref, normed_ref, attended_ref, branch_ref, *refs
 ):
     carried, refs = list(zip(ways, refs[: len(ways)])), refs[len(ways) :]
-    grad_ref, sums_ref = refs[:2]
-    targets, refs = refs[2 : 2 + len(ways)], refs[2 + len(ways) :]
-    landed, raw, local, send, recv, carry_send, carry_recv = refs
+    grad_ref, sums_ref, qk_part_ref, v_part_ref, out_part_ref = refs[:5]
+    targets, refs = refs[5 : 5 + len(ways)], refs[5 + len(ways) :]
+    landed, raw, wide, narrow, part_sem, local, send, recv, carry_send, carry_recv = refs
     me = lax.axis_index("mp")
     tall = landed.shape[1]
     rows_here = grad_ref.shape[1]
@@ -859,6 +768,15 @@
     carries = carry_copies(carried, targets, carry_send, carry_recv)
     for copy in carries:
         copy.start()
+
+    def out_part(at):
+        lanes = head_lanes(at)
+        return (
+            left_t_right(attended_ref[0, :, lanes], branch_ref[0])
+            + left_t_right(attended_ref[1, :, lanes], branch_ref[1])
+        ).astype(LOW)
+
+    stream_out(heads // 2, out_part, narrow, out_part_ref, part_sem)
     own.wait()
     load.wait()
     for _, landing in copies:
@@ -891,31 +809,56 @@
             return carry
 
         lax.fori_loop(0, heads, back, 0)
+
+    def pair(at):
+        return pl.ds(pl.multiple_of(at * 256, 256), 256)
+
+    def qk_part(at):
+        return (
+            left_t_right(grad_ref[0, :, pair(at)], normed_ref[0])
+            + left_t_right(grad_ref[1, :, pair(at)], normed_ref[1])
+        ).astype(LOW)
+
+    def v_part(at):
+        side = grad_ref[2, :, pair(at)]
+        zero, one = left_t_right(side, normed_ref[0]), left_t_right(side, normed_ref[1])
+        return jnp.concatenate(
+            [zero[:HD] + one[HD : 2 * HD], zero[2 * HD : 3 * HD] + one[3 * HD :]], axis=0
+        ).astype(LOW)
+
+    stream_out(heads // 2, qk_part, wide, qk_part_ref, part_sem)
+    stream_out(heads // 2, v_part, narrow, v_part_ref, part_sem)
     for leaving, _ in copies:
         leaving.wait_send()
     for copy in carries:
         copy.wait()
 
 
-def project_back(x, raw, taps, masks, carried):
+def project_back(x, raw, taps, masks, normed, attended, branch, carried):
     mp = lax.axis_size("mp")
-    rows_here = masks.shape[2]
+    rows_here, depth = normed.shape[1:]
     tall = raw.shape[1]
     anywhere = pl.BlockSpec(memory_space=pl.ANY)
     dma = pltpu.SemaphoreType.DMA
     vmem = pl.BlockSpec(memory_space=pltpu.VMEM)
     return pl.pallas_call(
         partial(project_back_kernel, tuple(way for way, _ in carried)),
-        in_specs=[vmem, anywhere, vmem, vmem] + [anywhere] * len(carried),
-        out_specs=[vmem] * 2 + [anywhere] * len(carried),
+        in_specs=[vmem, anywhere] + [vmem] * 5 + [anywhere] * len(carried),
+        out_specs=[vmem] * 2 + [anywhere] * (3 + len(carried)),
         out_shape=[
             jax.ShapeDtypeStruct((3, rows_here, mp * 128), LOW),
             jax.ShapeDtypeStruct((3, 8, mp * 128), F32),
+            jax.ShapeDtypeStruct((mp // 2, 4 * HD, depth), LOW),
+            jax.ShapeDtypeStruct((mp // 2, 2 * HD, depth), LOW),
+            jax.ShapeDtypeStruct((mp // 2, 2 * HD, depth), LOW),
         ]
         + [jax.ShapeDtypeStruct(block.shape, block.dtype) for _, block in carried],
         scratch_shapes=[
             pltpu.VMEM((3, tall, mp * 128), LOW),
             pltpu.VMEM((3, tall, mp * 128), F32),
+            pltpu.VMEM((2, 4 * HD, depth), LOW),
+            pltpu.VMEM((2, 2 * HD, depth), LOW),
+            dma((2,)),
             dma((2,)),
             dma((mp,)),
             dma((mp,)),
@@ -927,60 +870,82 @@
         ),
         cost_estimate=pl.CostEstimate(flops=2**35, bytes_accessed=2**24, transcendentals=0),
         name="project_back",
-    )(x, raw, taps, masks, *(block for _, block in carried))
-
-
-def exchange(x, shape, halo, number, name, left=None, right=(), carried=()):
+    )(x, raw, taps, masks, normed, attended, branch, *(block for _, block in carried))
+
+
+def attended_kernel(x_ref, o_ref, landed, local, send, recv):
+    me = lax.axis_index("mp")
+    tall = o_ref.shape[1]
+
+    def source(at):
+        return x_ref.at[:, pl.ds(pl.multiple_of(at * tall, 16), tall), :]
+
+    def target(at):
+        return landed.at[:, :, head_lanes(at)]
+
+    own = pltpu.make_async_copy(source(me), target(me), local.at[0])
+    own.start()
+    greet_members(())
+    copies = member_copies(source, target, send, recv)
+    for leaving, _ in copies:
+        leaving.start()
+    own.wait()
+    for _, landing in copies:
+        landing.wait_recv()
+    save = pltpu.make_async_copy(landed, o_ref, local.at[1])
+    save.start()
+    for leaving, _ in copies:
+        leaving.wait_send()
+    save.wait()
+
+
+def attended_back(x, rows_here):
     mp = lax.axis_size("mp")
-    anywhere = pl.BlockSpec(memory_space=pl.ANY)
+    shape = (x.shape[0], rows_here, mp * 128)
     dma = pltpu.SemaphoreType.DMA
-    scratch = [pltpu.VMEM(shape, x.dtype), dma((2,)), dma((mp,)), dma((mp,))]
-    if carried:
-        scratch += [dma((len(carried),)), dma((len(carried),))]
-    outs = [jax.ShapeDtypeStruct(shape, x.dtype)]
-    extra = ()
-    if left is not None:
-        rows, units = left.shape
-        depth = right[0].shape[-1]
-        outs.append(jax.ShapeDtypeStruct((units, depth), LOW))
-        scratch += weight_grad_scratch(rows, depth, len(right))
-        extra = (left,) + tuple(right)
-    ways = tuple(way for way, _ in carried)
-    extra += tuple(block for _, block in carried)
-    outs += [jax.ShapeDtypeStruct(block.shape, block.dtype) for _, block in carried]
     return pl.pallas_call(
-        partial(exchange_kernel, halo, len(right), ways),
-        in_specs=[pl.BlockSpec(memory_space=pltpu.VMEM)] + [anywhere] * len(extra),
-        out_specs=[anywhere] * len(outs),
-        out_shape=outs,
-        scratch_shapes=scratch,
+        attended_kernel,
+        in_specs=[pl.BlockSpec(memory_space=pltpu.VMEM)],
+        out_specs=pl.BlockSpec(memory_space=pl.ANY),
+        out_shape=jax.ShapeDtypeStruct(shape, x.dtype),
+        scratch_shapes=[pltpu.VMEM(shape, x.dtype), dma((2,)), dma((mp,)), dma((mp,))],
         compiler_params=pltpu.CompilerParams(
-            collective_id=number, has_side_effects=True, vmem_limit_bytes=48 * 2**20
+            collective_id=5, has_side_effects=True, vmem_limit_bytes=48 * 2**20
         ),
-        cost_estimate=pl.CostEstimate(flops=2**35, bytes_accessed=2**24, transcendentals=0),
-        name=name,
-    )(x, *extra)
-
-
-def heads_out(x, number, name, left=None, right=(), carried=()):
-    parts, rows_here, width = x.shape
-    mp = lax.axis_size("mp")
-    shape = (parts, mp, rows_here, 128)
-    out, *more = exchange(x, shape, None, number, name, left, right, carried)
-    return [out.reshape(parts, mp * rows_here, 128)] + more
-
-
-def heads_back(x, rows_here, halo, number, name, left=None, right=(), carried=()):
-    mp = lax.axis_size("mp")
-    shape = (x.shape[0], rows_here + halo, mp * 128)
-    return exchange(x, shape, halo, number, name, left, right, carried)
+        cost_estimate=pl.CostEstimate(flops=2**34, bytes_accessed=2**24, transcendentals=0),
+        name="attended_back",
+    )(x)
+
+
+def line_blocks(place, sources, local, send, recv):
+    z, core = mesh_place()
+    count = lax.axis_size("mp") // 2
+    out = []
+    for number, (step, way, ref) in enumerate(sources):
+        at = z - way * step
+        there = (at >= 0) & (at < count)
+        at = jnp.clip(at, 0, count - 1)
+        sems = (send.at[number], recv.at[number], other_core())
+        out.append(
+            (
+                there,
+                pltpu.make_async_copy(ref, place(at, core), local.at[number]),
+                wire(ref, place(at, core), *sems),
+                wire(ref, place(at, 1 - core), *sems),
+            )
+        )
+    return out
 
 
 def feed_in_kernel(
-    second_ref, up_ref, down_ref, cot_0, cot_1, cot_2, cot_3, cot_4, cot_5, cot_6,
-    all_ref, relu_ref, hidden_ref, down_all_ref, up_all_ref, first_ref,
-    rows, up, relu, hidden, down, cot, tiles, sums, local, outs, send, recv, cot_sem, tile_sem, sum_sem, *line_sems,
+    late, second_ref, up_ref, down_ref, cot_0, cot_1, cot_2, cot_3, cot_4, cot_5, cot_6, *refs
 ):
+    late_sources = [(step, way, ref) for (step, way), ref in zip(late, refs)]
+    (
+        all_ref, relu_ref, hidden_ref, down_all_ref, up_all_ref, down_part_ref,
+        rows, up, relu, hidden, down, cot, tiles, sums, before, local, outs, send, recv, cot_sem, tile_sem, sum_sem,
+        before_sem, late_local, late_send, late_recv, *line_sems,
+    ) = refs[len(late) :]
     count = lax.axis_size("mp") // 2
     depth = rows.shape[3]
     units = up.shape[0]
@@ -1003,8 +968,8 @@
     for copy in own:
         copy.wait()
     greet_line(True)
-    up_line = LineGather(line_place(up), *line_sems[:4])
-    down_line = LineGather(line_place(down), *line_sems[4:])
+    late_blocks = line_blocks(line_place(up), late_sources, late_local, late_send, late_recv)
+    down_line = LineGather(line_place(down), *line_sems)
 
     def remote(s, source, target, half, partner, number):
         return wire(
@@ -1054,38 +1019,50 @@
 
     for number in range(4):
         copies[0][number].start()
-    late = range(early_steps(count)[-1] + 1, count)
-    for step in late:
-        up_line.start(step)
-        if step != late[-1]:
-            up_line.arrive(step)
-    cot_loads = []
-    for m in range(4):
-        cot_loads += piece_copies(pieces, 0, m, cot.at[m], cot_sem.at[m])
-    for copy in cot_loads:
+    for there, here, leaving, _ in late_blocks:
+
+        @pl.when(there)
+        def _(here=here, leaving=leaving):
+            here.start()
+            leaving.start()
+
+    down_line.start(1)
+    down_line.swap_own()
+
+    def cot_loads(s):
+        copies = []
+        for m in range(4):
+            copies += piece_copies(pieces, s, m, cot.at[m], cot_sem.at[m])
+        return copies
+
+    for copy in cot_loads(0):
         copy.start()
+    for there, here, leaving, landing in late_blocks:
+
+        @pl.when(there)
+        def _(here=here, leaving=leaving, landing=landing):
+            here.wait()
+            leaving.wait_send()
+            landing.wait_recv()
+
+    whole_up = pltpu.make_async_copy(up, up_all_ref, local.at[2])
+    whole_up.start()
+    tile(0, 0)
     copies[0][0].wait_recv()
     copies[0][4].start()
     copies[0][1].wait_recv()
     copies[0][5].start()
     copies[1][0].start()
     copies[1][1].start()
-    up_line.arrive(late[-1])
-    down_line.start(1)
-    down_line.swap_own()
-    up_line.finish(late, False)
-    whole_up = pltpu.make_async_copy(up, up_all_ref, local.at[2])
-    whole_up.start()
-    tile(0, 0)
+    tile(1, 0)
+    down_line.arrive(1)
+    down_line.start(2)
     copies[0][3].wait_recv()
     tile(0, 1)
     copies[0][2].wait_recv()
     copies[1][2].start()
     copies[1][3].start()
     tile(0, 2)
-    down_line.arrive(1)
-    if count > 2:
-        down_line.start(2)
     copies[1][0].wait_recv()
     copies[1][4].start()
     copies[1][1].wait_recv()
@@ -1093,19 +1070,16 @@
     copies[0][4].wait_recv()
     copies[0][5].wait_recv()
     tile(0, 3)
-    tile(1, 0)
-    settle(0)
-    settle(1)
-    for copy in cot_loads:
-        copy.wait()
-
-    def first_half():
-        gradient_tiles(hidden_ref.at[0], cot, tiles, sums, first_ref, tile_sem, sum_sem)
-
-    first_half()
     for step in range(3, count):
         down_line.arrive(step - 1)
         down_line.start(step)
+    settle(0)
+    settle(1)
+    for copy in cot_loads(0):
+        copy.wait()
+    gradient_tiles(hidden_ref.at[0], cot, tiles, sums, down_part_ref, tile_sem, sum_sem)
+    for copy in cot_loads(1):
+        copy.start()
     copies[1][3].wait_recv()
     tile(1, 1)
     copies[1][2].wait_recv()
@@ -1115,13 +1089,18 @@
     gathered = pltpu.make_async_copy(rows, all_ref, local.at[0])
     gathered.start()
     tile(1, 3)
-    if count > 2:
-        down_line.arrive(count - 1)
+    down_line.arrive(count - 1)
     down_line.finish(range(1, count), True)
     whole_down = pltpu.make_async_copy(down, down_all_ref, local.at[1])
     whole_down.start()
     settle(0)
     settle(1)
+    for copy in cot_loads(1):
+        copy.wait()
+    gradient_tiles(
+        hidden_ref.at[1], cot, tiles, sums, down_part_ref, tile_sem, sum_sem,
+        (down_part_ref, before, before_sem),
+    )
     for s in range(2):
         for copy in copies[s]:
             copy.wait_send()
@@ -1130,13 +1109,19 @@
     whole_down.wait()
 
 
-def gradient_tiles(left_ref, right, tiles, sums, out_ref, tile_sem, sum_sem, before=None):
-    wide = tiles.shape[3]
-    steps = left_ref.shape[2] // wide
+def gradient_tiles(
+    left_ref, right, tiles, sums, out_ref, tile_sem, sum_sem, before=None, span=None
+):
+    wide = tiles.shape[-1]
+    first, steps = span if span is not None else (0, left_ref.shape[-1] // wide)
+    lead = (slice(None),) * (len(left_ref.shape) - 1)
+    tall = math.prod(tiles.shape[1:-1])
 
     def load(at, slot):
         columns = pl.ds(pl.multiple_of(at * wide, wide), wide)
-        return pltpu.make_async_copy(left_ref.at[:, :, columns], tiles.at[slot], tile_sem.at[slot])
+        return pltpu.make_async_copy(
+            left_ref.at[lead + (columns,)], tiles.at[slot], tile_sem.at[slot]
+        )
 
     def rows_of(at):
         return pl.ds(pl.multiple_of(at * wide, wide), wide)
@@ -1148,9 +1133,9 @@
         before_ref, buffer, sem = before
         return pltpu.make_async_copy(before_ref.at[rows_of(at), :], buffer.at[slot], sem.at[slot])
 
-    load(0, 0).start()
+    load(first, first % 2).start()
     if before is not None:
-        load_before(0, 0).start()
+        load_before(first, first % 2).start()
 
     def one(at, carry):
         slot = lax.rem(at, 2)
@@ -1164,14 +1149,13 @@
             if before is not None:
                 load_before(at + 1, 1 - slot).start()
 
-        @pl.when(at >= 2)
+        @pl.when(at >= first + 2)
         def _():
             save(at - 2, slot).wait()
 
-        blocks, tall = right.shape[:2]
         result = lax.dot_general(
-            tiles[slot].reshape(blocks * tall, wide),
-            right[...].reshape(blocks * tall, right.shape[2]),
+            tiles[slot].reshape(tall, wide),
+            right[...].reshape(tall, right.shape[-1]),
             (((0,), (0,)), ((), ())),
             preferred_element_type=F32,
         )
@@ -1181,63 +1165,20 @@
         save(at, slot).start()
         return carry
 
-    lax.fori_loop(0, steps, one, 0)
+    lax.fori_loop(first, steps, one, 0)
     save(steps - 2, (steps - 2) % 2).wait()
     save(steps - 1, (steps - 1) % 2).wait()
 
 
-def down_grad_rest(hidden, cot_pieces, first):
-    rows_here, units = hidden.shape[2:]
-    depth = first.shape[1]
-    anywhere = pl.BlockSpec(memory_space=pl.ANY)
-    dma = pltpu.SemaphoreType.DMA
-
-    def kernel(hidden_ref, first_ref, *refs):
-        pieces, out_ref = refs[:7], refs[7]
-        cot, tiles, sums, buffer, cot_sem, tile_sem, sum_sem, first_sem = refs[8:]
-        loads = []
-        for m in range(4):
-            loads += piece_copies(pieces, 1, m, cot.at[m], cot_sem.at[m])
-        for copy in loads:
-            copy.start()
-        for copy in loads:
-            copy.wait()
-        gradient_tiles(
-            hidden_ref.at[1], cot, tiles, sums, out_ref, tile_sem, sum_sem, (first_ref, buffer, first_sem)
-        )
-
-    return pl.pallas_call(
-        kernel,
-        in_specs=[anywhere] * 9,
-        out_specs=anywhere,
-        out_shape=jax.ShapeDtypeStruct((units, depth), LOW),
-        scratch_shapes=[
-            pltpu.VMEM((4, rows_here, depth), LOW),
-            pltpu.VMEM((2, 4, rows_here, WIDE), LOW),
-            pltpu.VMEM((2, WIDE, depth), LOW),
-            pltpu.VMEM((2, WIDE, depth), LOW),
-            dma((4, 2)),
-            dma((2,)),
-            dma((2,)),
-            dma((2,)),
-        ],
-        compiler_params=pltpu.CompilerParams(vmem_limit_bytes=48 * 2**20),
-        cost_estimate=pl.CostEstimate(
-            flops=2 * 4 * rows_here * units * depth, bytes_accessed=2**25, transcendentals=0
-        ),
-        name="down_grad_rest",
-    )(hidden, first, *cot_pieces)
-
-
-def feed_in(second, up_early, down, cot_pieces):
+def feed_in(second, up_early, down, cot_pieces, up_late):
     rows_here, depth = second.shape[1:]
     units = up_early.shape[0]
     count = lax.axis_size("mp") // 2
     anywhere = pl.BlockSpec(memory_space=pl.ANY)
     dma = pltpu.SemaphoreType.DMA
     return pl.pallas_call(
-        feed_in_kernel,
-        in_specs=[anywhere] * 10,
+        partial(feed_in_kernel, tuple(up_late)),
+        in_specs=[anywhere] * (10 + len(up_late)),
         out_specs=[anywhere] * 6,
         out_shape=[
             jax.ShapeDtypeStruct((2, 4, rows_here, depth), LOW),
@@ -1256,6 +1197,7 @@
             pltpu.VMEM((4, rows_here, depth), LOW),
             pltpu.VMEM((2, 4, rows_here, WIDE), LOW),
             pltpu.VMEM((2, WIDE, depth), LOW),
+            pltpu.VMEM((2, WIDE, depth), LOW),
             dma((4,)),
             dma((2, 2)),
             dma((2, 6)),
@@ -1263,8 +1205,10 @@
             dma((4, 2)),
             dma((2,)),
             dma((2,)),
+            dma((2,)),
         ]
-        + line_semaphores(count) * 2,
+        + [dma((len(up_late),))] * 3
+        + line_semaphores(count),
         compiler_params=pltpu.CompilerParams(
             collective_id=1, has_side_effects=True, vmem_limit_bytes=VMEM_LIMIT
         ),
@@ -1274,7 +1218,7 @@
             transcendentals=0,
         ),
         name="feed_in",
-    )(second, up_early, down, *cot_pieces)
+    )(second, up_early, down, *cot_pieces, *up_late.values())
 
 
 def piece_copies(pieces, s, m, target, sems):
@@ -1290,11 +1234,14 @@
 
 
 def feed_out_kernel(
-    cot_0, cot_1, cot_2, cot_3, cot_4, cot_5, cot_6, relu_ref, hidden_ref, up_ref, down_ref,
-    grad_ref, feed_x0_ref, feed_x1_ref, feed_y0_ref, feed_y1_ref, keep_a_ref, keep_b_ref, back_ref,
-    up, down, cot, relu, grad, part, arrived, feed, result, local, loads, outs, send, recv,
+    cot_0, cot_1, cot_2, cot_3, cot_4, cot_5, cot_6, relu_ref, second_ref, up_ref, down_ref,
+    grad_ref, up_part_ref, back_ref,
+    up, shared, cot, relu, grad, part, arrived, tiles, sums, result, local, loads, outs, send, recv,
+    tile_sem, sum_sem,
 ):
     units, depth = up.shape
+    down = shared.at[pl.ds(0, units), :]
+    second = shared.at[pl.ds(0, 8 * cot.shape[1]), :]
     half = depth // 2
     lanes = (pl.ds(0, half), pl.ds(half, half))
     to_x, to_y = plane_partners()
@@ -1303,7 +1250,6 @@
         pltpu.make_async_copy(up_ref, up, local.at[1]),
     ]
     order = [(s, m) for s in range(2) for m in (3, 1, 2, 0)]
-    feed_x_refs, feed_y_refs = (feed_x0_ref, feed_x1_ref), (feed_y0_ref, feed_y1_ref)
     pieces = (cot_0, cot_1, cot_2, cot_3, cot_4, cot_5, cot_6)
 
     def load(at):
@@ -1318,7 +1264,6 @@
     greet([to_x, to_y])
     for copy in weights:
         copy.wait()
-
     def remote(s, source, number, side, partner):
         return pltpu.make_async_remote_copy(
             src_ref=part.at[s, source, :, lanes[side]],
@@ -1341,6 +1286,7 @@
         for s in range(2)
     ]
     saving = [None, None]
+    load_second = pltpu.make_async_copy(second_ref, second, local.at[0])
 
     def tile(at):
         s, m = order[at]
@@ -1360,6 +1306,8 @@
             return carry
 
         lax.fori_loop(0, units // CHUNK, back, 0)
+        if at + 1 == len(order):
+            load_second.start()
         saving[slot] = pltpu.make_async_copy(grad.at[slot], grad_ref.at[s, m], outs.at[slot])
         saving[slot].start()
 
@@ -1409,87 +1357,56 @@
         send_after(at)
     done = finish(0)
 
-    feeding = [None, None]
-
-    def feed_load(at):
-        s, m = order[at]
-        return pltpu.make_async_copy(hidden_ref.at[s, m], cot.at[at % 2], loads.at[at % 2, 0])
-
-    def feed_tile(at):
-        s, m = order[at]
-        slot = at % 2
-        feed_load(at).wait()
-        if at + 1 < len(order):
-            feed_load(at + 1).start()
-        if feeding[slot] is not None:
-            for copy in feeding[slot]:
-                copy.wait()
-
-        def one(step, carry):
-            columns = pl.ds(pl.multiple_of(step * CHUNK, CHUNK), CHUNK)
-            feed[slot, :, columns] = dot(cot[slot], down[:, columns]).astype(LOW)
-            return carry
-
-        lax.fori_loop(0, depth // CHUNK, one, 0)
-        targets = (
-            (keep_a_ref.at[s, 0], feed_x_refs[s].at[0], keep_a_ref.at[s, 1], feed_x_refs[s].at[1])[m],
-            (keep_b_ref.at[s, 0], keep_b_ref.at[s, 1], feed_y_refs[s].at[0], feed_y_refs[s].at[1])[m],
-        )
-        feeding[slot] = [
-            pltpu.make_async_copy(feed.at[slot, :, lanes[side]], target, outs.at[2 + 2 * slot + side])
-            for side, target in enumerate(targets)
-        ]
-        for copy in feeding[slot]:
-            copy.start()
-
-    feed_load(0).start()
-    for at in range(2):
-        feed_tile(at)
+    for slot in range(2):
+        saving[slot].wait()
+    load_second.wait()
+    halves = units // WIDE // 2
+
+    def some(span):
+        gradient_tiles(grad_ref, second, tiles, sums, up_part_ref, tile_sem, sum_sem, span=span)
+
+    some((0, halves))
     second_leg(1)
-    for at in range(2, 8):
-        feed_tile(at)
+    some((halves, 2 * halves))
     done.wait()
     finish(1).wait()
-    for slot in range(2):
-        saving[slot].wait()
-        for copy in feeding[slot]:
-            copy.wait()
     for s in range(2):
         for number in range(6):
             copies[s][number].wait_send()
 
 
-def feed_out(cot_pieces, relu, hidden, up_all, down_all):
+def feed_out(cot_pieces, relu, second_all, up_all, down_all):
     rows_here, units = relu.shape[2:]
     depth = up_all.shape[1]
     anywhere = pl.BlockSpec(memory_space=pl.ANY)
+    dma = pltpu.SemaphoreType.DMA
     return pl.pallas_call(
         feed_out_kernel,
         in_specs=[anywhere] * 11,
-        out_specs=[anywhere] * 8,
+        out_specs=[anywhere] * 3,
         out_shape=[
             jax.ShapeDtypeStruct((2, 4, rows_here, units), LOW),
-        ]
-        + [jax.ShapeDtypeStruct((2, rows_here, depth // 2), LOW)] * 4
-        + [jax.ShapeDtypeStruct((2, 2, rows_here, depth // 2), LOW)] * 2
-        + [
+            jax.ShapeDtypeStruct((units, depth), LOW),
             jax.ShapeDtypeStruct((2, rows_here, depth), F32),
         ],
         scratch_shapes=[
             pltpu.VMEM((units, depth), LOW),
-            pltpu.VMEM((units, depth), LOW),
+            pltpu.VMEM((max(units, 8 * rows_here), depth), LOW),
             pltpu.VMEM((2, rows_here, depth), LOW),
             pltpu.VMEM((2, rows_here, units), F32),
             pltpu.VMEM((2, rows_here, units), LOW),
             pltpu.VMEM((2, 4, rows_here, depth), LOW),
             pltpu.VMEM((2, 6, rows_here, depth // 2), LOW),
-            pltpu.VMEM((2, rows_here, depth), LOW),
+            pltpu.VMEM((2, 2, 4, rows_here, WIDE), LOW),
+            pltpu.VMEM((2, WIDE, depth), LOW),
             pltpu.VMEM((rows_here, depth), F32),
-            pltpu.SemaphoreType.DMA((3,)),
-            pltpu.SemaphoreType.DMA((2, 3)),
-            pltpu.SemaphoreType.DMA((6,)),
-            pltpu.SemaphoreType.DMA((2, 6)),
-            pltpu.SemaphoreType.DMA((2, 6)),
+            dma((3,)),
+            dma((2, 3)),
+            dma((2,)),
+            dma((2, 6)),
+            dma((2, 6)),
+            dma((2,)),
+            dma((2,)),
         ],
         compiler_params=pltpu.CompilerParams(
             collective_id=2, has_side_effects=True, vmem_limit_bytes=VMEM_LIMIT
@@ -1500,7 +1417,113 @@
             transcendentals=0,
         ),
         name="feed_out",
-    )(*cot_pieces, relu, hidden, up_all, down_all)
+    )(*cot_pieces, relu, second_all.reshape(8 * rows_here, depth), up_all, down_all)
+
+
+def feed_heads_kernel(
+    x_ref, hidden_ref, down_ref,
+    o_ref, feed_x0_ref, feed_x1_ref, feed_y0_ref, feed_y1_ref, keep_a_ref, keep_b_ref,
+    landed, down, hidden, feed, local, send, recv, loads, outs,
+):
+    me = lax.axis_index("mp")
+    units, depth = down.shape
+    half = depth // 2
+    lanes = (pl.ds(0, half), pl.ds(half, half))
+    feed_x_refs, feed_y_refs = (feed_x0_ref, feed_x1_ref), (feed_y0_ref, feed_y1_ref)
+
+    def source(at):
+        return x_ref.at[:, :, head_lanes(at)]
+
+    def target(at):
+        return landed.at[:, at]
+
+    weights = pltpu.make_async_copy(down_ref, down, local.at[2])
+    weights.start()
+    own = pltpu.make_async_copy(source(me), target(me), local.at[0])
+    own.start()
+    greet_members(())
+    copies = member_copies(source, target, send, recv)
+    for leaving, _ in copies:
+        leaving.start()
+    order = [(s, m) for s in range(2) for m in (3, 1, 2, 0)]
+
+    def load(at):
+        s, m = order[at]
+        return pltpu.make_async_copy(hidden_ref.at[s, m], hidden.at[at % 2], loads.at[at % 2])
+
+    load(0).start()
+    weights.wait()
+    feeding = [None, None]
+    for at, (s, m) in enumerate(order):
+        slot = at % 2
+        load(at).wait()
+        if at + 1 < len(order):
+            load(at + 1).start()
+        if feeding[slot] is not None:
+            for copy in feeding[slot]:
+                copy.wait()
+
+        def one(step, carry, slot=slot):
+            columns = pl.ds(pl.multiple_of(step * CHUNK, CHUNK), CHUNK)
+            feed[slot, :, columns] = dot(hidden[slot], down[:, columns]).astype(LOW)
+            return carry
+
+        lax.fori_loop(0, depth // CHUNK, one, 0)
+        targets = (
+            (keep_a_ref.at[s, 0], feed_x_refs[s].at[0], keep_a_ref.at[s, 1], feed_x_refs[s].at[1])[m],
+            (keep_b_ref.at[s, 0], keep_b_ref.at[s, 1], feed_y_refs[s].at[0], feed_y_refs[s].at[1])[m],
+        )
+        feeding[slot] = [
+            pltpu.make_async_copy(feed.at[slot, :, lanes[side]], there, outs.at[slot, side])
+            for side, there in enumerate(targets)
+        ]
+        for copy in feeding[slot]:
+            copy.start()
+    own.wait()
+    for _, landing in copies:
+        landing.wait_recv()
+    save = pltpu.make_async_copy(landed, o_ref, local.at[1])
+    save.start()
+    for leaving, _ in copies:
+        leaving.wait_send()
+    for slot in feeding:
+        for copy in slot:
+            copy.wait()
+    save.wait()
+
+
+def feed_heads(x, hidden, down_all):
+    parts, rows_here, width = x.shape
+    mp = lax.axis_size("mp")
+    units, depth = down_all.shape
+    anywhere = pl.BlockSpec(memory_space=pl.ANY)
+    dma = pltpu.SemaphoreType.DMA
+    shape = (parts, mp, rows_here, 128)
+    out, *terms = pl.pallas_call(
+        feed_heads_kernel,
+        in_specs=[pl.BlockSpec(memory_space=pltpu.VMEM)] + [anywhere] * 2,
+        out_specs=[anywhere] * 7,
+        out_shape=[jax.ShapeDtypeStruct(shape, LOW)]
+        + [jax.ShapeDtypeStruct((2, rows_here, depth // 2), LOW)] * 4
+        + [jax.ShapeDtypeStruct((2, 2, rows_here, depth // 2), LOW)] * 2,
+        scratch_shapes=[
+            pltpu.VMEM(shape, LOW),
+            pltpu.VMEM((units, depth), LOW),
+            pltpu.VMEM((2, rows_here, units), LOW),
+            pltpu.VMEM((2, rows_here, depth), LOW),
+            dma((3,)),
+            dma((mp,)),
+            dma((mp,)),
+            dma((2,)),
+            dma((2, 2)),
+        ],
+        compiler_params=pltpu.CompilerParams(
+            collective_id=6, has_side_effects=True, vmem_limit_bytes=48 * 2**20
+        ),
+        cost_estimate=pl.CostEstimate(flops=2**35, bytes_accessed=2**24, transcendentals=0),
+        name="feed_heads",
+    )(x, hidden, down_all)
+    return [out.reshape(parts, mp * rows_here, 128)] + terms
 
 
 def finish_kernel(
@@ -1573,11 +1596,12 @@
         pltpu.make_async_copy(norms_ref, norms_all.at[me], local.at[3]),
         pltpu.make_async_copy(taps_ref.at[me], taps_all.at[me], local.at[4]),
     ]
-    for copy in own_small:
-        copy.start()
     over_mp = small("mp", me, mp, lambda to: norms_ref, norms_all, 0, None) + small(
         "mp", me, mp, lambda to: taps_ref.at[to], taps_all, 1, None
     )
+
+    for copy in own_small:
+        copy.start()
     for leaving, _ in over_mp:
         leaving.start()
 
@@ -1615,6 +1639,12 @@
     add_core(2, dp_y)
     sends[2].start()
     add_core(3, dp)
+    sends[1].wait_recv()
+    add(dp_y, 0, 1)
+    sends[4].start()
+    sends[3].wait_recv()
+    add(dp_x, 1, 3)
+    sends[5].start()
     for _, landing in over_mp:
         landing.wait_recv()
     for copy in own_small:
@@ -1626,12 +1656,6 @@
     )
     for leaving, _ in over_dp:
         leaving.start()
-    sends[1].wait_recv()
-    add(dp_y, 0, 1)
-    sends[4].start()
-    sends[3].wait_recv()
-    add(dp_x, 1, 3)
-    sends[5].start()
     sends[0].wait_recv()
     add(dp, 0, 0)
     sends[2].wait_recv()
@@ -1742,7 +1766,7 @@
             pltpu.VMEM((count, 4, HD, depth), LOW),
             pltpu.VMEM((count, 4, HD, depth), LOW),
             pltpu.VMEM((6, count, HD, depth // 2), LOW),
-            pltpu.VMEM((2, count, HD, depth), LOW),
+            pltpu.VMEM((2, count - 1, HD, depth), LOW),
             pltpu.VMEM((4, HD, depth), LOW),
             pltpu.VMEM((mp,) + norms.shape, F32),
             pltpu.VMEM(taps.shape, F32),
@@ -1767,11 +1791,60 @@
         ),
         cost_estimate=pl.CostEstimate(flops=2**36, bytes_accessed=2**26, transcendentals=0),
         name="finish",
-    )(qk, v, out, norms, taps, *(block for _, block in carried))
+    )(
+        qk, v, out, norms, taps, *(block for _, block in carried),
+    )
 
 
 def plane_send(block, mask):
     return lax.ppermute(block, "dp", [(d, d ^ mask) for d in range(lax.axis_size("dp"))])
+
+
+def placed(own, legs, last, me, turn):
+    one_x, two_y, one_y, two_x = legs
+    units, width = own.shape
+    wide = 256
+    steps = width // 2 // wide
+
+    def kernel(me_ref, own_ref, one_x, two_x, one_y, two_y, one_xy, two_xy, o_ref):
+        first = pl.program_id(0) < steps
+        blocks = [own_ref[...]] + [
+            jnp.where(first, one[...], two[...])
+            for one, two in ((one_x, two_x), (one_y, two_y), (one_xy, two_xy))
+        ]
+        odd, high = lax.rem(me_ref[0], 2) == 1, me_ref[0] >= 2
+        blocks = [jnp.where(odd, blocks[at ^ 1], blocks[at]) for at in range(4)]
+        blocks = [jnp.where(high, blocks[at ^ 2], blocks[at]) for at in range(4)]
+        for at, block in enumerate(blocks):
+            if turn:
+                o_ref[:, at * units : (at + 1) * units] = block.astype(F32).T
+            else:
+                o_ref[at * units : (at + 1) * units, :] = block.astype(F32)
+
+    def half(side):
+        if side == 0:
+            return pl.BlockSpec((units, wide), lambda i, me: (0, jnp.minimum(i, steps - 1)))
+        return pl.BlockSpec((units, wide), lambda i, me: (0, jnp.maximum(i - steps, 0)))
+
+    if turn:
+        shape = (width, 4 * units)
+        out_spec = pl.BlockSpec((wide, 4 * units), lambda i, me: (i, 0))
+    else:
+        shape = (4 * units, width)
+        out_spec = pl.BlockSpec((4 * units, wide), lambda i, me: (0, i))
+    return pl.pallas_call(
+        kernel,
+        grid_spec=pltpu.PrefetchScalarGridSpec(
+            num_scalar_prefetch=1,
+            grid=(2 * steps,),
+            in_specs=[pl.BlockSpec((units, wide), lambda i, me: (0, i))] + [half(0), half(1)] * 3,
+            out_specs=out_spec,
+        ),
+        out_shape=jax.ShapeDtypeStruct(shape, F32),
+        compiler_params=pltpu.CompilerParams(vmem_limit_bytes=32 * 2**20),
+        cost_estimate=pl.CostEstimate(flops=0, bytes_accessed=2**24, transcendentals=0),
+        name="placed",
+    )(me.reshape(1).astype(jnp.int32), own, one_x, two_x, one_y, two_y, *last)
 
 
 def plane_gather_begin(block, axis=-1):
@@ -1785,22 +1858,11 @@
     return plane_send(one_x, 2), plane_send(two_y, 1)
 
 
-def plane_blocks(block, legs, last, axis=-1):
-    one_x, two_y, one_y, two_x = legs
-    return [
-        block,
-        jnp.concatenate([one_x, two_x], axis=axis),
-        jnp.concatenate([one_y, two_y], axis=axis),
-        jnp.concatenate(last, axis=axis),
-    ]
-
-
-def plane_order(blocks, axis):
-    me = lax.axis_index("dp")
-    stacked = jnp.stack(blocks, axis=0)
-    return jnp.concatenate(
-        [lax.dynamic_index_in_dim(stacked, me ^ d, 0, keepdims=False) for d in range(4)], axis=axis
-    )
+def line_step(blocks, step):
+    count = lax.axis_size("mp") // 2
+    up = [(2 * z + c, 2 * z + 2 + c) for z in range(step - 1, count - 1) for c in range(2)]
+    down = [(2 * z + c, 2 * z - 2 + c) for z in range(1, count - step + 1) for c in range(2)]
+    return lax.ppermute(blocks[0], "mp", up), lax.ppermute(blocks[1], "mp", down)
 
 
 def per_device(
@@ -1829,6 +1891,7 @@
     me_dp = lax.axis_index("dp")
     me_mp = lax.axis_index("mp")
     group = rows_here * mp
+    chips = mp // 2
     hidden_here = up_weight.shape[1]
     share = hidden_here // dp
 
@@ -1875,7 +1938,18 @@
     v_all = v_all.reshape(mp * HD, width)
     out_all = out_all.reshape(mp * HD, width)
     mixed = mixed.reshape(3, group, 128)
-    cot, mixed = lax.optimization_barrier((cotangent, mixed))
+    cot, mixed, up_early = lax.optimization_barrier((cotangent, mixed, up_early))
+
+    def early_block(at):
+        start = (2 * jnp.clip(at, 0, chips - 1) + me_mp % 2) * share
+        return lax.dynamic_slice_in_dim(up_early, start, share, 0)
+
+    late = range(early_steps(chips)[-1] + 1, chips)
+    up_late = {}
+    blocks = (early_block(me_mp // 2 - late[0] + 1), early_block(me_mp // 2 + late[0] - 1))
+    for step in late:
+        blocks = line_step(blocks, step)
+        up_late[step, 1], up_late[step, -1] = blocks
     one_y, two_x = plane_send(cot[:, :, : width // 2], 2), plane_send(cot[:, :, width // 2 :], 1)
     one_xy, two_xy = plane_send(one_x, 2), plane_send(two_y, 1)
 
@@ -1888,8 +1962,8 @@
         return split.transpose(2, 0, 1, 3).reshape(2, joint.shape[1], mp * HD)
 
     attended_head, wide, total = attend(mixed, starts)
-    (attended,) = heads_back(attended_head, rows_here, 0, 5, "attended_back")
-    attended = apart(attended)
+    attended_head, up_late = lax.optimization_barrier((attended_head, up_late))
+    attended = apart(attended_back(attended_head, rows_here))
     middle = rows + dot(attended, out_all)
     second = layer_norm(middle, norm2_gain, norm2_bias).astype(LOW)
 
@@ -1897,15 +1971,17 @@
         (second, one_y, two_x, one_xy, two_xy)
     )
     cot_pieces = (cot, one_x, two_x, one_y, two_y, one_xy, two_xy)
-    second_all, relu, hidden, down_all, up_all, down_first = feed_in(
-        second, up_early, down_own, cot_pieces
+    second_all, relu, hidden, down_all, up_all, down_part = feed_in(
+        second, up_early, down_own, cot_pieces, up_late
     )
-    down_part = down_grad_rest(hidden, cot_pieces, down_first)
     down_mine = lax.psum_scatter(down_part, "mp", scatter_dimension=0, tiled=True)
-    down_part, relu = lax.optimization_barrier((down_part, relu))
-    grad_pre, feed_x0, feed_x1, feed_y0, feed_y1, keep_a, keep_b, grad_second = feed_out(
-        cot_pieces, relu, hidden, up_all, down_all
+    grad_pre, up_part, grad_second = feed_out(
+        cot_pieces, relu, second_all, up_all, down_all
     )
+    up_mine = lax.psum_scatter(up_part, "mp", scatter_dimension=0, tiled=True)
+    grad_second, down_mine = lax.optimization_barrier((grad_second, down_mine))
+    down_legs = plane_gather_begin(down_mine)
+
     def norm_back(values, gain, grad):
         flat = values.reshape(-1, width)
         unused, pull = jax.vjp(layer_norm, flat, gain, norm1_bias)
@@ -1915,68 +1991,67 @@
     grad_middle, gain_two, shift_two = norm_back(middle, norm2_gain, grad_second)
     grad_middle = grad_middle + cotangent.astype(F32)
     branch = grad_middle.astype(LOW)
-    out_part = jnp.einsum("srh,srd->hd", attended, branch, preferred_element_type=F32).astype(LOW)
     grad_attended = jnp.einsum("srd,hd->srh", branch, out_all, preferred_element_type=F32).astype(LOW)
-    grad_head, up_part, x_first, y_first = heads_out(
-        side_by_side(grad_attended), 6, "attended_grad_out", grad_pre.reshape(-1, hidden.shape[3]),
-        (second_all.reshape(-1, width),), ((0, feed_x0), (1, feed_y0)),
+    grad_head, feed_x0, feed_x1, feed_y0, feed_y1, keep_a, keep_b = feed_heads(
+        side_by_side(grad_attended), hidden, down_all
     )
-    up_mine = lax.psum_scatter(up_part, "mp", scatter_dimension=0, tiled=True)
-    grad_head, down_mine = lax.optimization_barrier((grad_head, down_mine))
-    down_legs = plane_gather_begin(down_mine)
+    grad_head, down_legs, feed_x0, feed_y0 = lax.optimization_barrier(
+        (grad_head, down_legs, feed_x0, feed_y0)
+    )
+    down_last = plane_gather_end(down_legs)
+    x_first, y_first = plane_send(feed_x0, 1), plane_send(feed_y0, 2)
     grad_mixed_head = attend_back(mixed, grad_head, wide, total, starts, HALO)
-    grad_mixed_head, down_legs = lax.optimization_barrier((grad_mixed_head, down_legs))
-    down_last = plane_gather_end(down_legs)
-    grad_raw, tap_sums, x_second, y_second = project_back(
-        grad_mixed_head, raw, taps, masks, ((0, feed_x1), (1, feed_y1))
+    grad_mixed_head, down_last, x_first, y_first = lax.optimization_barrier(
+        (grad_mixed_head, down_last, x_first, y_first)
+    )
+    down_grad = placed(down_mine, down_legs, down_last, me_dp, False)
+
+    def add(left, right):
+        return left.astype(F32) + right.astype(F32)
+
+    feed_a0, feed_b0 = add(keep_a[0, 1], x_first[1]).astype(LOW), add(keep_b[0, 1], y_first[1]).astype(LOW)
+    grad_raw, tap_sums, qk_part, v_part, out_part, x_second, y_second, feed_a0, feed_b0 = project_back(
+        grad_mixed_head, raw, taps, masks, normed, attended, branch,
+        ((0, feed_x1), (1, feed_y1), (1, feed_a0), (0, feed_b0)),
     )
     grad_raw, down_last = lax.optimization_barrier((grad_raw, down_last))
-    down_grad = plane_order(plane_blocks(down_mine, down_legs, down_last), axis=0).astype(F32)
-    x_in, y_in = jnp.stack([x_first, x_second]), jnp.stack([y_first, y_second])
-
-    def add(left, right):
-        return left.astype(F32) + right.astype(F32)
-
-    feed_a = add(keep_a[:, 1], x_in[:, 1]).astype(LOW)
-    feed_b = add(keep_b[:, 1], y_in[:, 1]).astype(LOW)
-    grad_raw_qk, grad_raw_v = grad_raw[:2], apart(grad_raw[2:])
-    grad_raw_qk, up_mine = lax.optimization_barrier((grad_raw_qk, up_mine))
-    up_mine = up_mine.T
-    up_legs = plane_gather_begin(up_mine, 0)
-    qk_part = jnp.einsum("src,srd->cd", grad_raw_qk, normed, preferred_element_type=F32).astype(LOW)
-    v_part = jnp.einsum("src,srd->cd", grad_raw_v, normed, preferred_element_type=F32).astype(LOW)
-    grad_normed = dot(grad_raw_qk, qk_all) + dot(grad_raw_v, v_all)
+    grad_raw, up_mine = lax.optimization_barrier((grad_raw, up_mine))
+    up_legs = plane_gather_begin(up_mine)
+    feed_a1, feed_b1 = add(keep_a[1, 1], x_second[1]).astype(LOW), add(keep_b[1, 1], y_second[1]).astype(LOW)
+
+    def split_parts(part):
+        return part.reshape(mp // 2, 2, 4, part.shape[1] // 8, width)
+
+    grad_normed = dot(grad_raw[:2], qk_all) + dot(apart(grad_raw[2:]), v_all)
     grad_input, gain_one, shift_one = norm_back(rows, norm1_gain, grad_normed)
     input_grads = grad_middle + grad_input
-
-    def split_parts(part):
-        return part.reshape(mp // 2, 2, 4, part.shape[0] // (4 * mp), width)
-
-    norms = jnp.stack([gain_one, shift_one, gain_two, shift_two]).reshape(8, width // 2)
+    norms = jnp.pad(jnp.stack([gain_one, shift_one, gain_two, shift_two]), ((0, 4), (0, 0)))
     qk_sums = (tap_sums[0] + tap_sums[1]).reshape(8, mp, 2 * HD)
     v_sums = tap_sums[2].reshape(8, mp, 2, HD).sum(axis=2)
     taps_part = jnp.concatenate([qk_sums, v_sums, jnp.zeros_like(v_sums)], axis=2)
     taps_part = taps_part.transpose(1, 0, 2)
     norms, up_legs = lax.optimization_barrier((norms, up_legs))
-    up_last = plane_gather_end(up_legs)
-    joint_grad, norms_sum, taps_sum, feed_a, feed_b = finish(
+    joint_grad, small_sum, taps_sum, feed_a1, feed_b1, one_xy, two_xy = finish(
         split_parts(qk_part), split_parts(v_part), split_parts(out_part), norms, taps_part,
-        ((1, feed_a), (0, feed_b)),
+        ((1, feed_a1), (0, feed_b1), (1, up_legs[0]), (0, up_legs[1])),
     )
-    results = (
-        middle
-        + jnp.concatenate(
-            [
-                add(keep_a[:, 0], x_in[:, 0]) + feed_a.astype(F32),
-                add(keep_b[:, 0], y_in[:, 0]) + feed_b.astype(F32),
-            ],
-            axis=2,
-        )
+    results = jnp.stack(
+        [
+            middle[s]
+            + jnp.concatenate(
+                [
+                    add(keep_a[s, 0], x_in[0]) + a_in.astype(F32),
+                    add(keep_b[s, 0], y_in[0]) + b_in.astype(F32),
+                ],
+                axis=1,
+            )
+            for s, (x_in, y_in, a_in, b_in) in enumerate(
+                ((x_first, y_first, feed_a0, feed_b0), (x_second, y_second, feed_a1, feed_b1))
+            )
+        ]
     ).astype(LOW)
-    joint_grad, up_last = lax.optimization_barrier((joint_grad, up_last))
-    up_grad = plane_order(plane_blocks(up_mine, up_legs, up_last, 0), axis=1).astype(F32)
+    up_grad = placed(up_mine, up_legs, (one_xy, two_xy), me_dp, True)
     joint_grad = joint_grad.astype(F32)
-    small_sum = norms_sum.reshape(4, width)
     qk_grad = joint_grad[:, : HD // 2].reshape(2 * HD, width).T
     v_grad = joint_grad[:, HD // 2 : 3 * HD // 4].reshape(HD, width).T
     out_grad = joint_grad[:, 3 * HD // 4 :].reshape(HD, width)

time: 807 us -> 766 us (0.949)
  Pallas kernels: 618 us -> 595 us
  other arithmetic: 62.5 us -> 46.7 us
  waiting for transfers between devices: 1.01 us -> 11.9 us
  matrix products: 29.5 us -> 20.5 us
    dot_general x3 -> x0, matrix products: 15.4 us -> none  [the longest x1 5.47 us: per_device(): jnp.einsum('src,srd->cd', grad_raw_qk, normed, preferred_element_type=F32)]
    pallas_call x4 -> x5, Pallas kernels: 198 us -> 187 us  [the longest x1 121 us: feed_in(): pl.pallas_call(partial(feed_in_kernel, tuple(up_late)), in_specs=[anywher...]
    pallas_call x1, Pallas kernels: 64.5 us -> 54 us  [project_back(): pl.pallas_call(partial(project_back_kernel, tuple((way for way, _ in carr...]
    convert_element_type x5 -> x3, other arithmetic: 16.8 us -> 7.12 us  [the longest x1 2.64 us: per_device(): add(keep_a[0, 1], x_first[1]).astype(LOW)]
    another operation x11 -> x5, other arithmetic: 14.2 us -> 5.41 us  [the longest x8 12.5 us: plane_order(): stacked = jnp.stack(blocks, axis=0)]
    unnamed x143 -> x144, local copies, waits for them, and re-layouts: 17.8 us -> 15.4 us
  transfers between devices with their start and end apart: 18 -> 20, of which waited for: 1 -> 2; matrix products, arithmetic and copies ran while one was open for 12% -> 10% of each run, Pallas kernels for 46% -> 35%
where the time goes in v5:
time: 766 us; the launch traced here: 757 us
  Pallas kernels  595 us (78%)
  other arithmetic  46.7 us (6%)
  local copies, waits for them, and re-layouts  44.9 us (6%)
  starting transfers between devices  22.7 us (3%)
  matrix products  20.5 us (3%)
  between operations  15.3 us (2%)
  waiting for transfers between devices  11.9 us (2%)
    pallas_call x1, Pallas kernels, feed_in(): pl.pallas_call(partial(feed_in_kernel, tuple(up_late)), in_specs=[anywher...  121 us
    pallas_call x1, Pallas kernels, feed_out(): pl.pallas_call(feed_out_kernel, in_specs=[anywhere] * 11, out_specs=[anyw...  107 us
    pallas_call x1, Pallas kernels, front(): pl.pallas_call(front_kernel, in_specs=[anywhere, vmem, vmem] + [anywhere]...  106 us
    pallas_call x1, Pallas kernels, finish(): pl.pallas_call(partial(finish_kernel, tuple((way for way, _ in carried)))...  96.2 us
    pallas_call x1, Pallas kernels, project_back(): pl.pallas_call(partial(project_back_kernel, tuple((way for way, _ in carr...  54 us
    pallas_call x1, Pallas kernels, feed_heads(): pl.pallas_call(feed_heads_kernel, in_specs=[pl.BlockSpec(memory_space=plt...  34.1 us
    pallas_call x1, Pallas kernels, attend_back(): pl.pallas_call(attend_back_kernel, grid_spec=pltpu.PrefetchScalarGridSpec...  26.4 us
    pallas_call x1, Pallas kernels, attended_back(): pl.pallas_call(attended_kernel, in_specs=[pl.BlockSpec(memory_space=pltpu...  19.5 us
  transfers between devices with their start and end apart: 20, of which 2 were waited for; matrix products, arithmetic and copies ran while one was open for 10% of the time, Pallas kernels for 35%

profile of v5, /device:TPU:0, one launch (start us, length us, event | category | flops | bytes accessed | tf_op | source)
XLA Modules:
  0.0 756.5 jit_solution(729637981838820807)
XLA Ops:
  17.3 106.3 %front.1 = (bf16[4,2,4,32,2048]{4,3,2,1,0:T(8,128)(2,1)}, bf16[4,2,4,16,2048]{4,3,2,1,0:T(8,128)(2,1)}, bf16[4,2,4,16,2048]{4,3,2,1,0:T(8,128)(2,1)}, f32[3,8,10...) custom-call(bf16[2,320,2048]{2,1,0:T(8,128)(2,1)} %inputs_ref.1, ...), custom_call_target="tpu_custom_call" | custom-call | flops 68719476736 | bytes 67108864 | tf_op jit(solution)/shard_map/front/pallas_call | solution.py:679
  123.7 2.5 collective-permute-start.4
  126.2 2.9 constant_dynamic-slice_fusion.1
  129.1 1.6 collective-permute-start.1
  132.1 1.8 fusion.31
  133.9 2.0 collective-permute-start.3
  136.0 2.4 constant_dynamic-slice_fusion.down_ref
  138.4 17.9 %attend.1 = (bf16[1,2560,128]{2,1,0:T(8,128)(2,1)S(1)}, f32[2,64,2560]{2,1,0:T(8,128)S(1)}, f32[2,1,2560]{2,1,0:T(1,128)S(1)}) custom-call(s32[2,5]{1,0:T(2,128)S(1)} %and_select_fusion.first_ref, s32[2,1,2560]{2,1,0:T(1,128)S(1)} %broadcast_in_dim.20.start_ref, bf16[3,2560,128]{2,1,0:T(8,128)(2,1)S(1)} %bitcast.149, bf16[3,2560,128]{2,1,0:T(8,128)(2,1)S(1)} %bitcast.150), custom_call_target="tpu_custom_call" | custom-call | flops 17179869184 | bytes 5242880 | tf_op jit(solution)/shard_map/attend/pallas_call | solution.py:108
  157.3 2.3 collective-permute-start.2
  159.6 3.8 collective-permute-done.refs_0_
  163.5 19.5 %attended_back.1 = bf16[1,320,1024]{2,1,0:T(8,128)(2,1)S(1)} custom-call(bf16[1,2560,128]{2,1,0:T(8,128)(2,1)S(1)} %get-tuple-element.97.x_ref), custom_call_target="tpu_custom_call" | custom-call | flops 17179869184 | bytes 16777216 | tf_op jit(solution)/shard_map/attended_back/pallas_call | solution.py:906
  183.4 4.5 fusion.39
  190.3 2.4 add_convert_fusion.second_ref
  192.7 120.9 %feed_in.1 = (bf16[2,4,320,2048]{3,2,1,0:T(8,128)(2,1)}, f32[2,4,320,2048]{3,2,1,0:T(8,128)}, bf16[2,4,320,2048]{3,2,1,0:T(8,128)(2,1)}, bf16[2048,2048]{1,0:T(8...) custom-call(bf16[2,320,2048]{2,1,0:T(8,128)(2,1)} %add_convert_fusion.second_ref, ...), custom_call_target="tpu_custom_call" | custom-call | flops 64424509440 | bytes 62914560 | tf_op jit(solution)/shard_map/feed_in/pallas_call | solution.py:1179
  314.2 106.8 %feed_out.1 = (bf16[2,4,320,2048]{3,2,1,0:T(8,128)(2,1)}, bf16[2048,2048]{1,0:T(8,128)(2,1)}, f32[2,320,2048]{2,1,0:T(8,128)}) custom-call(bf16[2,320,2048]{2,1,0:T(8,128)(2,1)} %cot_0.1, bf16[2,320,1024]{2,1,0:T(8,128)(2,1)} %get-tuple-element.100.cot_1, bf16[2,320,1024]{2,1,0:T(8,128)(2,1)} %collective-permute-done.3.cot_2, ...), custom_call_target="tpu_custom_call" | custom-call | flops 85899345920 | bytes 62914560 | tf_op jit(solution)/shard_map/feed_out/pallas_call | solution.py:1383
  421.2 1.6 copy-done.29
  423.2 2.3 copy.66.attended_ref
  425.5 2.6 fusion.35
  428.1 1.8 collective-permute-start.7
  430.2 2.0 collective-permute-start.6
  432.2 5.2 multiply_reduce_fusion
  437.4 3.5 fusion.30
  440.9 2.3 copy-done.31
  445.5 1.6 convolution_convert_fusion
  448.2 2.2 copy.64
  451.8 34.1 %feed_heads.1 = (bf16[1,8,320,128]{3,2,1,0:T(8,128)(2,1)S(1)}, bf16[2,320,1024]{2,1,0:T(8,128)(2,1)S(1)}, bf16[2,320,1024]{2,1,0:T(8,128)(2,1)S(1)}, bf16[2,320,...) custom-call(bf16[1,320,1024]{2,1,0:T(8,128)(2,1)S(1)} %copy.65.x_ref, ...), custom_call_target="tpu_custom_call" | custom-call | flops 34359738368 | bytes 16777216 | tf_op jit(solution)/shard_map/feed_heads/pallas_call | solution.py:1502
  486.2 1.7 collective-permute-start.11
  488.2 1.9 collective-permute-start.13
  490.1 26.4 %attend_back.1.x_ref = bf16[3,2576,128]{2,1,0:T(8,128)(2,1)S(1)} custom-call(s32[2,5]{1,0:T(2,128)S(1)} %copy-done.21, s32[2,1,2560]{2,1,0:T(1,128)S(1)} %copy-done.19, bf16[3,2560,128]{2,1,0:T(8,128)(2,1)S(1)} %bitcast.151, bf16[3,2560,128]{2,1,0:T(8,128)(2,1)S(1)} %bitcast.152, bf16[1,2560,128]{2,1,0:T(8,128)(2,1)S(1)} %bitcast.153, ...), custom_call_target="tpu_custom_call" | custom-call | flops 34359738368 | bytes 5242880 | tf_op jit(solution)/shard_map/attend_back/pallas_call | solution.py:203
  519.5 7.9 %collective-permute-done.12 = bf16[2,320,1024]{2,1,0:T(8,128)(2,1)S(1)} collective-permute-done((bf16[2,320,1024]{2,1,0:T(8,128)(2,1)S(1)}, bf16[2,320,1024]{2,1,0:T(8,128)(2,1)S(1)}, u32[]{:S(2)}, u32[]{:S(2)}) %collective-permute-start.12) | collective-permute-done | bytes 1310752 | tf_op jit(solution)/shard_map/ppermute | solution.py:1800
  527.4 2.6 fusion.21.refs_2_
  530.1 2.2 fusion.20.refs_3_
  532.2 54.0 %project_back.1 = (bf16[3,320,1024]{2,1,0:T(8,128)(2,1)}, f32[3,8,1024]{2,1,0:T(8,128)}, bf16[4,256,2048]{2,1,0:T(8,128)(2,1)}, bf16[4,128,2048]{2,1,0:T(8,128)(...) custom-call(bf16[3,2576,128]{2,1,0:T(8,128)(2,1)} %copy-done.26, ...), custom_call_target="tpu_custom_call" | custom-call | flops 34359738368 | bytes 16777216 | tf_op jit(solution)/shard_map/project_back/pallas_call | solution.py:844
  586.3 2.2 fusion.34
  588.5 1.6 collective-permute-start.17
  590.5 1.6 collective-permute-start.16
  594.7 7.8 %fusion.40 = f32[2,320,2048]{2,1,0:T(8,128)} fusion(bf16[3,320,1024]{2,1,0:T(8,128)(2,1)} %get-tuple-element.149, bf16[1024,2048,1]{1,0,2:T(8,128)(2,1)} %bitcast.192), kind=kOutput, calls=%fused_computation.111 | convolution fusion | flops 2684354560 | bytes 11403264 | tf_op jit(solution)/shard_map/dot_general | solution.py:22
  604.9 6.7 fusion.7
  611.6 2.6 fusion.11
  614.3 5.7 add_add_fusion.2
  620.0 2.3 fusion.14.refs_1_
  623.0 5.2 placed.3
  628.9 1.9 fusion.23
  632.6 96.2 %finish.1 = (bf16[4,64,2048]{2,1,0:T(8,128)(2,1)}, f32[8,2048]{1,0:T(8,128)}, f32[8,256]{1,0:T(8,128)}, bf16[320,1024]{1,0:T(8,128)(2,1)}, bf16[320,1024]{1,0:T(...) custom-call(bf16[4,2,4,32,2048]{4,3,2,1,0:T(8,128)(2,1)} %bitcast.193, ...), custom_call_target="tpu_custom_call" | custom-call | flops 68719476736 | bytes 67108864 | tf_op jit(solution)/shard_map/finish/pallas_call | solution.py:1755
  731.2 2.4 fusion.17
  735.9 2.2 fusion.19
  739.5 1.7 pad_maximum_fusion
  742.3 7.2 placed.2
  (227 shorter events, 40.6 us)
Async XLA Ops:
  7.2 7.0 copy-start.50
  7.2 6.9 copy-start.51
  7.2 418.3 %reduce-scatter.3.cloned.1.call-start = ((), (), s32[]{:S(2)}) async-start(), calls=%async_computation.2 | async-start | bytes 9437184 | tf_op jit(solution)/shard_map/reduce_scatter | solution.py:1977
  123.7 69.0 %collective-permute-start.4 = (bf16[2,320,1024]{2,1,0:T(8,128)(2,1)}, bf16[2,320,1024]{2,1,0:T(8,128)(2,1)}, u32[]{:S(2)}, u32[]{:S(2)}) collective-permute-start(bf16[2,320,1024]{2,1,0:T(8,128)(2,1)} %get-tuple-element.100.cot_1), channel_id=1, source_target_pairs={{0,16},{8,24},{16,0},{24,8},{1,17},{9,25},{17,1},{25,9},{2,18},{10... | collective-permute-start | bytes 3932168 | tf_op jit(solution)/shard_map/ppermute | solution.py:1800
  126.2 66.5 %collective-permute-start.5 = (bf16[2,320,1024]{2,1,0:T(8,128)(2,1)}, bf16[2,320,1024]{2,1,0:T(8,128)(2,1)}, u32[]{:S(2)}, u32[]{:S(2)}) collective-permute-start(bf16[2,320,1024]{2,1,0:T(8,128)(2,1)} %get-tuple-element.101.cot_4), channel_id=1, source_target_pairs={{0,8},{8,0},{16,24},{24,16},{1,9},{9,1},{17,25},{25,17},{2,10},{10... | collective-permute-start | bytes 3932168 | tf_op jit(solution)/shard_map/ppermute | solution.py:1800
  129.1 28.3 %collective-permute-start.1 = (bf16[256,2048]{1,0:T(8,128)(2,1)}, bf16[256,2048]{1,0:T(8,128)(2,1)}, u32[]{:S(2)}, u32[]{:S(2)}) collective-permute-start(bf16[256,2048]{1,0:T(8,128)(2,1)} %get-tuple-element.181), channel_id=1, source_target_pairs={{4,6},{5,7},{12,14},{13,15},{20,22},{21,23},{28,30},{29,31}} | collective-permute-start | bytes 3145736 | tf_op jit(solution)/shard_map/ppermute | solution.py:1865
  130.7 7.7 %copy-start.22 = (bf16[3,8,320,128]{3,2,1,0:T(8,128)(2,1)S(1)}, bf16[3,8,320,128]{3,2,1,0:T(8,128)(2,1)}, u32[]{:S(2)}) copy-start(bf16[3,8,320,128]{3,2,1,0:T(8,128)(2,1)} %get-tuple-element.92) | copy-start | bytes 5898244
  130.7 32.7 %collective-permute-start = (bf16[256,2048]{1,0:T(8,128)(2,1)S(1)}, bf16[256,2048]{1,0:T(8,128)(2,1)}, u32[]{:S(2)}, u32[]{:S(2)}) collective-permute-start(bf16[256,2048]{1,0:T(8,128)(2,1)S(1)} %get-tuple-element.182), channel_id=1, source_target_pairs={{2,0},{3,1},{10,8},{11,9},{18,16},{19,17},{26,24},{27,25}} | collective-permute-start | bytes 3145736 | tf_op jit(solution)/shard_map/ppermute | solution.py:1865
  133.9 58.8 %collective-permute-start.3 = (bf16[2,320,1024]{2,1,0:T(8,128)(2,1)}, bf16[2,320,1024]{2,1,0:T(8,128)(2,1)}, u32[]{:S(2)}, u32[]{:S(2)}) collective-permute-start(bf16[2,320,1024]{2,1,0:T(8,128)(2,1)} %get-tuple-element.189), channel_id=1, source_target_pairs={{0,8},{8,0},{16,24},{24,16},{1,9},{9,1},{17,25},{25,17},{2,10},{10... | collective-permute-start | bytes 3932168 | tf_op jit(solution)/shard_map/ppermute | solution.py:1800
  136.0 20.3 %copy-start.18 = (s32[2,1,2560]{2,1,0:T(1,128)}, s32[2,1,2560]{2,1,0:T(1,128)S(1)}, u32[]{:S(2)}) copy-start(s32[2,1,2560]{2,1,0:T(1,128)S(1)} %broadcast_in_dim.20.start_ref) | copy-start | bytes 61444
  136.0 20.3 %copy-start.20 = (s32[2,5]{1,0:T(2,128)}, s32[2,5]{1,0:T(2,128)S(1)}, u32[]{:S(2)}) copy-start(s32[2,5]{1,0:T(2,128)S(1)} %and_select_fusion.first_ref) | copy-start | bytes 124
  157.3 35.4 %collective-permute-start.2 = (bf16[2,320,1024]{2,1,0:T(8,128)(2,1)}, bf16[2,320,1024]{2,1,0:T(8,128)(2,1)}, u32[]{:S(2)}, u32[]{:S(2)}) collective-permute-start(bf16[2,320,1024]{2,1,0:T(8,128)(2,1)} %get-tuple-element.190), channel_id=1, source_target_pairs={{0,16},{8,24},{16,0},{24,8},{1,17},{9,25},{17,1},{25,9},{2,18},{10... | collective-permute-start | bytes 3932168 | tf_op jit(solution)/shard_map/ppermute | solution.py:1800
  313.7 272.6 %reduce-scatter.5.cloned.1.call-start = ((), (), s32[]{:S(2)}) async-start(), calls=%async_computation.3 | async-start | bytes 9437184 | tf_op jit(solution)/shard_map/reduce_scatter | solution.py:1981
  422.8 9.4 %copy-start.54 = (f32[2,320]{1,0:T(2,128)S(1)}, f32[2,320]{1,0:T(2,128)}, u32[]{:S(2)}) copy-start(f32[2,320]{1,0:T(2,128)} %copy-done.53) | copy-start | bytes 7684
  422.8 9.4 %copy-start.56 = (f32[2048]{0:T(1024)S(1)}, f32[2048]{0:T(1024)}, u32[]{:S(2)}) copy-start(f32[2048]{0:T(1024)} %param.30) | copy-start | bytes 24580
  422.8 9.4 %copy-start.58 = (f32[2,320]{1,0:T(2,128)S(1)}, f32[2,320]{1,0:T(2,128)}, u32[]{:S(2)}) copy-start(f32[2,320]{1,0:T(2,128)} %copy-done.57) | copy-start | bytes 7684
  425.5 11.9 %slice-start.2 = ((s8[5242880]{0:T(1024)(128)(4,1)}), s8[4194304]{0:T(1024)(128)(4,1)S(1)}, s32[]{:S(2)}) async-start(s8[5242880]{0:T(1024)(128)(4,1)} %bitcast.156), calls=%async_computation.6 | async-start | bytes 8388608
  428.1 57.8 %collective-permute-start.9 = (bf16[256,1024]{1,0:T(8,128)(2,1)}, bf16[256,1024]{1,0:T(8,128)(2,1)S(1)}, u32[]{:S(2)}, u32[]{:S(2)}) collective-permute-start(bf16[256,1024]{1,0:T(8,128)(2,1)} %get-tuple-element.197), channel_id=1, source_target_pairs={{0,8},{8,0},{16,24},{24,16},{1,9},{9,1},{17,25},{25,17},{2,10},{10... | collective-permute-start | bytes 1572872 | tf_op jit(solution)/shard_map/ppermute | solution.py:1800
  428.1 57.8 %collective-permute-start.7 = (bf16[256,1024]{1,0:T(8,128)(2,1)}, bf16[256,1024]{1,0:T(8,128)(2,1)S(1)}, u32[]{:S(2)}, u32[]{:S(2)}) collective-permute-start(bf16[256,1024]{1,0:T(8,128)(2,1)} %get-tuple-element.197), channel_id=1, source_target_pairs={{0,16},{8,24},{16,0},{24,8},{1,17},{9,25},{17,1},{25,9},{2,18},{10... | collective-permute-start | bytes 1572872 | tf_op jit(solution)/shard_map/ppermute | solution.py:1800
  429.9 7.5 copy-start.60
  429.9 7.5 slice-start.3
  429.9 56.1 %collective-permute-start.8 = (bf16[256,1024]{1,0:T(8,128)(2,1)}, bf16[256,1024]{1,0:T(8,128)(2,1)S(1)}, u32[]{:S(2)}, u32[]{:S(2)}) collective-permute-start(bf16[256,1024]{1,0:T(8,128)(2,1)} %get-tuple-element.198), channel_id=1, source_target_pairs={{0,16},{8,24},{16,0},{24,8},{1,17},{9,25},{17,1},{25,9},{2,18},{10... | collective-permute-start | bytes 1572872 | tf_op jit(solution)/shard_map/ppermute | solution.py:1800
  430.2 55.8 %collective-permute-start.6 = (bf16[256,1024]{1,0:T(8,128)(2,1)}, bf16[256,1024]{1,0:T(8,128)(2,1)S(1)}, u32[]{:S(2)}, u32[]{:S(2)}) collective-permute-start(bf16[256,1024]{1,0:T(8,128)(2,1)} %get-tuple-element.198), channel_id=1, source_target_pairs={{0,8},{8,0},{16,24},{24,16},{1,9},{9,1},{17,25},{25,17},{2,10},{10... | collective-permute-start | bytes 1572872 | tf_op jit(solution)/shard_map/ppermute | solution.py:1800
  451.7 38.4 %copy-start.19 = (s32[2,1,2560]{2,1,0:T(1,128)S(1)}, s32[2,1,2560]{2,1,0:T(1,128)}, u32[]{:S(2)}) copy-start(s32[2,1,2560]{2,1,0:T(1,128)} %copy-done.18) | copy-start | bytes 61444
  451.8 38.4 %copy-start.21 = (s32[2,5]{1,0:T(2,128)S(1)}, s32[2,5]{1,0:T(2,128)}, u32[]{:S(2)}) copy-start(s32[2,5]{1,0:T(2,128)} %copy-done.20) | copy-start | bytes 124
  451.8 38.4 %copy-start.23 = (bf16[3,8,320,128]{3,2,1,0:T(8,128)(2,1)S(1)}, bf16[3,8,320,128]{3,2,1,0:T(8,128)(2,1)}, u32[]{:S(2)}) copy-start(bf16[3,8,320,128]{3,2,1,0:T(8,128)(2,1)} %get-tuple-element.92) | copy-start | bytes 5898244
  451.8 38.4 %copy-start.25 = (f32[2,64,2560]{2,1,0:T(8,128)S(1)}, f32[2,64,2560]{2,1,0:T(8,128)}, u32[]{:S(2)}) copy-start(f32[2,64,2560]{2,1,0:T(8,128)} %copy-done.24) | copy-start | bytes 3932164
  485.9 30.6 %copy-start.27 = (bf16[2,320,1024]{2,1,0:T(8,128)(2,1)}, bf16[2,320,1024]{2,1,0:T(8,128)(2,1)S(1)}, u32[]{:S(2)}) copy-start(bf16[2,320,1024]{2,1,0:T(8,128)(2,1)S(1)} %get-tuple-element.134.refs_0_) | copy-start | bytes 3932164
  486.0 30.6 %copy-start.2 = (bf16[256,1024]{1,0:T(8,128)(2,1)}, bf16[256,1024]{1,0:T(8,128)(2,1)S(1)}, u32[]{:S(2)}) copy-start(bf16[256,1024]{1,0:T(8,128)(2,1)S(1)} %collective-permute-done.7.two_y) | copy-start | bytes 1572868
  486.0 30.6 %copy-start.4 = (bf16[256,1024]{1,0:T(8,128)(2,1)}, bf16[256,1024]{1,0:T(8,128)(2,1)S(1)}, u32[]{:S(2)}) copy-start(bf16[256,1024]{1,0:T(8,128)(2,1)S(1)} %collective-permute-done.8.one_y) | copy-start | bytes 1572868
  486.0 30.6 %copy-start.6 = (bf16[256,1024]{1,0:T(8,128)(2,1)}, bf16[256,1024]{1,0:T(8,128)(2,1)S(1)}, u32[]{:S(2)}) copy-start(bf16[256,1024]{1,0:T(8,128)(2,1)S(1)} %collective-permute-done.6.one_x) | copy-start | bytes 1572868
  486.0 31.9 %collective-permute-start.10 = (bf16[256,1024]{1,0:T(8,128)(2,1)S(1)}, bf16[256,1024]{1,0:T(8,128)(2,1)S(1)}, u32[]{:S(2)}, u32[]{:S(2)}) collective-permute-start(bf16[256,1024]{1,0:T(8,128)(2,1)S(1)} %collective-permute-done.6.one_x), channel_id=1, source_target_pairs={{0,16},{8,24},{16,0},{24,8},{1,17},{9,25},{17,1},{25,9},{2,18},{10... | collective-permute-start | bytes 1572872 | tf_op jit(solution)/shard_map/ppermute | solution.py:1800
  486.2 32.5 %collective-permute-start.11 = (bf16[256,1024]{1,0:T(8,128)(2,1)S(1)}, bf16[256,1024]{1,0:T(8,128)(2,1)S(1)}, u32[]{:S(2)}, u32[]{:S(2)}) collective-permute-start(bf16[256,1024]{1,0:T(8,128)(2,1)S(1)} %collective-permute-done.7.two_y), channel_id=1, source_target_pairs={{0,8},{8,0},{16,24},{24,16},{1,9},{9,1},{17,25},{25,17},{2,10},{10... | collective-permute-start | bytes 1572872 | tf_op jit(solution)/shard_map/ppermute | solution.py:1800
  487.9 39.5 %collective-permute-start.12 = (bf16[2,320,1024]{2,1,0:T(8,128)(2,1)S(1)}, bf16[2,320,1024]{2,1,0:T(8,128)(2,1)S(1)}, u32[]{:S(2)}, u32[]{:S(2)}) collective-permute-start(bf16[2,320,1024]{2,1,0:T(8,128)(2,1)S(1)} %get-tuple-element.127), channel_id=1, source_target_pairs={{0,8},{8,0},{16,24},{24,16},{1,9},{9,1},{17,25},{25,17},{2,10},{10... | collective-permute-start | bytes 3932168 | tf_op jit(solution)/shard_map/ppermute | solution.py:1800
  488.2 39.2 %collective-permute-start.13 = (bf16[2,320,1024]{2,1,0:T(8,128)(2,1)S(1)}, bf16[2,320,1024]{2,1,0:T(8,128)(2,1)S(1)}, u32[]{:S(2)}, u32[]{:S(2)}) collective-permute-start(bf16[2,320,1024]{2,1,0:T(8,128)(2,1)S(1)} %get-tuple-element.128), channel_id=1, source_target_pairs={{0,16},{8,24},{16,0},{24,8},{1,17},{9,25},{17,1},{25,9},{2,18},{10... | collective-permute-start | bytes 3932168 | tf_op jit(solution)/shard_map/ppermute | solution.py:1800
  588.5 42.3 %collective-permute-start.17 = (bf16[256,1024]{1,0:T(8,128)(2,1)}, bf16[256,1024]{1,0:T(8,128)(2,1)S(1)}, u32[]{:S(2)}, u32[]{:S(2)}) collective-permute-start(bf16[256,1024]{1,0:T(8,128)(2,1)} %get-tuple-element.195), channel_id=1, source_target_pairs={{0,8},{8,0},{16,24},{24,16},{1,9},{9,1},{17,25},{25,17},{2,10},{10... | collective-permute-start | bytes 1572872 | tf_op jit(solution)/shard_map/ppermute | solution.py:1800
  590.1 41.6 %collective-permute-start.15 = (bf16[256,1024]{1,0:T(8,128)(2,1)}, bf16[256,1024]{1,0:T(8,128)(2,1)}, u32[]{:S(2)}, u32[]{:S(2)}) collective-permute-start(bf16[256,1024]{1,0:T(8,128)(2,1)} %get-tuple-element.195), channel_id=1, source_target_pairs={{0,16},{8,24},{16,0},{24,8},{1,17},{9,25},{17,1},{25,9},{2,18},{10... | collective-permute-start | bytes 1572872 | tf_op jit(solution)/shard_map/ppermute | solution.py:1800
  590.5 41.2 %collective-permute-start.16 = (bf16[256,1024]{1,0:T(8,128)(2,1)}, bf16[256,1024]{1,0:T(8,128)(2,1)S(1)}, u32[]{:S(2)}, u32[]{:S(2)}) collective-permute-start(bf16[256,1024]{1,0:T(8,128)(2,1)} %get-tuple-element.196), channel_id=1, source_target_pairs={{0,16},{8,24},{16,0},{24,8},{1,17},{9,25},{17,1},{25,9},{2,18},{10... | collective-permute-start | bytes 1572872 | tf_op jit(solution)/shard_map/ppermute | solution.py:1800
  592.1 40.4 %collective-permute-start.14 = (bf16[256,1024]{1,0:T(8,128)(2,1)}, bf16[256,1024]{1,0:T(8,128)(2,1)}, u32[]{:S(2)}, u32[]{:S(2)}) collective-permute-start(bf16[256,1024]{1,0:T(8,128)(2,1)} %get-tuple-element.196), channel_id=1, source_target_pairs={{0,8},{8,0},{16,24},{24,16},{1,9},{9,1},{17,25},{25,17},{2,10},{10... | collective-permute-start | bytes 1572872 | tf_op jit(solution)/shard_map/ppermute | solution.py:1800
  604.9 6.7 copy-start.30
  614.2 8.7 %copy-start.3 = (bf16[256,1024]{1,0:T(8,128)(2,1)S(1)}, bf16[256,1024]{1,0:T(8,128)(2,1)}, u32[]{:S(2)}) copy-start(bf16[256,1024]{1,0:T(8,128)(2,1)} %copy-done.2) | copy-start | bytes 1572868
  614.3 8.7 %copy-start.5 = (bf16[256,1024]{1,0:T(8,128)(2,1)S(1)}, bf16[256,1024]{1,0:T(8,128)(2,1)}, u32[]{:S(2)}) copy-start(bf16[256,1024]{1,0:T(8,128)(2,1)} %copy-done.4) | copy-start | bytes 1572868
  614.3 8.7 %copy-start.7 = (bf16[256,1024]{1,0:T(8,128)(2,1)S(1)}, bf16[256,1024]{1,0:T(8,128)(2,1)}, u32[]{:S(2)}) copy-start(bf16[256,1024]{1,0:T(8,128)(2,1)} %copy-done.6) | copy-start | bytes 1572868
  614.3 8.7 %copy-start.13 = (bf16[256,1024]{1,0:T(8,128)(2,1)S(1)}, bf16[256,1024]{1,0:T(8,128)(2,1)}, u32[]{:S(2)}) copy-start(bf16[256,1024]{1,0:T(8,128)(2,1)} %copy-done.12) | copy-start | bytes 1572868
  614.3 8.7 %copy-start.15 = (bf16[256,1024]{1,0:T(8,128)(2,1)S(1)}, bf16[256,1024]{1,0:T(8,128)(2,1)}, u32[]{:S(2)}) copy-start(bf16[256,1024]{1,0:T(8,128)(2,1)} %copy-done.14) | copy-start | bytes 1572868
  632.6 103.4 %copy-start.48 = (bf16[320,1024]{1,0:T(8,128)(2,1)S(1)}, bf16[320,1024]{1,0:T(8,128)(2,1)}, u32[]{:S(2)}) copy-start(bf16[320,1024]{1,0:T(8,128)(2,1)} %get-tuple-element.139) | copy-start | bytes 1966084
  728.7 7.2 copy-start.43
  730.1 8.0 %slice-start = ((s8[5242880]{0:T(1024)(128)(4,1)}), s8[4194304]{0:T(1024)(128)(4,1)S(1)}, s32[]{:S(2)}) async-start(s8[5242880]{0:T(1024)(128)(4,1)} %bitcast.154), calls=%async_computation.4 | async-start | bytes 8388608
  (43 other events, 136.6 us)
Sparse Core Ops, SparseCore 0:
  313.8 89.0 reduce-scatter.2
  421.2 99.6 reduce-scatter.4

commit v6 on v5

--- a/solution.py
+++ b/solution.py
@@ -30,10 +30,12 @@
 
 
 def document_starts(lengths, count):
-    ends = jnp.cumsum(lengths)
     places = jnp.arange(count, dtype=jnp.int32)
-    passed = (places[:, None] >= ends[None, :]).astype(jnp.int32)
-    return jnp.sum(passed * lengths[None, :], axis=1)
+    starts, end = jnp.zeros_like(places), 0
+    for at in range(lengths.shape[0]):
+        end = end + lengths[at]
+        starts = starts + jnp.where(places >= end, lengths[at], 0)
+    return starts
 
 
 def allowed_pairs(start_row, key_block, query_block):
@@ -1527,13 +1529,15 @@
 
 
 def finish_kernel(
-    ways, qk_ref, v_ref, out_ref, norms_ref, taps_ref, *refs
+    ways, qk_ref, v_ref, out_ref, norms_ref, taps_ref, grad_raw_ref, inputs_ref, gain_ref,
+    qk_all_ref, v_all_ref, middle_ref, *refs
 ):
     carried, refs = list(zip(ways, refs[: len(ways)])), refs[len(ways) :]
-    joint_ref, norms_sum_ref, taps_sum_ref = refs[:3]
-    targets, refs = refs[3 : 3 + len(ways)], refs[3 + len(ways) :]
+    joint_ref, norms_sum_ref, taps_sum_ref, input_grad_ref = refs[:4]
+    targets, refs = refs[4 : 4 + len(ways)], refs[4 + len(ways) :]
     (
     acc, got, plane_in, line_in, gathered, norms_all, taps_all, norms_dp, taps_dp,
+    weights, result, middle, norms, sums, weight_sem,
     local, swap_send, swap_recv, plane_send_sem, plane_recv_sem, line_send_sem, line_recv_sem,
     gather_send, gather_recv, small_send, small_recv, carry_send, carry_recv,
     ) = refs
@@ -1592,18 +1596,98 @@
             out.append((wire(source(to), target.at[at], *sems), wire(source(to), target.at[frm], *sems)))
         return out
 
+    load_middle = pltpu.make_async_copy(middle_ref, middle, local.at[6])
+    load_middle.start()
     own_small = [
-        pltpu.make_async_copy(norms_ref, norms_all.at[me], local.at[3]),
+        pltpu.make_async_copy(norms, norms_all.at[me], local.at[3]),
         pltpu.make_async_copy(taps_ref.at[me], taps_all.at[me], local.at[4]),
     ]
-    over_mp = small("mp", me, mp, lambda to: norms_ref, norms_all, 0, None) + small(
+    over_mp = small("mp", me, mp, lambda to: norms, norms_all, 0, None) + small(
         "mp", me, mp, lambda to: taps_ref.at[to], taps_all, 1, None
     )
 
-    for copy in own_small:
-        copy.start()
-    for leaving, _ in over_mp:
-        leaving.start()
+    rows_here = inputs_ref.shape[1]
+    slots = weights.shape[0]
+
+    def load_weights(at, slot):
+        return [
+            pltpu.make_async_copy(
+                qk_all_ref.at[at], weights.at[slot, pl.ds(0, 4 * HD), :], weight_sem.at[slot, 0]
+            )
+        ] + [
+            pltpu.make_async_copy(
+                v_all_ref.at[at, pl.ds(head * HD, HD), :],
+                weights.at[slot, pl.ds((4 + 2 * head + copy) * HD, HD), :],
+                weight_sem.at[slot, 1 + 2 * head + copy],
+            )
+            for head in range(2)
+            for copy in range(2)
+        ]
+
+    def normed_grad():
+        if slots == 2:
+            for copy in load_weights(0, 0):
+                copy.start()
+        lane = lax.rem(lax.broadcasted_iota(jnp.int32, (rows_here, 4 * HD), 1), 2 * HD)
+
+        def one(at, carry):
+            slot = lax.rem(at, slots)
+            if slots == 1:
+                for copy in load_weights(at, slot):
+                    copy.start()
+            for copy in load_weights(at, slot):
+                copy.wait()
+            if slots == 2:
+
+                @pl.when(at + 1 < count)
+                def _():
+                    for copy in load_weights(at + 1, 1 - slot):
+                        copy.start()
+
+            pair = pl.ds(pl.multiple_of(at * 4 * HD, 4 * HD), 4 * HD)
+            side = grad_raw_ref[2, :, pair]
+            for s in range(2):
+                mine = lane < HD if s == 0 else lane >= HD
+                left = jnp.concatenate(
+                    [grad_raw_ref[s, :, pair], jnp.where(mine, side, jnp.zeros_like(side))], axis=1
+                )
+                for first in range(0, depth, CHUNK):
+                    columns = pl.ds(first, CHUNK)
+                    product = dot(left, weights[slot, :, columns])
+
+                    @pl.when(at == 0)
+                    def _(s=s, columns=columns, product=product):
+                        result[s, :, columns] = product
+
+                    @pl.when(at > 0)
+                    def _(s=s, columns=columns, product=product):
+                        result[s, :, columns] += product
+
+            return carry
+
+        lax.fori_loop(0, count, one, 0)
+
+    tall = 16
+    tiles = rows_here // tall
+
+    def norm_back(s, first, last):
+        def some(at, carry):
+            here = pl.ds(pl.multiple_of(at * tall, tall), tall)
+            values = inputs_ref[s, here, :].astype(F32)
+            centered = values - jnp.mean(values, axis=1, keepdims=True)
+            scale = lax.rsqrt(jnp.mean(centered * centered, axis=1, keepdims=True) + 1e-05)
+            hat = centered * scale
+            grad = result[s, here, :]
+            wide = grad * gain_ref[...]
+            back = wide - jnp.mean(wide, axis=1, keepdims=True)
+            back = scale * (back - hat * jnp.mean(wide * hat, axis=1, keepdims=True))
+            result[s, here, :] = middle[s, here, :] + back
+            product = grad * hat
+            sums[0] += product[:8] + product[8:]
+            sums[1] += grad[:8] + grad[8:]
+            return carry
+
+        lax.fori_loop(first, last, some, 0)
 
     def add(quarter, side, number):
         acc[:, quarter, :, lanes[side]] = (
@@ -1639,23 +1723,21 @@
     add_core(2, dp_y)
     sends[2].start()
     add_core(3, dp)
+    normed_grad()
+    load_middle.wait()
+    sums[...] = jnp.zeros(sums.shape, F32)
+    norm_back(0, 0, tiles)
+    saved_rows = [
+        pltpu.make_async_copy(result.at[s], input_grad_ref.at[s], local.at[7 + s]) for s in range(2)
+    ]
+    saved_rows[0].start()
     sends[1].wait_recv()
     add(dp_y, 0, 1)
     sends[4].start()
     sends[3].wait_recv()
     add(dp_x, 1, 3)
     sends[5].start()
-    for _, landing in over_mp:
-        landing.wait_recv()
-    for copy in own_small:
-        copy.wait()
-    norms_dp[dp] = jnp.sum(norms_all[...], axis=0)
-    taps_dp[dp] = jnp.sum(taps_all[...], axis=0)
-    over_dp = small("dp", dp, 4, lambda to: norms_dp.at[dp], norms_dp, 2, None) + small(
-        "dp", dp, 4, lambda to: taps_dp.at[dp], taps_dp, 3, None
-    )
-    for leaving, _ in over_dp:
-        leaving.start()
+    norm_back(1, 0, tiles // 2)
     sends[0].wait_recv()
     add(dp, 0, 0)
     sends[2].wait_recv()
@@ -1687,10 +1769,33 @@
             out.append((sends, receives, to, copy))
         return out
 
+    over_dp = []
     for step in range(1, count):
         legs = line(step)
         for sends_now, _, _, copy in legs:
             pl.when(sends_now)(copy.start)
+        if step == 1:
+            norm_back(1, tiles // 2, tiles)
+            saved_rows[1].start()
+            norms[...] = norms_ref[...]
+            norms[0:1, :] = jnp.sum(sums[0], axis=0, keepdims=True)
+            norms[1:2, :] = jnp.sum(sums[1], axis=0, keepdims=True)
+            for copy in own_small:
+                copy.start()
+            for leaving, _ in over_mp:
+                leaving.start()
+        if step == count - 1:
+            for _, landed in over_mp:
+                landed.wait_recv()
+            for copy in own_small:
+                copy.wait()
+            norms_dp[dp] = jnp.sum(norms_all[...], axis=0)
+            taps_dp[dp] = jnp.sum(taps_all[...], axis=0)
+            over_dp = small("dp", dp, 4, lambda to: norms_dp.at[dp], norms_dp, 2, None) + small(
+                "dp", dp, 4, lambda to: taps_dp.at[dp], taps_dp, 3, None
+            )
+            for leaving, _ in over_dp:
+                leaving.start()
         for way, (_, receives, to, copy) in enumerate(legs):
 
             @pl.when(receives)
@@ -1740,12 +1845,12 @@
         copy.wait_send()
     for copy, _ in over_mp + over_dp:
         copy.wait_send()
-    for copy in carries:
+    for copy in carries + saved_rows:
         copy.wait()
     save.wait()
 
 
-def finish(qk, v, out, norms, taps, carried):
+def finish(qk, v, out, norms, taps, grad_raw, inputs, gain, qk_all, v_all, middle, carried):
     mp = lax.axis_size("mp")
     count = mp // 2
     depth = qk.shape[-1]
@@ -1754,12 +1859,13 @@
     dma = pltpu.SemaphoreType.DMA
     return pl.pallas_call(
         partial(finish_kernel, tuple(way for way, _ in carried)),
-        in_specs=[anywhere] * 3 + [vmem] * 2 + [anywhere] * len(carried),
-        out_specs=[anywhere, vmem, vmem] + [anywhere] * len(carried),
+        in_specs=[anywhere] * 3 + [vmem] * 5 + [anywhere] * (3 + len(carried)),
+        out_specs=[anywhere, vmem, vmem, anywhere] + [anywhere] * len(carried),
         out_shape=[
             jax.ShapeDtypeStruct((4, HD, depth), LOW),
             jax.ShapeDtypeStruct(norms.shape, F32),
             jax.ShapeDtypeStruct(taps.shape[1:], F32),
+            jax.ShapeDtypeStruct(middle.shape, F32),
         ]
         + [jax.ShapeDtypeStruct(block.shape, block.dtype) for _, block in carried],
         scratch_shapes=[
@@ -1772,7 +1878,13 @@
             pltpu.VMEM(taps.shape, F32),
             pltpu.VMEM((4,) + norms.shape, F32),
             pltpu.VMEM((4,) + taps.shape[1:], F32),
-            dma((6,)),
+            pltpu.VMEM((2 if count <= 8 else 1, 8 * HD, depth), LOW),
+            pltpu.VMEM(middle.shape, F32),
+            pltpu.VMEM(middle.shape, F32),
+            pltpu.VMEM(norms.shape, F32),
+            pltpu.VMEM((2, 8, depth), F32),
+            dma((2, 5)),
+            dma((9,)),
             dma((3, 4)),
             dma((3, 4)),
             dma((6,)),
@@ -1787,12 +1899,12 @@
             dma((len(carried),)),
         ],
         compiler_params=pltpu.CompilerParams(
-            collective_id=8, has_side_effects=True, vmem_limit_bytes=VMEM_LIMIT
+            collective_id=8, has_side_effects=True, vmem_limit_bytes=VMEM_LIMIT + 2**19
         ),
         cost_estimate=pl.CostEstimate(flops=2**36, bytes_accessed=2**26, transcendentals=0),
         name="finish",
     )(
-        qk, v, out, norms, taps, *(block for _, block in carried),
+        qk, v, out, norms, taps, grad_raw, inputs, gain.reshape(1, depth), qk_all, v_all, middle, *(block for _, block in carried),
     )
 
 
@@ -2022,17 +2134,16 @@
     def split_parts(part):
         return part.reshape(mp // 2, 2, 4, part.shape[1] // 8, width)
 
-    grad_normed = dot(grad_raw[:2], qk_all) + dot(apart(grad_raw[2:]), v_all)
-    grad_input, gain_one, shift_one = norm_back(rows, norm1_gain, grad_normed)
-    input_grads = grad_middle + grad_input
-    norms = jnp.pad(jnp.stack([gain_one, shift_one, gain_two, shift_two]), ((0, 4), (0, 0)))
+    norms = jnp.pad(jnp.stack([gain_two, shift_two]), ((2, 4), (0, 0)))
     qk_sums = (tap_sums[0] + tap_sums[1]).reshape(8, mp, 2 * HD)
     v_sums = tap_sums[2].reshape(8, mp, 2, HD).sum(axis=2)
     taps_part = jnp.concatenate([qk_sums, v_sums, jnp.zeros_like(v_sums)], axis=2)
     taps_part = taps_part.transpose(1, 0, 2)
     norms, up_legs = lax.optimization_barrier((norms, up_legs))
-    joint_grad, small_sum, taps_sum, feed_a1, feed_b1, one_xy, two_xy = finish(
+    joint_grad, small_sum, taps_sum, input_grads, feed_a1, feed_b1, one_xy, two_xy = finish(
         split_parts(qk_part), split_parts(v_part), split_parts(out_part), norms, taps_part,
+        grad_raw, inputs, norm1_gain, qk_all.reshape(chips, 4 * HD, width), v_all.reshape(chips, 2 * HD, width),
+        grad_middle,
         ((1, feed_a1), (0, feed_b1), (1, up_legs[0]), (0, up_legs[1])),
     )
     results = jnp.stack(

time: 766 us -> 763 us (level)
  matrix products: 20.5 us -> 6.04 us
  Pallas kernels: 595 us -> 605 us
    dot_general x3 -> x1, matrix products: 19 us -> 4.49 us  [dot(): return jnp.dot(left, right, preferred_element_type=F32)]
    reduce_sum x5 -> x0, other arithmetic: 7.98 us -> none  [the longest x2 6.04 us: layer_norm(): centered = rows - row_mean]
    unnamed x144 -> x134, local copies, waits for them, and re-layouts: 15.4 us -> 16.2 us
  transfers between devices with their start and end apart: 20 -> 20, of which waited for: 2 -> 3; matrix products, arithmetic and copies ran while one was open for 10% -> 7% of each run, Pallas kernels for 35% -> 35%
where the time goes in v6:
time: 763 us; the launch traced here: 754 us
  Pallas kernels  605 us (79%)
  local copies, waits for them, and re-layouts  43.6 us (6%)
  other arithmetic  43 us (6%)
  starting transfers between devices  21.1 us (3%)
  between operations  19.3 us (3%)
  waiting for transfers between devices  15.5 us (2%)
    pallas_call x1, Pallas kernels, feed_in(): pl.pallas_call(partial(feed_in_kernel, tuple(up_late)), in_specs=[anywher...  122 us
    pallas_call x1, Pallas kernels, feed_out(): pl.pallas_call(feed_out_kernel, in_specs=[anywhere] * 11, out_specs=[anyw...  107 us
    pallas_call x1, Pallas kernels, front(): pl.pallas_call(front_kernel, in_specs=[anywhere, vmem, vmem] + [anywhere]...  106 us
    pallas_call x1, Pallas kernels, finish(): pl.pallas_call(partial(finish_kernel, tuple((way for way, _ in carried)))...  102 us
    pallas_call x1, Pallas kernels, project_back(): pl.pallas_call(partial(project_back_kernel, tuple((way for way, _ in carr...  54 us
    pallas_call x1, Pallas kernels, feed_heads(): pl.pallas_call(feed_heads_kernel, in_specs=[pl.BlockSpec(memory_space=plt...  34.1 us
    pallas_call x1, Pallas kernels, attend_back(): pl.pallas_call(attend_back_kernel, grid_spec=pltpu.PrefetchScalarGridSpec...  28.3 us
    pallas_call x1, Pallas kernels, attended_back(): pl.pallas_call(attended_kernel, in_specs=[pl.BlockSpec(memory_space=pltpu...  19.4 us
  transfers between devices with their start and end apart: 20, of which 3 were waited for; matrix products, arithmetic and copies ran while one was open for 7% of the time, Pallas kernels for 35%

profile of v6, /device:TPU:0, one launch (start us, length us, event | category | flops | bytes accessed | tf_op | source)
XLA Modules:
  0.0 753.8 jit_solution(440804105949294380)
XLA Ops:
  13.9 3.9 fusion.21
  19.3 1.4 copy.55
  23.2 1.4 pad_maximum_fusion.1.masks_ref
  24.6 106.3 %front.1 = (bf16[4,2,4,32,2048]{4,3,2,1,0:T(8,128)(2,1)}, bf16[4,2,4,16,2048]{4,3,2,1,0:T(8,128)(2,1)}, bf16[4,2,4,16,2048]{4,3,2,1,0:T(8,128)(2,1)}, f32[3,8,10...) custom-call(bf16[2,320,2048]{2,1,0:T(8,128)(2,1)} %inputs_ref.3, ...), custom_call_target="tpu_custom_call" | custom-call | flops 68719476736 | bytes 67108864 | tf_op jit(solution)/shard_map/front/pallas_call | solution.py:681
  130.9 2.5 collective-permute-start.4
  133.5 2.9 constant_dynamic-slice_fusion.1
  136.4 1.6 collective-permute-start.1
  138.0 1.4 collective-permute-start
  139.5 1.8 fusion.25
  141.2 1.9 collective-permute-start.3
  143.3 2.3 constant_dynamic-slice_fusion.down_ref
  145.6 19.4 %attend.1 = (bf16[1,2560,128]{2,1,0:T(8,128)(2,1)S(1)}, f32[2,64,2560]{2,1,0:T(8,128)S(1)}, f32[2,1,2560]{2,1,0:T(1,128)S(1)}) custom-call(s32[2,5]{1,0:T(2,128)S(1)} %and_select_fusion.first_ref, s32[2,1,2560]{2,1,0:T(1,128)S(1)} %broadcast_in_dim.62.start_ref, bf16[3,2560,128]{2,1,0:T(8,128)(2,1)S(1)} %bitcast.137, bf16[3,2560,128]{2,1,0:T(8,128)(2,1)S(1)} %bitcast.138), custom_call_target="tpu_custom_call" | custom-call | flops 17179869184 | bytes 5242880 | tf_op jit(solution)/shard_map/attend/pallas_call | solution.py:110
  166.9 3.9 collective-permute-done.refs_0_
  170.8 19.4 %attended_back.1 = bf16[1,320,1024]{2,1,0:T(8,128)(2,1)S(1)} custom-call(bf16[1,2560,128]{2,1,0:T(8,128)(2,1)S(1)} %get-tuple-element.98.x_ref), custom_call_target="tpu_custom_call" | custom-call | flops 17179869184 | bytes 16777216 | tf_op jit(solution)/shard_map/attended_back/pallas_call | solution.py:908
  190.7 4.5 fusion.35
  197.5 2.4 add_convert_fusion.second_ref
  200.0 121.7 %feed_in.1 = (bf16[2,4,320,2048]{3,2,1,0:T(8,128)(2,1)}, f32[2,4,320,2048]{3,2,1,0:T(8,128)}, bf16[2,4,320,2048]{3,2,1,0:T(8,128)(2,1)}, bf16[2048,2048]{1,0:T(8...) custom-call(bf16[2,320,2048]{2,1,0:T(8,128)(2,1)} %add_convert_fusion.second_ref, ...), custom_call_target="tpu_custom_call" | custom-call | flops 64424509440 | bytes 62914560 | tf_op jit(solution)/shard_map/feed_in/pallas_call | solution.py:1181
  322.2 106.7 %feed_out.1 = (bf16[2,4,320,2048]{3,2,1,0:T(8,128)(2,1)}, bf16[2048,2048]{1,0:T(8,128)(2,1)}, f32[2,320,2048]{2,1,0:T(8,128)}) custom-call(bf16[2,320,2048]{2,1,0:T(8,128)(2,1)} %cot_0.1, bf16[2,320,1024]{2,1,0:T(8,128)(2,1)} %get-tuple-element.101.cot_1, bf16[2,320,1024]{2,1,0:T(8,128)(2,1)} %collective-permute-done.3.cot_2, ...), custom_call_target="tpu_custom_call" | custom-call | flops 85899345920 | bytes 62914560 | tf_op jit(solution)/shard_map/feed_out/pallas_call | solution.py:1385
  431.2 2.4 fusion.29
  433.6 2.0 collective-permute-start.7
  435.6 2.0 collective-permute-start.6
  437.6 4.9 multiply_reduce_fusion.1
  442.6 4.6 multiply_reduce_fusion
  447.5 3.9 fusion.24
  451.4 1.5 copy-done.31
  452.9 1.6 convolution_convert_fusion
  455.6 2.1 copy.48
  459.2 34.1 %feed_heads.1 = (bf16[1,8,320,128]{3,2,1,0:T(8,128)(2,1)S(1)}, bf16[2,320,1024]{2,1,0:T(8,128)(2,1)S(1)}, bf16[2,320,1024]{2,1,0:T(8,128)(2,1)S(1)}, bf16[2,320,...) custom-call(bf16[1,320,1024]{2,1,0:T(8,128)(2,1)S(1)} %copy.49.x_ref, ...), custom_call_target="tpu_custom_call" | custom-call | flops 34359738368 | bytes 16777216 | tf_op jit(solution)/shard_map/feed_heads/pallas_call | solution.py:1504
  494.4 1.9 collective-permute-start.11
  496.4 1.8 collective-permute-start.13
  498.2 28.3 %attend_back.1.x_ref = bf16[3,2576,128]{2,1,0:T(8,128)(2,1)S(1)} custom-call(s32[2,5]{1,0:T(2,128)S(1)} %copy-done.17, s32[2,1,2560]{2,1,0:T(1,128)S(1)} %copy-done.15, bf16[3,2560,128]{2,1,0:T(8,128)(2,1)S(1)} %bitcast.139, bf16[3,2560,128]{2,1,0:T(8,128)(2,1)S(1)} %bitcast.140, bf16[1,2560,128]{2,1,0:T(8,128)(2,1)S(1)} %bitcast.141, ...), custom_call_target="tpu_custom_call" | custom-call | flops 34359738368 | bytes 5242880 | tf_op jit(solution)/shard_map/attend_back/pallas_call | solution.py:205
  529.5 6.3 collective-permute-done.12
  535.9 2.7 fusion.11.refs_2_
  538.5 2.1 fusion.10.refs_3_
  540.7 54.0 %project_back.1 = (bf16[3,320,1024]{2,1,0:T(8,128)(2,1)}, f32[3,8,1024]{2,1,0:T(8,128)}, bf16[4,256,2048]{2,1,0:T(8,128)(2,1)}, bf16[4,128,2048]{2,1,0:T(8,128)(...) custom-call(bf16[3,2576,128]{2,1,0:T(8,128)(2,1)} %copy-done.22, ...), custom_call_target="tpu_custom_call" | custom-call | flops 34359738368 | bytes 16777216 | tf_op jit(solution)/shard_map/project_back/pallas_call | solution.py:846
  594.7 2.4 fusion.28
  597.1 1.6 collective-permute-start.17
  599.1 1.6 collective-permute-start.16
  602.2 2.3 fusion.4.refs_1_
  607.7 5.5 placed.3
  613.8 1.9 fusion.13
  615.7 5.2 collective-permute-done.16.one_y
  620.9 101.9 %finish.1 = (bf16[4,64,2048]{2,1,0:T(8,128)(2,1)}, f32[8,2048]{1,0:T(8,128)}, f32[8,256]{1,0:T(8,128)}, f32[2,320,2048]{2,1,0:T(8,128)}, bf16[320,1024]{1,0:T(8,...) custom-call(bf16[4,2,4,32,2048]{4,3,2,1,0:T(8,128)(2,1)} %bitcast.177, ...), custom_call_target="tpu_custom_call" | custom-call | flops 68719476736 | bytes 67108864 | tf_op jit(solution)/shard_map/finish/pallas_call | solution.py:1860
  725.3 2.4 fusion.7
  730.0 2.4 fusion.9
  733.8 1.7 pad_maximum_fusion
  736.2 8.0 %placed.2 = f32[2048,1024]{1,0:T(8,128)} custom-call(s32[1]{0:T(128)} %bitcast.74.me_ref, bf16[256,2048]{1,0:T(8,128)(2,1)S(1)} %copy-done, bf16[256,1024]{1,0:T(8,128)(2,1)} %collective-permute-done.14.refs_2_.one_x, bf16[256,1024]{1,0:T(8,128)(2,1)} %collective-permute-done.17.two_x, bf16[256,1024]{1,0:T(8,128)(2,1)} %collective-permute-done.16.one_y, ...), custom_call_target="tpu_custom_call" | custom-call | bytes 16777216 | tf_op jit(solution)/shard_map/placed/pallas_call | solution.py:1947
  744.2 2.4 copy.61
  (205 shorter events, 33.7 us)
Async XLA Ops:
  7.2 13.6 %copy-start.56 = (f32[3,64]{1,0:T(4,128)S(1)}, f32[3,64]{1,0:T(4,128)}, u32[]{:S(2)}) copy-start(f32[3,64]{1,0:T(4,128)} %param.28) | copy-start | bytes 2308
  7.2 13.6 %copy-start.54 = (f32[3,64]{1,0:T(4,128)S(1)}, f32[3,64]{1,0:T(4,128)}, u32[]{:S(2)}) copy-start(f32[3,64]{1,0:T(4,128)} %param.27) | copy-start | bytes 2308
  7.2 13.6 %copy-start.55 = (f32[3,64]{1,0:T(4,128)S(1)}, f32[3,64]{1,0:T(4,128)}, u32[]{:S(2)}) copy-start(f32[3,64]{1,0:T(4,128)} %param.26) | copy-start | bytes 2308
  7.2 14.2 %copy-start.41 = (bf16[2048,64]{0,1:T(8,128)(2,1)S(1)}, bf16[2048,64]{0,1:T(8,128)(2,1)}, u32[]{:S(2)}) copy-start(bf16[2048,64]{0,1:T(8,128)(2,1)} %param.24) | copy-start | bytes 786436
  7.2 14.2 %copy-start.42 = (bf16[2048,64]{0,1:T(8,128)(2,1)S(1)}, bf16[2048,64]{0,1:T(8,128)(2,1)}, u32[]{:S(2)}) copy-start(bf16[2048,64]{0,1:T(8,128)(2,1)} %param.23) | copy-start | bytes 786436
  7.2 424.0 %reduce-scatter.3.cloned.1.call-start = ((), (), s32[]{:S(2)}) async-start(), calls=%async_computation.2 | async-start | bytes 9437184 | tf_op jit(solution)/shard_map/reduce_scatter | solution.py:2089
  130.9 69.1 %collective-permute-start.4 = (bf16[2,320,1024]{2,1,0:T(8,128)(2,1)}, bf16[2,320,1024]{2,1,0:T(8,128)(2,1)}, u32[]{:S(2)}, u32[]{:S(2)}) collective-permute-start(bf16[2,320,1024]{2,1,0:T(8,128)(2,1)} %get-tuple-element.101.cot_1), channel_id=1, source_target_pairs={{0,16},{8,24},{16,0},{24,8},{1,17},{9,25},{17,1},{25,9},{2,18},{10... | collective-permute-start | bytes 3932168 | tf_op jit(solution)/shard_map/ppermute | solution.py:1912
  133.4 66.5 %collective-permute-start.5 = (bf16[2,320,1024]{2,1,0:T(8,128)(2,1)}, bf16[2,320,1024]{2,1,0:T(8,128)(2,1)}, u32[]{:S(2)}, u32[]{:S(2)}) collective-permute-start(bf16[2,320,1024]{2,1,0:T(8,128)(2,1)} %get-tuple-element.102.cot_4), channel_id=1, source_target_pairs={{0,8},{8,0},{16,24},{24,16},{1,9},{9,1},{17,25},{25,17},{2,10},{10... | collective-permute-start | bytes 3932168 | tf_op jit(solution)/shard_map/ppermute | solution.py:1912
  136.4 29.7 %collective-permute-start.1 = (bf16[256,2048]{1,0:T(8,128)(2,1)}, bf16[256,2048]{1,0:T(8,128)(2,1)}, u32[]{:S(2)}, u32[]{:S(2)}) collective-permute-start(bf16[256,2048]{1,0:T(8,128)(2,1)} %get-tuple-element.178), channel_id=1, source_target_pairs={{4,6},{5,7},{12,14},{13,15},{20,22},{21,23},{28,30},{29,31}} | collective-permute-start | bytes 3145736 | tf_op jit(solution)/shard_map/ppermute | solution.py:1977
  138.0 7.6 %copy-start.18 = (bf16[3,8,320,128]{3,2,1,0:T(8,128)(2,1)S(1)}, bf16[3,8,320,128]{3,2,1,0:T(8,128)(2,1)}, u32[]{:S(2)}) copy-start(bf16[3,8,320,128]{3,2,1,0:T(8,128)(2,1)} %get-tuple-element.93) | copy-start | bytes 5898244
  138.0 32.7 %collective-permute-start = (bf16[256,2048]{1,0:T(8,128)(2,1)S(1)}, bf16[256,2048]{1,0:T(8,128)(2,1)}, u32[]{:S(2)}, u32[]{:S(2)}) collective-permute-start(bf16[256,2048]{1,0:T(8,128)(2,1)S(1)} %get-tuple-element.179), channel_id=1, source_target_pairs={{2,0},{3,1},{10,8},{11,9},{18,16},{19,17},{26,24},{27,25}} | collective-permute-start | bytes 3145736 | tf_op jit(solution)/shard_map/ppermute | solution.py:1977
  141.2 58.8 %collective-permute-start.3 = (bf16[2,320,1024]{2,1,0:T(8,128)(2,1)}, bf16[2,320,1024]{2,1,0:T(8,128)(2,1)}, u32[]{:S(2)}, u32[]{:S(2)}) collective-permute-start(bf16[2,320,1024]{2,1,0:T(8,128)(2,1)} %get-tuple-element.186), channel_id=1, source_target_pairs={{0,8},{8,0},{16,24},{24,16},{1,9},{9,1},{17,25},{25,17},{2,10},{10... | collective-permute-start | bytes 3932168 | tf_op jit(solution)/shard_map/ppermute | solution.py:1912
  143.2 21.7 %copy-start.14 = (s32[2,1,2560]{2,1,0:T(1,128)}, s32[2,1,2560]{2,1,0:T(1,128)S(1)}, u32[]{:S(2)}) copy-start(s32[2,1,2560]{2,1,0:T(1,128)S(1)} %broadcast_in_dim.62.start_ref) | copy-start | bytes 61444
  143.3 21.7 %copy-start.16 = (s32[2,5]{1,0:T(2,128)}, s32[2,5]{1,0:T(2,128)S(1)}, u32[]{:S(2)}) copy-start(s32[2,5]{1,0:T(2,128)S(1)} %and_select_fusion.first_ref) | copy-start | bytes 124
  166.0 33.9 %collective-permute-start.2 = (bf16[2,320,1024]{2,1,0:T(8,128)(2,1)}, bf16[2,320,1024]{2,1,0:T(8,128)(2,1)}, u32[]{:S(2)}, u32[]{:S(2)}) collective-permute-start(bf16[2,320,1024]{2,1,0:T(8,128)(2,1)} %get-tuple-element.187), channel_id=1, source_target_pairs={{0,16},{8,24},{16,0},{24,8},{1,17},{9,25},{17,1},{25,9},{2,18},{10... | collective-permute-start | bytes 3932168 | tf_op jit(solution)/shard_map/ppermute | solution.py:1912
  321.7 273.0 %reduce-scatter.5.cloned.1.call-start = ((), (), s32[]{:S(2)}) async-start(), calls=%async_computation.3 | async-start | bytes 9437184 | tf_op jit(solution)/shard_map/reduce_scatter | solution.py:2093
  428.9 8.7 %copy-start.44 = (f32[2048]{0:T(1024)S(1)}, f32[2048]{0:T(1024)}, u32[]{:S(2)}) copy-start(f32[2048]{0:T(1024)} %param.30) | copy-start | bytes 24580
  429.0 8.7 %copy-start.46 = (f32[2,320]{1,0:T(2,128)S(1)}, f32[2,320]{1,0:T(2,128)}, u32[]{:S(2)}) copy-start(f32[2,320]{1,0:T(2,128)} %copy-done.45) | copy-start | bytes 7684
  431.2 11.4 %slice-start.4 = ((s8[5242880]{0:T(1024)(128)(4,1)}), s8[4194304]{0:T(1024)(128)(4,1)S(1)}, s32[]{:S(2)}) async-start(s8[5242880]{0:T(1024)(128)(4,1)} %bitcast.146), calls=%async_computation.8 | async-start | bytes 8388608
  433.6 60.5 %collective-permute-start.9 = (bf16[256,1024]{1,0:T(8,128)(2,1)}, bf16[256,1024]{1,0:T(8,128)(2,1)S(1)}, u32[]{:S(2)}, u32[]{:S(2)}) collective-permute-start(bf16[256,1024]{1,0:T(8,128)(2,1)} %get-tuple-element.194), channel_id=1, source_target_pairs={{0,8},{8,0},{16,24},{24,16},{1,9},{9,1},{17,25},{25,17},{2,10},{10... | collective-permute-start | bytes 1572872 | tf_op jit(solution)/shard_map/ppermute | solution.py:1912
  433.6 60.5 %collective-permute-start.7 = (bf16[256,1024]{1,0:T(8,128)(2,1)}, bf16[256,1024]{1,0:T(8,128)(2,1)S(1)}, u32[]{:S(2)}, u32[]{:S(2)}) collective-permute-start(bf16[256,1024]{1,0:T(8,128)(2,1)} %get-tuple-element.194), channel_id=1, source_target_pairs={{0,16},{8,24},{16,0},{24,8},{1,17},{9,25},{17,1},{25,9},{2,18},{10... | collective-permute-start | bytes 1572872 | tf_op jit(solution)/shard_map/ppermute | solution.py:1912
  435.5 7.0 slice-start.5
  435.5 7.0 copy-start.48
  435.6 58.5 %collective-permute-start.8 = (bf16[256,1024]{1,0:T(8,128)(2,1)}, bf16[256,1024]{1,0:T(8,128)(2,1)S(1)}, u32[]{:S(2)}, u32[]{:S(2)}) collective-permute-start(bf16[256,1024]{1,0:T(8,128)(2,1)} %get-tuple-element.195), channel_id=1, source_target_pairs={{0,16},{8,24},{16,0},{24,8},{1,17},{9,25},{17,1},{25,9},{2,18},{10... | collective-permute-start | bytes 1572872 | tf_op jit(solution)/shard_map/ppermute | solution.py:1912
  435.6 58.4 %collective-permute-start.6 = (bf16[256,1024]{1,0:T(8,128)(2,1)}, bf16[256,1024]{1,0:T(8,128)(2,1)S(1)}, u32[]{:S(2)}, u32[]{:S(2)}) collective-permute-start(bf16[256,1024]{1,0:T(8,128)(2,1)} %get-tuple-element.195), channel_id=1, source_target_pairs={{0,8},{8,0},{16,24},{24,16},{1,9},{9,1},{17,25},{25,17},{2,10},{10... | collective-permute-start | bytes 1572872 | tf_op jit(solution)/shard_map/ppermute | solution.py:1912
  459.2 39.0 %copy-start.15 = (s32[2,1,2560]{2,1,0:T(1,128)S(1)}, s32[2,1,2560]{2,1,0:T(1,128)}, u32[]{:S(2)}) copy-start(s32[2,1,2560]{2,1,0:T(1,128)} %copy-done.14) | copy-start | bytes 61444
  459.2 39.0 %copy-start.17 = (s32[2,5]{1,0:T(2,128)S(1)}, s32[2,5]{1,0:T(2,128)}, u32[]{:S(2)}) copy-start(s32[2,5]{1,0:T(2,128)} %copy-done.16) | copy-start | bytes 124
  459.2 39.0 %copy-start.19 = (bf16[3,8,320,128]{3,2,1,0:T(8,128)(2,1)S(1)}, bf16[3,8,320,128]{3,2,1,0:T(8,128)(2,1)}, u32[]{:S(2)}) copy-start(bf16[3,8,320,128]{3,2,1,0:T(8,128)(2,1)} %get-tuple-element.93) | copy-start | bytes 5898244
  459.2 39.0 %copy-start.21 = (f32[2,64,2560]{2,1,0:T(8,128)S(1)}, f32[2,64,2560]{2,1,0:T(8,128)}, u32[]{:S(2)}) copy-start(f32[2,64,2560]{2,1,0:T(8,128)} %copy-done.20) | copy-start | bytes 3932164
  493.3 33.3 %copy-start.23 = (bf16[2,320,1024]{2,1,0:T(8,128)(2,1)}, bf16[2,320,1024]{2,1,0:T(8,128)(2,1)S(1)}, u32[]{:S(2)}) copy-start(bf16[2,320,1024]{2,1,0:T(8,128)(2,1)S(1)} %get-tuple-element.135.refs_0_) | copy-start | bytes 3932164
  494.0 32.5 %copy-start.2 = (bf16[256,1024]{1,0:T(8,128)(2,1)}, bf16[256,1024]{1,0:T(8,128)(2,1)S(1)}, u32[]{:S(2)}) copy-start(bf16[256,1024]{1,0:T(8,128)(2,1)S(1)} %collective-permute-done.7.two_y) | copy-start | bytes 1572868
  494.0 32.5 %copy-start.4 = (bf16[256,1024]{1,0:T(8,128)(2,1)}, bf16[256,1024]{1,0:T(8,128)(2,1)S(1)}, u32[]{:S(2)}) copy-start(bf16[256,1024]{1,0:T(8,128)(2,1)S(1)} %collective-permute-done.8.one_y) | copy-start | bytes 1572868
  494.1 32.5 %copy-start.6 = (bf16[256,1024]{1,0:T(8,128)(2,1)}, bf16[256,1024]{1,0:T(8,128)(2,1)S(1)}, u32[]{:S(2)}) copy-start(bf16[256,1024]{1,0:T(8,128)(2,1)S(1)} %collective-permute-done.6.one_x) | copy-start | bytes 1572868
  494.1 33.8 %collective-permute-start.10 = (bf16[256,1024]{1,0:T(8,128)(2,1)S(1)}, bf16[256,1024]{1,0:T(8,128)(2,1)S(1)}, u32[]{:S(2)}, u32[]{:S(2)}) collective-permute-start(bf16[256,1024]{1,0:T(8,128)(2,1)S(1)} %collective-permute-done.6.one_x), channel_id=1, source_target_pairs={{0,16},{8,24},{16,0},{24,8},{1,17},{9,25},{17,1},{25,9},{2,18},{10... | collective-permute-start | bytes 1572872 | tf_op jit(solution)/shard_map/ppermute | solution.py:1912
  494.4 34.3 %collective-permute-start.11 = (bf16[256,1024]{1,0:T(8,128)(2,1)S(1)}, bf16[256,1024]{1,0:T(8,128)(2,1)S(1)}, u32[]{:S(2)}, u32[]{:S(2)}) collective-permute-start(bf16[256,1024]{1,0:T(8,128)(2,1)S(1)} %collective-permute-done.7.two_y), channel_id=1, source_target_pairs={{0,8},{8,0},{16,24},{24,16},{1,9},{9,1},{17,25},{25,17},{2,10},{10... | collective-permute-start | bytes 1572872 | tf_op jit(solution)/shard_map/ppermute | solution.py:1912
  496.2 39.6 %collective-permute-start.12 = (bf16[2,320,1024]{2,1,0:T(8,128)(2,1)S(1)}, bf16[2,320,1024]{2,1,0:T(8,128)(2,1)S(1)}, u32[]{:S(2)}, u32[]{:S(2)}) collective-permute-start(bf16[2,320,1024]{2,1,0:T(8,128)(2,1)S(1)} %get-tuple-element.128), channel_id=1, source_target_pairs={{0,8},{8,0},{16,24},{24,16},{1,9},{9,1},{17,25},{25,17},{2,10},{10... | collective-permute-start | bytes 3932168 | tf_op jit(solution)/shard_map/ppermute | solution.py:1912
  496.4 39.5 %collective-permute-start.13 = (bf16[2,320,1024]{2,1,0:T(8,128)(2,1)S(1)}, bf16[2,320,1024]{2,1,0:T(8,128)(2,1)S(1)}, u32[]{:S(2)}, u32[]{:S(2)}) collective-permute-start(bf16[2,320,1024]{2,1,0:T(8,128)(2,1)S(1)} %get-tuple-element.129), channel_id=1, source_target_pairs={{0,16},{8,24},{16,0},{24,8},{1,17},{9,25},{17,1},{25,9},{2,18},{10... | collective-permute-start | bytes 3932168 | tf_op jit(solution)/shard_map/ppermute | solution.py:1912
  594.7 9.8 %copy-start.1 = (bf16[256,2048]{1,0:T(8,128)(2,1)S(1)}, bf16[256,2048]{1,0:T(8,128)(2,1)}, u32[]{:S(2)}) copy-start(bf16[256,2048]{1,0:T(8,128)(2,1)} %reduce-scatter.3.cloned.1.call-done.own_ref) | copy-start | bytes 3145732
  594.7 9.8 %copy-start.3 = (bf16[256,1024]{1,0:T(8,128)(2,1)S(1)}, bf16[256,1024]{1,0:T(8,128)(2,1)}, u32[]{:S(2)}) copy-start(bf16[256,1024]{1,0:T(8,128)(2,1)} %copy-done.2) | copy-start | bytes 1572868
  594.7 9.8 %copy-start.5 = (bf16[256,1024]{1,0:T(8,128)(2,1)S(1)}, bf16[256,1024]{1,0:T(8,128)(2,1)}, u32[]{:S(2)}) copy-start(bf16[256,1024]{1,0:T(8,128)(2,1)} %copy-done.4) | copy-start | bytes 1572868
  597.1 18.6 %collective-permute-start.17 = (bf16[256,1024]{1,0:T(8,128)(2,1)}, bf16[256,1024]{1,0:T(8,128)(2,1)}, u32[]{:S(2)}, u32[]{:S(2)}) collective-permute-start(bf16[256,1024]{1,0:T(8,128)(2,1)} %get-tuple-element.192), channel_id=1, source_target_pairs={{0,8},{8,0},{16,24},{24,16},{1,9},{9,1},{17,25},{25,17},{2,10},{10... | collective-permute-start | bytes 1572872 | tf_op jit(solution)/shard_map/ppermute | solution.py:1912
  598.7 17.0 %collective-permute-start.15 = (bf16[256,1024]{1,0:T(8,128)(2,1)}, bf16[256,1024]{1,0:T(8,128)(2,1)}, u32[]{:S(2)}, u32[]{:S(2)}) collective-permute-start(bf16[256,1024]{1,0:T(8,128)(2,1)} %get-tuple-element.192), channel_id=1, source_target_pairs={{0,16},{8,24},{16,0},{24,8},{1,17},{9,25},{17,1},{25,9},{2,18},{10... | collective-permute-start | bytes 1572872 | tf_op jit(solution)/shard_map/ppermute | solution.py:1912
  599.1 21.8 %collective-permute-start.16 = (bf16[256,1024]{1,0:T(8,128)(2,1)}, bf16[256,1024]{1,0:T(8,128)(2,1)}, u32[]{:S(2)}, u32[]{:S(2)}) collective-permute-start(bf16[256,1024]{1,0:T(8,128)(2,1)} %get-tuple-element.193), channel_id=1, source_target_pairs={{0,16},{8,24},{16,0},{24,8},{1,17},{9,25},{17,1},{25,9},{2,18},{10... | collective-permute-start | bytes 1572872 | tf_op jit(solution)/shard_map/ppermute | solution.py:1912
  600.7 20.2 %collective-permute-start.14 = (bf16[256,1024]{1,0:T(8,128)(2,1)}, bf16[256,1024]{1,0:T(8,128)(2,1)}, u32[]{:S(2)}, u32[]{:S(2)}) collective-permute-start(bf16[256,1024]{1,0:T(8,128)(2,1)} %get-tuple-element.193), channel_id=1, source_target_pairs={{0,8},{8,0},{16,24},{24,16},{1,9},{9,1},{17,25},{25,17},{2,10},{10... | collective-permute-start | bytes 1572872 | tf_op jit(solution)/shard_map/ppermute | solution.py:1912
  722.8 7.2 copy-start.36
  724.2 8.2 %slice-start.2 = ((s8[5242880]{0:T(1024)(128)(4,1)}), s8[4194304]{0:T(1024)(128)(4,1)S(1)}, s32[]{:S(2)}) async-start(s8[5242880]{0:T(1024)(128)(4,1)} %bitcast.144), calls=%async_computation.6 | async-start | bytes 8388608
  735.5 8.7 %slice-start.6 = ((s8[5242880]{0:T(1024)(128)(4,1)}), s8[4194304]{0:T(1024)(128)(4,1)S(1)}, s32[]{:S(2)}) async-start(s8[5242880]{0:T(1024)(128)(4,1)} %bitcast.150), calls=%async_computation.10 | async-start | bytes 8388608
  736.2 8.0 %slice-start.7 = ((s8[5242880]{0:T(1024)(128)(4,1)}), s8[1048576]{0:T(1024)(128)(4,1)S(1)}, s32[]{:S(2)}) async-start(s8[5242880]{0:T(1024)(128)(4,1)} %bitcast.150), calls=%async_computation.11 | async-start | bytes 2097152
  (37 other events, 117.2 us)
Sparse Core Ops, SparseCore 0:
  321.8 89.0 reduce-scatter.2
  429.1 99.6 reduce-scatter.4

commit v7 on v6

--- a/solution.py
+++ b/solution.py
@@ -30,12 +30,10 @@
 
 
 def document_starts(lengths, count):
+    ends = jnp.cumsum(lengths)
     places = jnp.arange(count, dtype=jnp.int32)
-    starts, end = jnp.zeros_like(places), 0
-    for at in range(lengths.shape[0]):
-        end = end + lengths[at]
-        starts = starts + jnp.where(places >= end, lengths[at], 0)
-    return starts
+    passed = (places[:, None] >= ends[None, :]).astype(jnp.int32)
+    return jnp.sum(passed * lengths[None, :], axis=1)
 
 
 def allowed_pairs(start_row, key_block, query_block):
@@ -2113,10 +2111,9 @@
     down_last = plane_gather_end(down_legs)
     x_first, y_first = plane_send(feed_x0, 1), plane_send(feed_y0, 2)
     grad_mixed_head = attend_back(mixed, grad_head, wide, total, starts, HALO)
-    grad_mixed_head, down_last, x_first, y_first = lax.optimization_barrier(
-        (grad_mixed_head, down_last, x_first, y_first)
+    grad_mixed_head, x_first, y_first = lax.optimization_barrier(
+        (grad_mixed_head, x_first, y_first)
     )
-    down_grad = placed(down_mine, down_legs, down_last, me_dp, False)
 
     def add(left, right):
         return left.astype(F32) + right.astype(F32)
@@ -2127,7 +2124,8 @@
         ((0, feed_x1), (1, feed_y1), (1, feed_a0), (0, feed_b0)),
     )
     grad_raw, down_last = lax.optimization_barrier((grad_raw, down_last))
-    grad_raw, up_mine = lax.optimization_barrier((grad_raw, up_mine))
+    grad_raw, up_mine, down_last = lax.optimization_barrier((grad_raw, up_mine, down_last))
+    down_grad = placed(down_mine, down_legs, down_last, me_dp, False)
     up_legs = plane_gather_begin(up_mine)
     feed_a1, feed_b1 = add(keep_a[1, 1], x_second[1]).astype(LOW), add(keep_b[1, 1], y_second[1]).astype(LOW)
 

time: 763 us -> 754 us (0.988)
  local copies, waits for them, and re-layouts: 43.6 us -> 35.2 us
    unnamed x134 -> x121, local copies, waits for them, and re-layouts: 16.2 us -> 12.5 us
  transfers between devices with their start and end apart: 20 -> 20, of which waited for: 3 -> 3; matrix products, arithmetic and copies ran while one was open for 7% -> 6% of each run, Pallas kernels for 35% -> 37%
where the time goes in v7:
time: 754 us; the launch traced here: 745 us
  Pallas kernels  610 us (81%)
  other arithmetic  42.4 us (6%)
  local copies, waits for them, and re-layouts  35.2 us (5%)
  starting transfers between devices  20.4 us (3%)
  between operations  15.4 us (2%)
  waiting for transfers between devices  15.2 us (2%)
    pallas_call x1, Pallas kernels, feed_in(): pl.pallas_call(partial(feed_in_kernel, tuple(up_late)), in_specs=[anywher...  122 us
    pallas_call x1, Pallas kernels, feed_out(): pl.pallas_call(feed_out_kernel, in_specs=[anywhere] * 11, out_specs=[anyw...  107 us
    pallas_call x1, Pallas kernels, front(): pl.pallas_call(front_kernel, in_specs=[anywhere, vmem, vmem] + [anywhere]...  106 us
    pallas_call x1, Pallas kernels, finish(): pl.pallas_call(partial(finish_kernel, tuple((way for way, _ in carried)))...  102 us
    pallas_call x1, Pallas kernels, project_back(): pl.pallas_call(partial(project_back_kernel, tuple((way for way, _ in carr...  54 us
    pallas_call x1, Pallas kernels, feed_heads(): pl.pallas_call(feed_heads_kernel, in_specs=[pl.BlockSpec(memory_space=plt...  34.1 us
    pallas_call x1, Pallas kernels, attend_back(): pl.pallas_call(attend_back_kernel, grid_spec=pltpu.PrefetchScalarGridSpec...  29.3 us
    pallas_call x1, Pallas kernels, attend(): pl.pallas_call(attend_kernel, grid_spec=pltpu.PrefetchScalarGridSpec(num_...  20.1 us
  transfers between devices with their start and end apart: 20, of which 3 were waited for; matrix products, arithmetic and copies ran while one was open for 6% of the time, Pallas kernels for 37%

profile of v7, /device:TPU:0, one launch (start us, length us, event | category | flops | bytes accessed | tf_op | source)
XLA Modules:
  0.0 744.7 jit_solution(8000384724166800115)
XLA Ops:
  12.0 1.4 copy.64
  15.9 1.4 pad_maximum_fusion.1.masks_ref
  17.3 106.3 %front.1 = (bf16[4,2,4,32,2048]{4,3,2,1,0:T(8,128)(2,1)}, bf16[4,2,4,16,2048]{4,3,2,1,0:T(8,128)(2,1)}, bf16[4,2,4,16,2048]{4,3,2,1,0:T(8,128)(2,1)}, f32[3,8,10...) custom-call(bf16[2,320,2048]{2,1,0:T(8,128)(2,1)} %inputs_ref.3, ...), custom_call_target="tpu_custom_call" | custom-call | flops 68719476736 | bytes 67108864 | tf_op jit(solution)/shard_map/front/pallas_call | solution.py:679
  123.6 2.5 collective-permute-start.4
  126.3 2.9 constant_dynamic-slice_fusion.1
  129.1 1.6 collective-permute-start.1
  130.7 1.4 collective-permute-start
  132.2 1.8 fusion.22
  133.9 1.9 collective-permute-start.3
  136.0 2.3 constant_dynamic-slice_fusion.down_ref
  138.3 20.1 %attend.1 = (bf16[1,2560,128]{2,1,0:T(8,128)(2,1)S(1)}, f32[2,64,2560]{2,1,0:T(8,128)S(1)}, f32[2,1,2560]{2,1,0:T(1,128)S(1)}) custom-call(s32[2,5]{1,0:T(2,128)S(1)} %and_select_fusion.first_ref, s32[2,1,2560]{2,1,0:T(1,128)S(1)} %broadcast_in_dim.16.start_ref, bf16[3,2560,128]{2,1,0:T(8,128)(2,1)S(1)} %bitcast.135, bf16[3,2560,128]{2,1,0:T(8,128)(2,1)S(1)} %bitcast.136), custom_call_target="tpu_custom_call" | custom-call | flops 17179869184 | bytes 5242880 | tf_op jit(solution)/shard_map/attend/pallas_call | solution.py:108
  159.6 3.8 collective-permute-done.refs_0_
  163.5 19.5 %attended_back.1 = bf16[1,320,1024]{2,1,0:T(8,128)(2,1)S(1)} custom-call(bf16[1,2560,128]{2,1,0:T(8,128)(2,1)S(1)} %get-tuple-element.100.x_ref), custom_call_target="tpu_custom_call" | custom-call | flops 17179869184 | bytes 16777216 | tf_op jit(solution)/shard_map/attended_back/pallas_call | solution.py:906
  183.4 4.5 fusion.30
  190.3 2.4 add_convert_fusion.second_ref
  192.7 121.6 %feed_in.1 = (bf16[2,4,320,2048]{3,2,1,0:T(8,128)(2,1)}, f32[2,4,320,2048]{3,2,1,0:T(8,128)}, bf16[2,4,320,2048]{3,2,1,0:T(8,128)(2,1)}, bf16[2048,2048]{1,0:T(8...) custom-call(bf16[2,320,2048]{2,1,0:T(8,128)(2,1)} %add_convert_fusion.second_ref, ...), custom_call_target="tpu_custom_call" | custom-call | flops 64424509440 | bytes 62914560 | tf_op jit(solution)/shard_map/feed_in/pallas_call | solution.py:1179
  314.9 106.8 %feed_out.1 = (bf16[2,4,320,2048]{3,2,1,0:T(8,128)(2,1)}, bf16[2048,2048]{1,0:T(8,128)(2,1)}, f32[2,320,2048]{2,1,0:T(8,128)}) custom-call(bf16[2,320,2048]{2,1,0:T(8,128)(2,1)} %cot_0.1, bf16[2,320,1024]{2,1,0:T(8,128)(2,1)} %get-tuple-element.103.cot_1, bf16[2,320,1024]{2,1,0:T(8,128)(2,1)} %collective-permute-done.3.cot_2, ...), custom_call_target="tpu_custom_call" | custom-call | flops 85899345920 | bytes 62914560 | tf_op jit(solution)/shard_map/feed_out/pallas_call | solution.py:1383
  424.0 2.4 fusion.26
  426.3 2.0 collective-permute-start.7
  428.4 2.0 collective-permute-start.6
  430.4 4.9 multiply_reduce_fusion.1
  435.4 4.6 multiply_reduce_fusion
  440.3 3.9 fusion.21
  444.2 1.5 copy-done.25
  445.7 1.6 convolution_convert_fusion
  448.6 1.4 copy.58.x_ref
  450.0 34.1 %feed_heads.1 = (bf16[1,8,320,128]{3,2,1,0:T(8,128)(2,1)S(1)}, bf16[2,320,1024]{2,1,0:T(8,128)(2,1)S(1)}, bf16[2,320,1024]{2,1,0:T(8,128)(2,1)S(1)}, bf16[2,320,...) custom-call(bf16[1,320,1024]{2,1,0:T(8,128)(2,1)S(1)} %copy.58.x_ref, ...), custom_call_target="tpu_custom_call" | custom-call | flops 34359738368 | bytes 16777216 | tf_op jit(solution)/shard_map/feed_heads/pallas_call | solution.py:1502
  485.2 1.8 collective-permute-start.13
  487.2 1.8 collective-permute-start.11
  489.0 29.3 %attend_back.1.x_ref = bf16[3,2576,128]{2,1,0:T(8,128)(2,1)S(1)} custom-call(s32[2,5]{1,0:T(2,128)S(1)} %copy-done.11, s32[2,1,2560]{2,1,0:T(1,128)S(1)} %copy-done.9, bf16[3,2560,128]{2,1,0:T(8,128)(2,1)S(1)} %bitcast.137, bf16[3,2560,128]{2,1,0:T(8,128)(2,1)S(1)} %bitcast.138, bf16[1,2560,128]{2,1,0:T(8,128)(2,1)S(1)} %bitcast.139, ...), custom_call_target="tpu_custom_call" | custom-call | flops 34359738368 | bytes 5242880 | tf_op jit(solution)/shard_map/attend_back/pallas_call | solution.py:203
  519.6 7.1 collective-permute-done.10
  526.8 2.6 fusion.11.refs_2_
  529.4 2.2 fusion.10.refs_3_
  531.6 54.0 %project_back.1 = (bf16[3,320,1024]{2,1,0:T(8,128)(2,1)}, f32[3,8,1024]{2,1,0:T(8,128)}, bf16[4,256,2048]{2,1,0:T(8,128)(2,1)}, bf16[4,128,2048]{2,1,0:T(8,128)(...) custom-call(bf16[3,2576,128]{2,1,0:T(8,128)(2,1)} %copy-done.16, ...), custom_call_target="tpu_custom_call" | custom-call | flops 34359738368 | bytes 16777216 | tf_op jit(solution)/shard_map/project_back/pallas_call | solution.py:844
  585.7 2.3 fusion.25
  588.0 1.6 collective-permute-start.17
  590.0 1.7 collective-permute-start.16
  593.1 2.4 fusion.4.refs_1_
  595.5 8.7 %placed.3 = f32[1024,2048]{1,0:T(8,128)} custom-call(s32[1]{0:T(128)} %bitcast.74.me_ref, bf16[256,2048]{1,0:T(8,128)(2,1)S(1)} %copy-done.1, bf16[256,1024]{1,0:T(8,128)(2,1)} %collective-permute-done.6.one_x, bf16[256,1024]{1,0:T(8,128)(2,1)S(1)} %collective-permute-done.9.two_x, bf16[256,1024]{1,0:T(8,128)(2,1)S(1)} %copy-done.3, ...), custom_call_target="tpu_custom_call" | custom-call | bytes 16777216 | tf_op jit(solution)/shard_map/placed/pallas_call | solution.py:1945
  604.9 1.9 fusion.13
  607.7 4.2 collective-permute-done.16.one_y
  611.8 101.9 %finish.1 = (bf16[4,64,2048]{2,1,0:T(8,128)(2,1)}, f32[8,2048]{1,0:T(8,128)}, f32[8,256]{1,0:T(8,128)}, f32[2,320,2048]{2,1,0:T(8,128)}, bf16[320,1024]{1,0:T(8,...) custom-call(bf16[4,2,4,32,2048]{4,3,2,1,0:T(8,128)(2,1)} %bitcast.179, ...), custom_call_target="tpu_custom_call" | custom-call | flops 68719476736 | bytes 67108864 | tf_op jit(solution)/shard_map/finish/pallas_call | solution.py:1858
  716.2 2.4 fusion.7
  720.9 2.4 fusion.9
  723.3 1.3 fusion.1
  724.7 1.7 pad_maximum_fusion
  727.3 7.8 %placed.2 = f32[2048,1024]{1,0:T(8,128)} custom-call(s32[1]{0:T(128)} %bitcast.74.me_ref, bf16[256,2048]{1,0:T(8,128)(2,1)S(1)} %copy-done, bf16[256,1024]{1,0:T(8,128)(2,1)} %collective-permute-done.14.refs_2_.one_x, bf16[256,1024]{1,0:T(8,128)(2,1)S(1)} %copy-done.5, bf16[256,1024]{1,0:T(8,128)(2,1)} %collective-permute-done.16.one_y, ...), custom_call_target="tpu_custom_call" | custom-call | bytes 16777216 | tf_op jit(solution)/shard_map/placed/pallas_call | solution.py:1945
  735.1 2.4 copy.68
  (195 shorter events, 27.2 us)
Async XLA Ops:
  7.2 6.3 copy-start.50
  7.2 7.0 copy-start.35
  7.2 6.9 copy-start.36
  7.2 416.7 %reduce-scatter.3.cloned.1.call-start = ((), (), s32[]{:S(2)}) async-start(), calls=%async_computation.2 | async-start | bytes 9437184 | tf_op jit(solution)/shard_map/reduce_scatter | solution.py:2087
  123.6 69.1 %collective-permute-start.4 = (bf16[2,320,1024]{2,1,0:T(8,128)(2,1)}, bf16[2,320,1024]{2,1,0:T(8,128)(2,1)}, u32[]{:S(2)}, u32[]{:S(2)}) collective-permute-start(bf16[2,320,1024]{2,1,0:T(8,128)(2,1)} %get-tuple-element.103.cot_1), channel_id=1, source_target_pairs={{0,16},{8,24},{16,0},{24,8},{1,17},{9,25},{17,1},{25,9},{2,18},{10... | collective-permute-start | bytes 3932168 | tf_op jit(solution)/shard_map/ppermute | solution.py:1910
  126.2 66.6 %collective-permute-start.5 = (bf16[2,320,1024]{2,1,0:T(8,128)(2,1)}, bf16[2,320,1024]{2,1,0:T(8,128)(2,1)}, u32[]{:S(2)}, u32[]{:S(2)}) collective-permute-start(bf16[2,320,1024]{2,1,0:T(8,128)(2,1)} %get-tuple-element.104.cot_4), channel_id=1, source_target_pairs={{0,8},{8,0},{16,24},{24,16},{1,9},{9,1},{17,25},{25,17},{2,10},{10... | collective-permute-start | bytes 3932168 | tf_op jit(solution)/shard_map/ppermute | solution.py:1910
  129.1 30.4 %collective-permute-start.1 = (bf16[256,2048]{1,0:T(8,128)(2,1)}, bf16[256,2048]{1,0:T(8,128)(2,1)}, u32[]{:S(2)}, u32[]{:S(2)}) collective-permute-start(bf16[256,2048]{1,0:T(8,128)(2,1)} %get-tuple-element.182), channel_id=1, source_target_pairs={{4,6},{5,7},{12,14},{13,15},{20,22},{21,23},{28,30},{29,31}} | collective-permute-start | bytes 3145736 | tf_op jit(solution)/shard_map/ppermute | solution.py:1975
  130.7 7.6 %copy-start.12 = (bf16[3,8,320,128]{3,2,1,0:T(8,128)(2,1)S(1)}, bf16[3,8,320,128]{3,2,1,0:T(8,128)(2,1)}, u32[]{:S(2)}) copy-start(bf16[3,8,320,128]{3,2,1,0:T(8,128)(2,1)} %get-tuple-element.95) | copy-start | bytes 5898244
  130.7 32.7 %collective-permute-start = (bf16[256,2048]{1,0:T(8,128)(2,1)S(1)}, bf16[256,2048]{1,0:T(8,128)(2,1)}, u32[]{:S(2)}, u32[]{:S(2)}) collective-permute-start(bf16[256,2048]{1,0:T(8,128)(2,1)S(1)} %get-tuple-element.183), channel_id=1, source_target_pairs={{2,0},{3,1},{10,8},{11,9},{18,16},{19,17},{26,24},{27,25}} | collective-permute-start | bytes 3145736 | tf_op jit(solution)/shard_map/ppermute | solution.py:1975
  133.9 58.8 %collective-permute-start.3 = (bf16[2,320,1024]{2,1,0:T(8,128)(2,1)}, bf16[2,320,1024]{2,1,0:T(8,128)(2,1)}, u32[]{:S(2)}, u32[]{:S(2)}) collective-permute-start(bf16[2,320,1024]{2,1,0:T(8,128)(2,1)} %get-tuple-element.190), channel_id=1, source_target_pairs={{0,8},{8,0},{16,24},{24,16},{1,9},{9,1},{17,25},{25,17},{2,10},{10... | collective-permute-start | bytes 3932168 | tf_op jit(solution)/shard_map/ppermute | solution.py:1910
  136.0 22.5 %copy-start.8 = (s32[2,1,2560]{2,1,0:T(1,128)}, s32[2,1,2560]{2,1,0:T(1,128)S(1)}, u32[]{:S(2)}) copy-start(s32[2,1,2560]{2,1,0:T(1,128)S(1)} %broadcast_in_dim.16.start_ref) | copy-start | bytes 61444
  136.0 22.5 %copy-start.10 = (s32[2,5]{1,0:T(2,128)}, s32[2,5]{1,0:T(2,128)S(1)}, u32[]{:S(2)}) copy-start(s32[2,5]{1,0:T(2,128)S(1)} %and_select_fusion.first_ref) | copy-start | bytes 124
  159.6 33.2 %collective-permute-start.2 = (bf16[2,320,1024]{2,1,0:T(8,128)(2,1)}, bf16[2,320,1024]{2,1,0:T(8,128)(2,1)}, u32[]{:S(2)}, u32[]{:S(2)}) collective-permute-start(bf16[2,320,1024]{2,1,0:T(8,128)(2,1)} %get-tuple-element.191), channel_id=1, source_target_pairs={{0,16},{8,24},{16,0},{24,8},{1,17},{9,25},{17,1},{25,9},{2,18},{10... | collective-permute-start | bytes 3932168 | tf_op jit(solution)/shard_map/ppermute | solution.py:1910
  314.4 271.2 %reduce-scatter.5.cloned.1.call-start = ((), (), s32[]{:S(2)}) async-start(), calls=%async_computation.3 | async-start | bytes 9437184 | tf_op jit(solution)/shard_map/reduce_scatter | solution.py:2091
  421.7 8.7 %copy-start.38 = (f32[2048]{0:T(1024)S(1)}, f32[2048]{0:T(1024)}, u32[]{:S(2)}) copy-start(f32[2048]{0:T(1024)} %param.30) | copy-start | bytes 24580
  421.7 8.7 %copy-start.40 = (f32[2,320]{1,0:T(2,128)S(1)}, f32[2,320]{1,0:T(2,128)}, u32[]{:S(2)}) copy-start(f32[2,320]{1,0:T(2,128)} %copy-done.39) | copy-start | bytes 7684
  424.0 11.4 %slice-start.4 = ((s8[5242880]{0:T(1024)(128)(4,1)}), s8[4194304]{0:T(1024)(128)(4,1)S(1)}, s32[]{:S(2)}) async-start(s8[5242880]{0:T(1024)(128)(4,1)} %bitcast.144), calls=%async_computation.8 | async-start | bytes 8388608
  426.3 58.5 %collective-permute-start.9 = (bf16[256,1024]{1,0:T(8,128)(2,1)}, bf16[256,1024]{1,0:T(8,128)(2,1)S(1)}, u32[]{:S(2)}, u32[]{:S(2)}) collective-permute-start(bf16[256,1024]{1,0:T(8,128)(2,1)} %get-tuple-element.198), channel_id=1, source_target_pairs={{0,8},{8,0},{16,24},{24,16},{1,9},{9,1},{17,25},{25,17},{2,10},{10... | collective-permute-start | bytes 1572872 | tf_op jit(solution)/shard_map/ppermute | solution.py:1910
  426.3 58.5 %collective-permute-start.7 = (bf16[256,1024]{1,0:T(8,128)(2,1)}, bf16[256,1024]{1,0:T(8,128)(2,1)}, u32[]{:S(2)}, u32[]{:S(2)}) collective-permute-start(bf16[256,1024]{1,0:T(8,128)(2,1)} %get-tuple-element.198), channel_id=1, source_target_pairs={{0,16},{8,24},{16,0},{24,8},{1,17},{9,25},{17,1},{25,9},{2,18},{10... | collective-permute-start | bytes 1572872 | tf_op jit(solution)/shard_map/ppermute | solution.py:1910
  428.3 7.0 copy-start.44
  428.3 7.0 slice-start.5
  428.3 7.0 copy-start.42
  428.3 56.6 %collective-permute-start.8 = (bf16[256,1024]{1,0:T(8,128)(2,1)}, bf16[256,1024]{1,0:T(8,128)(2,1)S(1)}, u32[]{:S(2)}, u32[]{:S(2)}) collective-permute-start(bf16[256,1024]{1,0:T(8,128)(2,1)} %get-tuple-element.199), channel_id=1, source_target_pairs={{0,16},{8,24},{16,0},{24,8},{1,17},{9,25},{17,1},{25,9},{2,18},{10... | collective-permute-start | bytes 1572872 | tf_op jit(solution)/shard_map/ppermute | solution.py:1910
  428.4 56.5 %collective-permute-start.6 = (bf16[256,1024]{1,0:T(8,128)(2,1)}, bf16[256,1024]{1,0:T(8,128)(2,1)}, u32[]{:S(2)}, u32[]{:S(2)}) collective-permute-start(bf16[256,1024]{1,0:T(8,128)(2,1)} %get-tuple-element.199), channel_id=1, source_target_pairs={{0,8},{8,0},{16,24},{24,16},{1,9},{9,1},{17,25},{25,17},{2,10},{10... | collective-permute-start | bytes 1572872 | tf_op jit(solution)/shard_map/ppermute | solution.py:1910
  450.0 39.0 %copy-start.9 = (s32[2,1,2560]{2,1,0:T(1,128)S(1)}, s32[2,1,2560]{2,1,0:T(1,128)}, u32[]{:S(2)}) copy-start(s32[2,1,2560]{2,1,0:T(1,128)} %copy-done.8) | copy-start | bytes 61444
  450.0 39.0 %copy-start.11 = (s32[2,5]{1,0:T(2,128)S(1)}, s32[2,5]{1,0:T(2,128)}, u32[]{:S(2)}) copy-start(s32[2,5]{1,0:T(2,128)} %copy-done.10) | copy-start | bytes 124
  450.0 39.0 %copy-start.13 = (bf16[3,8,320,128]{3,2,1,0:T(8,128)(2,1)S(1)}, bf16[3,8,320,128]{3,2,1,0:T(8,128)(2,1)}, u32[]{:S(2)}) copy-start(bf16[3,8,320,128]{3,2,1,0:T(8,128)(2,1)} %get-tuple-element.95) | copy-start | bytes 5898244
  450.0 39.0 %copy-start.15 = (f32[2,64,2560]{2,1,0:T(8,128)S(1)}, f32[2,64,2560]{2,1,0:T(8,128)}, u32[]{:S(2)}) copy-start(f32[2,64,2560]{2,1,0:T(8,128)} %copy-done.14) | copy-start | bytes 3932164
  484.1 34.2 %copy-start.17 = (bf16[2,320,1024]{2,1,0:T(8,128)(2,1)}, bf16[2,320,1024]{2,1,0:T(8,128)(2,1)S(1)}, u32[]{:S(2)}) copy-start(bf16[2,320,1024]{2,1,0:T(8,128)(2,1)S(1)} %get-tuple-element.135.refs_0_) | copy-start | bytes 3932164
  484.9 33.5 %copy-start.2 = (bf16[256,1024]{1,0:T(8,128)(2,1)}, bf16[256,1024]{1,0:T(8,128)(2,1)S(1)}, u32[]{:S(2)}) copy-start(bf16[256,1024]{1,0:T(8,128)(2,1)S(1)} %collective-permute-done.8.one_y) | copy-start | bytes 1572868
  484.9 100.7 %collective-permute-start.12 = (bf16[256,1024]{1,0:T(8,128)(2,1)}, bf16[256,1024]{1,0:T(8,128)(2,1)}, u32[]{:S(2)}, u32[]{:S(2)}) collective-permute-start(bf16[256,1024]{1,0:T(8,128)(2,1)} %collective-permute-done.6.one_x), channel_id=1, source_target_pairs={{0,16},{8,24},{16,0},{24,8},{1,17},{9,25},{17,1},{25,9},{2,18},{10... | collective-permute-start | bytes 1572872 | tf_op jit(solution)/shard_map/ppermute | solution.py:1910
  485.2 100.5 %collective-permute-start.13 = (bf16[256,1024]{1,0:T(8,128)(2,1)}, bf16[256,1024]{1,0:T(8,128)(2,1)}, u32[]{:S(2)}, u32[]{:S(2)}) collective-permute-start(bf16[256,1024]{1,0:T(8,128)(2,1)} %collective-permute-done.7.two_y), channel_id=1, source_target_pairs={{0,8},{8,0},{16,24},{24,16},{1,9},{9,1},{17,25},{25,17},{2,10},{10... | collective-permute-start | bytes 1572872 | tf_op jit(solution)/shard_map/ppermute | solution.py:1910
  487.0 39.8 %collective-permute-start.10 = (bf16[2,320,1024]{2,1,0:T(8,128)(2,1)S(1)}, bf16[2,320,1024]{2,1,0:T(8,128)(2,1)S(1)}, u32[]{:S(2)}, u32[]{:S(2)}) collective-permute-start(bf16[2,320,1024]{2,1,0:T(8,128)(2,1)S(1)} %get-tuple-element.128), channel_id=1, source_target_pairs={{0,8},{8,0},{16,24},{24,16},{1,9},{9,1},{17,25},{25,17},{2,10},{10... | collective-permute-start | bytes 3932168 | tf_op jit(solution)/shard_map/ppermute | solution.py:1910
  487.2 39.5 %collective-permute-start.11 = (bf16[2,320,1024]{2,1,0:T(8,128)(2,1)S(1)}, bf16[2,320,1024]{2,1,0:T(8,128)(2,1)S(1)}, u32[]{:S(2)}, u32[]{:S(2)}) collective-permute-start(bf16[2,320,1024]{2,1,0:T(8,128)(2,1)S(1)} %get-tuple-element.129), channel_id=1, source_target_pairs={{0,16},{8,24},{16,0},{24,8},{1,17},{9,25},{17,1},{25,9},{2,18},{10... | collective-permute-start | bytes 3932168 | tf_op jit(solution)/shard_map/ppermute | solution.py:1910
  585.6 9.9 %copy-start.1 = (bf16[256,2048]{1,0:T(8,128)(2,1)S(1)}, bf16[256,2048]{1,0:T(8,128)(2,1)}, u32[]{:S(2)}) copy-start(bf16[256,2048]{1,0:T(8,128)(2,1)} %reduce-scatter.3.cloned.1.call-done.own_ref) | copy-start | bytes 3145732
  585.6 9.9 %copy-start.3 = (bf16[256,1024]{1,0:T(8,128)(2,1)S(1)}, bf16[256,1024]{1,0:T(8,128)(2,1)}, u32[]{:S(2)}) copy-start(bf16[256,1024]{1,0:T(8,128)(2,1)} %copy-done.2) | copy-start | bytes 1572868
  588.0 18.8 %collective-permute-start.17 = (bf16[256,1024]{1,0:T(8,128)(2,1)}, bf16[256,1024]{1,0:T(8,128)(2,1)S(1)}, u32[]{:S(2)}, u32[]{:S(2)}) collective-permute-start(bf16[256,1024]{1,0:T(8,128)(2,1)} %get-tuple-element.196), channel_id=1, source_target_pairs={{0,8},{8,0},{16,24},{24,16},{1,9},{9,1},{17,25},{25,17},{2,10},{10... | collective-permute-start | bytes 1572872 | tf_op jit(solution)/shard_map/ppermute | solution.py:1910
  589.6 18.0 %collective-permute-start.15 = (bf16[256,1024]{1,0:T(8,128)(2,1)}, bf16[256,1024]{1,0:T(8,128)(2,1)}, u32[]{:S(2)}, u32[]{:S(2)}) collective-permute-start(bf16[256,1024]{1,0:T(8,128)(2,1)} %get-tuple-element.196), channel_id=1, source_target_pairs={{0,16},{8,24},{16,0},{24,8},{1,17},{9,25},{17,1},{25,9},{2,18},{10... | collective-permute-start | bytes 1572872 | tf_op jit(solution)/shard_map/ppermute | solution.py:1910
  590.0 21.8 %collective-permute-start.16 = (bf16[256,1024]{1,0:T(8,128)(2,1)}, bf16[256,1024]{1,0:T(8,128)(2,1)}, u32[]{:S(2)}, u32[]{:S(2)}) collective-permute-start(bf16[256,1024]{1,0:T(8,128)(2,1)} %get-tuple-element.197), channel_id=1, source_target_pairs={{0,16},{8,24},{16,0},{24,8},{1,17},{9,25},{17,1},{25,9},{2,18},{10... | collective-permute-start | bytes 1572872 | tf_op jit(solution)/shard_map/ppermute | solution.py:1910
  591.7 20.2 %collective-permute-start.14 = (bf16[256,1024]{1,0:T(8,128)(2,1)}, bf16[256,1024]{1,0:T(8,128)(2,1)}, u32[]{:S(2)}, u32[]{:S(2)}) collective-permute-start(bf16[256,1024]{1,0:T(8,128)(2,1)} %get-tuple-element.197), channel_id=1, source_target_pairs={{0,8},{8,0},{16,24},{24,16},{1,9},{9,1},{17,25},{25,17},{2,10},{10... | collective-permute-start | bytes 1572872 | tf_op jit(solution)/shard_map/ppermute | solution.py:1910
  595.5 9.4 %copy-start.26 = (bf16[2,2,320,1024]{3,2,1,0:T(8,128)(2,1)S(1)}, bf16[2,2,320,1024]{3,2,1,0:T(8,128)(2,1)}, u32[]{:S(2)}) copy-start(bf16[2,2,320,1024]{3,2,1,0:T(8,128)(2,1)} %get-tuple-element.120) | copy-start | bytes 7864324
  595.5 9.4 %copy-start.31 = (bf16[2,320,1024]{2,1,0:T(8,128)(2,1)S(1)}, bf16[2,320,1024]{2,1,0:T(8,128)(2,1)}, u32[]{:S(2)}) copy-start(bf16[2,320,1024]{2,1,0:T(8,128)(2,1)} %get-tuple-element.141) | copy-start | bytes 3932164
  595.5 9.4 %copy-start.33 = (bf16[2,320,1024]{2,1,0:T(8,128)(2,1)S(1)}, bf16[2,320,1024]{2,1,0:T(8,128)(2,1)}, u32[]{:S(2)}) copy-start(bf16[2,320,1024]{2,1,0:T(8,128)(2,1)} %copy-done.32) | copy-start | bytes 3932164
  595.5 9.4 %copy-start.34 = (bf16[320,1024]{1,0:T(8,128)(2,1)S(1)}, bf16[320,1024]{1,0:T(8,128)(2,1)}, u32[]{:S(2)}) copy-start(bf16[320,1024]{1,0:T(8,128)(2,1)} %get-tuple-element.139) | copy-start | bytes 1966084
  713.7 7.2 copy-start.30
  715.1 8.2 %slice-start.2 = ((s8[5242880]{0:T(1024)(128)(4,1)}), s8[4194304]{0:T(1024)(128)(4,1)S(1)}, s32[]{:S(2)}) async-start(s8[5242880]{0:T(1024)(128)(4,1)} %bitcast.142), calls=%async_computation.6 | async-start | bytes 8388608
  726.4 8.7 %slice-start.6 = ((s8[5242880]{0:T(1024)(128)(4,1)}), s8[4194304]{0:T(1024)(128)(4,1)S(1)}, s32[]{:S(2)}) async-start(s8[5242880]{0:T(1024)(128)(4,1)} %bitcast.148), calls=%async_computation.10 | async-start | bytes 8388608
  727.3 7.8 %slice-start.7 = ((s8[5242880]{0:T(1024)(128)(4,1)}), s8[1048576]{0:T(1024)(128)(4,1)S(1)}, s32[]{:S(2)}) async-start(s8[5242880]{0:T(1024)(128)(4,1)} %bitcast.148), calls=%async_computation.11 | async-start | bytes 2097152
  (31 other events, 97.0 us)
Sparse Core Ops, SparseCore 0:
  314.5 89.0 reduce-scatter.2
  421.8 99.5 reduce-scatter.4

commit v8 on v7

--- a/solution.py
+++ b/solution.py
@@ -2108,12 +2108,12 @@
     grad_head, down_legs, feed_x0, feed_y0 = lax.optimization_barrier(
         (grad_head, down_legs, feed_x0, feed_y0)
     )
-    down_last = plane_gather_end(down_legs)
     x_first, y_first = plane_send(feed_x0, 1), plane_send(feed_y0, 2)
     grad_mixed_head = attend_back(mixed, grad_head, wide, total, starts, HALO)
-    grad_mixed_head, x_first, y_first = lax.optimization_barrier(
-        (grad_mixed_head, x_first, y_first)
+    grad_mixed_head, x_first, y_first, down_legs = lax.optimization_barrier(
+        (grad_mixed_head, x_first, y_first, down_legs)
     )
+    down_last = plane_gather_end(down_legs)
 
     def add(left, right):
         return left.astype(F32) + right.astype(F32)

time: 754 us -> 749 us (level)
  transfers between devices with their start and end apart: 20 -> 20, of which waited for: 3 -> 2; matrix products, arithmetic and copies ran while one was open for 6% -> 7% of each run, Pallas kernels for 37% -> 37%
where the time goes in v8:
time: 749 us; the launch traced here: 740 us
  Pallas kernels  610 us (81%)
  other arithmetic  43.9 us (6%)
  local copies, waits for them, and re-layouts  35.2 us (5%)
  starting transfers between devices  19 us (3%)
  between operations  15.4 us (2%)
  waiting for transfers between devices  10.5 us (1%)
    pallas_call x1, Pallas kernels, feed_in(): pl.pallas_call(partial(feed_in_kernel, tuple(up_late)), in_specs=[anywher...  121 us
    pallas_call x1, Pallas kernels, feed_out(): pl.pallas_call(feed_out_kernel, in_specs=[anywhere] * 11, out_specs=[anyw...  106 us
    pallas_call x1, Pallas kernels, front(): pl.pallas_call(front_kernel, in_specs=[anywhere, vmem, vmem] + [anywhere]...  106 us
    pallas_call x1, Pallas kernels, finish(): pl.pallas_call(partial(finish_kernel, tuple((way for way, _ in carried)))...  103 us
    pallas_call x1, Pallas kernels, project_back(): pl.pallas_call(partial(project_back_kernel, tuple((way for way, _ in carr...  54 us
    pallas_call x1, Pallas kernels, feed_heads(): pl.pallas_call(feed_heads_kernel, in_specs=[pl.BlockSpec(memory_space=plt...  34 us
    pallas_call x1, Pallas kernels, attend_back(): pl.pallas_call(attend_back_kernel, grid_spec=pltpu.PrefetchScalarGridSpec...  30.3 us
    pallas_call x1, Pallas kernels, attend(): pl.pallas_call(attend_kernel, grid_spec=pltpu.PrefetchScalarGridSpec(num_...  20.8 us
  transfers between devices with their start and end apart: 20, of which 2 were waited for; matrix products, arithmetic and copies ran while one was open for 7% of the time, Pallas kernels for 37%

profile of v8, /device:TPU:0, one launch (start us, length us, event | category | flops | bytes accessed | tf_op | source)
XLA Modules:
  0.0 740.4 jit_solution(11666024329466731049)
XLA Ops:
  10.7 1.3 constant_dynamic-slice_fusion.3
  12.0 1.4 copy.64
  15.9 1.5 pad_maximum_fusion.1.masks_ref
  17.4 106.3 %front.1 = (bf16[4,2,4,32,2048]{4,3,2,1,0:T(8,128)(2,1)}, bf16[4,2,4,16,2048]{4,3,2,1,0:T(8,128)(2,1)}, bf16[4,2,4,16,2048]{4,3,2,1,0:T(8,128)(2,1)}, f32[3,8,10...) custom-call(bf16[2,320,2048]{2,1,0:T(8,128)(2,1)} %inputs_ref.3, ...), custom_call_target="tpu_custom_call" | custom-call | flops 68719476736 | bytes 67108864 | tf_op jit(solution)/shard_map/front/pallas_call | solution.py:679
  123.7 2.5 collective-permute-start.4
  126.3 2.9 constant_dynamic-slice_fusion.1
  129.1 1.6 collective-permute-start.1
  130.8 1.4 collective-permute-start
  132.2 1.8 fusion.22
  133.9 1.9 collective-permute-start.3
  136.0 2.3 constant_dynamic-slice_fusion.down_ref
  138.4 20.8 %attend.1 = (bf16[1,2560,128]{2,1,0:T(8,128)(2,1)S(1)}, f32[2,64,2560]{2,1,0:T(8,128)S(1)}, f32[2,1,2560]{2,1,0:T(1,128)S(1)}) custom-call(s32[2,5]{1,0:T(2,128)S(1)} %and_select_fusion.first_ref, s32[2,1,2560]{2,1,0:T(1,128)S(1)} %broadcast_in_dim.16.start_ref, bf16[3,2560,128]{2,1,0:T(8,128)(2,1)S(1)} %bitcast.135, bf16[3,2560,128]{2,1,0:T(8,128)(2,1)S(1)} %bitcast.136), custom_call_target="tpu_custom_call" | custom-call | flops 17179869184 | bytes 5242880 | tf_op jit(solution)/shard_map/attend/pallas_call | solution.py:108
  160.3 3.2 collective-permute-done.refs_0_
  163.5 20.0 %attended_back.1 = bf16[1,320,1024]{2,1,0:T(8,128)(2,1)S(1)} custom-call(bf16[1,2560,128]{2,1,0:T(8,128)(2,1)S(1)} %get-tuple-element.104.x_ref), custom_call_target="tpu_custom_call" | custom-call | flops 17179869184 | bytes 16777216 | tf_op jit(solution)/shard_map/attended_back/pallas_call | solution.py:906
  184.0 4.5 fusion.30
  190.9 2.4 add_convert_fusion.second_ref
  193.3 120.7 %feed_in.1 = (bf16[2,4,320,2048]{3,2,1,0:T(8,128)(2,1)}, f32[2,4,320,2048]{3,2,1,0:T(8,128)}, bf16[2,4,320,2048]{3,2,1,0:T(8,128)(2,1)}, bf16[2048,2048]{1,0:T(8...) custom-call(bf16[2,320,2048]{2,1,0:T(8,128)(2,1)} %add_convert_fusion.second_ref, ...), custom_call_target="tpu_custom_call" | custom-call | flops 64424509440 | bytes 62914560 | tf_op jit(solution)/shard_map/feed_in/pallas_call | solution.py:1179
  314.5 106.4 %feed_out.1 = (bf16[2,4,320,2048]{3,2,1,0:T(8,128)(2,1)}, bf16[2048,2048]{1,0:T(8,128)(2,1)}, f32[2,320,2048]{2,1,0:T(8,128)}) custom-call(bf16[2,320,2048]{2,1,0:T(8,128)(2,1)} %cot_0.1, bf16[2,320,1024]{2,1,0:T(8,128)(2,1)} %get-tuple-element.107.cot_1, bf16[2,320,1024]{2,1,0:T(8,128)(2,1)} %collective-permute-done.3.cot_2, ...), custom_call_target="tpu_custom_call" | custom-call | flops 85899345920 | bytes 62914560 | tf_op jit(solution)/shard_map/feed_out/pallas_call | solution.py:1383
  423.2 2.4 fusion.26
  425.6 2.0 collective-permute-start.7
  427.7 2.0 collective-permute-start.6
  429.7 4.9 multiply_reduce_fusion.1
  434.6 4.6 multiply_reduce_fusion
  439.6 3.9 fusion.21
  443.5 1.5 copy-done.27
  445.0 1.6 convolution_convert_fusion
  447.9 1.4 copy.58.x_ref
  449.3 34.0 %feed_heads.1 = (bf16[1,8,320,128]{3,2,1,0:T(8,128)(2,1)S(1)}, bf16[2,320,1024]{2,1,0:T(8,128)(2,1)S(1)}, bf16[2,320,1024]{2,1,0:T(8,128)(2,1)S(1)}, bf16[2,320,...) custom-call(bf16[1,320,1024]{2,1,0:T(8,128)(2,1)S(1)} %copy.58.x_ref, ...), custom_call_target="tpu_custom_call" | custom-call | flops 34359738368 | bytes 16777216 | tf_op jit(solution)/shard_map/feed_heads/pallas_call | solution.py:1502
  484.1 1.6 collective-permute-start.10
  486.3 30.3 %attend_back.1.x_ref = bf16[3,2576,128]{2,1,0:T(8,128)(2,1)S(1)} custom-call(s32[2,5]{1,0:T(2,128)S(1)} %copy-done.13, s32[2,1,2560]{2,1,0:T(1,128)S(1)} %copy-done.11, bf16[3,2560,128]{2,1,0:T(8,128)(2,1)S(1)} %bitcast.137, bf16[3,2560,128]{2,1,0:T(8,128)(2,1)S(1)} %bitcast.138, bf16[1,2560,128]{2,1,0:T(8,128)(2,1)S(1)} %bitcast.139, ...), custom_call_target="tpu_custom_call" | custom-call | flops 34359738368 | bytes 5242880 | tf_op jit(solution)/shard_map/attend_back/pallas_call | solution.py:203
  518.4 2.6 fusion.11.refs_2_
  521.0 2.2 fusion.10.refs_3_
  523.2 54.0 %project_back.1 = (bf16[3,320,1024]{2,1,0:T(8,128)(2,1)}, f32[3,8,1024]{2,1,0:T(8,128)}, bf16[4,256,2048]{2,1,0:T(8,128)(2,1)}, bf16[4,128,2048]{2,1,0:T(8,128)(...) custom-call(bf16[3,2576,128]{2,1,0:T(8,128)(2,1)} %copy-done.18, ...), custom_call_target="tpu_custom_call" | custom-call | flops 34359738368 | bytes 16777216 | tf_op jit(solution)/shard_map/project_back/pallas_call | solution.py:844
  578.4 2.4 fusion.4.refs_1_
  580.8 1.4 fusion.25
  582.2 1.9 collective-permute-start.17
  584.1 1.3 collective-permute-start.15
  587.0 3.3 fusion.13
  590.3 7.6 %placed.3 = f32[1024,2048]{1,0:T(8,128)} custom-call(s32[1]{0:T(128)} %bitcast.74.me_ref, bf16[256,2048]{1,0:T(8,128)(2,1)S(1)} %copy-done.1, bf16[256,1024]{1,0:T(8,128)(2,1)} %collective-permute-done.6.one_x, bf16[256,1024]{1,0:T(8,128)(2,1)S(1)} %collective-permute-done.9.two_x, bf16[256,1024]{1,0:T(8,128)(2,1)S(1)} %copy-done.3, ...), custom_call_target="tpu_custom_call" | custom-call | bytes 16777216 | tf_op jit(solution)/shard_map/placed/pallas_call | solution.py:1945
  598.7 7.3 collective-permute-done.16.one_y
  606.8 102.6 %finish.1 = (bf16[4,64,2048]{2,1,0:T(8,128)(2,1)}, f32[8,2048]{1,0:T(8,128)}, f32[8,256]{1,0:T(8,128)}, f32[2,320,2048]{2,1,0:T(8,128)}, bf16[320,1024]{1,0:T(8,...) custom-call(bf16[4,2,4,32,2048]{4,3,2,1,0:T(8,128)(2,1)} %bitcast.179, ...), custom_call_target="tpu_custom_call" | custom-call | flops 68719476736 | bytes 67108864 | tf_op jit(solution)/shard_map/finish/pallas_call | solution.py:1858
  709.5 1.3 slice.182
  711.9 2.4 fusion.7
  716.7 2.4 fusion.9
  719.1 1.3 fusion.1
  720.4 1.7 pad_maximum_fusion
  723.2 7.6 %placed.2 = f32[2048,1024]{1,0:T(8,128)} custom-call(s32[1]{0:T(128)} %bitcast.74.me_ref, bf16[256,2048]{1,0:T(8,128)(2,1)S(1)} %copy-done, bf16[256,1024]{1,0:T(8,128)(2,1)} %collective-permute-done.14.refs_2_.one_x, bf16[256,1024]{1,0:T(8,128)(2,1)S(1)} %copy-done.5, bf16[256,1024]{1,0:T(8,128)(2,1)S(1)} %copy-done.7, ...), custom_call_target="tpu_custom_call" | custom-call | bytes 16777216 | tf_op jit(solution)/shard_map/placed/pallas_call | solution.py:1945
  730.8 2.4 copy.68
  (197 shorter events, 26.4 us)
Async XLA Ops:
  7.2 6.3 copy-start.51
  7.2 6.3 copy-start.49
  7.2 6.3 copy-start.50
  7.2 7.0 copy-start.36
  7.2 6.9 copy-start.37
  7.2 416.0 %reduce-scatter.3.cloned.1.call-start = ((), (), s32[]{:S(2)}) async-start(), calls=%async_computation.2 | async-start | bytes 9437184 | tf_op jit(solution)/shard_map/reduce_scatter | solution.py:2087
  123.7 69.6 %collective-permute-start.4 = (bf16[2,320,1024]{2,1,0:T(8,128)(2,1)}, bf16[2,320,1024]{2,1,0:T(8,128)(2,1)}, u32[]{:S(2)}, u32[]{:S(2)}) collective-permute-start(bf16[2,320,1024]{2,1,0:T(8,128)(2,1)} %get-tuple-element.107.cot_1), channel_id=1, source_target_pairs={{0,16},{8,24},{16,0},{24,8},{1,17},{9,25},{17,1},{25,9},{2,18},{10... | collective-permute-start | bytes 3932168 | tf_op jit(solution)/shard_map/ppermute | solution.py:1910
  126.2 67.1 %collective-permute-start.5 = (bf16[2,320,1024]{2,1,0:T(8,128)(2,1)}, bf16[2,320,1024]{2,1,0:T(8,128)(2,1)}, u32[]{:S(2)}, u32[]{:S(2)}) collective-permute-start(bf16[2,320,1024]{2,1,0:T(8,128)(2,1)} %get-tuple-element.108.cot_4), channel_id=1, source_target_pairs={{0,8},{8,0},{16,24},{24,16},{1,9},{9,1},{17,25},{25,17},{2,10},{10... | collective-permute-start | bytes 3932168 | tf_op jit(solution)/shard_map/ppermute | solution.py:1910
  126.3 5.9 copy-start.21
  129.1 31.2 %collective-permute-start.1 = (bf16[256,2048]{1,0:T(8,128)(2,1)}, bf16[256,2048]{1,0:T(8,128)(2,1)}, u32[]{:S(2)}, u32[]{:S(2)}) collective-permute-start(bf16[256,2048]{1,0:T(8,128)(2,1)} %get-tuple-element.190), channel_id=1, source_target_pairs={{4,6},{5,7},{12,14},{13,15},{20,22},{21,23},{28,30},{29,31}} | collective-permute-start | bytes 3145736 | tf_op jit(solution)/shard_map/ppermute | solution.py:1975
  130.8 7.6 %copy-start.14 = (bf16[3,8,320,128]{3,2,1,0:T(8,128)(2,1)S(1)}, bf16[3,8,320,128]{3,2,1,0:T(8,128)(2,1)}, u32[]{:S(2)}) copy-start(bf16[3,8,320,128]{3,2,1,0:T(8,128)(2,1)} %get-tuple-element.99) | copy-start | bytes 5898244
  130.8 32.7 %collective-permute-start = (bf16[256,2048]{1,0:T(8,128)(2,1)S(1)}, bf16[256,2048]{1,0:T(8,128)(2,1)}, u32[]{:S(2)}, u32[]{:S(2)}) collective-permute-start(bf16[256,2048]{1,0:T(8,128)(2,1)S(1)} %get-tuple-element.191), channel_id=1, source_target_pairs={{2,0},{3,1},{10,8},{11,9},{18,16},{19,17},{26,24},{27,25}} | collective-permute-start | bytes 3145736 | tf_op jit(solution)/shard_map/ppermute | solution.py:1975
  133.9 59.4 %collective-permute-start.3 = (bf16[2,320,1024]{2,1,0:T(8,128)(2,1)}, bf16[2,320,1024]{2,1,0:T(8,128)(2,1)}, u32[]{:S(2)}, u32[]{:S(2)}) collective-permute-start(bf16[2,320,1024]{2,1,0:T(8,128)(2,1)} %get-tuple-element.198), channel_id=1, source_target_pairs={{0,8},{8,0},{16,24},{24,16},{1,9},{9,1},{17,25},{25,17},{2,10},{10... | collective-permute-start | bytes 3932168 | tf_op jit(solution)/shard_map/ppermute | solution.py:1910
  136.0 23.2 %copy-start.10 = (s32[2,1,2560]{2,1,0:T(1,128)}, s32[2,1,2560]{2,1,0:T(1,128)S(1)}, u32[]{:S(2)}) copy-start(s32[2,1,2560]{2,1,0:T(1,128)S(1)} %broadcast_in_dim.16.start_ref) | copy-start | bytes 61444
  136.0 23.2 %copy-start.12 = (s32[2,5]{1,0:T(2,128)}, s32[2,5]{1,0:T(2,128)S(1)}, u32[]{:S(2)}) copy-start(s32[2,5]{1,0:T(2,128)S(1)} %and_select_fusion.first_ref) | copy-start | bytes 124
  160.3 33.0 %collective-permute-start.2 = (bf16[2,320,1024]{2,1,0:T(8,128)(2,1)}, bf16[2,320,1024]{2,1,0:T(8,128)(2,1)}, u32[]{:S(2)}, u32[]{:S(2)}) collective-permute-start(bf16[2,320,1024]{2,1,0:T(8,128)(2,1)} %get-tuple-element.199), channel_id=1, source_target_pairs={{0,16},{8,24},{16,0},{24,8},{1,17},{9,25},{17,1},{25,9},{2,18},{10... | collective-permute-start | bytes 3932168 | tf_op jit(solution)/shard_map/ppermute | solution.py:1910
  314.1 266.7 %reduce-scatter.5.cloned.1.call-start = ((), (), s32[]{:S(2)}) async-start(), calls=%async_computation.3 | async-start | bytes 9437184 | tf_op jit(solution)/shard_map/reduce_scatter | solution.py:2091
  421.0 8.7 %copy-start.39 = (f32[2048]{0:T(1024)S(1)}, f32[2048]{0:T(1024)}, u32[]{:S(2)}) copy-start(f32[2048]{0:T(1024)} %param.30) | copy-start | bytes 24580
  421.0 8.7 %copy-start.41 = (f32[2,320]{1,0:T(2,128)S(1)}, f32[2,320]{1,0:T(2,128)}, u32[]{:S(2)}) copy-start(f32[2,320]{1,0:T(2,128)} %copy-done.40) | copy-start | bytes 7684
  423.2 11.4 %slice-start.4 = ((s8[5242880]{0:T(1024)(128)(4,1)}), s8[4194304]{0:T(1024)(128)(4,1)S(1)}, s32[]{:S(2)}) async-start(s8[5242880]{0:T(1024)(128)(4,1)} %bitcast.144), calls=%async_computation.8 | async-start | bytes 8388608
  425.6 58.5 %collective-permute-start.9 = (bf16[256,1024]{1,0:T(8,128)(2,1)}, bf16[256,1024]{1,0:T(8,128)(2,1)S(1)}, u32[]{:S(2)}, u32[]{:S(2)}) collective-permute-start(bf16[256,1024]{1,0:T(8,128)(2,1)} %get-tuple-element.206), channel_id=1, source_target_pairs={{0,8},{8,0},{16,24},{24,16},{1,9},{9,1},{17,25},{25,17},{2,10},{10... | collective-permute-start | bytes 1572872 | tf_op jit(solution)/shard_map/ppermute | solution.py:1910
  425.6 58.5 %collective-permute-start.7 = (bf16[256,1024]{1,0:T(8,128)(2,1)}, bf16[256,1024]{1,0:T(8,128)(2,1)}, u32[]{:S(2)}, u32[]{:S(2)}) collective-permute-start(bf16[256,1024]{1,0:T(8,128)(2,1)} %get-tuple-element.206), channel_id=1, source_target_pairs={{0,16},{8,24},{16,0},{24,8},{1,17},{9,25},{17,1},{25,9},{2,18},{10... | collective-permute-start | bytes 1572872 | tf_op jit(solution)/shard_map/ppermute | solution.py:1910
  427.6 7.0 copy-start.45
  427.6 7.0 slice-start.5
  427.6 7.0 copy-start.43
  427.6 56.5 %collective-permute-start.8 = (bf16[256,1024]{1,0:T(8,128)(2,1)}, bf16[256,1024]{1,0:T(8,128)(2,1)S(1)}, u32[]{:S(2)}, u32[]{:S(2)}) collective-permute-start(bf16[256,1024]{1,0:T(8,128)(2,1)} %get-tuple-element.207), channel_id=1, source_target_pairs={{0,16},{8,24},{16,0},{24,8},{1,17},{9,25},{17,1},{25,9},{2,18},{10... | collective-permute-start | bytes 1572872 | tf_op jit(solution)/shard_map/ppermute | solution.py:1910
  427.7 56.4 %collective-permute-start.6 = (bf16[256,1024]{1,0:T(8,128)(2,1)}, bf16[256,1024]{1,0:T(8,128)(2,1)}, u32[]{:S(2)}, u32[]{:S(2)}) collective-permute-start(bf16[256,1024]{1,0:T(8,128)(2,1)} %get-tuple-element.207), channel_id=1, source_target_pairs={{0,8},{8,0},{16,24},{24,16},{1,9},{9,1},{17,25},{25,17},{2,10},{10... | collective-permute-start | bytes 1572872 | tf_op jit(solution)/shard_map/ppermute | solution.py:1910
  449.3 37.0 %copy-start.11 = (s32[2,1,2560]{2,1,0:T(1,128)S(1)}, s32[2,1,2560]{2,1,0:T(1,128)}, u32[]{:S(2)}) copy-start(s32[2,1,2560]{2,1,0:T(1,128)} %copy-done.10) | copy-start | bytes 61444
  449.3 37.0 %copy-start.13 = (s32[2,5]{1,0:T(2,128)S(1)}, s32[2,5]{1,0:T(2,128)}, u32[]{:S(2)}) copy-start(s32[2,5]{1,0:T(2,128)} %copy-done.12) | copy-start | bytes 124
  449.3 37.0 %copy-start.15 = (bf16[3,8,320,128]{3,2,1,0:T(8,128)(2,1)S(1)}, bf16[3,8,320,128]{3,2,1,0:T(8,128)(2,1)}, u32[]{:S(2)}) copy-start(bf16[3,8,320,128]{3,2,1,0:T(8,128)(2,1)} %get-tuple-element.99) | copy-start | bytes 5898244
  449.3 37.0 %copy-start.17 = (f32[2,64,2560]{2,1,0:T(8,128)S(1)}, f32[2,64,2560]{2,1,0:T(8,128)}, u32[]{:S(2)}) copy-start(f32[2,64,2560]{2,1,0:T(8,128)} %copy-done.16) | copy-start | bytes 3932164
  483.3 33.2 %copy-start.19 = (bf16[2,320,1024]{2,1,0:T(8,128)(2,1)}, bf16[2,320,1024]{2,1,0:T(8,128)(2,1)S(1)}, u32[]{:S(2)}) copy-start(bf16[2,320,1024]{2,1,0:T(8,128)(2,1)S(1)} %get-tuple-element.143.refs_0_) | copy-start | bytes 3932164
  484.1 32.5 %copy-start.2 = (bf16[256,1024]{1,0:T(8,128)(2,1)}, bf16[256,1024]{1,0:T(8,128)(2,1)S(1)}, u32[]{:S(2)}) copy-start(bf16[256,1024]{1,0:T(8,128)(2,1)S(1)} %collective-permute-done.8.one_y) | copy-start | bytes 1572868
  484.1 33.8 %collective-permute-start.10 = (bf16[2,320,1024]{2,1,0:T(8,128)(2,1)S(1)}, bf16[2,320,1024]{2,1,0:T(8,128)(2,1)S(1)}, u32[]{:S(2)}, u32[]{:S(2)}) collective-permute-start(bf16[2,320,1024]{2,1,0:T(8,128)(2,1)S(1)} %get-tuple-element.132), channel_id=1, source_target_pairs={{0,8},{8,0},{16,24},{24,16},{1,9},{9,1},{17,25},{25,17},{2,10},{10... | collective-permute-start | bytes 3932168 | tf_op jit(solution)/shard_map/ppermute | solution.py:1910
  485.7 32.2 %collective-permute-start.11 = (bf16[2,320,1024]{2,1,0:T(8,128)(2,1)S(1)}, bf16[2,320,1024]{2,1,0:T(8,128)(2,1)S(1)}, u32[]{:S(2)}, u32[]{:S(2)}) collective-permute-start(bf16[2,320,1024]{2,1,0:T(8,128)(2,1)S(1)} %get-tuple-element.133), channel_id=1, source_target_pairs={{0,16},{8,24},{16,0},{24,8},{1,17},{9,25},{17,1},{25,9},{2,18},{10... | collective-permute-start | bytes 3932168 | tf_op jit(solution)/shard_map/ppermute | solution.py:1910
  517.9 62.9 %collective-permute-start.12 = (bf16[256,1024]{1,0:T(8,128)(2,1)}, bf16[256,1024]{1,0:T(8,128)(2,1)}, u32[]{:S(2)}, u32[]{:S(2)}) collective-permute-start(bf16[256,1024]{1,0:T(8,128)(2,1)} %collective-permute-done.6.one_x), channel_id=1, source_target_pairs={{0,16},{8,24},{16,0},{24,8},{1,17},{9,25},{17,1},{25,9},{2,18},{10... | collective-permute-start | bytes 1572872 | tf_op jit(solution)/shard_map/ppermute | solution.py:1910
  518.4 62.3 %collective-permute-start.13 = (bf16[256,1024]{1,0:T(8,128)(2,1)}, bf16[256,1024]{1,0:T(8,128)(2,1)}, u32[]{:S(2)}, u32[]{:S(2)}) collective-permute-start(bf16[256,1024]{1,0:T(8,128)(2,1)} %collective-permute-done.7.two_y), channel_id=1, source_target_pairs={{0,8},{8,0},{16,24},{24,16},{1,9},{9,1},{17,25},{25,17},{2,10},{10... | collective-permute-start | bytes 1572872 | tf_op jit(solution)/shard_map/ppermute | solution.py:1910
  577.2 9.7 %copy-start.32 = (bf16[2,320,1024]{2,1,0:T(8,128)(2,1)S(1)}, bf16[2,320,1024]{2,1,0:T(8,128)(2,1)}, u32[]{:S(2)}) copy-start(bf16[2,320,1024]{2,1,0:T(8,128)(2,1)} %get-tuple-element.149) | copy-start | bytes 3932164
  577.2 9.7 %copy-start.35 = (bf16[320,1024]{1,0:T(8,128)(2,1)S(1)}, bf16[320,1024]{1,0:T(8,128)(2,1)}, u32[]{:S(2)}) copy-start(bf16[320,1024]{1,0:T(8,128)(2,1)} %get-tuple-element.147) | copy-start | bytes 1966084
  580.8 6.2 copy-start.34
  582.2 15.7 %collective-permute-start.17 = (bf16[256,1024]{1,0:T(8,128)(2,1)S(1)}, bf16[256,1024]{1,0:T(8,128)(2,1)S(1)}, u32[]{:S(2)}, u32[]{:S(2)}) collective-permute-start(bf16[256,1024]{1,0:T(8,128)(2,1)S(1)} %get-tuple-element.204), channel_id=1, source_target_pairs={{0,8},{8,0},{16,24},{24,16},{1,9},{9,1},{17,25},{25,17},{2,10},{10... | collective-permute-start | bytes 1572872 | tf_op jit(solution)/shard_map/ppermute | solution.py:1910
  584.1 14.6 %collective-permute-start.15 = (bf16[256,1024]{1,0:T(8,128)(2,1)S(1)}, bf16[256,1024]{1,0:T(8,128)(2,1)}, u32[]{:S(2)}, u32[]{:S(2)}) collective-permute-start(bf16[256,1024]{1,0:T(8,128)(2,1)S(1)} %get-tuple-element.204), channel_id=1, source_target_pairs={{0,16},{8,24},{16,0},{24,8},{1,17},{9,25},{17,1},{25,9},{2,18},{10... | collective-permute-start | bytes 1572872 | tf_op jit(solution)/shard_map/ppermute | solution.py:1910
  585.4 20.5 %collective-permute-start.16 = (bf16[256,1024]{1,0:T(8,128)(2,1)S(1)}, bf16[256,1024]{1,0:T(8,128)(2,1)S(1)}, u32[]{:S(2)}, u32[]{:S(2)}) collective-permute-start(bf16[256,1024]{1,0:T(8,128)(2,1)S(1)} %get-tuple-element.205), channel_id=1, source_target_pairs={{0,16},{8,24},{16,0},{24,8},{1,17},{9,25},{17,1},{25,9},{2,18},{10... | collective-permute-start | bytes 1572872 | tf_op jit(solution)/shard_map/ppermute | solution.py:1910
  586.1 20.7 %collective-permute-start.14 = (bf16[256,1024]{1,0:T(8,128)(2,1)S(1)}, bf16[256,1024]{1,0:T(8,128)(2,1)}, u32[]{:S(2)}, u32[]{:S(2)}) collective-permute-start(bf16[256,1024]{1,0:T(8,128)(2,1)S(1)} %get-tuple-element.205), channel_id=1, source_target_pairs={{0,8},{8,0},{16,24},{24,16},{1,9},{9,1},{17,25},{25,17},{2,10},{10... | collective-permute-start | bytes 1572872 | tf_op jit(solution)/shard_map/ppermute | solution.py:1910
  709.5 7.2 copy-start.31
  710.8 8.2 %slice-start.2 = ((s8[5242880]{0:T(1024)(128)(4,1)}), s8[4194304]{0:T(1024)(128)(4,1)S(1)}, s32[]{:S(2)}) async-start(s8[5242880]{0:T(1024)(128)(4,1)} %bitcast.142), calls=%async_computation.6 | async-start | bytes 8388608
  722.2 8.6 %slice-start.6 = ((s8[5242880]{0:T(1024)(128)(4,1)}), s8[4194304]{0:T(1024)(128)(4,1)S(1)}, s32[]{:S(2)}) async-start(s8[5242880]{0:T(1024)(128)(4,1)} %bitcast.148), calls=%async_computation.10 | async-start | bytes 8388608
  723.2 7.6 %slice-start.7 = ((s8[5242880]{0:T(1024)(128)(4,1)}), s8[1048576]{0:T(1024)(128)(4,1)S(1)}, s32[]{:S(2)}) async-start(s8[5242880]{0:T(1024)(128)(4,1)} %bitcast.148), calls=%async_computation.11 | async-start | bytes 2097152
  (32 other events, 89.7 us)
Sparse Core Ops, SparseCore 0:
  314.2 89.3 reduce-scatter.2
  421.1 100.2 reduce-scatter.4

commit v9 on v8

--- a/solution.py
+++ b/solution.py
@@ -1724,18 +1724,17 @@
     normed_grad()
     load_middle.wait()
     sums[...] = jnp.zeros(sums.shape, F32)
-    norm_back(0, 0, tiles)
     saved_rows = [
         pltpu.make_async_copy(result.at[s], input_grad_ref.at[s], local.at[7 + s]) for s in range(2)
     ]
-    saved_rows[0].start()
     sends[1].wait_recv()
     add(dp_y, 0, 1)
     sends[4].start()
     sends[3].wait_recv()
     add(dp_x, 1, 3)
     sends[5].start()
-    norm_back(1, 0, tiles // 2)
+    norm_back(0, 0, tiles)
+    saved_rows[0].start()
     sends[0].wait_recv()
     add(dp, 0, 0)
     sends[2].wait_recv()
@@ -1773,6 +1772,8 @@
         for sends_now, _, _, copy in legs:
             pl.when(sends_now)(copy.start)
         if step == 1:
+            norm_back(1, 0, tiles // 2)
+        if step == 2:
             norm_back(1, tiles // 2, tiles)
             saved_rows[1].start()
             norms[...] = norms_ref[...]

time: 749 us -> 749 us (level)
  transfers between devices with their start and end apart: 20 -> 20, of which waited for: 2 -> 2; matrix products, arithmetic and copies ran while one was open for 7% -> 7% of each run, Pallas kernels for 37% -> 36%
where the time goes in v9:
time: 749 us; the launch traced here: 739 us
  Pallas kernels  608 us (81%)
  other arithmetic  43.5 us (6%)
  local copies, waits for them, and re-layouts  35.2 us (5%)
  starting transfers between devices  21.4 us (3%)
  between operations  15.4 us (2%)
  waiting for transfers between devices  9.95 us (1%)
    pallas_call x1, Pallas kernels, feed_in(): pl.pallas_call(partial(feed_in_kernel, tuple(up_late)), in_specs=[anywher...  123 us
    pallas_call x1, Pallas kernels, feed_out(): pl.pallas_call(feed_out_kernel, in_specs=[anywhere] * 11, out_specs=[anyw...  107 us
    pallas_call x1, Pallas kernels, front(): pl.pallas_call(front_kernel, in_specs=[anywhere, vmem, vmem] + [anywhere]...  106 us
    pallas_call x1, Pallas kernels, finish(): pl.pallas_call(partial(finish_kernel, tuple((way for way, _ in carried)))...  103 us
    pallas_call x1, Pallas kernels, project_back(): pl.pallas_call(partial(project_back_kernel, tuple((way for way, _ in carr...  54 us
    pallas_call x1, Pallas kernels, feed_heads(): pl.pallas_call(feed_heads_kernel, in_specs=[pl.BlockSpec(memory_space=plt...  34.1 us
    pallas_call x1, Pallas kernels, attend_back(): pl.pallas_call(attend_back_kernel, grid_spec=pltpu.PrefetchScalarGridSpec...  28.4 us
    pallas_call x1, Pallas kernels, attend(): pl.pallas_call(attend_kernel, grid_spec=pltpu.PrefetchScalarGridSpec(num_...  19.4 us
  transfers between devices with their start and end apart: 20, of which 2 were waited for; matrix products, arithmetic and copies ran while one was open for 7% of the time, Pallas kernels for 36%

profile of v9, /device:TPU:0, one launch (start us, length us, event | category | flops | bytes accessed | tf_op | source)
XLA Modules:
  0.0 739.4 jit_solution(10042696997698895129)
XLA Ops:
  10.7 1.3 constant_dynamic-slice_fusion.3
  12.0 1.4 copy.64
  15.9 1.5 pad_maximum_fusion.1.masks_ref
  17.4 106.3 %front.1 = (bf16[4,2,4,32,2048]{4,3,2,1,0:T(8,128)(2,1)}, bf16[4,2,4,16,2048]{4,3,2,1,0:T(8,128)(2,1)}, bf16[4,2,4,16,2048]{4,3,2,1,0:T(8,128)(2,1)}, f32[3,8,10...) custom-call(bf16[2,320,2048]{2,1,0:T(8,128)(2,1)} %inputs_ref.3, ...), custom_call_target="tpu_custom_call" | custom-call | flops 68719476736 | bytes 67108864 | tf_op jit(solution)/shard_map/front/pallas_call | solution.py:679
  123.7 2.5 collective-permute-start.4
  126.3 2.9 constant_dynamic-slice_fusion.1
  129.1 1.6 collective-permute-start.1
  130.8 1.4 collective-permute-start
  132.2 1.8 fusion.22
  133.9 1.9 collective-permute-start.3
  136.0 2.3 constant_dynamic-slice_fusion.down_ref
  138.4 19.4 %attend.1 = (bf16[1,2560,128]{2,1,0:T(8,128)(2,1)S(1)}, f32[2,64,2560]{2,1,0:T(8,128)S(1)}, f32[2,1,2560]{2,1,0:T(1,128)S(1)}) custom-call(s32[2,5]{1,0:T(2,128)S(1)} %and_select_fusion.first_ref, s32[2,1,2560]{2,1,0:T(1,128)S(1)} %broadcast_in_dim.16.start_ref, bf16[3,2560,128]{2,1,0:T(8,128)(2,1)S(1)} %bitcast.135, bf16[3,2560,128]{2,1,0:T(8,128)(2,1)S(1)} %bitcast.136), custom_call_target="tpu_custom_call" | custom-call | flops 17179869184 | bytes 5242880 | tf_op jit(solution)/shard_map/attend/pallas_call | solution.py:108
  158.9 4.6 collective-permute-done.refs_0_
  163.5 18.6 %attended_back.1 = bf16[1,320,1024]{2,1,0:T(8,128)(2,1)S(1)} custom-call(bf16[1,2560,128]{2,1,0:T(8,128)(2,1)S(1)} %get-tuple-element.104.x_ref), custom_call_target="tpu_custom_call" | custom-call | flops 17179869184 | bytes 16777216 | tf_op jit(solution)/shard_map/attended_back/pallas_call | solution.py:906
  182.5 4.5 fusion.30
  189.4 2.4 add_convert_fusion.second_ref
  191.9 122.6 %feed_in.1 = (bf16[2,4,320,2048]{3,2,1,0:T(8,128)(2,1)}, f32[2,4,320,2048]{3,2,1,0:T(8,128)}, bf16[2,4,320,2048]{3,2,1,0:T(8,128)(2,1)}, bf16[2048,2048]{1,0:T(8...) custom-call(bf16[2,320,2048]{2,1,0:T(8,128)(2,1)} %add_convert_fusion.second_ref, ...), custom_call_target="tpu_custom_call" | custom-call | flops 64424509440 | bytes 62914560 | tf_op jit(solution)/shard_map/feed_in/pallas_call | solution.py:1179
  314.9 106.8 %feed_out.1 = (bf16[2,4,320,2048]{3,2,1,0:T(8,128)(2,1)}, bf16[2048,2048]{1,0:T(8,128)(2,1)}, f32[2,320,2048]{2,1,0:T(8,128)}) custom-call(bf16[2,320,2048]{2,1,0:T(8,128)(2,1)} %cot_0.1, bf16[2,320,1024]{2,1,0:T(8,128)(2,1)} %get-tuple-element.107.cot_1, bf16[2,320,1024]{2,1,0:T(8,128)(2,1)} %collective-permute-done.3.cot_2, ...), custom_call_target="tpu_custom_call" | custom-call | flops 85899345920 | bytes 62914560 | tf_op jit(solution)/shard_map/feed_out/pallas_call | solution.py:1383
  424.0 2.4 fusion.26
  426.4 2.0 collective-permute-start.7
  428.4 2.0 collective-permute-start.6
  430.4 4.9 multiply_reduce_fusion.1
  435.4 4.6 multiply_reduce_fusion
  440.3 3.9 fusion.21
  444.2 1.5 copy-done.27
  445.7 1.6 convolution_convert_fusion
  448.6 1.4 copy.58.x_ref
  450.1 34.1 %feed_heads.1 = (bf16[1,8,320,128]{3,2,1,0:T(8,128)(2,1)S(1)}, bf16[2,320,1024]{2,1,0:T(8,128)(2,1)S(1)}, bf16[2,320,1024]{2,1,0:T(8,128)(2,1)S(1)}, bf16[2,320,...) custom-call(bf16[1,320,1024]{2,1,0:T(8,128)(2,1)S(1)} %copy.58.x_ref, ...), custom_call_target="tpu_custom_call" | custom-call | flops 34359738368 | bytes 16777216 | tf_op jit(solution)/shard_map/feed_heads/pallas_call | solution.py:1502
  485.2 1.8 collective-permute-start.11
  487.0 28.4 %attend_back.1.x_ref = bf16[3,2576,128]{2,1,0:T(8,128)(2,1)S(1)} custom-call(s32[2,5]{1,0:T(2,128)S(1)} %copy-done.13, s32[2,1,2560]{2,1,0:T(1,128)S(1)} %copy-done.11, bf16[3,2560,128]{2,1,0:T(8,128)(2,1)S(1)} %bitcast.137, bf16[3,2560,128]{2,1,0:T(8,128)(2,1)S(1)} %bitcast.138, bf16[1,2560,128]{2,1,0:T(8,128)(2,1)S(1)} %bitcast.139, ...), custom_call_target="tpu_custom_call" | custom-call | flops 34359738368 | bytes 5242880 | tf_op jit(solution)/shard_map/attend_back/pallas_call | solution.py:203
  517.0 2.8 collective-permute-start.13
  519.8 2.2 fusion.11.refs_2_
  521.9 2.2 fusion.10.refs_3_
  524.1 54.0 %project_back.1 = (bf16[3,320,1024]{2,1,0:T(8,128)(2,1)}, f32[3,8,1024]{2,1,0:T(8,128)}, bf16[4,256,2048]{2,1,0:T(8,128)(2,1)}, bf16[4,128,2048]{2,1,0:T(8,128)(...) custom-call(bf16[3,2576,128]{2,1,0:T(8,128)(2,1)} %copy-done.18, ...), custom_call_target="tpu_custom_call" | custom-call | flops 34359738368 | bytes 16777216 | tf_op jit(solution)/shard_map/project_back/pallas_call | solution.py:844
  579.3 2.4 fusion.4.refs_1_
  581.7 1.4 fusion.25
  585.3 1.9 collective-permute-start.14
  587.9 3.3 fusion.13
  591.2 7.6 %placed.3 = f32[1024,2048]{1,0:T(8,128)} custom-call(s32[1]{0:T(128)} %bitcast.74.me_ref, bf16[256,2048]{1,0:T(8,128)(2,1)S(1)} %copy-done.1, bf16[256,1024]{1,0:T(8,128)(2,1)} %collective-permute-done.6.one_x, bf16[256,1024]{1,0:T(8,128)(2,1)S(1)} %collective-permute-done.9.two_x, bf16[256,1024]{1,0:T(8,128)(2,1)S(1)} %copy-done.3, ...), custom_call_target="tpu_custom_call" | custom-call | bytes 16777216 | tf_op jit(solution)/shard_map/placed/pallas_call | solution.py:1946
  599.6 5.2 collective-permute-done.16.one_y
  605.7 102.7 %finish.1 = (bf16[4,64,2048]{2,1,0:T(8,128)(2,1)}, f32[8,2048]{1,0:T(8,128)}, f32[8,256]{1,0:T(8,128)}, f32[2,320,2048]{2,1,0:T(8,128)}, bf16[320,1024]{1,0:T(8,...) custom-call(bf16[4,2,4,32,2048]{4,3,2,1,0:T(8,128)(2,1)} %bitcast.179, ...), custom_call_target="tpu_custom_call" | custom-call | flops 68719476736 | bytes 67108864 | tf_op jit(solution)/shard_map/finish/pallas_call | solution.py:1859
  708.4 1.3 slice.182
  710.9 2.4 fusion.7
  715.6 2.4 fusion.9
  718.0 1.3 fusion.1
  719.4 1.7 pad_maximum_fusion
  722.1 7.6 %placed.2 = f32[2048,1024]{1,0:T(8,128)} custom-call(s32[1]{0:T(128)} %bitcast.74.me_ref, bf16[256,2048]{1,0:T(8,128)(2,1)S(1)} %copy-done, bf16[256,1024]{1,0:T(8,128)(2,1)} %collective-permute-done.14.refs_2_.one_x, bf16[256,1024]{1,0:T(8,128)(2,1)S(1)} %copy-done.5, bf16[256,1024]{1,0:T(8,128)(2,1)S(1)} %copy-done.7, ...), custom_call_target="tpu_custom_call" | custom-call | bytes 16777216 | tf_op jit(solution)/shard_map/placed/pallas_call | solution.py:1946
  729.7 2.4 copy.68
  (197 shorter events, 27.0 us)
Async XLA Ops:
  7.2 6.3 copy-start.51
  7.2 6.3 copy-start.49
  7.2 6.3 copy-start.50
  7.2 7.0 copy-start.36
  7.2 6.9 copy-start.37
  7.2 416.8 %reduce-scatter.3.cloned.1.call-start = ((), (), s32[]{:S(2)}) async-start(), calls=%async_computation.2 | async-start | bytes 9437184 | tf_op jit(solution)/shard_map/reduce_scatter | solution.py:2088
  123.7 68.2 %collective-permute-start.4 = (bf16[2,320,1024]{2,1,0:T(8,128)(2,1)}, bf16[2,320,1024]{2,1,0:T(8,128)(2,1)}, u32[]{:S(2)}, u32[]{:S(2)}) collective-permute-start(bf16[2,320,1024]{2,1,0:T(8,128)(2,1)} %get-tuple-element.107.cot_1), channel_id=1, source_target_pairs={{0,16},{8,24},{16,0},{24,8},{1,17},{9,25},{17,1},{25,9},{2,18},{10... | collective-permute-start | bytes 3932168 | tf_op jit(solution)/shard_map/ppermute | solution.py:1911
  126.2 65.7 %collective-permute-start.5 = (bf16[2,320,1024]{2,1,0:T(8,128)(2,1)}, bf16[2,320,1024]{2,1,0:T(8,128)(2,1)}, u32[]{:S(2)}, u32[]{:S(2)}) collective-permute-start(bf16[2,320,1024]{2,1,0:T(8,128)(2,1)} %get-tuple-element.108.cot_4), channel_id=1, source_target_pairs={{0,8},{8,0},{16,24},{24,16},{1,9},{9,1},{17,25},{25,17},{2,10},{10... | collective-permute-start | bytes 3932168 | tf_op jit(solution)/shard_map/ppermute | solution.py:1911
  129.1 29.8 %collective-permute-start.1 = (bf16[256,2048]{1,0:T(8,128)(2,1)}, bf16[256,2048]{1,0:T(8,128)(2,1)}, u32[]{:S(2)}, u32[]{:S(2)}) collective-permute-start(bf16[256,2048]{1,0:T(8,128)(2,1)} %get-tuple-element.190), channel_id=1, source_target_pairs={{4,6},{5,7},{12,14},{13,15},{20,22},{21,23},{28,30},{29,31}} | collective-permute-start | bytes 3145736 | tf_op jit(solution)/shard_map/ppermute | solution.py:1976
  130.8 7.6 %copy-start.14 = (bf16[3,8,320,128]{3,2,1,0:T(8,128)(2,1)S(1)}, bf16[3,8,320,128]{3,2,1,0:T(8,128)(2,1)}, u32[]{:S(2)}) copy-start(bf16[3,8,320,128]{3,2,1,0:T(8,128)(2,1)} %get-tuple-element.99) | copy-start | bytes 5898244
  130.8 32.7 %collective-permute-start = (bf16[256,2048]{1,0:T(8,128)(2,1)S(1)}, bf16[256,2048]{1,0:T(8,128)(2,1)}, u32[]{:S(2)}, u32[]{:S(2)}) collective-permute-start(bf16[256,2048]{1,0:T(8,128)(2,1)S(1)} %get-tuple-element.191), channel_id=1, source_target_pairs={{2,0},{3,1},{10,8},{11,9},{18,16},{19,17},{26,24},{27,25}} | collective-permute-start | bytes 3145736 | tf_op jit(solution)/shard_map/ppermute | solution.py:1976
  133.9 57.9 %collective-permute-start.3 = (bf16[2,320,1024]{2,1,0:T(8,128)(2,1)}, bf16[2,320,1024]{2,1,0:T(8,128)(2,1)}, u32[]{:S(2)}, u32[]{:S(2)}) collective-permute-start(bf16[2,320,1024]{2,1,0:T(8,128)(2,1)} %get-tuple-element.198), channel_id=1, source_target_pairs={{0,8},{8,0},{16,24},{24,16},{1,9},{9,1},{17,25},{25,17},{2,10},{10... | collective-permute-start | bytes 3932168 | tf_op jit(solution)/shard_map/ppermute | solution.py:1911
  136.0 21.8 %copy-start.10 = (s32[2,1,2560]{2,1,0:T(1,128)}, s32[2,1,2560]{2,1,0:T(1,128)S(1)}, u32[]{:S(2)}) copy-start(s32[2,1,2560]{2,1,0:T(1,128)S(1)} %broadcast_in_dim.16.start_ref) | copy-start | bytes 61444
  136.0 21.7 %copy-start.12 = (s32[2,5]{1,0:T(2,128)}, s32[2,5]{1,0:T(2,128)S(1)}, u32[]{:S(2)}) copy-start(s32[2,5]{1,0:T(2,128)S(1)} %and_select_fusion.first_ref) | copy-start | bytes 124
  158.9 33.0 %collective-permute-start.2 = (bf16[2,320,1024]{2,1,0:T(8,128)(2,1)}, bf16[2,320,1024]{2,1,0:T(8,128)(2,1)}, u32[]{:S(2)}, u32[]{:S(2)}) collective-permute-start(bf16[2,320,1024]{2,1,0:T(8,128)(2,1)} %get-tuple-element.199), channel_id=1, source_target_pairs={{0,16},{8,24},{16,0},{24,8},{1,17},{9,25},{17,1},{25,9},{2,18},{10... | collective-permute-start | bytes 3932168 | tf_op jit(solution)/shard_map/ppermute | solution.py:1911
  314.5 267.2 %reduce-scatter.5.cloned.1.call-start = ((), (), s32[]{:S(2)}) async-start(), calls=%async_computation.3 | async-start | bytes 9437184 | tf_op jit(solution)/shard_map/reduce_scatter | solution.py:2092
  421.7 8.7 %copy-start.39 = (f32[2048]{0:T(1024)S(1)}, f32[2048]{0:T(1024)}, u32[]{:S(2)}) copy-start(f32[2048]{0:T(1024)} %param.30) | copy-start | bytes 24580
  421.8 8.7 %copy-start.41 = (f32[2,320]{1,0:T(2,128)S(1)}, f32[2,320]{1,0:T(2,128)}, u32[]{:S(2)}) copy-start(f32[2,320]{1,0:T(2,128)} %copy-done.40) | copy-start | bytes 7684
  424.0 11.4 %slice-start.4 = ((s8[5242880]{0:T(1024)(128)(4,1)}), s8[4194304]{0:T(1024)(128)(4,1)S(1)}, s32[]{:S(2)}) async-start(s8[5242880]{0:T(1024)(128)(4,1)} %bitcast.144), calls=%async_computation.8 | async-start | bytes 8388608
  426.4 58.5 %collective-permute-start.9 = (bf16[256,1024]{1,0:T(8,128)(2,1)}, bf16[256,1024]{1,0:T(8,128)(2,1)S(1)}, u32[]{:S(2)}, u32[]{:S(2)}) collective-permute-start(bf16[256,1024]{1,0:T(8,128)(2,1)} %get-tuple-element.206), channel_id=1, source_target_pairs={{0,8},{8,0},{16,24},{24,16},{1,9},{9,1},{17,25},{25,17},{2,10},{10... | collective-permute-start | bytes 1572872 | tf_op jit(solution)/shard_map/ppermute | solution.py:1911
  426.4 58.5 %collective-permute-start.7 = (bf16[256,1024]{1,0:T(8,128)(2,1)}, bf16[256,1024]{1,0:T(8,128)(2,1)}, u32[]{:S(2)}, u32[]{:S(2)}) collective-permute-start(bf16[256,1024]{1,0:T(8,128)(2,1)} %get-tuple-element.206), channel_id=1, source_target_pairs={{0,16},{8,24},{16,0},{24,8},{1,17},{9,25},{17,1},{25,9},{2,18},{10... | collective-permute-start | bytes 1572872 | tf_op jit(solution)/shard_map/ppermute | solution.py:1911
  428.4 7.0 copy-start.45
  428.4 7.0 slice-start.5
  428.4 7.0 copy-start.43
  428.4 56.5 %collective-permute-start.8 = (bf16[256,1024]{1,0:T(8,128)(2,1)}, bf16[256,1024]{1,0:T(8,128)(2,1)S(1)}, u32[]{:S(2)}, u32[]{:S(2)}) collective-permute-start(bf16[256,1024]{1,0:T(8,128)(2,1)} %get-tuple-element.207), channel_id=1, source_target_pairs={{0,16},{8,24},{16,0},{24,8},{1,17},{9,25},{17,1},{25,9},{2,18},{10... | collective-permute-start | bytes 1572872 | tf_op jit(solution)/shard_map/ppermute | solution.py:1911
  428.4 56.5 %collective-permute-start.6 = (bf16[256,1024]{1,0:T(8,128)(2,1)}, bf16[256,1024]{1,0:T(8,128)(2,1)}, u32[]{:S(2)}, u32[]{:S(2)}) collective-permute-start(bf16[256,1024]{1,0:T(8,128)(2,1)} %get-tuple-element.207), channel_id=1, source_target_pairs={{0,8},{8,0},{16,24},{24,16},{1,9},{9,1},{17,25},{25,17},{2,10},{10... | collective-permute-start | bytes 1572872 | tf_op jit(solution)/shard_map/ppermute | solution.py:1911
  450.0 37.0 %copy-start.11 = (s32[2,1,2560]{2,1,0:T(1,128)S(1)}, s32[2,1,2560]{2,1,0:T(1,128)}, u32[]{:S(2)}) copy-start(s32[2,1,2560]{2,1,0:T(1,128)} %copy-done.10) | copy-start | bytes 61444
  450.0 37.0 %copy-start.13 = (s32[2,5]{1,0:T(2,128)S(1)}, s32[2,5]{1,0:T(2,128)}, u32[]{:S(2)}) copy-start(s32[2,5]{1,0:T(2,128)} %copy-done.12) | copy-start | bytes 124
  450.0 37.0 %copy-start.15 = (bf16[3,8,320,128]{3,2,1,0:T(8,128)(2,1)S(1)}, bf16[3,8,320,128]{3,2,1,0:T(8,128)(2,1)}, u32[]{:S(2)}) copy-start(bf16[3,8,320,128]{3,2,1,0:T(8,128)(2,1)} %get-tuple-element.99) | copy-start | bytes 5898244
  450.0 37.0 %copy-start.17 = (f32[2,64,2560]{2,1,0:T(8,128)S(1)}, f32[2,64,2560]{2,1,0:T(8,128)}, u32[]{:S(2)}) copy-start(f32[2,64,2560]{2,1,0:T(8,128)} %copy-done.16) | copy-start | bytes 3932164
  484.2 31.2 %copy-start.19 = (bf16[2,320,1024]{2,1,0:T(8,128)(2,1)}, bf16[2,320,1024]{2,1,0:T(8,128)(2,1)S(1)}, u32[]{:S(2)}) copy-start(bf16[2,320,1024]{2,1,0:T(8,128)(2,1)S(1)} %get-tuple-element.143.refs_0_) | copy-start | bytes 3932164
  484.9 30.5 %copy-start.2 = (bf16[256,1024]{1,0:T(8,128)(2,1)}, bf16[256,1024]{1,0:T(8,128)(2,1)S(1)}, u32[]{:S(2)}) copy-start(bf16[256,1024]{1,0:T(8,128)(2,1)S(1)} %collective-permute-done.8.one_y) | copy-start | bytes 1572868
  484.9 31.8 %collective-permute-start.10 = (bf16[2,320,1024]{2,1,0:T(8,128)(2,1)S(1)}, bf16[2,320,1024]{2,1,0:T(8,128)(2,1)S(1)}, u32[]{:S(2)}, u32[]{:S(2)}) collective-permute-start(bf16[2,320,1024]{2,1,0:T(8,128)(2,1)S(1)} %get-tuple-element.132), channel_id=1, source_target_pairs={{0,8},{8,0},{16,24},{24,16},{1,9},{9,1},{17,25},{25,17},{2,10},{10... | collective-permute-start | bytes 3932168 | tf_op jit(solution)/shard_map/ppermute | solution.py:1911
  485.2 31.5 %collective-permute-start.11 = (bf16[2,320,1024]{2,1,0:T(8,128)(2,1)S(1)}, bf16[2,320,1024]{2,1,0:T(8,128)(2,1)S(1)}, u32[]{:S(2)}, u32[]{:S(2)}) collective-permute-start(bf16[2,320,1024]{2,1,0:T(8,128)(2,1)S(1)} %get-tuple-element.133), channel_id=1, source_target_pairs={{0,16},{8,24},{16,0},{24,8},{1,17},{9,25},{17,1},{25,9},{2,18},{10... | collective-permute-start | bytes 3932168 | tf_op jit(solution)/shard_map/ppermute | solution.py:1911
  516.7 7.4 %copy-start.33 = (bf16[2,320,1024]{2,1,0:T(8,128)(2,1)}, bf16[2,320,1024]{2,1,0:T(8,128)(2,1)S(1)}, u32[]{:S(2)}) copy-start(bf16[2,320,1024]{2,1,0:T(8,128)(2,1)S(1)} %collective-permute-done.10) | copy-start | bytes 3932164
  516.7 65.0 %collective-permute-start.12 = (bf16[256,1024]{1,0:T(8,128)(2,1)}, bf16[256,1024]{1,0:T(8,128)(2,1)}, u32[]{:S(2)}, u32[]{:S(2)}) collective-permute-start(bf16[256,1024]{1,0:T(8,128)(2,1)} %collective-permute-done.6.one_x), channel_id=1, source_target_pairs={{0,16},{8,24},{16,0},{24,8},{1,17},{9,25},{17,1},{25,9},{2,18},{10... | collective-permute-start | bytes 1572872 | tf_op jit(solution)/shard_map/ppermute | solution.py:1911
  517.0 64.7 %collective-permute-start.13 = (bf16[256,1024]{1,0:T(8,128)(2,1)}, bf16[256,1024]{1,0:T(8,128)(2,1)}, u32[]{:S(2)}, u32[]{:S(2)}) collective-permute-start(bf16[256,1024]{1,0:T(8,128)(2,1)} %collective-permute-done.7.two_y), channel_id=1, source_target_pairs={{0,8},{8,0},{16,24},{24,16},{1,9},{9,1},{17,25},{25,17},{2,10},{10... | collective-permute-start | bytes 1572872 | tf_op jit(solution)/shard_map/ppermute | solution.py:1911
  578.1 9.7 %copy-start.32 = (bf16[2,320,1024]{2,1,0:T(8,128)(2,1)S(1)}, bf16[2,320,1024]{2,1,0:T(8,128)(2,1)}, u32[]{:S(2)}) copy-start(bf16[2,320,1024]{2,1,0:T(8,128)(2,1)} %get-tuple-element.149) | copy-start | bytes 3932164
  578.2 9.7 %copy-start.35 = (bf16[320,1024]{1,0:T(8,128)(2,1)S(1)}, bf16[320,1024]{1,0:T(8,128)(2,1)}, u32[]{:S(2)}) copy-start(bf16[320,1024]{1,0:T(8,128)(2,1)} %get-tuple-element.147) | copy-start | bytes 1966084
  581.7 6.2 copy-start.34
  583.1 15.7 %collective-permute-start.17 = (bf16[256,1024]{1,0:T(8,128)(2,1)S(1)}, bf16[256,1024]{1,0:T(8,128)(2,1)S(1)}, u32[]{:S(2)}, u32[]{:S(2)}) collective-permute-start(bf16[256,1024]{1,0:T(8,128)(2,1)S(1)} %get-tuple-element.204), channel_id=1, source_target_pairs={{0,8},{8,0},{16,24},{24,16},{1,9},{9,1},{17,25},{25,17},{2,10},{10... | collective-permute-start | bytes 1572872 | tf_op jit(solution)/shard_map/ppermute | solution.py:1911
  583.2 16.4 %collective-permute-start.15 = (bf16[256,1024]{1,0:T(8,128)(2,1)S(1)}, bf16[256,1024]{1,0:T(8,128)(2,1)}, u32[]{:S(2)}, u32[]{:S(2)}) collective-permute-start(bf16[256,1024]{1,0:T(8,128)(2,1)S(1)} %get-tuple-element.204), channel_id=1, source_target_pairs={{0,16},{8,24},{16,0},{24,8},{1,17},{9,25},{17,1},{25,9},{2,18},{10... | collective-permute-start | bytes 1572872 | tf_op jit(solution)/shard_map/ppermute | solution.py:1911
  584.3 20.6 %collective-permute-start.16 = (bf16[256,1024]{1,0:T(8,128)(2,1)S(1)}, bf16[256,1024]{1,0:T(8,128)(2,1)S(1)}, u32[]{:S(2)}, u32[]{:S(2)}) collective-permute-start(bf16[256,1024]{1,0:T(8,128)(2,1)S(1)} %get-tuple-element.205), channel_id=1, source_target_pairs={{0,16},{8,24},{16,0},{24,8},{1,17},{9,25},{17,1},{25,9},{2,18},{10... | collective-permute-start | bytes 1572872 | tf_op jit(solution)/shard_map/ppermute | solution.py:1911
  585.3 20.4 %collective-permute-start.14 = (bf16[256,1024]{1,0:T(8,128)(2,1)S(1)}, bf16[256,1024]{1,0:T(8,128)(2,1)}, u32[]{:S(2)}, u32[]{:S(2)}) collective-permute-start(bf16[256,1024]{1,0:T(8,128)(2,1)S(1)} %get-tuple-element.205), channel_id=1, source_target_pairs={{0,8},{8,0},{16,24},{24,16},{1,9},{9,1},{17,25},{25,17},{2,10},{10... | collective-permute-start | bytes 1572872 | tf_op jit(solution)/shard_map/ppermute | solution.py:1911
  708.4 7.2 copy-start.31
  709.8 8.2 %slice-start.2 = ((s8[5242880]{0:T(1024)(128)(4,1)}), s8[4194304]{0:T(1024)(128)(4,1)S(1)}, s32[]{:S(2)}) async-start(s8[5242880]{0:T(1024)(128)(4,1)} %bitcast.142), calls=%async_computation.6 | async-start | bytes 8388608
  721.1 8.6 %slice-start.6 = ((s8[5242880]{0:T(1024)(128)(4,1)}), s8[4194304]{0:T(1024)(128)(4,1)S(1)}, s32[]{:S(2)}) async-start(s8[5242880]{0:T(1024)(128)(4,1)} %bitcast.148), calls=%async_computation.10 | async-start | bytes 8388608
  722.1 7.6 %slice-start.7 = ((s8[5242880]{0:T(1024)(128)(4,1)}), s8[1048576]{0:T(1024)(128)(4,1)S(1)}, s32[]{:S(2)}) async-start(s8[5242880]{0:T(1024)(128)(4,1)} %bitcast.148), calls=%async_computation.11 | async-start | bytes 2097152
  (32 other events, 92.3 us)
Sparse Core Ops, SparseCore 0:
  314.6 89.0 reduce-scatter.2
  421.9 99.5 reduce-scatter.4
